TPU v7x, 128 devices: a whole 4x4x4 slice. The times are simulated.
128 devices in a mesh: ctx: 16 (over y_hi, z, core), tp: 8 (over x, y_lo).
Axes of the slice: x: 4, y: 4 (y_hi: 2, y_lo: 2; y = y_hi * 2 + y_lo), z: 4, core: 2. Of those that a mesh axis runs over, the one named last changes fastest.
Arguments:
- tokens: bfloat16 [8192, 8192], P('ctx', 'tp'), may hold values from -6 to 6
- old_map: int32 [16, 16], replicated, may hold values from 0 to 255, as said below
- new_map: int32 [16, 16], replicated, may hold values from 0 to 255, as said below
- w_query: bfloat16 [8192, 4096], P(None, 'tp'), may hold values from -16 to 16
- key_projection_weight: bfloat16 [8192, 1024], P(None, 'tp'), may hold values from -16 to 16
- value_projection_weight: bfloat16 [8192, 1024], P(None, 'tp'), may hold values from -0.0625 to 0.0625
Outputs:
- attended: bfloat16 [8192, 4096], P('ctx', 'tp')
Inputs may be any that keep to these rules, and one draw needn't show every extreme that they name: A permutation of the fine blocks: row a lists the fine blocks of device a in the order of its rows; for every pair of devices a and b exactly one fine block of device a in old_map lies in row b of new_map. `new_map`: row b holds the 8 fine blocks of one coarse block c < 16 in increasing order (fine blocks c*16/2 onwards), then those of coarse block 31-c; each coarse block of the 32 stands in one row.
All inputs are finite; a program needn't handle non-finite values.
Results may differ from a plain program's by a relative error of at most 0.008.
The roundings to bfloat16 on the way count: a program that leaves them out, or rounds other values in their place, can miss the bound.
Values may be sent and summed in bfloat16 or wider, within the bound.
No kernel may reach another device: no remote copies, remote signals or barrier semaphores. Data moves between devices by JAX's collectives and lax.ppermute only.
A program may use at most 128 MiB of HBM per device.

v0:
```python
import math

import jax
import jax.numpy as jnp
from jax import lax
from jax.sharding import PartitionSpec as P

HEAD_SIZE = 128


THETA = 500000.0


def layout_positions(table, fine):
    offsets = jnp.arange(fine, dtype=jnp.int32)
    return (table[:, :, None] * fine + offsets[None, None, :]).reshape(-1)


def apply_rotation(vectors, positions):
    head_dim = vectors.shape[-1]
    half = head_dim // 2
    freqs = jnp.exp(jnp.arange(half, dtype=jnp.float32) * (-2.0 * math.log(THETA) / head_dim))
    angles = positions.astype(jnp.float32)[:, None] * freqs[None, :]
    cosine = jnp.cos(angles)[:, None, :]
    sine = jnp.sin(angles)[:, None, :]
    first = vectors[..., :half]
    second = vectors[..., half:]
    return jnp.concatenate(
        [first * cosine - second * sine, second * cosine + first * sine], axis=-1
    )


def routing(old_map, new_map, own_index, count):
    devices = jnp.arange(count, dtype=jnp.int32)
    old_mine = lax.dynamic_index_in_dim(old_map, own_index, 0, keepdims=False)
    new_mine = lax.dynamic_index_in_dim(new_map, own_index, 0, keepdims=False)
    outward = jnp.any(new_map[:, :, None] == old_mine[None, None, :], axis=1)
    send_order = jnp.sum(outward.astype(jnp.int32) * devices[None, :], axis=1)
    inward = jnp.any(old_map[:, :, None] == new_mine[None, None, :], axis=1)
    from_device = jnp.sum(inward.astype(jnp.int32) * devices[:, None], axis=0)
    return (send_order, from_device)


def outgoing(rows, send_order, count):
    blocks = rows.reshape(count, rows.shape[0] // count, rows.shape[1])
    return jnp.take(blocks, send_order, axis=0)


def incoming(received, from_device):
    placed = jnp.take(received, from_device, axis=0)
    return placed.reshape(-1, received.shape[-1])


def finish(query_matrix, key, value_matrix, positions):
    rows = query_matrix.shape[0]
    query_rot = (
        apply_rotation(query_matrix.reshape(rows, -1, HEAD_SIZE), positions)
        .reshape(rows, -1)
        .astype(jnp.bfloat16)
    )
    key_rot = (
        apply_rotation(key.reshape(rows, -1, HEAD_SIZE), positions)
        .reshape(rows, -1)
        .astype(jnp.bfloat16)
    )
    return (query_rot, key_rot, value_matrix.astype(jnp.bfloat16))


def fresh_state(heads_kv, query_group, rows):
    return (
        jnp.full((heads_kv, query_group, rows), -1e30, jnp.float32),
        jnp.zeros((heads_kv, query_group, rows), jnp.float32),
        jnp.zeros((heads_kv, query_group, rows, HEAD_SIZE), jnp.float32),
    )


def absorb_one(state, queries, query_pos, keys, values, key_pos):
    top, total, accum = state
    heads_kv = queries.shape[1]
    keys = keys.reshape(keys.shape[0], heads_kv, HEAD_SIZE)
    values = values.reshape(values.shape[0], heads_kv, HEAD_SIZE)
    scores = jnp.einsum(
        "rkgd,skd->kgrs", queries, keys, preferred_element_type=jnp.float32
    ) * HEAD_SIZE ** (-0.5)
    visible = key_pos[None, None, None, :] <= query_pos[None, None, :, None]
    new_top = jnp.maximum(top, jnp.max(jnp.where(visible, scores, -1e30), axis=-1))
    weights = jnp.where(visible, jnp.exp(scores - new_top[..., None]), 0.0)
    factor = jnp.exp(top - new_top)
    total = total * factor + jnp.sum(weights, axis=-1)
    accum = accum * factor[..., None] + jnp.einsum(
        "kgrs,skd->kgrd", weights.astype(jnp.bfloat16), values, preferred_element_type=jnp.float32
    )
    return (new_top, total, accum)


def blockwise(state, queries, query_pos, keys, values, key_pos, block):
    width = keys.shape[0]
    parts = width // block

    def advance(carry, items):
        return (absorb_one(carry, queries, query_pos, items[0], items[1], items[2]), None)

    state, unused = lax.scan(
        advance,
        state,
        (
            keys.reshape(parts, block, keys.shape[1]),
            values.reshape(parts, block, values.shape[1]),
            key_pos.reshape(parts, block),
        ),
    )
    return state


def normalize(state):
    top, total, accum = state
    result = accum / total[..., None]
    rows = result.shape[2]
    return jnp.transpose(result, (2, 0, 1, 3)).reshape(rows, -1).astype(jnp.bfloat16)


def local(tokens, old_map, new_map, w_query, key_projection_weight, value_projection_weight):
    count = lax.axis_size("ctx")
    own_index = lax.axis_index("ctx")
    rows = tokens.shape[0]
    fine = rows // count
    new_all = layout_positions(new_map, fine)
    new_rows = lax.dynamic_slice_in_dim(new_all, own_index * rows, rows, 0)
    send_order, from_device = routing(old_map, new_map, own_index, count)
    features = lax.all_gather(tokens, "tp", axis=1, tiled=True)
    moved = lax.all_to_all(
        outgoing(features, send_order, count), "ctx", split_axis=0, concat_axis=0, tiled=True
    )
    placed = incoming(moved, from_device)
    query_matrix = jnp.dot(placed, w_query, preferred_element_type=jnp.float32)
    key = jnp.dot(placed, key_projection_weight, preferred_element_type=jnp.float32)
    value_matrix = jnp.dot(placed, value_projection_weight, preferred_element_type=jnp.float32)
    query_rot, key_rot, value_low = finish(query_matrix, key, value_matrix, new_rows)
    heads_kv = key_rot.shape[1] // HEAD_SIZE
    query_group = query_rot.shape[1] // key_rot.shape[1]
    queries = query_rot.reshape(rows, heads_kv, query_group, HEAD_SIZE)
    state = blockwise(
        fresh_state(heads_kv, query_group, rows),
        queries,
        new_rows,
        lax.all_gather(key_rot, "ctx", axis=0, tiled=True),
        lax.all_gather(value_low, "ctx", axis=0, tiled=True),
        new_all,
        rows,
    )
    return normalize(state)


def solution(mesh):
    return jax.shard_map(
        local,
        mesh=mesh,
        in_specs=(P("ctx", "tp"), P(), P(), P(None, "tp"), P(None, "tp"), P(None, "tp")),
        out_specs=P("ctx", "tp"),
        check_vma=False,
    )
```

profile of v0, /device:TPU:1, one launch (start us, length us, event | category | flops | bytes accessed | tf_op | source)
XLA Modules:
  0.0 622.5 jit_solution(12318619433109487482)
XLA Ops:
  8.9 171.6 %all-gather.5.cloned.1.call-done = bf16[512,8192]{1,0:T(8,128)(2,1)} async-done(((bf16[512,1024]{1,0:T(8,128)(2,1)}), bf16[512,8192]{1,0:T(8,128)(2,1)}) %all-gather.5.cloned.1.call-update) | async-done | bytes 8388624 | tf_op jit(solution)/shard_map/all_gather | solution.py:130
  180.6 8.1 %gather_fusion = bf16[16,32,8192]{2,1,0:T(8,128)(2,1)} fusion(bf16[16,32,8192]{2,1,0:T(8,128)(2,1)} %bitcast.117, s32[1024]{0:T(1024)S(1)} %pad_clamp_fusion.1), kind=kCustom, calls=%fused_computation.clone | custom fusion | bytes 16777280 | tf_op jit(solution)/shard_map/jit(_take)/gather | solution.py:46
  188.7 7.5 %broadcast_select_fusion.1 = bf16[16,32,8192]{2,1,0:T(8,128)(2,1)} fusion(bf16[16,32,8192]{2,1,0:T(8,128)(2,1)} %gather_fusion, pred[16]{0:T(512)(128)(4,1)S(1)} %compare_and_fusion.1), kind=kLoop, calls=%fused_computation.33 | loop fusion | flops 4194304 | bytes 16777232 | tf_op jit(solution)/shard_map/jit(_take)/select_n | solution.py:46
  196.2 7.4 %all-to-all-start = ((bf16[16,32,8192]{2,1,0:T(8,128)(2,1)}), bf16[16,32,8192]{2,1,0:T(8,128)(2,1)}, u32[]{:S(2)}, u32[]{:S(2)}) async-start(bf16[16,32,8192]{2,1,0:T(8,128)(2,1)} %broadcast_select_fusion.1), calls=%async_computation | async-start | bytes 16777216 | tf_op jit(solution)/shard_map/all_to_all | solution.py:131
  204.2 118.9 %all-to-all-done = bf16[16,32,8192]{2,1,0:T(8,128)(2,1)} async-done(((bf16[16,32,8192]{2,1,0:T(8,128)(2,1)}), bf16[16,32,8192]{2,1,0:T(8,128)(2,1)}, u32[]{:S(2)}, u32[]{:S(2)}) %all-to-all-start) | async-done | bytes 8388640 | tf_op jit(solution)/shard_map/all_to_all | solution.py:131
  323.0 8.1 %gather_fusion.1 = bf16[16,32,8192]{2,1,0:T(8,128)(2,1)} fusion(bf16[16,32,8192]{2,1,0:T(8,128)(2,1)} %all-to-all-done, s32[1024]{0:T(1024)S(1)} %pad_clamp_fusion), kind=kCustom, calls=%fused_computation.1.clone | custom fusion | bytes 16777280 | tf_op jit(solution)/shard_map/jit(_take)/gather | solution.py:50
  331.2 7.5 %broadcast_select_fusion = bf16[16,32,8192]{2,1,0:T(8,128)(2,1)} fusion(bf16[16,32,8192]{2,1,0:T(8,128)(2,1)} %gather_fusion.1, pred[16]{0:T(512)(128)(4,1)S(1)} %compare_and_fusion), kind=kLoop, calls=%fused_computation.32 | loop fusion | flops 4194304 | bytes 16777232 | tf_op jit(solution)/shard_map/jit(_take)/select_n | solution.py:50
  338.7 6.3 %convolution_bitcast_fusion = f32[512,1,128]{0,2,1:T(8,128)S(1)} fusion(bf16[512,8192]{1,0:T(8,128)(2,1)} %bitcast.114, bf16[8192,128]{1,0:T(8,128)(2,1)S(1)} %copy-done), kind=kOutput, calls=%fused_computation.34 | convolution fusion | flops 1073741824 | bytes 10747904 | tf_op jit(solution)/shard_map/dot_general | solution.py:136
  346.4 7.0 %convolution_convert_fusion = bf16[512,128]{1,0:T(8,128)(2,1)} fusion(bf16[512,8192]{1,0:T(8,128)(2,1)} %bitcast.115, bf16[8192,128]{1,0:T(8,128)(2,1)} %param.15), kind=kOutput, calls=%fused_computation.35 | convolution fusion | flops 1073807360 | bytes 10616832 | tf_op jit(solution)/shard_map/dot_general | solution.py:137
  353.4 11.7 %copy.19 = bf16[512,8192]{1,0:T(8,128)(2,1)} copy(bf16[512,8192]{0,1:T(8,128)(2,1)} %bitcast.118) | data formatting | bytes 16777216 | tf_op jit(solution)/shard_map/dot_general | solution.py:135
  366.0 9.6 %fusion.38 = f32[512,4,128]{0,2,1:T(8,128)S(1)} fusion(bf16[512,8192,1]{1,0,2:T(8,128)(2,1)} %bitcast.116, bf16[4,128,8192]{2,1,0:T(8,128)(2,1)} %bitcast.119), kind=kOutput, calls=%fused_computation.74 | convolution fusion | flops 4294967296 | bytes 17825792 | tf_op jit(solution)/shard_map/dot_general | solution.py:135
  376.1 30.8 %all-gather.9.cloned.1.call-done = bf16[8192,1,128]{0,2,1:T(8,128)(2,1)} async-done(((bf16[512,1,128]{0,2,1:T(8,128)(2,1)}), bf16[8192,1,128]{0,2,1:T(8,128)(2,1)}) %all-gather.9.cloned.1.call-update) | async-done | bytes 2097168 | tf_op jit(solution)/shard_map/all_gather | solution.py:146
  406.9 4.1 copy.18
  411.0 44.1 %all-gather.7.cloned.1.call-done = bf16[8192,128]{1,0:T(8,128)(2,1)} async-done(((bf16[512,128]{1,0:T(8,128)(2,1)}), bf16[8192,128]{1,0:T(8,128)(2,1)}) %all-gather.7.cloned.1.call-update) | async-done | bytes 2097168 | tf_op jit(solution)/shard_map/all_gather | solution.py:147
  455.1 157.8 %while.15 = (s32[]{:T(128)}, f32[1,4,512]{2,1,0:T(4,128)S(1)}, f32[1,4,512]{2,1,0:T(4,128)S(1)}, f32[1,4,512,128]{3,2,1,0:T(8,128)}, s32[16,512]{1,0:T(8,128)S(1...) while((s32[]{:T(128)}, f32[1,4,512]{2,1,0:T(4,128)S(1)}, ...), condition=%wide.region_7.9_spmd.clone, body=%wide.region_4.8_spmd.clone.sunk | while | flops 549466112 | bytes 33432728 | solution.py:103
  455.3 3.7 fusion.53
  459.0 4.6 fusion.56
  463.7 0.9 fusion.55
  464.9 3.7 fusion.53
  468.6 5.0 fusion.56
  473.6 0.9 fusion.55
  474.8 3.7 fusion.53
  478.5 5.0 fusion.56
  483.4 0.9 fusion.55
  484.6 3.7 fusion.53
  488.4 5.0 fusion.56
  493.3 0.9 fusion.55
  494.5 3.7 fusion.53
  498.3 5.0 fusion.56
  503.2 0.9 fusion.55
  504.4 3.7 fusion.53
  508.1 5.0 fusion.56
  513.1 0.9 fusion.55
  514.3 3.7 fusion.53
  518.0 5.0 fusion.56
  523.0 0.9 fusion.55
  524.2 3.7 fusion.53
  527.9 5.0 fusion.56
  532.9 0.9 fusion.55
  534.1 3.7 fusion.53
  537.8 5.0 fusion.56
  542.8 0.9 fusion.55
  544.0 3.7 fusion.53
  547.7 5.0 fusion.56
  552.6 0.9 fusion.55
  553.8 3.7 fusion.53
  557.6 5.0 fusion.56
  562.5 0.9 fusion.55
  563.7 3.7 fusion.53
  567.5 5.0 fusion.56
  572.4 0.9 fusion.55
  573.6 3.7 fusion.53
  577.3 5.0 fusion.56
  582.3 0.9 fusion.55
  583.5 3.7 fusion.53
  587.2 5.0 fusion.56
  592.2 0.9 fusion.55
  593.4 3.7 fusion.53
  597.1 5.0 fusion.56
  602.1 0.9 fusion.55
  603.3 3.7 fusion.53
  607.0 5.0 fusion.56
  612.0 0.9 fusion.55
  612.9 1.7 fusion.26
  (158 shorter events, 11.1 us)
Async XLA Ops:
  6.5 332.1 %copy-start = (bf16[8192,128]{1,0:T(8,128)(2,1)S(1)}, bf16[8192,128]{1,0:T(8,128)(2,1)}, u32[]{:S(2)}) copy-start(bf16[8192,128]{1,0:T(8,128)(2,1)} %param.14) | copy-start | bytes 6291460
  6.5 174.0 %all-gather.5.cloned.1.call-start = ((), (), s32[]{:S(2)}) async-start(), calls=%async_computation.1 | async-start | bytes 9437184 | tf_op jit(solution)/shard_map/all_gather | solution.py:130
  196.2 7.5 %copy-start.3 = (s32[16,16]{1,0:T(8,128)S(1)}, s32[16,16]{1,0:T(8,128)}, u32[]{:S(2)}) copy-start(s32[16,16]{1,0:T(8,128)} %param.12) | copy-start | bytes 3076
  196.2 7.7 %copy-start.4 = (s32[16,16]{1,0:T(8,128)S(1)}, s32[16,16]{1,0:T(8,128)}, u32[]{:S(2)}) copy-start(s32[16,16]{1,0:T(8,128)} %param.11) | copy-start | bytes 3076
  196.2 126.8 %all-to-all-start = ((bf16[16,32,8192]{2,1,0:T(8,128)(2,1)}), bf16[16,32,8192]{2,1,0:T(8,128)(2,1)}, u32[]{:S(2)}, u32[]{:S(2)}) async-start(bf16[16,32,8192]{2,1,0:T(8,128)(2,1)} %broadcast_select_fusion.1), calls=%async_computation | async-start | bytes 16777216 | tf_op jit(solution)/shard_map/all_to_all | solution.py:131
  203.6 203.3 %all-gather.9.cloned.1.call-start = ((), (), s32[]{:S(2)}) async-start(), calls=%async_computation.3 | async-start | bytes 2228224 | tf_op jit(solution)/shard_map/all_gather | solution.py:146
  346.2 108.9 %all-gather.7.cloned.1.call-start = ((), (), s32[]{:S(2)}) async-start(), calls=%async_computation.2 | async-start | bytes 2228224 | tf_op jit(solution)/shard_map/all_gather | solution.py:147
  459.0 4.6 copy-start.2
  468.6 5.0 copy-start.2
  478.5 5.0 copy-start.2
  488.4 5.0 copy-start.2
  498.2 5.0 copy-start.2
  508.1 5.0 copy-start.2
  518.0 5.0 copy-start.2
  527.9 5.0 copy-start.2
  537.8 5.0 copy-start.2
  547.7 5.0 copy-start.2
  557.6 5.0 copy-start.2
  567.4 5.0 copy-start.2
  577.3 5.0 copy-start.2
  587.2 5.0 copy-start.2
  597.1 5.0 copy-start.2
  607.0 5.0 copy-start.2
  612.9 3.0 copy-start.1
Sparse Core Ops, SparseCore 0:
  9.0 171.5 all-gather.4
  346.3 60.5 all-gather.8
  409.4 45.6 all-gather.6
where the time goes:
time: 624 us; the launch traced here: 622 us
  waiting for transfers between devices  366 us (59%)
  matrix products  161 us (26%)
  other arithmetic  38.4 us (6%)
  local copies, waits for them, and re-layouts  35 us (6%)
  between operations  13.3 us (2%)
  starting transfers between devices  7.66 us (1%)
    all_gather x1, waiting for transfers between devices, local(): features = lax.all_gather(tokens, 'tp', axis=1, tiled=True)  172 us
    all_to_all x1, waiting for transfers between devices, local(): lax.all_to_all(outgoing(features, send_order, count), 'ctx', split_axis=0...  119 us
    dot_general x16, matrix products, absorb_one(): jnp.einsum('kgrs,skd->kgrd', weights.astype(jnp.bfloat16), values, prefer...  79 us
    dot_general x16, matrix products, absorb_one(): jnp.einsum('rkgd,skd->kgrs', queries, keys, preferred_element_type=jnp.fl...  59.4 us
    all_gather x1, waiting for transfers between devices, local(): lax.all_gather(value_low, 'ctx', axis=0, tiled=True)  44.1 us
    all_gather x1, waiting for transfers between devices, local(): lax.all_gather(key_rot, 'ctx', axis=0, tiled=True)  30.8 us
    reduce_sum x16, other arithmetic, absorb_one(): total = total * factor + jnp.sum(weights, axis=-1)  14.6 us
  transfers between devices with their start and end apart: 4, of which 4 were waited for; matrix products, arithmetic and copies ran while one was open for 6% of the time, Pallas kernels for 0%

commit v1 on v0

v1 whole, which is shorter than its diff:
```python
import functools
import math

import jax
import jax.numpy as jnp
from jax import lax
from jax.experimental import pallas as pl
from jax.experimental.pallas import tpu as pltpu
from jax.sharding import PartitionSpec as P

HEAD = 128
THETA = 500000.0
SCALE = HEAD ** -0.5
FINE = 32
CHUNKS = 2
W = FINE // CHUNKS
ROWS = 16 * W
PAYLOAD = 20 * W
KB = 512
VMEM = pl.BlockSpec(memory_space=pltpu.VMEM)
SMEM = pl.BlockSpec(memory_space=pltpu.SMEM)

CHIPS = [(dh, dz) for dh in range(2) for dz in range(4)]


def shift_x(block, step):
    perm = [(i * 2 + j, ((i + step) % 4) * 2 + j) for i in range(4) for j in range(2)]
    return lax.ppermute(block, "tp", perm)


def swap_y(block):
    return lax.ppermute(block, "tp", [(i, i ^ 1) for i in range(8)])


def shift_ctx(block, dh, dz):
    perm = [
        (h * 8 + z * 2 + c, (h ^ dh) * 8 + ((z + dz) % 4) * 2 + c)
        for h in range(2)
        for z in range(4)
        for c in range(2)
    ]
    return lax.ppermute(block, "ctx", perm)


def swap_core(block):
    return lax.ppermute(block, "ctx", [(i, i ^ 1) for i in range(16)])


def dot(a, b):
    return lax.dot_general(a, b, (((1,), (0,)), ((), ())), preferred_element_type=jnp.float32)


def dot_t(a, b):
    return lax.dot_general(a, b, (((1,), (1,)), ((), ())), preferred_element_type=jnp.float32)


def project_kernel(groups, has_acc, last, *refs):
    features, refs = refs[0], refs[1:]
    blocks, at = [], 0
    for n in groups:
        blocks.append(refs[at : at + n])
        at += n
    wq, wk, wv = refs[at : at + 3]
    at += 3
    acc_in = None
    if has_acc:
        acc_in = refs[at]
        at += 1
    if last:
        info, cosine, sine = refs[at : at + 3]
        at += 3
        outs = refs[at : at + 8]
        acc, heads = refs[at + 8 : at + 10]
    else:
        out, acc = refs[at : at + 2]
    step = pl.program_id(0)

    for i, parts in enumerate(blocks):

        @pl.when(step == i)
        def add(i=i, parts=parts):
            block = parts[0][...] if len(parts) == 1 else jnp.concatenate([p[...] for p in parts], axis=0)
            for lo, hi, w in ((0, 512, wq), (512, 640, wk), (640, 768, wv)):
                value = dot(block, w[...])
                if i > 0:
                    value = value + acc[:, lo:hi]
                elif has_acc:
                    value = value + acc_in[:, lo:hi]
                acc[:, lo:hi] = value

    @pl.when(step == len(blocks) - 1)
    def finish():
        if not last:
            out[...] = acc[...]
            return
        cos, sin = cosine[...], sine[...]

        def rotated(lo):
            vector = acc[:, lo : lo + HEAD]
            return (vector * cos + pltpu.roll(vector, HEAD // 2, 1) * sin).astype(jnp.bfloat16)

        for h in range(4):
            heads[:, h * HEAD : (h + 1) * HEAD] = rotated(h * HEAD)
        key = rotated(512)
        value = acc[:, 640:768].astype(jnp.bfloat16)
        me = info[0]
        high, z = me // 8, lax.rem(me // 2, 4)
        for r, (dh, dz) in enumerate(CHIPS):
            outs[r][0:ROWS, 0:HEAD] = key
            outs[r][0:ROWS, HEAD : 2 * HEAD] = value
            chip = lax.rem(high + dh, 2) * 8 + lax.rem(z + dz, 4) * 2
            for core in range(2):
                k = info[1 + chip + core]
                rows = pl.ds(pl.multiple_of(k * W, W), W)
                for half in range(2):
                    at = ROWS + (core * 2 + half) * W
                    outs[r][at : at + W, :] = heads[rows, half * 256 : half * 256 + 256]


def project(features, blocks, weights, acc=None, tables=None):
    groups = [len(b) for b in blocks]
    flat = [p for b in blocks for p in b]
    whole = lambda shape: pl.BlockSpec(shape, lambda i, f: (0,) * len(shape))
    last = tables is not None
    specs = [whole(p.shape) for p in flat]
    specs += [pl.BlockSpec((1024, w.shape[1]), lambda i, f: (f[i], 0)) for w in weights]
    operands = flat + list(weights)
    if acc is not None:
        specs.append(whole(acc.shape))
        operands.append(acc)
    scratch = [pltpu.VMEM((ROWS, 768), jnp.float32)]
    if last:
        specs += [SMEM, whole((ROWS, HEAD)), whole((ROWS, HEAD))]
        operands += list(tables)
        out_shape = [jax.ShapeDtypeStruct((PAYLOAD, 256), jnp.bfloat16)] * 8
        out_specs = [whole((PAYLOAD, 256))] * 8
        scratch.append(pltpu.VMEM((ROWS, 512), jnp.bfloat16))
    else:
        out_shape = jax.ShapeDtypeStruct((ROWS, 768), jnp.float32)
        out_specs = whole((ROWS, 768))
    return pl.pallas_call(
        functools.partial(project_kernel, groups, acc is not None, last),
        grid_spec=pltpu.PrefetchScalarGridSpec(
            num_scalar_prefetch=1,
            grid=(len(blocks),),
            in_specs=specs,
            out_specs=out_specs,
            scratch_shapes=scratch,
        ),
        out_shape=out_shape,
        compiler_params=pltpu.CompilerParams(vmem_limit_bytes=48 * 2**20),
        name="project",
    )(features, *operands)


def attend_kernel(info, old_map, *refs):
    own = refs[: 8 * CHUNKS]
    other = refs[8 * CHUNKS : 9 * CHUNKS]
    out, query, keys, values, top, total, accum = refs[9 * CHUNKS :]
    me = info[0]
    high, z, core = me // 8, lax.rem(me // 2, 4), lax.rem(me, 2)
    for r, (dh, dz) in enumerate(CHIPS):
        for swapped in range(2):
            source = lax.rem(high + dh, 2) * 8 + lax.rem(z + 4 - dz, 4) * 2 + lax.rem(core + swapped, 2)
            slot = info[3 + source]
            for j in range(CHUNKS):
                ref = other[j].at[r] if swapped else own[j * 8 + r]
                for k in range(16):
                    at = pl.ds(pl.multiple_of(old_map[source * 16 + k] * FINE + j * W, W), W)
                    keys[at, :] = ref[k * W : (k + 1) * W, 0:HEAD]
                    values[at, :] = ref[k * W : (k + 1) * W, HEAD : 2 * HEAD]
                for h in range(4):
                    at = pl.ds(pl.multiple_of(ROWS + (core * 2 + h // 2) * W, W), W)
                    to = (slot // 8) * 1024 + h * 256 + lax.rem(slot, 8) * FINE + j * W
                    query[pl.ds(pl.multiple_of(to, W), W), :] = ref[at, (h % 2) * HEAD : (h % 2 + 1) * HEAD]

    for u in range(2):
        coarse = info[1 + u]
        queries = query[u * 1024 : (u + 1) * 1024, :]
        top[...] = jnp.full(top.shape, -1e30, jnp.float32)
        total[...] = jnp.zeros_like(total)
        accum[...] = jnp.zeros_like(accum)
        whole = (coarse * 256) // KB

        def absorb(block, masked, coarse=coarse, queries=queries):
            start = pl.multiple_of(block * KB, KB)
            scores = dot_t(queries, keys[pl.ds(start, KB), :])
            if masked:
                row = lax.rem(lax.broadcasted_iota(jnp.int32, (1024, KB), 0), 256) + coarse * 256
                visible = lax.broadcasted_iota(jnp.int32, (1024, KB), 1) + start <= row
                scores = jnp.where(visible, scores, -1e30)
            old = top[...]
            new = jnp.maximum(old, jnp.max(scores, axis=-1, keepdims=True))
            factor = jnp.exp((old - new) * SCALE)
            weights = jnp.exp((scores - new[:, :1]) * SCALE)
            if masked:
                weights = jnp.where(visible, weights, 0.0)
            sums = total[...] * factor
            for i in range(KB // HEAD):
                sums = sums + weights[:, i * HEAD : (i + 1) * HEAD]
            total[...] = sums
            accum[...] = accum[...] * factor + dot(
                weights.astype(jnp.bfloat16), values[pl.ds(start, KB), :]
            )
            top[...] = new

        def body(block, carry, absorb=absorb):
            absorb(block, False)
            return carry

        lax.fori_loop(0, whole, body, 0)
        absorb(whole, True)
        result = accum[...] / jnp.sum(total[...], axis=-1, keepdims=True)
        for h in range(4):
            out[u * 256 : (u + 1) * 256, h * HEAD : (h + 1) * HEAD] = result[h * 256 : (h + 1) * 256].astype(
                jnp.bfloat16
            )


def attend(info, old_map, own, other):
    return pl.pallas_call(
        attend_kernel,
        out_shape=jax.ShapeDtypeStruct((512, 512), jnp.bfloat16),
        in_specs=[SMEM, SMEM] + [VMEM] * (9 * CHUNKS),
        out_specs=VMEM,
        scratch_shapes=[
            pltpu.VMEM((2048, HEAD), jnp.bfloat16),
            pltpu.VMEM((8192, HEAD), jnp.bfloat16),
            pltpu.VMEM((8192, HEAD), jnp.bfloat16),
            pltpu.VMEM((1024, HEAD), jnp.float32),
            pltpu.VMEM((1024, HEAD), jnp.float32),
            pltpu.VMEM((1024, HEAD), jnp.float32),
        ],
        compiler_params=pltpu.CompilerParams(vmem_limit_bytes=56 * 2**20),
        name="attend",
    )(info, old_map, *own, *other)


def routing(old_map, new_map, own_index):
    devices = jnp.arange(16, dtype=jnp.int32)
    old_mine = lax.dynamic_index_in_dim(old_map, own_index, 0, keepdims=False)
    new_mine = lax.dynamic_index_in_dim(new_map, own_index, 0, keepdims=False)
    outward = jnp.any(new_map[:, :, None] == old_mine[None, None, :], axis=1)
    send_order = jnp.sum(outward.astype(jnp.int32) * devices[None, :], axis=1)
    inward = jnp.any(old_map[:, :, None] == new_mine[None, None, :], axis=1)
    slot_of = jnp.sum(inward.astype(jnp.int32) * devices[None, :], axis=1)
    coarse = jnp.stack([new_mine[0] // 8, new_mine[8] // 8])
    return (
        jnp.concatenate([own_index[None], send_order]).astype(jnp.int32),
        jnp.concatenate([own_index[None], coarse, slot_of]).astype(jnp.int32),
        old_mine,
    )


def angle_tables(positions):
    half = HEAD // 2
    freqs = jnp.exp(jnp.arange(half, dtype=jnp.float32) * (-2.0 * math.log(THETA) / HEAD))
    angles = positions.astype(jnp.float32)[:, None] * freqs[None, :]
    cosine = jnp.cos(angles)
    sine = jnp.sin(angles)
    return jnp.concatenate([cosine, cosine], axis=1), jnp.concatenate([-sine, sine], axis=1)


def local(tokens, old_map, new_map, w_query, key_projection_weight, value_projection_weight):
    me = lax.axis_index("ctx").astype(jnp.int32)
    place = lax.axis_index("tp").astype(jnp.int32)
    weights = (w_query, key_projection_weight, value_projection_weight)
    send_info, attend_info, old_mine = routing(old_map, new_map, me)
    x, y = place // 2, place % 2
    feature = lambda dx, dy: ((x + dx) % 4) * 2 + (y + dy) % 2
    order = [(0, 0), (3, 0), (1, 0), (0, 1), (3, 1), (2, 0), (1, 1), (2, 1)]
    features = jnp.stack([feature(dx, dy) for dx, dy in order]).astype(jnp.int32)
    chunks = tokens.reshape(16, CHUNKS, W, 1024)
    third = (ROWS // 3) // 16 * 16

    own_side, other_side = [], []
    for j in range(CHUNKS):
        mine = chunks[:, j].reshape(ROWS, 1024)
        left = shift_x(mine, 1)
        right = shift_x(mine, -1)
        across = swap_y(mine)
        left_across = shift_x(across, 1)
        far = shift_x(right, -1)
        right_across = swap_y(right)
        far_across = (
            swap_y(far[:third]),
            shift_x(left_across[third : 2 * third], 1),
            shift_x(right_across[2 * third :], -1),
        )
        positions = old_mine[:, None] * FINE + j * W + jnp.arange(W, dtype=jnp.int32)[None, :]
        cosine, sine = angle_tables(positions.reshape(-1))
        acc = project(features[:4], [(mine,), (left,), (right,), (across,)], weights)
        acc = project(features[4:7], [(left_across,), (far,), (right_across,)], weights, acc)
        sent = project(features[7:], [far_across], weights, acc, (send_info, cosine, sine))
        received = [sent[0]] + [shift_ctx(sent[r], *CHIPS[r]) for r in range(1, 8)]
        own_side += received
        other_side.append(swap_core(jnp.stack(received)))
    return attend(attend_info, old_map.reshape(-1), own_side, other_side)


def solution(mesh):
    return jax.shard_map(
        local,
        mesh=mesh,
        in_specs=(P("ctx", "tp"), P(), P(), P(None, "tp"), P(None, "tp"), P(None, "tp")),
        out_specs=P("ctx", "tp"),
        check_vma=False,
    )
```

time: 624 us -> 179 us (0.29)
  waiting for transfers between devices: 366 us -> 25.3 us
  matrix products: 161 us -> 0 us
  starting transfers between devices: 7.66 us -> 64.3 us
  Pallas kernels: 0 us -> 53.3 us
  other arithmetic: 38.4 us -> 5.11 us
  local copies, waits for them, and re-layouts: 35 us -> 25.1 us
  between operations: 13.3 us -> 5.23 us
    all_gather x3 -> x0, waiting for transfers between devices: 247 us -> none  [the longest x1 172 us: local(): features = lax.all_gather(tokens, 'tp', axis=1, tiled=True)]
    dot_general x35 -> x0, matrix products: 161 us -> none  [the longest x16 79 us: absorb_one(): jnp.einsum('kgrs,skd->kgrd', weights.astype(jnp.bfloat16), values, prefer...]
    all_to_all x1 -> x0, waiting for transfers between devices: 119 us -> none  [local(): lax.all_to_all(outgoing(features, send_order, count), 'ctx', split_axis=0...]
    ppermute x0 -> x34, starting transfers between devices: none -> 64.3 us  [the longest x14 26.2 us: shift_ctx(): return lax.ppermute(block, 'ctx', perm)]
    pallas_call x0 -> x7, Pallas kernels: none -> 53.3 us  [the longest x1 27.7 us: attend(): pl.pallas_call(attend_kernel, out_shape=jax.ShapeDtypeStruct((512, 512),...]
    ppermute x0 -> x34, waiting for transfers between devices: none -> 25.3 us  [the longest x12 24.3 us: shift_x(): return lax.ppermute(block, 'tp', perm)]
    gather x2 -> x0, local copies, waits for them, and re-layouts: 16.3 us -> none  [the longest x1 8.15 us: outgoing(): return jnp.take(blocks, send_order, axis=0)]
    select_n x4 -> x0, other arithmetic: 15 us -> none  [the longest x2 7.48 us: outgoing(): return jnp.take(blocks, send_order, axis=0)]
  transfers between devices with their start and end apart: 4 -> 34, of which waited for: 4 -> 5; matrix products, arithmetic and copies ran while one was open for 6% -> 14% of each run, Pallas kernels for 0% -> 14%
where the time goes in v1:
time: 179 us; the launch traced here: 178 us
  starting transfers between devices  64.3 us (36%)
  Pallas kernels  53.3 us (30%)
  waiting for transfers between devices  25.3 us (14%)
  local copies, waits for them, and re-layouts  25.1 us (14%)
  between operations  5.23 us (3%)
  other arithmetic  5.11 us (3%)
    pallas_call x1, Pallas kernels, attend(): pl.pallas_call(attend_kernel, out_shape=jax.ShapeDtypeStruct((512, 512),...  27.7 us
    ppermute x14, starting transfers between devices, shift_ctx(): return lax.ppermute(block, 'ctx', perm)  26.2 us
    pallas_call x6, Pallas kernels, project(): pl.pallas_call(functools.partial(project_kernel, groups, acc is not None,...  25.6 us
    ppermute x12, waiting for transfers between devices, shift_x(): return lax.ppermute(block, 'tp', perm)  24.3 us
    ppermute x12, starting transfers between devices, shift_x(): return lax.ppermute(block, 'tp', perm)  17.6 us
    ppermute x2, starting transfers between devices, swap_core(): return lax.ppermute(block, 'ctx', [(i, i ^ 1) for i in range(16)])  14.7 us
    unnamed x72, local copies, waits for them, and re-layouts  13.3 us
    ppermute x6, starting transfers between devices, swap_y(): return lax.ppermute(block, 'tp', [(i, i ^ 1) for i in range(8)])  5.78 us
  transfers between devices with their start and end apart: 34, of which 5 were waited for; matrix products, arithmetic and copies ran while one was open for 14% of the time, Pallas kernels for 14%

profile of v1, /device:TPU:1, one launch (start us, length us, event | category | flops | bytes accessed | tf_op | source)
XLA Modules:
  0.0 178.4 jit_solution(13805787529930377494)
XLA Ops:
  0.0 1.3 fusion.2
  1.3 3.4 %collective-permute-start.16 = (bf16[256,1024]{1,0:T(8,128)(2,1)S(1)}, bf16[256,1024]{1,0:T(8,128)(2,1)}, u32[]{:S(2)}, u32[]{:S(2)}) collective-permute-start(bf16[256,1024]{1,0:T(8,128)(2,1)S(1)} %bitcast.61), channel_id=1, source_target_pairs={{0,6},{1,7},{2,0},{3,1},{4,2},{5,3},{6,4},{7,5},{8,14},{9,15},{10,... | collective-permute-start | bytes 1572872 | tf_op jit(solution)/shard_map/ppermute | solution.py:28
  4.7 1.3 collective-permute-start.19
  6.8 8.5 %collective-permute-done.16.refs_3_ = bf16[256,1024]{1,0:T(8,128)(2,1)} collective-permute-done((bf16[256,1024]{1,0:T(8,128)(2,1)S(1)}, bf16[256,1024]{1,0:T(8,128)(2,1)}, u32[]{:S(2)}, u32[]{:S(2)}) %collective-permute-start.16) | collective-permute-done | bytes 524320 | tf_op jit(solution)/shard_map/ppermute | solution.py:28
  15.3 3.5 %collective-permute-start.17 = (bf16[256,1024]{1,0:T(8,128)(2,1)}, bf16[256,1024]{1,0:T(8,128)(2,1)S(1)}, u32[]{:S(2)}, u32[]{:S(2)}) collective-permute-start(bf16[256,1024]{1,0:T(8,128)(2,1)} %collective-permute-done.16.refs_3_), channel_id=1, source_target_pairs={{0,6},{1,7},{2,0},{3,1},{4,2},{5,3},{6,4},{7,5},{8,14},{9,15},{10,... | collective-permute-start | bytes 1572872 | tf_op jit(solution)/shard_map/ppermute | solution.py:28
  18.9 1.3 collective-permute-start.22
  20.7 5.8 %collective-permute-done.refs_3_ = bf16[256,1024]{1,0:T(8,128)(2,1)} collective-permute-done((bf16[256,1024]{1,0:T(8,128)(2,1)S(1)}, bf16[256,1024]{1,0:T(8,128)(2,1)}, u32[]{:S(2)}, u32[]{:S(2)}) %collective-permute-start) | collective-permute-done | bytes 524320 | tf_op jit(solution)/shard_map/ppermute | solution.py:28
  26.5 1.0 collective-permute-start.24
  27.6 0.9 collective-permute-done.3.refs_4_
  28.8 9.1 %collective-permute-done.17.refs_2_ = bf16[256,1024]{1,0:T(8,128)(2,1)S(1)} collective-permute-done((bf16[256,1024]{1,0:T(8,128)(2,1)}, bf16[256,1024]{1,0:T(8,128)(2,1)S(1)}, u32[]{:S(2)}, u32[]{:S(2)}) %collective-permute-start.17) | collective-permute-done | bytes 524320 | tf_op jit(solution)/shard_map/ppermute | solution.py:28
  37.9 1.3 collective-permute-start.6
  39.2 1.6 fusion.1
  40.8 3.4 %collective-permute-start.1 = (bf16[256,1024]{1,0:T(8,128)(2,1)}, bf16[256,1024]{1,0:T(8,128)(2,1)}, u32[]{:S(2)}, u32[]{:S(2)}) collective-permute-start(bf16[256,1024]{1,0:T(8,128)(2,1)} %collective-permute-done.refs_3_), channel_id=1, source_target_pairs={{0,6},{1,7},{2,0},{3,1},{4,2},{5,3},{6,4},{7,5},{8,14},{9,15},{10,... | collective-permute-start | bytes 1572872 | tf_op jit(solution)/shard_map/ppermute | solution.py:28
  44.3 0.8 pad_maximum_fusion.2
  45.1 1.6 slice.55
  46.7 1.6 slice.53
  48.3 1.6 slice.54
  49.9 0.8 copy-done.8
  50.7 2.7 %collective-permute-start.23 = (bf16[96,1024]{1,0:T(8,128)(2,1)}, bf16[96,1024]{1,0:T(8,128)(2,1)S(1)}, u32[]{:S(2)}, u32[]{:S(2)}) collective-permute-start(bf16[96,1024]{1,0:T(8,128)(2,1)} %slice.55), channel_id=1, source_target_pairs={{0,6},{1,7},{2,0},{3,1},{4,2},{5,3},{6,4},{7,5},{8,14},{9,15},{10,... | collective-permute-start | bytes 589832 | tf_op jit(solution)/shard_map/ppermute | solution.py:28
  53.3 0.9 collective-permute-done.8.refs_2_
  54.3 0.8 copy-done.10
  55.1 0.9 collective-permute-start.18
  56.0 1.2 pad_maximum_fusion
  57.3 1.0 copy-done.9
  58.3 5.8 %project.9.refs_7_ = f32[256,768]{1,0:T(8,128)S(1)} custom-call(s32[4]{0:T(128)S(1)} %pad_add_fusion.2.refs_0_, bf16[256,1024]{1,0:T(8,128)(2,1)S(1)} %bitcast.64, bf16[256,1024]{1,0:T(8,128)(2,1)S(1)} %copy-done.9, bf16[256,1024]{1,0:T(8,128)(2,1)} %collective-permute-done.16.refs_3_, bf16[256,1024]{1,0:T(8,128)(2,1)} %collective-permute-done.19.refs_4_, ...), custom_call_target="tpu_custom_call" | custom-call | tf_op jit(solution)/shard_map/project/pallas_call | solution.py:141
  64.1 5.6 %project.6.refs_7_ = f32[256,768]{1,0:T(8,128)S(1)} custom-call(s32[4]{0:T(128)S(1)} %pad_add_fusion.2.refs_0_, bf16[256,1024]{1,0:T(8,128)(2,1)S(1)} %bitcast.60, bf16[256,1024]{1,0:T(8,128)(2,1)S(1)} %copy-done.11, bf16[256,1024]{1,0:T(8,128)(2,1)} %collective-permute-done.refs_3_, bf16[256,1024]{1,0:T(8,128)(2,1)S(1)} %copy-done.7, ...), custom_call_target="tpu_custom_call" | custom-call | tf_op jit(solution)/shard_map/project/pallas_call | solution.py:141
  69.8 1.0 slice.51
  70.8 2.7 %collective-permute-start.7 = (bf16[96,1024]{1,0:T(8,128)(2,1)S(1)}, bf16[96,1024]{1,0:T(8,128)(2,1)S(1)}, u32[]{:S(2)}, u32[]{:S(2)}) collective-permute-start(bf16[96,1024]{1,0:T(8,128)(2,1)S(1)} %slice.51), channel_id=1, source_target_pairs={{0,6},{1,7},{2,0},{3,1},{4,2},{5,3},{6,4},{7,5},{8,14},{9,15},{10,... | collective-permute-start | bytes 589832 | tf_op jit(solution)/shard_map/ppermute | solution.py:28
  73.5 0.9 slice.49
  74.5 0.8 collective-permute-start.2
  75.3 0.9 slice.50
  76.2 4.9 %project.10.refs_7_ = f32[256,768]{1,0:T(8,128)S(1)} custom-call(s32[3]{0:T(128)S(1)} %pad_add_fusion.1.refs_0_, bf16[256,1024]{1,0:T(8,128)(2,1)} %collective-permute-done.20.refs_1_, bf16[256,1024]{1,0:T(8,128)(2,1)S(1)} %copy-done.2, bf16[256,1024]{1,0:T(8,128)(2,1)} %collective-permute-done.22.refs_3_, bf16[8192,512]{1,0:T(8,128)(2,1)} %refs_4_.7, ...), custom_call_target="tpu_custom_call" | custom-call | tf_op jit(solution)/shard_map/project/pallas_call | solution.py:141
  81.2 5.1 %project.7.refs_7_ = f32[256,768]{1,0:T(8,128)S(1)} custom-call(s32[3]{0:T(128)S(1)} %pad_add_fusion.1.refs_0_, bf16[256,1024]{1,0:T(8,128)(2,1)} %collective-permute-done.4.refs_1_, bf16[256,1024]{1,0:T(8,128)(2,1)} %collective-permute-done.1.refs_2_, bf16[256,1024]{1,0:T(8,128)(2,1)} %collective-permute-done.6.refs_3_, bf16[8192,512]{1,0:T(8,128)(2,1)} %refs_4_.7, ...), custom_call_target="tpu_custom_call" | custom-call | tf_op jit(solution)/shard_map/project/pallas_call | solution.py:141
  86.4 2.2 %project.11 = (bf16[320,256]{1,0:T(8,128)(2,1)S(1)}, bf16[320,256]{1,0:T(8,128)(2,1)S(1)}, bf16[320,256]{1,0:T(8,128)(2,1)S(1)}, bf16[320,256]{1,0:T(8,128)(2,1)...) custom-call(s32[1]{0:T(128)} %bitcast.6.refs_0_, ...), custom_call_target="tpu_custom_call" | custom-call | tf_op jit(solution)/shard_map/project/pallas_call | solution.py:141
  88.6 1.7 collective-permute-start.25
  90.3 3.3 %collective-permute-start.26 = (bf16[320,256]{1,0:T(8,128)(2,1)S(1)}, bf16[320,256]{1,0:T(8,128)(2,1)S(1)}, u32[]{:S(2)}, u32[]{:S(2)}) collective-permute-start(bf16[320,256]{1,0:T(8,128)(2,1)S(1)} %get-tuple-element.31), channel_id=1, source_target_pairs={{0,32},{8,40},{16,48},{24,56},{32,0},{40,8},{48,16},{56,24},{64,96... | collective-permute-start | bytes 491528 | tf_op jit(solution)/shard_map/ppermute | solution.py:42
  94.3 0.7 collective-permute-start.27
  95.0 2.6 %collective-permute-start.28 = (bf16[320,256]{1,0:T(8,128)(2,1)S(1)}, bf16[320,256]{1,0:T(8,128)(2,1)S(1)}, u32[]{:S(2)}, u32[]{:S(2)}) collective-permute-start(bf16[320,256]{1,0:T(8,128)(2,1)S(1)} %get-tuple-element.33), channel_id=1, source_target_pairs={{0,64},{8,72},{16,80},{24,88},{32,96},{40,104},{48,112},{56,120},{... | collective-permute-start | bytes 491528 | tf_op jit(solution)/shard_map/ppermute | solution.py:42
  97.6 0.8 collective-permute-start.29
  98.4 2.0 %project.8 = (bf16[320,256]{1,0:T(8,128)(2,1)S(1)}, bf16[320,256]{1,0:T(8,128)(2,1)S(1)}, bf16[320,256]{1,0:T(8,128)(2,1)S(1)}, bf16[320,256]{1,0:T(8,128)(2,1)S...) custom-call(s32[1]{0:T(128)} %bitcast.6.refs_0_, ...), custom_call_target="tpu_custom_call" | custom-call | tf_op jit(solution)/shard_map/project/pallas_call | solution.py:141
  100.5 0.7 bitcast_dynamic-update-slice_fusion.15
  101.2 3.2 %collective-permute-start.30 = (bf16[320,256]{1,0:T(8,128)(2,1)S(1)}, bf16[320,256]{1,0:T(8,128)(2,1)S(1)}, u32[]{:S(2)}, u32[]{:S(2)}) collective-permute-start(bf16[320,256]{1,0:T(8,128)(2,1)S(1)} %get-tuple-element.35), channel_id=1, source_target_pairs={{0,96},{8,104},{16,112},{24,120},{32,64},{40,72},{48,80},{56,88},{... | collective-permute-start | bytes 491528 | tf_op jit(solution)/shard_map/ppermute | solution.py:42
  104.5 0.7 bitcast_dynamic-update-slice_fusion.6
  105.1 1.5 collective-permute-start.31
  107.5 0.7 bitcast_dynamic-update-slice_fusion.4
  108.2 1.9 %collective-permute-start.10 = (bf16[320,256]{1,0:T(8,128)(2,1)S(1)}, bf16[320,256]{1,0:T(8,128)(2,1)S(1)}, u32[]{:S(2)}, u32[]{:S(2)}) collective-permute-start(bf16[320,256]{1,0:T(8,128)(2,1)S(1)} %get-tuple-element.23), channel_id=1, source_target_pairs={{0,32},{8,40},{16,48},{24,56},{32,0},{40,8},{48,16},{56,24},{64,96... | collective-permute-start | bytes 491528 | tf_op jit(solution)/shard_map/ppermute | solution.py:42
  110.8 1.9 %collective-permute-start.11 = (bf16[320,256]{1,0:T(8,128)(2,1)S(1)}, bf16[320,256]{1,0:T(8,128)(2,1)S(1)}, u32[]{:S(2)}, u32[]{:S(2)}) collective-permute-start(bf16[320,256]{1,0:T(8,128)(2,1)S(1)} %get-tuple-element.24), channel_id=1, source_target_pairs={{0,48},{8,56},{16,0},{24,8},{32,16},{40,24},{48,32},{56,40},{64,11... | collective-permute-start | bytes 491528 | tf_op jit(solution)/shard_map/ppermute | solution.py:42
  112.7 0.7 bitcast_dynamic-update-slice_fusion.2
  113.4 2.6 %collective-permute-start.12 = (bf16[320,256]{1,0:T(8,128)(2,1)S(1)}, bf16[320,256]{1,0:T(8,128)(2,1)S(1)}, u32[]{:S(2)}, u32[]{:S(2)}) collective-permute-start(bf16[320,256]{1,0:T(8,128)(2,1)S(1)} %get-tuple-element.25), channel_id=1, source_target_pairs={{0,64},{8,72},{16,80},{24,88},{32,96},{40,104},{48,112},{56,120},{... | collective-permute-start | bytes 491528 | tf_op jit(solution)/shard_map/ppermute | solution.py:42
  116.0 0.7 bitcast_dynamic-update-slice_fusion.1
  116.7 0.7 bitcast_dynamic-update-slice_fusion
  117.4 3.7 %collective-permute-start.14 = (bf16[320,256]{1,0:T(8,128)(2,1)S(1)}, bf16[320,256]{1,0:T(8,128)(2,1)S(1)}, u32[]{:S(2)}, u32[]{:S(2)}) collective-permute-start(bf16[320,256]{1,0:T(8,128)(2,1)S(1)} %get-tuple-element.27), channel_id=1, source_target_pairs={{0,96},{8,104},{16,112},{24,120},{32,64},{40,72},{48,80},{56,88},{... | collective-permute-start | bytes 491528 | tf_op jit(solution)/shard_map/ppermute | solution.py:42
  121.1 0.7 bitcast_dynamic-update-slice_fusion.14
  121.7 2.0 %collective-permute-start.15 = (bf16[320,256]{1,0:T(8,128)(2,1)S(1)}, bf16[320,256]{1,0:T(8,128)(2,1)S(1)}, u32[]{:S(2)}, u32[]{:S(2)}) collective-permute-start(bf16[320,256]{1,0:T(8,128)(2,1)S(1)} %get-tuple-element.28), channel_id=1, source_target_pairs={{0,112},{8,120},{16,64},{24,72},{32,80},{40,88},{48,96},{56,104},{... | collective-permute-start | bytes 491528 | tf_op jit(solution)/shard_map/ppermute | solution.py:42
  124.4 12.8 %collective-permute-start.33 = (bf16[8,320,256]{2,1,0:T(8,128)(2,1)}, bf16[8,320,256]{2,1,0:T(8,128)(2,1)S(1)}, u32[]{:S(2)}, u32[]{:S(2)}) collective-permute-start(bf16[8,320,256]{2,1,0:T(8,128)(2,1)} %bitcast_dynamic-update-slice_fusion), channel_id=1, source_target_pairs={{0,8},{8,0},{16,24},{24,16},{32,40},{40,32},{48,56},{56,48},{64,72... | collective-permute-start | bytes 3932168 | tf_op jit(solution)/shard_map/ppermute | solution.py:46
  137.2 0.7 bitcast_dynamic-update-slice_fusion.12
  137.9 0.7 bitcast_dynamic-update-slice_fusion.11
  138.6 0.7 bitcast_dynamic-update-slice_fusion.10
  139.3 0.7 bitcast_dynamic-update-slice_fusion.9
  140.0 0.7 bitcast_dynamic-update-slice_fusion.8
  140.8 1.9 %collective-permute-start.32 = (bf16[8,320,256]{2,1,0:T(8,128)(2,1)}, bf16[8,320,256]{2,1,0:T(8,128)(2,1)}, u32[]{:S(2)}, u32[]{:S(2)}) collective-permute-start(bf16[8,320,256]{2,1,0:T(8,128)(2,1)} %bitcast_dynamic-update-slice_fusion.8), channel_id=1, source_target_pairs={{0,8},{8,0},{16,24},{24,16},{32,40},{40,32},{48,56},{56,48},{64,72... | collective-permute-start | bytes 3932168 | tf_op jit(solution)/shard_map/ppermute | solution.py:46
  148.0 0.7 reshape.64.old_map
  149.7 1.0 copy-done.12
  150.7 27.7 %attend.1 = bf16[512,512]{1,0:T(8,128)(2,1)} custom-call(s32[19]{0:T(128)} %pad_add_fusion.info, s32[256]{0:T(256)} %reshape.64.old_map, bf16[320,256]{1,0:T(8,128)(2,1)} %copy-done.4, bf16[320,256]{1,0:T(8,128)(2,1)} %copy-done.20, bf16[320,256]{1,0:T(8,128)(2,1)} %copy-done.21, bf16[320,256]{1,0:T(8,128)(2,1)} %copy-done.22, bf16[320,256]{1,0:T(8,128)(2,1)} %copy-done.23, ...), custom_call_target="tpu_custom_call" | custom-call | tf_op jit(solution)/shard_map/attend/pallas_call | solution.py:221
  (114 shorter events, 6.3 us)
Async XLA Ops:
  0.0 6.7 %copy-start.27 = (s32[16,16]{1,0:T(8,128)S(1)}, s32[16,16]{1,0:T(8,128)}, u32[]{:S(2)}) copy-start(s32[16,16]{1,0:T(8,128)} %param.7) | copy-start | bytes 3076
  0.0 20.5 %copy-start.28 = (s32[16,16]{1,0:T(8,128)S(1)}, s32[16,16]{1,0:T(8,128)}, u32[]{:S(2)}) copy-start(s32[16,16]{1,0:T(8,128)} %param.8) | copy-start | bytes 3076
  1.3 14.0 %collective-permute-start.16 = (bf16[256,1024]{1,0:T(8,128)(2,1)S(1)}, bf16[256,1024]{1,0:T(8,128)(2,1)}, u32[]{:S(2)}, u32[]{:S(2)}) collective-permute-start(bf16[256,1024]{1,0:T(8,128)(2,1)S(1)} %bitcast.61), channel_id=1, source_target_pairs={{0,6},{1,7},{2,0},{3,1},{4,2},{5,3},{6,4},{7,5},{8,14},{9,15},{10,... | collective-permute-start | bytes 1572872 | tf_op jit(solution)/shard_map/ppermute | solution.py:28
  4.7 15.5 %collective-permute-start.19 = (bf16[256,1024]{1,0:T(8,128)(2,1)S(1)}, bf16[256,1024]{1,0:T(8,128)(2,1)}, u32[]{:S(2)}, u32[]{:S(2)}) collective-permute-start(bf16[256,1024]{1,0:T(8,128)(2,1)S(1)} %bitcast.62), channel_id=1, source_target_pairs={{0,1},{1,0},{2,3},{3,2},{4,5},{5,4},{6,7},{7,6},{8,9},{9,8},{10,11... | collective-permute-start | bytes 1572872 | tf_op jit(solution)/shard_map/ppermute | solution.py:32
  6.0 20.5 %collective-permute-start = (bf16[256,1024]{1,0:T(8,128)(2,1)S(1)}, bf16[256,1024]{1,0:T(8,128)(2,1)}, u32[]{:S(2)}, u32[]{:S(2)}) collective-permute-start(bf16[256,1024]{1,0:T(8,128)(2,1)S(1)} %bitcast.57), channel_id=1, source_target_pairs={{0,6},{1,7},{2,0},{3,1},{4,2},{5,3},{6,4},{7,5},{8,14},{9,15},{10,... | collective-permute-start | bytes 1572872 | tf_op jit(solution)/shard_map/ppermute | solution.py:28
  6.6 22.0 %collective-permute-start.3 = (bf16[256,1024]{1,0:T(8,128)(2,1)S(1)}, bf16[256,1024]{1,0:T(8,128)(2,1)S(1)}, u32[]{:S(2)}, u32[]{:S(2)}) collective-permute-start(bf16[256,1024]{1,0:T(8,128)(2,1)S(1)} %bitcast.58), channel_id=1, source_target_pairs={{0,1},{1,0},{2,3},{3,2},{4,5},{5,4},{6,7},{7,6},{8,9},{9,8},{10,11... | collective-permute-start | bytes 1572872 | tf_op jit(solution)/shard_map/ppermute | solution.py:32
  15.3 22.6 %collective-permute-start.17 = (bf16[256,1024]{1,0:T(8,128)(2,1)}, bf16[256,1024]{1,0:T(8,128)(2,1)S(1)}, u32[]{:S(2)}, u32[]{:S(2)}) collective-permute-start(bf16[256,1024]{1,0:T(8,128)(2,1)} %collective-permute-done.16.refs_3_), channel_id=1, source_target_pairs={{0,6},{1,7},{2,0},{3,1},{4,2},{5,3},{6,4},{7,5},{8,14},{9,15},{10,... | collective-permute-start | bytes 1572872 | tf_op jit(solution)/shard_map/ppermute | solution.py:28
  18.9 21.9 %collective-permute-start.22 = (bf16[256,1024]{1,0:T(8,128)(2,1)}, bf16[256,1024]{1,0:T(8,128)(2,1)}, u32[]{:S(2)}, u32[]{:S(2)}) collective-permute-start(bf16[256,1024]{1,0:T(8,128)(2,1)} %collective-permute-done.16.refs_3_), channel_id=1, source_target_pairs={{0,1},{1,0},{2,3},{3,2},{4,5},{5,4},{6,7},{7,6},{8,9},{9,8},{10,11... | collective-permute-start | bytes 1572872 | tf_op jit(solution)/shard_map/ppermute | solution.py:32
  20.2 23.9 %collective-permute-start.20 = (bf16[256,1024]{1,0:T(8,128)(2,1)}, bf16[256,1024]{1,0:T(8,128)(2,1)}, u32[]{:S(2)}, u32[]{:S(2)}) collective-permute-start(bf16[256,1024]{1,0:T(8,128)(2,1)} %collective-permute-done.19.refs_4_), channel_id=1, source_target_pairs={{0,2},{1,3},{2,4},{3,5},{4,6},{5,7},{6,0},{7,1},{8,10},{9,11},{10,... | collective-permute-start | bytes 1572872 | tf_op jit(solution)/shard_map/ppermute | solution.py:28
  26.5 23.3 %collective-permute-start.24 = (bf16[256,1024]{1,0:T(8,128)(2,1)S(1)}, bf16[256,1024]{1,0:T(8,128)(2,1)S(1)}, u32[]{:S(2)}, u32[]{:S(2)}) collective-permute-start(bf16[256,1024]{1,0:T(8,128)(2,1)S(1)} %bitcast.63), channel_id=1, source_target_pairs={{0,2},{1,3},{2,4},{3,5},{4,6},{5,7},{6,0},{7,1},{8,10},{9,11},{10,... | collective-permute-start | bytes 1572872 | tf_op jit(solution)/shard_map/ppermute | solution.py:28
  28.5 10.7 %copy-start.6 = (bf16[256,1024]{1,0:T(8,128)(2,1)}, bf16[256,1024]{1,0:T(8,128)(2,1)S(1)}, u32[]{:S(2)}) copy-start(bf16[256,1024]{1,0:T(8,128)(2,1)S(1)} %collective-permute-done.3.refs_4_) | copy-start | bytes 1572868
  28.5 25.7 %collective-permute-start.8 = (bf16[256,1024]{1,0:T(8,128)(2,1)S(1)}, bf16[256,1024]{1,0:T(8,128)(2,1)S(1)}, u32[]{:S(2)}, u32[]{:S(2)}) collective-permute-start(bf16[256,1024]{1,0:T(8,128)(2,1)S(1)} %bitcast.59), channel_id=1, source_target_pairs={{0,2},{1,3},{2,4},{3,5},{4,6},{5,7},{6,0},{7,1},{8,10},{9,11},{10,... | collective-permute-start | bytes 1572872 | tf_op jit(solution)/shard_map/ppermute | solution.py:28
  37.9 1.3 copy-start.1
  37.9 18.1 %collective-permute-start.6 = (bf16[256,1024]{1,0:T(8,128)(2,1)}, bf16[256,1024]{1,0:T(8,128)(2,1)}, u32[]{:S(2)}, u32[]{:S(2)}) collective-permute-start(bf16[256,1024]{1,0:T(8,128)(2,1)} %collective-permute-done.refs_3_), channel_id=1, source_target_pairs={{0,1},{1,0},{2,3},{3,2},{4,5},{5,4},{6,7},{7,6},{8,9},{9,8},{10,11... | collective-permute-start | bytes 1572872 | tf_op jit(solution)/shard_map/ppermute | solution.py:32
  40.8 16.5 %copy-start = (bf16[8192,128]{1,0:T(8,128)(2,1)S(1)}, bf16[8192,128]{1,0:T(8,128)(2,1)}, u32[]{:S(2)}) copy-start(bf16[8192,128]{1,0:T(8,128)(2,1)} %refs_5_.11) | copy-start | bytes 6291460
  40.8 30.0 %collective-permute-start.1 = (bf16[256,1024]{1,0:T(8,128)(2,1)}, bf16[256,1024]{1,0:T(8,128)(2,1)}, u32[]{:S(2)}, u32[]{:S(2)}) collective-permute-start(bf16[256,1024]{1,0:T(8,128)(2,1)} %collective-permute-done.refs_3_), channel_id=1, source_target_pairs={{0,6},{1,7},{2,0},{3,1},{4,2},{5,3},{6,4},{7,5},{8,14},{9,15},{10,... | collective-permute-start | bytes 1572872 | tf_op jit(solution)/shard_map/ppermute | solution.py:28
  44.1 30.3 %collective-permute-start.4 = (bf16[256,1024]{1,0:T(8,128)(2,1)}, bf16[256,1024]{1,0:T(8,128)(2,1)}, u32[]{:S(2)}, u32[]{:S(2)}) collective-permute-start(bf16[256,1024]{1,0:T(8,128)(2,1)} %copy-done.6), channel_id=1, source_target_pairs={{0,2},{1,3},{2,4},{3,5},{4,6},{5,7},{6,0},{7,1},{8,10},{9,11},{10,... | collective-permute-start | bytes 1572872 | tf_op jit(solution)/shard_map/ppermute | solution.py:28
  49.9 0.8 copy-start.8
  50.7 35.7 %collective-permute-start.23 = (bf16[96,1024]{1,0:T(8,128)(2,1)}, bf16[96,1024]{1,0:T(8,128)(2,1)S(1)}, u32[]{:S(2)}, u32[]{:S(2)}) collective-permute-start(bf16[96,1024]{1,0:T(8,128)(2,1)} %slice.55), channel_id=1, source_target_pairs={{0,6},{1,7},{2,0},{3,1},{4,2},{5,3},{6,4},{7,5},{8,14},{9,15},{10,... | collective-permute-start | bytes 589832 | tf_op jit(solution)/shard_map/ppermute | solution.py:28
  54.3 0.8 copy-start.10
  55.1 31.2 %collective-permute-start.18 = (bf16[80,1024]{1,0:T(8,128)(2,1)}, bf16[80,1024]{1,0:T(8,128)(2,1)}, u32[]{:S(2)}, u32[]{:S(2)}) collective-permute-start(bf16[80,1024]{1,0:T(8,128)(2,1)} %slice.53), channel_id=1, source_target_pairs={{0,1},{1,0},{2,3},{3,2},{4,5},{5,4},{6,7},{7,6},{8,9},{9,8},{10,11... | collective-permute-start | bytes 491528 | tf_op jit(solution)/shard_map/ppermute | solution.py:32
  55.9 30.4 %collective-permute-start.21 = (bf16[80,1024]{1,0:T(8,128)(2,1)}, bf16[80,1024]{1,0:T(8,128)(2,1)}, u32[]{:S(2)}, u32[]{:S(2)}) collective-permute-start(bf16[80,1024]{1,0:T(8,128)(2,1)} %slice.54), channel_id=1, source_target_pairs={{0,2},{1,3},{2,4},{3,5},{4,6},{5,7},{6,0},{7,1},{8,10},{9,11},{10,... | collective-permute-start | bytes 491528 | tf_op jit(solution)/shard_map/ppermute | solution.py:28
  57.3 1.0 copy-start.9
  58.3 5.8 %copy-start.7 = (bf16[256,1024]{1,0:T(8,128)(2,1)S(1)}, bf16[256,1024]{1,0:T(8,128)(2,1)}, u32[]{:S(2)}) copy-start(bf16[256,1024]{1,0:T(8,128)(2,1)} %copy-done.6) | copy-start | bytes 1572868
  58.3 5.8 %copy-start.11 = (bf16[256,1024]{1,0:T(8,128)(2,1)S(1)}, bf16[256,1024]{1,0:T(8,128)(2,1)}, u32[]{:S(2)}) copy-start(bf16[256,1024]{1,0:T(8,128)(2,1)} %copy-done.10) | copy-start | bytes 1572868
  69.7 6.5 %copy-start.2 = (bf16[256,1024]{1,0:T(8,128)(2,1)S(1)}, bf16[256,1024]{1,0:T(8,128)(2,1)}, u32[]{:S(2)}) copy-start(bf16[256,1024]{1,0:T(8,128)(2,1)} %copy-done.1) | copy-start | bytes 1572868
  70.8 26.9 %collective-permute-start.7 = (bf16[96,1024]{1,0:T(8,128)(2,1)S(1)}, bf16[96,1024]{1,0:T(8,128)(2,1)S(1)}, u32[]{:S(2)}, u32[]{:S(2)}) collective-permute-start(bf16[96,1024]{1,0:T(8,128)(2,1)S(1)} %slice.51), channel_id=1, source_target_pairs={{0,6},{1,7},{2,0},{3,1},{4,2},{5,3},{6,4},{7,5},{8,14},{9,15},{10,... | collective-permute-start | bytes 589832 | tf_op jit(solution)/shard_map/ppermute | solution.py:28
  74.5 19.8 %collective-permute-start.2 = (bf16[80,1024]{1,0:T(8,128)(2,1)S(1)}, bf16[80,1024]{1,0:T(8,128)(2,1)S(1)}, u32[]{:S(2)}, u32[]{:S(2)}) collective-permute-start(bf16[80,1024]{1,0:T(8,128)(2,1)S(1)} %slice.49), channel_id=1, source_target_pairs={{0,1},{1,0},{2,3},{3,2},{4,5},{5,4},{6,7},{7,6},{8,9},{9,8},{10,11... | collective-permute-start | bytes 491528 | tf_op jit(solution)/shard_map/ppermute | solution.py:32
  81.2 5.2 %copy-start.5 = (f32[256,128]{1,0:T(8,128)S(1)}, f32[256,128]{1,0:T(8,128)}, u32[]{:S(2)}) copy-start(f32[256,128]{1,0:T(8,128)} %get-tuple-element.55.refs_10_) | copy-start | bytes 393220
  86.3 8.8 %collective-permute-start.5 = (bf16[80,1024]{1,0:T(8,128)(2,1)S(1)}, bf16[80,1024]{1,0:T(8,128)(2,1)S(1)}, u32[]{:S(2)}, u32[]{:S(2)}) collective-permute-start(bf16[80,1024]{1,0:T(8,128)(2,1)S(1)} %slice.50), channel_id=1, source_target_pairs={{0,2},{1,3},{2,4},{3,5},{4,6},{5,7},{6,0},{7,1},{8,10},{9,11},{10,... | collective-permute-start | bytes 491528 | tf_op jit(solution)/shard_map/ppermute | solution.py:28
  88.6 11.9 %copy-start.3 = (bf16[320,256]{1,0:T(8,128)(2,1)}, bf16[320,256]{1,0:T(8,128)(2,1)S(1)}, u32[]{:S(2)}) copy-start(bf16[320,256]{1,0:T(8,128)(2,1)S(1)} %get-tuple-element.29.refs_8_) | copy-start | bytes 491524
  88.6 12.6 %collective-permute-start.25 = (bf16[320,256]{1,0:T(8,128)(2,1)S(1)}, bf16[320,256]{1,0:T(8,128)(2,1)S(1)}, u32[]{:S(2)}, u32[]{:S(2)}) collective-permute-start(bf16[320,256]{1,0:T(8,128)(2,1)S(1)} %get-tuple-element.30), channel_id=1, source_target_pairs={{0,16},{8,24},{16,32},{24,40},{32,48},{40,56},{48,0},{56,8},{64,80... | collective-permute-start | bytes 491528 | tf_op jit(solution)/shard_map/ppermute | solution.py:42
  90.3 14.8 %collective-permute-start.26 = (bf16[320,256]{1,0:T(8,128)(2,1)S(1)}, bf16[320,256]{1,0:T(8,128)(2,1)S(1)}, u32[]{:S(2)}, u32[]{:S(2)}) collective-permute-start(bf16[320,256]{1,0:T(8,128)(2,1)S(1)} %get-tuple-element.31), channel_id=1, source_target_pairs={{0,32},{8,40},{16,48},{24,56},{32,0},{40,8},{48,16},{56,24},{64,96... | collective-permute-start | bytes 491528 | tf_op jit(solution)/shard_map/ppermute | solution.py:42
  94.3 13.0 %collective-permute-start.27 = (bf16[320,256]{1,0:T(8,128)(2,1)S(1)}, bf16[320,256]{1,0:T(8,128)(2,1)S(1)}, u32[]{:S(2)}, u32[]{:S(2)}) collective-permute-start(bf16[320,256]{1,0:T(8,128)(2,1)S(1)} %get-tuple-element.32), channel_id=1, source_target_pairs={{0,48},{8,56},{16,0},{24,8},{32,16},{40,24},{48,32},{56,40},{64,11... | collective-permute-start | bytes 491528 | tf_op jit(solution)/shard_map/ppermute | solution.py:42
  95.0 13.1 %collective-permute-start.28 = (bf16[320,256]{1,0:T(8,128)(2,1)S(1)}, bf16[320,256]{1,0:T(8,128)(2,1)S(1)}, u32[]{:S(2)}, u32[]{:S(2)}) collective-permute-start(bf16[320,256]{1,0:T(8,128)(2,1)S(1)} %get-tuple-element.33), channel_id=1, source_target_pairs={{0,64},{8,72},{16,80},{24,88},{32,96},{40,104},{48,112},{56,120},{... | collective-permute-start | bytes 491528 | tf_op jit(solution)/shard_map/ppermute | solution.py:42
  97.6 13.1 %collective-permute-start.29 = (bf16[320,256]{1,0:T(8,128)(2,1)S(1)}, bf16[320,256]{1,0:T(8,128)(2,1)S(1)}, u32[]{:S(2)}, u32[]{:S(2)}) collective-permute-start(bf16[320,256]{1,0:T(8,128)(2,1)S(1)} %get-tuple-element.34), channel_id=1, source_target_pairs={{0,80},{8,88},{16,96},{24,104},{32,112},{40,120},{48,64},{56,72},{... | collective-permute-start | bytes 491528 | tf_op jit(solution)/shard_map/ppermute | solution.py:42
  100.5 16.9 %copy-start.4 = (bf16[320,256]{1,0:T(8,128)(2,1)}, bf16[320,256]{1,0:T(8,128)(2,1)S(1)}, u32[]{:S(2)}) copy-start(bf16[320,256]{1,0:T(8,128)(2,1)S(1)} %get-tuple-element.21.refs_0_) | copy-start | bytes 491524
  101.2 20.5 %copy-start.13 = (bf16[320,256]{1,0:T(8,128)(2,1)}, bf16[320,256]{1,0:T(8,128)(2,1)S(1)}, u32[]{:S(2)}) copy-start(bf16[320,256]{1,0:T(8,128)(2,1)S(1)} %collective-permute-done.25.refs_9_) | copy-start | bytes 491524
  101.2 12.2 %collective-permute-start.30 = (bf16[320,256]{1,0:T(8,128)(2,1)S(1)}, bf16[320,256]{1,0:T(8,128)(2,1)S(1)}, u32[]{:S(2)}, u32[]{:S(2)}) collective-permute-start(bf16[320,256]{1,0:T(8,128)(2,1)S(1)} %get-tuple-element.35), channel_id=1, source_target_pairs={{0,96},{8,104},{16,112},{24,120},{32,64},{40,72},{48,80},{56,88},{... | collective-permute-start | bytes 491528 | tf_op jit(solution)/shard_map/ppermute | solution.py:42
  105.1 19.2 %copy-start.14 = (bf16[320,256]{1,0:T(8,128)(2,1)}, bf16[320,256]{1,0:T(8,128)(2,1)S(1)}, u32[]{:S(2)}) copy-start(bf16[320,256]{1,0:T(8,128)(2,1)S(1)} %collective-permute-done.26.refs_10_) | copy-start | bytes 491524
  105.1 11.5 %collective-permute-start.31 = (bf16[320,256]{1,0:T(8,128)(2,1)S(1)}, bf16[320,256]{1,0:T(8,128)(2,1)S(1)}, u32[]{:S(2)}, u32[]{:S(2)}) collective-permute-start(bf16[320,256]{1,0:T(8,128)(2,1)S(1)} %get-tuple-element.36), channel_id=1, source_target_pairs={{0,112},{8,120},{16,64},{24,72},{32,80},{40,88},{48,96},{56,104},{... | collective-permute-start | bytes 491528 | tf_op jit(solution)/shard_map/ppermute | solution.py:42
  107.3 30.5 %copy-start.15 = (bf16[320,256]{1,0:T(8,128)(2,1)}, bf16[320,256]{1,0:T(8,128)(2,1)S(1)}, u32[]{:S(2)}) copy-start(bf16[320,256]{1,0:T(8,128)(2,1)S(1)} %collective-permute-done.27.refs_11_) | copy-start | bytes 491524
  107.3 10.1 %collective-permute-start.9 = (bf16[320,256]{1,0:T(8,128)(2,1)S(1)}, bf16[320,256]{1,0:T(8,128)(2,1)S(1)}, u32[]{:S(2)}, u32[]{:S(2)}) collective-permute-start(bf16[320,256]{1,0:T(8,128)(2,1)S(1)} %get-tuple-element.22), channel_id=1, source_target_pairs={{0,16},{8,24},{16,32},{24,40},{32,48},{40,56},{48,0},{56,8},{64,80... | collective-permute-start | bytes 491528 | tf_op jit(solution)/shard_map/ppermute | solution.py:42
  108.2 30.4 %copy-start.16 = (bf16[320,256]{1,0:T(8,128)(2,1)}, bf16[320,256]{1,0:T(8,128)(2,1)S(1)}, u32[]{:S(2)}) copy-start(bf16[320,256]{1,0:T(8,128)(2,1)S(1)} %collective-permute-done.28.refs_12_) | copy-start | bytes 491524
  108.2 13.6 %collective-permute-start.10 = (bf16[320,256]{1,0:T(8,128)(2,1)S(1)}, bf16[320,256]{1,0:T(8,128)(2,1)S(1)}, u32[]{:S(2)}, u32[]{:S(2)}) collective-permute-start(bf16[320,256]{1,0:T(8,128)(2,1)S(1)} %get-tuple-element.23), channel_id=1, source_target_pairs={{0,32},{8,40},{16,48},{24,56},{32,0},{40,8},{48,16},{56,24},{64,96... | collective-permute-start | bytes 491528 | tf_op jit(solution)/shard_map/ppermute | solution.py:42
  110.8 28.5 %copy-start.17 = (bf16[320,256]{1,0:T(8,128)(2,1)}, bf16[320,256]{1,0:T(8,128)(2,1)S(1)}, u32[]{:S(2)}) copy-start(bf16[320,256]{1,0:T(8,128)(2,1)S(1)} %collective-permute-done.29.refs_13_) | copy-start | bytes 491524
  110.8 13.6 %collective-permute-start.11 = (bf16[320,256]{1,0:T(8,128)(2,1)S(1)}, bf16[320,256]{1,0:T(8,128)(2,1)S(1)}, u32[]{:S(2)}, u32[]{:S(2)}) collective-permute-start(bf16[320,256]{1,0:T(8,128)(2,1)S(1)} %get-tuple-element.24), channel_id=1, source_target_pairs={{0,48},{8,56},{16,0},{24,8},{32,16},{40,24},{48,32},{56,40},{64,11... | collective-permute-start | bytes 491528 | tf_op jit(solution)/shard_map/ppermute | solution.py:42
  113.4 26.7 %copy-start.18 = (bf16[320,256]{1,0:T(8,128)(2,1)}, bf16[320,256]{1,0:T(8,128)(2,1)S(1)}, u32[]{:S(2)}) copy-start(bf16[320,256]{1,0:T(8,128)(2,1)S(1)} %collective-permute-done.30.refs_14_) | copy-start | bytes 491524
  113.4 24.5 %collective-permute-start.12 = (bf16[320,256]{1,0:T(8,128)(2,1)S(1)}, bf16[320,256]{1,0:T(8,128)(2,1)S(1)}, u32[]{:S(2)}, u32[]{:S(2)}) collective-permute-start(bf16[320,256]{1,0:T(8,128)(2,1)S(1)} %get-tuple-element.25), channel_id=1, source_target_pairs={{0,64},{8,72},{16,80},{24,88},{32,96},{40,104},{48,112},{56,120},{... | collective-permute-start | bytes 491528 | tf_op jit(solution)/shard_map/ppermute | solution.py:42
  116.7 24.1 %copy-start.19 = (bf16[320,256]{1,0:T(8,128)(2,1)}, bf16[320,256]{1,0:T(8,128)(2,1)S(1)}, u32[]{:S(2)}) copy-start(bf16[320,256]{1,0:T(8,128)(2,1)S(1)} %collective-permute-done.31.refs_15_) | copy-start | bytes 491524
  116.7 21.9 %collective-permute-start.13 = (bf16[320,256]{1,0:T(8,128)(2,1)S(1)}, bf16[320,256]{1,0:T(8,128)(2,1)S(1)}, u32[]{:S(2)}, u32[]{:S(2)}) collective-permute-start(bf16[320,256]{1,0:T(8,128)(2,1)S(1)} %get-tuple-element.26), channel_id=1, source_target_pairs={{0,80},{8,88},{16,96},{24,104},{32,112},{40,120},{48,64},{56,72},{... | collective-permute-start | bytes 491528 | tf_op jit(solution)/shard_map/ppermute | solution.py:42
  117.4 32.2 %copy-start.20 = (bf16[320,256]{1,0:T(8,128)(2,1)}, bf16[320,256]{1,0:T(8,128)(2,1)S(1)}, u32[]{:S(2)}) copy-start(bf16[320,256]{1,0:T(8,128)(2,1)S(1)} %collective-permute-done.9.refs_1_) | copy-start | bytes 491524
  117.4 21.9 %collective-permute-start.14 = (bf16[320,256]{1,0:T(8,128)(2,1)S(1)}, bf16[320,256]{1,0:T(8,128)(2,1)S(1)}, u32[]{:S(2)}, u32[]{:S(2)}) collective-permute-start(bf16[320,256]{1,0:T(8,128)(2,1)S(1)} %get-tuple-element.27), channel_id=1, source_target_pairs={{0,96},{8,104},{16,112},{24,120},{32,64},{40,72},{48,80},{56,88},{... | collective-permute-start | bytes 491528 | tf_op jit(solution)/shard_map/ppermute | solution.py:42
  121.7 27.9 %copy-start.21 = (bf16[320,256]{1,0:T(8,128)(2,1)}, bf16[320,256]{1,0:T(8,128)(2,1)S(1)}, u32[]{:S(2)}) copy-start(bf16[320,256]{1,0:T(8,128)(2,1)S(1)} %collective-permute-done.10.refs_2_) | copy-start | bytes 491524
  121.7 18.3 %collective-permute-start.15 = (bf16[320,256]{1,0:T(8,128)(2,1)S(1)}, bf16[320,256]{1,0:T(8,128)(2,1)S(1)}, u32[]{:S(2)}, u32[]{:S(2)}) collective-permute-start(bf16[320,256]{1,0:T(8,128)(2,1)S(1)} %get-tuple-element.28), channel_id=1, source_target_pairs={{0,112},{8,120},{16,64},{24,72},{32,80},{40,88},{48,96},{56,104},{... | collective-permute-start | bytes 491528 | tf_op jit(solution)/shard_map/ppermute | solution.py:42
  124.4 25.2 %copy-start.22 = (bf16[320,256]{1,0:T(8,128)(2,1)}, bf16[320,256]{1,0:T(8,128)(2,1)S(1)}, u32[]{:S(2)}) copy-start(bf16[320,256]{1,0:T(8,128)(2,1)S(1)} %collective-permute-done.11.refs_3_) | copy-start | bytes 491524
  124.4 25.2 %collective-permute-start.33 = (bf16[8,320,256]{2,1,0:T(8,128)(2,1)}, bf16[8,320,256]{2,1,0:T(8,128)(2,1)S(1)}, u32[]{:S(2)}, u32[]{:S(2)}) collective-permute-start(bf16[8,320,256]{2,1,0:T(8,128)(2,1)} %bitcast_dynamic-update-slice_fusion), channel_id=1, source_target_pairs={{0,8},{8,0},{16,24},{24,16},{32,40},{40,32},{48,56},{56,48},{64,72... | collective-permute-start | bytes 3932168 | tf_op jit(solution)/shard_map/ppermute | solution.py:46
  137.9 11.8 %copy-start.23 = (bf16[320,256]{1,0:T(8,128)(2,1)}, bf16[320,256]{1,0:T(8,128)(2,1)S(1)}, u32[]{:S(2)}) copy-start(bf16[320,256]{1,0:T(8,128)(2,1)S(1)} %collective-permute-done.12.refs_4_) | copy-start | bytes 491524
  138.6 11.1 %copy-start.24 = (bf16[320,256]{1,0:T(8,128)(2,1)}, bf16[320,256]{1,0:T(8,128)(2,1)S(1)}, u32[]{:S(2)}) copy-start(bf16[320,256]{1,0:T(8,128)(2,1)S(1)} %collective-permute-done.13.refs_5_) | copy-start | bytes 491524
  139.3 10.4 %copy-start.25 = (bf16[320,256]{1,0:T(8,128)(2,1)}, bf16[320,256]{1,0:T(8,128)(2,1)S(1)}, u32[]{:S(2)}) copy-start(bf16[320,256]{1,0:T(8,128)(2,1)S(1)} %collective-permute-done.14.refs_6_) | copy-start | bytes 491524
  140.0 9.6 %copy-start.26 = (bf16[320,256]{1,0:T(8,128)(2,1)}, bf16[320,256]{1,0:T(8,128)(2,1)S(1)}, u32[]{:S(2)}) copy-start(bf16[320,256]{1,0:T(8,128)(2,1)S(1)} %collective-permute-done.15.refs_7_) | copy-start | bytes 491524
  140.8 8.8 %collective-permute-start.32 = (bf16[8,320,256]{2,1,0:T(8,128)(2,1)}, bf16[8,320,256]{2,1,0:T(8,128)(2,1)}, u32[]{:S(2)}, u32[]{:S(2)}) collective-permute-start(bf16[8,320,256]{2,1,0:T(8,128)(2,1)} %bitcast_dynamic-update-slice_fusion.8), channel_id=1, source_target_pairs={{0,8},{8,0},{16,24},{24,16},{32,40},{40,32},{48,56},{56,48},{64,72... | collective-permute-start | bytes 3932168 | tf_op jit(solution)/shard_map/ppermute | solution.py:46
  149.6 1.1 copy-start.12

commit v2 on v1

--- a/solution.py
+++ b/solution.py
@@ -42,6 +42,14 @@
     return lax.ppermute(block, "ctx", perm)
 
 
+def together(*values):
+    return lax.optimization_barrier(values)
+
+
+def after(value, *others):
+    return lax.optimization_barrier((value, *others))[0]
+
+
 def swap_core(block):
     return lax.ppermute(block, "ctx", [(i, i ^ 1) for i in range(16)])
 
@@ -54,7 +62,7 @@
     return lax.dot_general(a, b, (((1,), (1,)), ((), ())), preferred_element_type=jnp.float32)
 
 
-def project_kernel(groups, has_acc, last, *refs):
+def project_kernel(groups, has_acc, last, joint, *refs):
     features, refs = refs[0], refs[1:]
     blocks, at = [], 0
     for n in groups:
@@ -69,8 +77,8 @@
     if last:
         info, cosine, sine = refs[at : at + 3]
         at += 3
-        outs = refs[at : at + 8]
-        acc, heads = refs[at + 8 : at + 10]
+        outs = refs[at:-2]
+        acc, heads = refs[-2:]
     else:
         out, acc = refs[at : at + 2]
     step = pl.program_id(0)
@@ -105,19 +113,21 @@
         value = acc[:, 640:768].astype(jnp.bfloat16)
         me = info[0]
         high, z = me // 8, lax.rem(me // 2, 4)
+        for payload in outs:
+            payload[0:ROWS, 0:HEAD] = key
+            payload[0:ROWS, HEAD : 2 * HEAD] = value
         for r, (dh, dz) in enumerate(CHIPS):
-            outs[r][0:ROWS, 0:HEAD] = key
-            outs[r][0:ROWS, HEAD : 2 * HEAD] = value
+            to, base = (outs[4], dz * 4 * W) if joint and dh else (outs[r], 0)
             chip = lax.rem(high + dh, 2) * 8 + lax.rem(z + dz, 4) * 2
             for core in range(2):
                 k = info[1 + chip + core]
                 rows = pl.ds(pl.multiple_of(k * W, W), W)
                 for half in range(2):
-                    at = ROWS + (core * 2 + half) * W
-                    outs[r][at : at + W, :] = heads[rows, half * 256 : half * 256 + 256]
-
-
-def project(features, blocks, weights, acc=None, tables=None):
+                    at = ROWS + base + (core * 2 + half) * W
+                    to[at : at + W, :] = heads[rows, half * 256 : half * 256 + 256]
+
+
+def project(features, blocks, weights, acc=None, tables=None, joint=False):
     groups = [len(b) for b in blocks]
     flat = [p for b in blocks for p in b]
     whole = lambda shape: pl.BlockSpec(shape, lambda i, f: (0,) * len(shape))
@@ -132,14 +142,15 @@
     if last:
         specs += [SMEM, whole((ROWS, HEAD)), whole((ROWS, HEAD))]
         operands += list(tables)
-        out_shape = [jax.ShapeDtypeStruct((PAYLOAD, 256), jnp.bfloat16)] * 8
-        out_specs = [whole((PAYLOAD, 256))] * 8
+        sizes = [PAYLOAD] * 4 + [2 * ROWS] if joint else [PAYLOAD] * 8
+        out_shape = [jax.ShapeDtypeStruct((n, 256), jnp.bfloat16) for n in sizes]
+        out_specs = [whole((n, 256)) for n in sizes]
         scratch.append(pltpu.VMEM((ROWS, 512), jnp.bfloat16))
     else:
         out_shape = jax.ShapeDtypeStruct((ROWS, 768), jnp.float32)
         out_specs = whole((ROWS, 768))
     return pl.pallas_call(
-        functools.partial(project_kernel, groups, acc is not None, last),
+        functools.partial(project_kernel, groups, acc is not None, last, joint),
         grid_spec=pltpu.PrefetchScalarGridSpec(
             num_scalar_prefetch=1,
             grid=(len(blocks),),
@@ -154,9 +165,8 @@
 
 
 def attend_kernel(info, old_map, *refs):
-    own = refs[: 8 * CHUNKS]
-    other = refs[8 * CHUNKS : 9 * CHUNKS]
-    out, query, keys, values, top, total, accum = refs[9 * CHUNKS :]
+    packed, packed_other, late, late_other = refs[:4], refs[4], refs[5:13], refs[13:15]
+    out, query, keys, values, top, total, accum = refs[15:]
     me = info[0]
     high, z, core = me // 8, lax.rem(me // 2, 4), lax.rem(me, 2)
     for r, (dh, dz) in enumerate(CHIPS):
@@ -164,13 +174,17 @@
             source = lax.rem(high + dh, 2) * 8 + lax.rem(z + 4 - dz, 4) * 2 + lax.rem(core + swapped, 2)
             slot = info[3 + source]
             for j in range(CHUNKS):
-                ref = other[j].at[r] if swapped else own[j * 8 + r]
+                if j == 0:
+                    ref, base = (packed_other, (dz * 2 + dh) * PAYLOAD) if swapped else (packed[dz], dh * PAYLOAD)
+                else:
+                    ref, base = (late_other[r // 4], (r % 4) * PAYLOAD) if swapped else (late[r], 0)
                 for k in range(16):
                     at = pl.ds(pl.multiple_of(old_map[source * 16 + k] * FINE + j * W, W), W)
-                    keys[at, :] = ref[k * W : (k + 1) * W, 0:HEAD]
-                    values[at, :] = ref[k * W : (k + 1) * W, HEAD : 2 * HEAD]
+                    rows = slice(base + k * W, base + (k + 1) * W)
+                    keys[at, :] = ref[rows, 0:HEAD]
+                    values[at, :] = ref[rows, HEAD : 2 * HEAD]
                 for h in range(4):
-                    at = pl.ds(pl.multiple_of(ROWS + (core * 2 + h // 2) * W, W), W)
+                    at = pl.ds(pl.multiple_of(base + ROWS + (core * 2 + h // 2) * W, W), W)
                     to = (slot // 8) * 1024 + h * 256 + lax.rem(slot, 8) * FINE + j * W
                     query[pl.ds(pl.multiple_of(to, W), W), :] = ref[at, (h % 2) * HEAD : (h % 2 + 1) * HEAD]
 
@@ -217,11 +231,11 @@
             )
 
 
-def attend(info, old_map, own, other):
+def attend(info, old_map, parts):
     return pl.pallas_call(
         attend_kernel,
         out_shape=jax.ShapeDtypeStruct((512, 512), jnp.bfloat16),
-        in_specs=[SMEM, SMEM] + [VMEM] * (9 * CHUNKS),
+        in_specs=[SMEM, SMEM] + [VMEM] * len(parts),
         out_specs=VMEM,
         scratch_shapes=[
             pltpu.VMEM((2048, HEAD), jnp.bfloat16),
@@ -233,7 +247,7 @@
         ],
         compiler_params=pltpu.CompilerParams(vmem_limit_bytes=56 * 2**20),
         name="attend",
-    )(info, old_map, *own, *other)
+    )(info, old_map, *parts)
 
 
 def routing(old_map, new_map, own_index):
@@ -271,31 +285,51 @@
     order = [(0, 0), (3, 0), (1, 0), (0, 1), (3, 1), (2, 0), (1, 1), (2, 1)]
     features = jnp.stack([feature(dx, dy) for dx, dy in order]).astype(jnp.int32)
     chunks = tokens.reshape(16, CHUNKS, W, 1024)
-    third = (ROWS // 3) // 16 * 16
-
-    own_side, other_side = [], []
+    tables = []
     for j in range(CHUNKS):
-        mine = chunks[:, j].reshape(ROWS, 1024)
-        left = shift_x(mine, 1)
-        right = shift_x(mine, -1)
-        across = swap_y(mine)
-        left_across = shift_x(across, 1)
-        far = shift_x(right, -1)
-        right_across = swap_y(right)
-        far_across = (
-            swap_y(far[:third]),
-            shift_x(left_across[third : 2 * third], 1),
-            shift_x(right_across[2 * third :], -1),
-        )
         positions = old_mine[:, None] * FINE + j * W + jnp.arange(W, dtype=jnp.int32)[None, :]
-        cosine, sine = angle_tables(positions.reshape(-1))
-        acc = project(features[:4], [(mine,), (left,), (right,), (across,)], weights)
-        acc = project(features[4:7], [(left_across,), (far,), (right_across,)], weights, acc)
-        sent = project(features[7:], [far_across], weights, acc, (send_info, cosine, sine))
-        received = [sent[0]] + [shift_ctx(sent[r], *CHIPS[r]) for r in range(1, 8)]
-        own_side += received
-        other_side.append(swap_core(jnp.stack(received)))
-    return attend(attend_info, old_map.reshape(-1), own_side, other_side)
+        tables.append((send_info, *angle_tables(positions.reshape(-1))))
+    early, late = (chunks[:, j].reshape(ROWS, 1024) for j in range(CHUNKS))
+
+    left = shift_x(early, 1)
+    right = shift_x(early, -1)
+    across = swap_y(early)
+    late_across = swap_y(after(late, early))
+    left, right, across = together(left, right, across)
+    left_across = shift_x(across, 1)
+    far = shift_x(right, -1)
+    right_across = swap_y(right)
+    total = project(features[:4], [(early,), (left,), (right,), (across,)], weights)
+    late_across, total = together(late_across, total)
+    late = after(late, total)
+    late_right = shift_x(late, -1)
+    left_across, far = together(left_across, far)
+    far_across = shift_x(left_across, 1)
+    late_left = shift_x(after(late, left_across), 1)
+    total = project(features[4:7], [(left_across,), (far,), (right_across,)], weights, total)
+    late_right, far_across, total = together(late_right, far_across, total)
+    late_far = shift_x(late_right, -1)
+    late_right_across = swap_y(late_right)
+    sent = project(features[7:], [(far_across,)], weights, total, tables[0], joint=True)
+    partner = shift_ctx(sent[4], 1, 0)
+    late_left, late_far, late_right_across, partner = together(late_left, late_far, late_right_across, partner)
+    late_left_across = shift_x(late_across, 1)
+    late_far_across = shift_x(late_right_across, -1)
+    early_parts = [
+        jnp.concatenate([sent[dz], partner[:ROWS], partner[ROWS + dz * 4 * W : ROWS + (dz + 1) * 4 * W]], axis=0)
+        for dz in range(4)
+    ]
+    early_parts[1:] = [shift_ctx(early_parts[dz], 0, dz) for dz in range(1, 4)]
+    blocks = [(late,), (late_left,), (late_right,), (late_across,)]
+    total = project(features[:4], blocks, weights)
+    late_far, late_right_across, total = together(late_far, late_right_across, total)
+    total = project(features[5:7], [(late_far,), (late_right_across,)], weights, total)
+    last = jnp.stack([features[4], features[7]])
+    sent = project(last, [(late_left_across,), (late_far_across,)], weights, total, tables[1])
+    early_other = swap_core(jnp.concatenate(early_parts, axis=0))
+    late_parts = [sent[0]] + [shift_ctx(sent[r], *CHIPS[r]) for r in range(1, 8)]
+    late_other = [swap_core(jnp.concatenate(late_parts[at : at + 4], axis=0)) for at in (0, 4)]
+    return attend(attend_info, old_map.reshape(-1), [*early_parts, early_other, *late_parts, *late_other])
 
 
 def solution(mesh):

time: 179 us -> 154 us (0.86)
  starting transfers between devices: 64.3 us -> 45.7 us
  local copies, waits for them, and re-layouts: 25.1 us -> 11.5 us
  waiting for transfers between devices: 25.3 us -> 32.1 us
    ppermute x12 -> x10, waiting for transfers between devices: 24.3 us -> 8.95 us  [shift_x(): return lax.ppermute(block, 'tp', perm)]
    ppermute x14 -> x11, waiting for transfers between devices: 0.04 us -> 13.9 us  [shift_ctx(): return lax.ppermute(block, 'ctx', perm)]
    ppermute x6 -> x4, waiting for transfers between devices: 0.96 us -> 9.23 us  [swap_y(): return lax.ppermute(block, 'tp', [(i, i ^ 1) for i in range(8)])]
    ppermute x12 -> x10, starting transfers between devices: 17.6 us -> 9.84 us  [shift_x(): return lax.ppermute(block, 'tp', perm)]
    slice x7 -> x3, local copies, waits for them, and re-layouts: 8.97 us -> 1.44 us  [the longest x1 1.43 us: local(): early, late = (chunks[:, j].reshape(ROWS, 1024) for j in range(CHUNKS))]
    unnamed x72 -> x44, local copies, waits for them, and re-layouts: 13.3 us -> 7.86 us
    ppermute x14 -> x11, starting transfers between devices: 26.2 us -> 21.2 us  [shift_ctx(): return lax.ppermute(block, 'ctx', perm)]
    ppermute x2 -> x3, starting transfers between devices: 14.7 us -> 10.3 us  [swap_core(): return lax.ppermute(block, 'ctx', [(i, i ^ 1) for i in range(16)])]
  transfers between devices with their start and end apart: 34 -> 28, of which waited for: 5 -> 7; matrix products, arithmetic and copies ran while one was open for 14% -> 7% of each run, Pallas kernels for 14% -> 17%
where the time goes in v2:
time: 154 us
  Pallas kernels  53.3 us (35%)
  starting transfers between devices  45.7 us (30%)
  waiting for transfers between devices  32.1 us (21%)
  local copies, waits for them, and re-layouts  11.5 us (7%)
  other arithmetic  5.52 us (4%)
  between operations  5.46 us (4%)
    pallas_call x1, Pallas kernels, attend(): pl.pallas_call(attend_kernel, out_shape=jax.ShapeDtypeStruct((512, 512),...  27.8 us
    pallas_call x6, Pallas kernels, project(): pl.pallas_call(functools.partial(project_kernel, groups, acc is not None,...  25.6 us
    ppermute x11, starting transfers between devices, shift_ctx(): return lax.ppermute(block, 'ctx', perm)  21.2 us
    ppermute x11, waiting for transfers between devices, shift_ctx(): return lax.ppermute(block, 'ctx', perm)  13.9 us
    ppermute x3, starting transfers between devices, swap_core(): return lax.ppermute(block, 'ctx', [(i, i ^ 1) for i in range(16)])  10.3 us
    ppermute x10, starting transfers between devices, shift_x(): return lax.ppermute(block, 'tp', perm)  9.84 us
    ppermute x4, waiting for transfers between devices, swap_y(): return lax.ppermute(block, 'tp', [(i, i ^ 1) for i in range(8)])  9.23 us
    ppermute x10, waiting for transfers between devices, shift_x(): return lax.ppermute(block, 'tp', perm)  8.95 us
  transfers between devices with their start and end apart: 28, of which 7 were waited for; matrix products, arithmetic and copies ran while one was open for 7% of the time, Pallas kernels for 17%

profile of v2, /device:TPU:1, one launch (start us, length us, event | category | flops | bytes accessed | tf_op | source)
XLA Modules:
  0.0 153.6 jit_solution(17246440505387183807)
XLA Ops:
  0.0 1.4 fusion.5
  1.4 2.1 %collective-permute-start.1 = (bf16[256,1024]{1,0:T(8,128)(2,1)S(1)}, bf16[256,1024]{1,0:T(8,128)(2,1)}, u32[]{:S(2)}, u32[]{:S(2)}) collective-permute-start(bf16[256,1024]{1,0:T(8,128)(2,1)S(1)} %bitcast.29), channel_id=1, source_target_pairs={{0,2},{1,3},{2,4},{3,5},{4,6},{5,7},{6,0},{7,1},{8,10},{9,11},{10,... | collective-permute-start | bytes 1572872 | tf_op jit(solution)/shard_map/ppermute | solution.py:28
  3.5 1.4 collective-permute-start.2
  4.9 1.4 collective-permute-start.3
  6.3 0.8 copy-done.1
  7.2 8.9 %collective-permute-done.1.refs_2_ = bf16[256,1024]{1,0:T(8,128)(2,1)} collective-permute-done((bf16[256,1024]{1,0:T(8,128)(2,1)S(1)}, bf16[256,1024]{1,0:T(8,128)(2,1)}, u32[]{:S(2)}, u32[]{:S(2)}) %collective-permute-start.1) | collective-permute-done | bytes 524320 | tf_op jit(solution)/shard_map/ppermute | solution.py:28
  16.1 1.0 collective-permute-done.3.refs_4_
  17.2 1.5 collective-permute-start.6
  18.9 1.5 collective-permute-start.8
  20.4 1.0 copy-done.2
  21.4 5.9 %project.6.refs_7_ = f32[256,768]{1,0:T(8,128)S(1)} custom-call(s32[4]{0:T(128)S(1)} %pad_add_fusion.1.refs_0_, bf16[256,1024]{1,0:T(8,128)(2,1)S(1)} %bitcast.32, bf16[256,1024]{1,0:T(8,128)(2,1)} %collective-permute-done.1.refs_2_, bf16[256,1024]{1,0:T(8,128)(2,1)} %collective-permute-done.2.refs_3_, bf16[256,1024]{1,0:T(8,128)(2,1)} %collective-permute-done.3.refs_4_, ...), custom_call_target="tpu_custom_call" | custom-call | tf_op jit(solution)/shard_map/project/pallas_call | solution.py:152
  27.3 1.0 collective-permute-done.refs_4_
  28.4 1.7 %collective-permute-start.4 = (bf16[256,1024]{1,0:T(8,128)(2,1)S(1)}, bf16[256,1024]{1,0:T(8,128)(2,1)}, u32[]{:S(2)}, u32[]{:S(2)}) collective-permute-start(bf16[256,1024]{1,0:T(8,128)(2,1)S(1)} %bitcast.26), channel_id=1, source_target_pairs={{0,6},{1,7},{2,0},{3,1},{4,2},{5,3},{6,4},{7,5},{8,14},{9,15},{10,... | collective-permute-start | bytes 1572872 | tf_op jit(solution)/shard_map/ppermute | solution.py:28
  30.1 0.8 copy-done.4
  31.1 0.1 convert_element_type.25
  31.1 0.1 compare_reduce_fusion
  31.3 0.1 select_reduce_fusion
  31.4 1.0 fusion.4
  32.5 7.2 %collective-permute-done.8.refs_3_ = bf16[256,1024]{1,0:T(8,128)(2,1)} collective-permute-done((bf16[256,1024]{1,0:T(8,128)(2,1)}, bf16[256,1024]{1,0:T(8,128)(2,1)}, u32[]{:S(2)}, u32[]{:S(2)}) %collective-permute-start.8) | collective-permute-done | bytes 524320 | tf_op jit(solution)/shard_map/ppermute | solution.py:32
  39.6 1.0 copy-done.5
  40.7 4.9 %project.7.refs_5_ = f32[256,768]{1,0:T(8,128)S(1)} custom-call(s32[3]{0:T(128)S(1)} %pad_add_fusion.2.refs_0_, bf16[256,1024]{1,0:T(8,128)(2,1)} %collective-permute-done.5.refs_1_, bf16[256,1024]{1,0:T(8,128)(2,1)S(1)} %copy-done.5, bf16[256,1024]{1,0:T(8,128)(2,1)} %collective-permute-done.8.refs_3_, bf16[8192,512]{1,0:T(8,128)(2,1)} %refs_3_.5, ...), custom_call_target="tpu_custom_call" | custom-call | tf_op jit(solution)/shard_map/project/pallas_call | solution.py:152
  45.6 1.5 collective-permute-start.10
  47.1 1.3 collective-permute-start.11
  48.5 0.1 pad_maximum_fusion.6
  48.6 2.2 %project.8 = (bf16[320,256]{1,0:T(8,128)(2,1)S(1)}, bf16[320,256]{1,0:T(8,128)(2,1)S(1)}, bf16[320,256]{1,0:T(8,128)(2,1)S(1)}, bf16[320,256]{1,0:T(8,128)(2,1)S(1)}, bf16[512,256]{1,0:T(8,128)(2,1)S(1)}) custom-call(s32[1]{0:T(128)} %bitcast.6.refs_0_, bf16[256,1024]{1,0:T(8,128)(2,1)} %collective-permute-done.7.refs_1_, bf16[8192,512]{1,0:T(8,128)(2,1)} %refs_3_.5, ...), custom_call_target="tpu_custom_call" | custom-call | tf_op jit(solution)/shard_map/project/pallas_call | solution.py:152
  50.8 2.7 %collective-permute-start.12 = (bf16[512,256]{1,0:T(8,128)(2,1)S(1)}, bf16[512,256]{1,0:T(8,128)(2,1)S(1)}, u32[]{:S(2)}, u32[]{:S(2)}) collective-permute-start(bf16[512,256]{1,0:T(8,128)(2,1)S(1)} %get-tuple-element.51), channel_id=1, source_target_pairs={{0,64},{8,72},{16,80},{24,88},{32,96},{40,104},{48,112},{56,120},{... | collective-permute-start | bytes 786440 | tf_op jit(solution)/shard_map/ppermute | solution.py:42
  53.6 0.1 pad_maximum_fusion.8
  53.8 0.3 collective-permute-start.17
  54.0 10.3 %collective-permute-done.12 = bf16[512,256]{1,0:T(8,128)(2,1)S(1)} collective-permute-done((bf16[512,256]{1,0:T(8,128)(2,1)S(1)}, bf16[512,256]{1,0:T(8,128)(2,1)S(1)}, u32[]{:S(2)}, u32[]{:S(2)}) %collective-permute-start.12) | collective-permute-done | bytes 262176 | tf_op jit(solution)/shard_map/ppermute | solution.py:42
  64.4 1.4 collective-permute-start.18
  65.7 0.1 fusion.2
  65.8 1.9 %collective-permute-start.13 = (bf16[640,256]{1,0:T(8,128)(2,1)S(1)}, bf16[640,256]{1,0:T(8,128)(2,1)S(1)}, u32[]{:S(2)}, u32[]{:S(2)}) collective-permute-start(bf16[640,256]{1,0:T(8,128)(2,1)S(1)} %get-tuple-element.82), channel_id=1, source_target_pairs={{0,16},{8,24},{16,32},{24,40},{32,48},{40,56},{48,0},{56,8},{64,80... | collective-permute-start | bytes 983048 | tf_op jit(solution)/shard_map/ppermute | solution.py:42
  67.7 0.7 constant_dynamic-update-slice_fusion.4
  68.4 3.3 %collective-permute-start.14 = (bf16[640,256]{1,0:T(8,128)(2,1)S(1)}, bf16[640,256]{1,0:T(8,128)(2,1)S(1)}, u32[]{:S(2)}, u32[]{:S(2)}) collective-permute-start(bf16[640,256]{1,0:T(8,128)(2,1)S(1)} %get-tuple-element.81), channel_id=1, source_target_pairs={{0,32},{8,40},{16,48},{24,56},{32,0},{40,8},{48,16},{56,24},{64,96... | collective-permute-start | bytes 983048 | tf_op jit(solution)/shard_map/ppermute | solution.py:42
  71.7 0.7 collective-permute-start.15
  72.4 0.7 constant_dynamic-update-slice_fusion.3
  73.1 5.8 %project.9.refs_6_ = f32[256,768]{1,0:T(8,128)S(1)} custom-call(s32[4]{0:T(128)S(1)} %pad_add_fusion.1.refs_0_, bf16[256,1024]{1,0:T(8,128)(2,1)S(1)} %bitcast.28, bf16[256,1024]{1,0:T(8,128)(2,1)S(1)} %collective-permute-done.9.refs_2_, bf16[256,1024]{1,0:T(8,128)(2,1)} %collective-permute-done.4.refs_3_, bf16[256,1024]{1,0:T(8,128)(2,1)} %collective-permute-done.refs_4_, ...), custom_call_target="tpu_custom_call" | custom-call | tf_op jit(solution)/shard_map/project/pallas_call | solution.py:152
  78.9 3.3 %project.10.refs_6_ = f32[256,768]{1,0:T(8,128)S(1)} custom-call(s32[2]{0:T(128)S(1)} %pad_add_fusion.5.refs_0_, bf16[256,1024]{1,0:T(8,128)(2,1)S(1)} %collective-permute-done.10.refs_1_, bf16[256,1024]{1,0:T(8,128)(2,1)S(1)} %collective-permute-done.11.refs_2_, bf16[8192,512]{1,0:T(8,128)(2,1)} %refs_3_.5, bf16[8192,128]{1,0:T(8,128)(2,1)S(1)} %copy-done, ...), custom_call_target="tpu_custom_call" | custom-call | tf_op jit(solution)/shard_map/project/pallas_call | solution.py:152
  82.3 0.8 constant_dynamic-update-slice_fusion.2
  83.1 0.8 constant_dynamic-update-slice_fusion.1
  83.9 3.4 %project.11 = (bf16[320,256]{1,0:T(8,128)(2,1)S(1)}, bf16[320,256]{1,0:T(8,128)(2,1)S(1)}, bf16[320,256]{1,0:T(8,128)(2,1)S(1)}, bf16[320,256]{1,0:T(8,128)(2,1)...) custom-call(s32[2]{0:T(128)S(1)} %pad_add_fusion.4.refs_0_, ...), custom_call_target="tpu_custom_call" | custom-call | tf_op jit(solution)/shard_map/project/pallas_call | solution.py:152
  87.4 0.4 collective-permute-start.22
  87.8 3.1 %collective-permute-start.23 = (bf16[320,256]{1,0:T(8,128)(2,1)S(1)}, bf16[320,256]{1,0:T(8,128)(2,1)S(1)}, u32[]{:S(2)}, u32[]{:S(2)}) collective-permute-start(bf16[320,256]{1,0:T(8,128)(2,1)S(1)} %get-tuple-element.68), channel_id=1, source_target_pairs={{0,80},{8,88},{16,96},{24,104},{32,112},{40,120},{48,64},{56,72},{... | collective-permute-start | bytes 491528 | tf_op jit(solution)/shard_map/ppermute | solution.py:42
  90.9 0.5 collective-permute-start.24
  91.4 3.7 %collective-permute-start.25 = (bf16[320,256]{1,0:T(8,128)(2,1)S(1)}, bf16[320,256]{1,0:T(8,128)(2,1)S(1)}, u32[]{:S(2)}, u32[]{:S(2)}) collective-permute-start(bf16[320,256]{1,0:T(8,128)(2,1)S(1)} %get-tuple-element.70), channel_id=1, source_target_pairs={{0,112},{8,120},{16,64},{24,72},{32,80},{40,88},{48,96},{56,104},{... | collective-permute-start | bytes 491528 | tf_op jit(solution)/shard_map/ppermute | solution.py:42
  95.1 0.8 constant_dynamic-update-slice_fusion
  95.9 6.6 %collective-permute-start.16 = (bf16[2560,256]{1,0:T(8,128)(2,1)}, bf16[2560,256]{1,0:T(8,128)(2,1)S(1)}, u32[]{:S(2)}, u32[]{:S(2)}) collective-permute-start(bf16[2560,256]{1,0:T(8,128)(2,1)} %constant_dynamic-update-slice_fusion), channel_id=1, source_target_pairs={{0,8},{8,0},{16,24},{24,16},{32,40},{40,32},{48,56},{56,48},{64,72... | collective-permute-start | bytes 3932168 | tf_op jit(solution)/shard_map/ppermute | solution.py:54
  102.5 0.2 collective-permute-start.19
  102.7 2.8 %collective-permute-start.20 = (bf16[320,256]{1,0:T(8,128)(2,1)S(1)}, bf16[320,256]{1,0:T(8,128)(2,1)S(1)}, u32[]{:S(2)}, u32[]{:S(2)}) collective-permute-start(bf16[320,256]{1,0:T(8,128)(2,1)S(1)} %get-tuple-element.65), channel_id=1, source_target_pairs={{0,32},{8,40},{16,48},{24,56},{32,0},{40,8},{48,16},{56,24},{64,96... | collective-permute-start | bytes 491528 | tf_op jit(solution)/shard_map/ppermute | solution.py:42
  105.5 1.9 %collective-permute-start.21 = (bf16[320,256]{1,0:T(8,128)(2,1)S(1)}, bf16[320,256]{1,0:T(8,128)(2,1)S(1)}, u32[]{:S(2)}, u32[]{:S(2)}) collective-permute-start(bf16[320,256]{1,0:T(8,128)(2,1)S(1)} %get-tuple-element.66), channel_id=1, source_target_pairs={{0,48},{8,56},{16,0},{24,8},{32,16},{40,24},{48,32},{56,40},{64,11... | collective-permute-start | bytes 491528 | tf_op jit(solution)/shard_map/ppermute | solution.py:42
  107.5 0.9 pad_maximum_fusion.1
  108.3 3.2 %collective-permute-start.27 = (bf16[1280,256]{1,0:T(8,128)(2,1)}, bf16[1280,256]{1,0:T(8,128)(2,1)}, u32[]{:S(2)}, u32[]{:S(2)}) collective-permute-start(bf16[1280,256]{1,0:T(8,128)(2,1)} %pad_maximum_fusion.1), channel_id=1, source_target_pairs={{0,8},{8,0},{16,24},{24,16},{32,40},{40,32},{48,56},{56,48},{64,72... | collective-permute-start | bytes 1966088 | tf_op jit(solution)/shard_map/ppermute | solution.py:54
  111.5 1.8 %collective-permute-done.20.refs_7_ = bf16[320,256]{1,0:T(8,128)(2,1)S(1)} collective-permute-done((bf16[320,256]{1,0:T(8,128)(2,1)S(1)}, bf16[320,256]{1,0:T(8,128)(2,1)S(1)}, u32[]{:S(2)}, u32[]{:S(2)}) %collective-permute-start.20) | collective-permute-done | bytes 163872 | tf_op jit(solution)/shard_map/ppermute | solution.py:42
  113.4 1.8 %collective-permute-done.21.refs_8_ = bf16[320,256]{1,0:T(8,128)(2,1)S(1)} collective-permute-done((bf16[320,256]{1,0:T(8,128)(2,1)S(1)}, bf16[320,256]{1,0:T(8,128)(2,1)S(1)}, u32[]{:S(2)}, u32[]{:S(2)}) %collective-permute-start.21) | collective-permute-done | bytes 163872 | tf_op jit(solution)/shard_map/ppermute | solution.py:42
  115.1 0.9 pad_maximum_fusion
  116.1 0.5 collective-permute-start.26
  116.6 0.6 fusion.7
  122.4 0.7 reshape.64.old_map
  123.1 0.1 compare_reduce_fusion.1
  123.2 0.1 select_reduce_fusion.1
  123.3 0.6 pad_add_fusion.info
  123.9 0.8 pad_maximum_fusion.5.refs_0_
  124.7 1.1 copy-done.9
  125.8 27.8 %attend.1 = bf16[512,512]{1,0:T(8,128)(2,1)} custom-call(s32[19]{0:T(128)} %pad_add_fusion.info, s32[256]{0:T(256)} %reshape.64.old_map, bf16[640,256]{1,0:T(8,128)(2,1)} %pad_maximum_fusion.5.refs_0_, bf16[640,256]{1,0:T(8,128)(2,1)} %copy-done.6, bf16[640,256]{1,0:T(8,128)(2,1)} %copy-done.7, bf16[640,256]{1,0:T(8,128)(2,1)} %copy-done.8, ...), custom_call_target="tpu_custom_call" | custom-call | tf_op jit(solution)/shard_map/attend/pallas_call | solution.py:235
  (75 shorter events, 0.9 us)
Async XLA Ops:
  0.0 7.2 %copy-start.18 = (s32[16,16]{1,0:T(8,128)S(1)}, s32[16,16]{1,0:T(8,128)}, u32[]{:S(2)}) copy-start(s32[16,16]{1,0:T(8,128)} %param.7) | copy-start | bytes 3076
  0.0 20.3 %copy-start = (bf16[8192,128]{1,0:T(8,128)(2,1)S(1)}, bf16[8192,128]{1,0:T(8,128)(2,1)}, u32[]{:S(2)}) copy-start(bf16[8192,128]{1,0:T(8,128)(2,1)} %refs_4_.7) | copy-start | bytes 6291460
  1.4 14.7 %collective-permute-start.1 = (bf16[256,1024]{1,0:T(8,128)(2,1)S(1)}, bf16[256,1024]{1,0:T(8,128)(2,1)}, u32[]{:S(2)}, u32[]{:S(2)}) collective-permute-start(bf16[256,1024]{1,0:T(8,128)(2,1)S(1)} %bitcast.29), channel_id=1, source_target_pairs={{0,2},{1,3},{2,4},{3,5},{4,6},{5,7},{6,0},{7,1},{8,10},{9,11},{10,... | collective-permute-start | bytes 1572872 | tf_op jit(solution)/shard_map/ppermute | solution.py:28
  3.5 12.6 %collective-permute-start.2 = (bf16[256,1024]{1,0:T(8,128)(2,1)S(1)}, bf16[256,1024]{1,0:T(8,128)(2,1)}, u32[]{:S(2)}, u32[]{:S(2)}) collective-permute-start(bf16[256,1024]{1,0:T(8,128)(2,1)S(1)} %bitcast.30), channel_id=1, source_target_pairs={{0,6},{1,7},{2,0},{3,1},{4,2},{5,3},{6,4},{7,5},{8,14},{9,15},{10,... | collective-permute-start | bytes 1572872 | tf_op jit(solution)/shard_map/ppermute | solution.py:28
  4.9 12.3 %collective-permute-start.3 = (bf16[256,1024]{1,0:T(8,128)(2,1)S(1)}, bf16[256,1024]{1,0:T(8,128)(2,1)}, u32[]{:S(2)}, u32[]{:S(2)}) collective-permute-start(bf16[256,1024]{1,0:T(8,128)(2,1)S(1)} %bitcast.31), channel_id=1, source_target_pairs={{0,1},{1,0},{2,3},{3,2},{4,5},{5,4},{6,7},{7,6},{8,9},{9,8},{10,11... | collective-permute-start | bytes 1572872 | tf_op jit(solution)/shard_map/ppermute | solution.py:32
  6.3 0.8 copy-start.1
  7.1 21.3 %collective-permute-start = (bf16[256,1024]{1,0:T(8,128)(2,1)S(1)}, bf16[256,1024]{1,0:T(8,128)(2,1)}, u32[]{:S(2)}, u32[]{:S(2)}) collective-permute-start(bf16[256,1024]{1,0:T(8,128)(2,1)S(1)} %bitcast.25), channel_id=1, source_target_pairs={{0,1},{1,0},{2,3},{3,2},{4,5},{5,4},{6,7},{7,6},{8,9},{9,8},{10,11... | collective-permute-start | bytes 1572872 | tf_op jit(solution)/shard_map/ppermute | solution.py:32
  17.2 12.9 %collective-permute-start.6 = (bf16[256,1024]{1,0:T(8,128)(2,1)}, bf16[256,1024]{1,0:T(8,128)(2,1)S(1)}, u32[]{:S(2)}, u32[]{:S(2)}) collective-permute-start(bf16[256,1024]{1,0:T(8,128)(2,1)} %collective-permute-done.2.refs_3_), channel_id=1, source_target_pairs={{0,6},{1,7},{2,0},{3,1},{4,2},{5,3},{6,4},{7,5},{8,14},{9,15},{10,... | collective-permute-start | bytes 1572872 | tf_op jit(solution)/shard_map/ppermute | solution.py:28
  18.7 12.2 %collective-permute-start.5 = (bf16[256,1024]{1,0:T(8,128)(2,1)}, bf16[256,1024]{1,0:T(8,128)(2,1)}, u32[]{:S(2)}, u32[]{:S(2)}) collective-permute-start(bf16[256,1024]{1,0:T(8,128)(2,1)} %collective-permute-done.3.refs_4_), channel_id=1, source_target_pairs={{0,2},{1,3},{2,4},{3,5},{4,6},{5,7},{6,0},{7,1},{8,10},{9,11},{10,... | collective-permute-start | bytes 1572872 | tf_op jit(solution)/shard_map/ppermute | solution.py:28
  18.9 20.7 %collective-permute-start.8 = (bf16[256,1024]{1,0:T(8,128)(2,1)}, bf16[256,1024]{1,0:T(8,128)(2,1)}, u32[]{:S(2)}, u32[]{:S(2)}) collective-permute-start(bf16[256,1024]{1,0:T(8,128)(2,1)} %collective-permute-done.2.refs_3_), channel_id=1, source_target_pairs={{0,1},{1,0},{2,3},{3,2},{4,5},{5,4},{6,7},{7,6},{8,9},{9,8},{10,11... | collective-permute-start | bytes 1572872 | tf_op jit(solution)/shard_map/ppermute | solution.py:32
  20.4 1.0 copy-start.2
  21.4 9.7 %copy-start.19 = (s32[16,16]{1,0:T(8,128)S(1)}, s32[16,16]{1,0:T(8,128)}, u32[]{:S(2)}) copy-start(s32[16,16]{1,0:T(8,128)} %param.8) | copy-start | bytes 3076
  28.4 17.2 %collective-permute-start.4 = (bf16[256,1024]{1,0:T(8,128)(2,1)S(1)}, bf16[256,1024]{1,0:T(8,128)(2,1)}, u32[]{:S(2)}, u32[]{:S(2)}) collective-permute-start(bf16[256,1024]{1,0:T(8,128)(2,1)S(1)} %bitcast.26), channel_id=1, source_target_pairs={{0,6},{1,7},{2,0},{3,1},{4,2},{5,3},{6,4},{7,5},{8,14},{9,15},{10,... | collective-permute-start | bytes 1572872 | tf_op jit(solution)/shard_map/ppermute | solution.py:28
  30.1 0.8 copy-start.4
  30.9 14.7 %collective-permute-start.7 = (bf16[256,1024]{1,0:T(8,128)(2,1)}, bf16[256,1024]{1,0:T(8,128)(2,1)}, u32[]{:S(2)}, u32[]{:S(2)}) collective-permute-start(bf16[256,1024]{1,0:T(8,128)(2,1)} %collective-permute-done.5.refs_1_), channel_id=1, source_target_pairs={{0,2},{1,3},{2,4},{3,5},{4,6},{5,7},{6,0},{7,1},{8,10},{9,11},{10,... | collective-permute-start | bytes 1572872 | tf_op jit(solution)/shard_map/ppermute | solution.py:28
  32.4 21.6 %collective-permute-start.9 = (bf16[256,1024]{1,0:T(8,128)(2,1)S(1)}, bf16[256,1024]{1,0:T(8,128)(2,1)S(1)}, u32[]{:S(2)}, u32[]{:S(2)}) collective-permute-start(bf16[256,1024]{1,0:T(8,128)(2,1)S(1)} %bitcast.27), channel_id=1, source_target_pairs={{0,2},{1,3},{2,4},{3,5},{4,6},{5,7},{6,0},{7,1},{8,10},{9,11},{10,... | collective-permute-start | bytes 1572872 | tf_op jit(solution)/shard_map/ppermute | solution.py:28
  39.6 1.0 copy-start.5
  45.6 18.7 %collective-permute-start.10 = (bf16[256,1024]{1,0:T(8,128)(2,1)}, bf16[256,1024]{1,0:T(8,128)(2,1)S(1)}, u32[]{:S(2)}, u32[]{:S(2)}) collective-permute-start(bf16[256,1024]{1,0:T(8,128)(2,1)} %collective-permute-done.4.refs_3_), channel_id=1, source_target_pairs={{0,6},{1,7},{2,0},{3,1},{4,2},{5,3},{6,4},{7,5},{8,14},{9,15},{10,... | collective-permute-start | bytes 1572872 | tf_op jit(solution)/shard_map/ppermute | solution.py:28
  47.1 17.2 %collective-permute-start.11 = (bf16[256,1024]{1,0:T(8,128)(2,1)}, bf16[256,1024]{1,0:T(8,128)(2,1)S(1)}, u32[]{:S(2)}, u32[]{:S(2)}) collective-permute-start(bf16[256,1024]{1,0:T(8,128)(2,1)} %collective-permute-done.4.refs_3_), channel_id=1, source_target_pairs={{0,1},{1,0},{2,3},{3,2},{4,5},{5,4},{6,7},{7,6},{8,9},{9,8},{10,11... | collective-permute-start | bytes 1572872 | tf_op jit(solution)/shard_map/ppermute | solution.py:32
  50.8 13.5 %collective-permute-start.12 = (bf16[512,256]{1,0:T(8,128)(2,1)S(1)}, bf16[512,256]{1,0:T(8,128)(2,1)S(1)}, u32[]{:S(2)}, u32[]{:S(2)}) collective-permute-start(bf16[512,256]{1,0:T(8,128)(2,1)S(1)} %get-tuple-element.51), channel_id=1, source_target_pairs={{0,64},{8,72},{16,80},{24,88},{32,96},{40,104},{48,112},{56,120},{... | collective-permute-start | bytes 786440 | tf_op jit(solution)/shard_map/ppermute | solution.py:42
  53.8 30.1 %collective-permute-start.17 = (bf16[256,1024]{1,0:T(8,128)(2,1)}, bf16[256,1024]{1,0:T(8,128)(2,1)S(1)}, u32[]{:S(2)}, u32[]{:S(2)}) collective-permute-start(bf16[256,1024]{1,0:T(8,128)(2,1)} %collective-permute-done.refs_4_), channel_id=1, source_target_pairs={{0,2},{1,3},{2,4},{3,5},{4,6},{5,7},{6,0},{7,1},{8,10},{9,11},{10,... | collective-permute-start | bytes 1572872 | tf_op jit(solution)/shard_map/ppermute | solution.py:28
  64.4 19.6 %collective-permute-start.18 = (bf16[256,1024]{1,0:T(8,128)(2,1)S(1)}, bf16[256,1024]{1,0:T(8,128)(2,1)S(1)}, u32[]{:S(2)}, u32[]{:S(2)}) collective-permute-start(bf16[256,1024]{1,0:T(8,128)(2,1)S(1)} %collective-permute-done.11.refs_2_), channel_id=1, source_target_pairs={{0,6},{1,7},{2,0},{3,1},{4,2},{5,3},{6,4},{7,5},{8,14},{9,15},{10,... | collective-permute-start | bytes 1572872 | tf_op jit(solution)/shard_map/ppermute | solution.py:28
  65.8 16.5 %collective-permute-start.13 = (bf16[640,256]{1,0:T(8,128)(2,1)S(1)}, bf16[640,256]{1,0:T(8,128)(2,1)S(1)}, u32[]{:S(2)}, u32[]{:S(2)}) collective-permute-start(bf16[640,256]{1,0:T(8,128)(2,1)S(1)} %get-tuple-element.82), channel_id=1, source_target_pairs={{0,16},{8,24},{16,32},{24,40},{32,48},{40,56},{48,0},{56,8},{64,80... | collective-permute-start | bytes 983048 | tf_op jit(solution)/shard_map/ppermute | solution.py:42
  68.4 14.7 %collective-permute-start.14 = (bf16[640,256]{1,0:T(8,128)(2,1)S(1)}, bf16[640,256]{1,0:T(8,128)(2,1)S(1)}, u32[]{:S(2)}, u32[]{:S(2)}) collective-permute-start(bf16[640,256]{1,0:T(8,128)(2,1)S(1)} %get-tuple-element.81), channel_id=1, source_target_pairs={{0,32},{8,40},{16,48},{24,56},{32,0},{40,8},{48,16},{56,24},{64,96... | collective-permute-start | bytes 983048 | tf_op jit(solution)/shard_map/ppermute | solution.py:42
  71.7 23.4 %collective-permute-start.15 = (bf16[640,256]{1,0:T(8,128)(2,1)S(1)}, bf16[640,256]{1,0:T(8,128)(2,1)S(1)}, u32[]{:S(2)}, u32[]{:S(2)}) collective-permute-start(bf16[640,256]{1,0:T(8,128)(2,1)S(1)} %get-tuple-element.80), channel_id=1, source_target_pairs={{0,48},{8,56},{16,0},{24,8},{32,16},{40,24},{48,32},{56,40},{64,11... | collective-permute-start | bytes 983048 | tf_op jit(solution)/shard_map/ppermute | solution.py:42
  82.3 5.0 %copy-start.6 = (bf16[640,256]{1,0:T(8,128)(2,1)}, bf16[640,256]{1,0:T(8,128)(2,1)S(1)}, u32[]{:S(2)}) copy-start(bf16[640,256]{1,0:T(8,128)(2,1)S(1)} %collective-permute-done.13.refs_1_) | copy-start | bytes 983044
  83.1 4.3 %copy-start.7 = (bf16[640,256]{1,0:T(8,128)(2,1)}, bf16[640,256]{1,0:T(8,128)(2,1)S(1)}, u32[]{:S(2)}) copy-start(bf16[640,256]{1,0:T(8,128)(2,1)S(1)} %collective-permute-done.14.refs_2_) | copy-start | bytes 983044
  87.3 28.7 %copy-start.3 = (bf16[320,256]{1,0:T(8,128)(2,1)}, bf16[320,256]{1,0:T(8,128)(2,1)S(1)}, u32[]{:S(2)}) copy-start(bf16[320,256]{1,0:T(8,128)(2,1)S(1)} %get-tuple-element.63.refs_5_) | copy-start | bytes 491524
  87.4 15.1 %collective-permute-start.22 = (bf16[320,256]{1,0:T(8,128)(2,1)S(1)}, bf16[320,256]{1,0:T(8,128)(2,1)S(1)}, u32[]{:S(2)}, u32[]{:S(2)}) collective-permute-start(bf16[320,256]{1,0:T(8,128)(2,1)S(1)} %get-tuple-element.67), channel_id=1, source_target_pairs={{0,64},{8,72},{16,80},{24,88},{32,96},{40,104},{48,112},{56,120},{... | collective-permute-start | bytes 491528 | tf_op jit(solution)/shard_map/ppermute | solution.py:42
  87.8 14.9 %collective-permute-start.23 = (bf16[320,256]{1,0:T(8,128)(2,1)S(1)}, bf16[320,256]{1,0:T(8,128)(2,1)S(1)}, u32[]{:S(2)}, u32[]{:S(2)}) collective-permute-start(bf16[320,256]{1,0:T(8,128)(2,1)S(1)} %get-tuple-element.68), channel_id=1, source_target_pairs={{0,80},{8,88},{16,96},{24,104},{32,112},{40,120},{48,64},{56,72},{... | collective-permute-start | bytes 491528 | tf_op jit(solution)/shard_map/ppermute | solution.py:42
  90.9 14.6 %collective-permute-start.24 = (bf16[320,256]{1,0:T(8,128)(2,1)S(1)}, bf16[320,256]{1,0:T(8,128)(2,1)S(1)}, u32[]{:S(2)}, u32[]{:S(2)}) collective-permute-start(bf16[320,256]{1,0:T(8,128)(2,1)S(1)} %get-tuple-element.69), channel_id=1, source_target_pairs={{0,96},{8,104},{16,112},{24,120},{32,64},{40,72},{48,80},{56,88},{... | collective-permute-start | bytes 491528 | tf_op jit(solution)/shard_map/ppermute | solution.py:42
  91.4 16.1 %collective-permute-start.25 = (bf16[320,256]{1,0:T(8,128)(2,1)S(1)}, bf16[320,256]{1,0:T(8,128)(2,1)S(1)}, u32[]{:S(2)}, u32[]{:S(2)}) collective-permute-start(bf16[320,256]{1,0:T(8,128)(2,1)S(1)} %get-tuple-element.70), channel_id=1, source_target_pairs={{0,112},{8,120},{16,64},{24,72},{32,80},{40,88},{48,96},{56,104},{... | collective-permute-start | bytes 491528 | tf_op jit(solution)/shard_map/ppermute | solution.py:42
  95.1 21.0 %copy-start.8 = (bf16[640,256]{1,0:T(8,128)(2,1)}, bf16[640,256]{1,0:T(8,128)(2,1)S(1)}, u32[]{:S(2)}) copy-start(bf16[640,256]{1,0:T(8,128)(2,1)S(1)} %collective-permute-done.15.refs_3_) | copy-start | bytes 983044
  95.9 28.8 %collective-permute-start.16 = (bf16[2560,256]{1,0:T(8,128)(2,1)}, bf16[2560,256]{1,0:T(8,128)(2,1)S(1)}, u32[]{:S(2)}, u32[]{:S(2)}) collective-permute-start(bf16[2560,256]{1,0:T(8,128)(2,1)} %constant_dynamic-update-slice_fusion), channel_id=1, source_target_pairs={{0,8},{8,0},{16,24},{24,16},{32,40},{40,32},{48,56},{56,48},{64,72... | collective-permute-start | bytes 3932168 | tf_op jit(solution)/shard_map/ppermute | solution.py:54
  102.5 13.5 %copy-start.10 = (bf16[320,256]{1,0:T(8,128)(2,1)}, bf16[320,256]{1,0:T(8,128)(2,1)S(1)}, u32[]{:S(2)}) copy-start(bf16[320,256]{1,0:T(8,128)(2,1)S(1)} %collective-permute-done.22.refs_9_) | copy-start | bytes 491524
  102.5 9.0 %collective-permute-start.19 = (bf16[320,256]{1,0:T(8,128)(2,1)S(1)}, bf16[320,256]{1,0:T(8,128)(2,1)S(1)}, u32[]{:S(2)}, u32[]{:S(2)}) collective-permute-start(bf16[320,256]{1,0:T(8,128)(2,1)S(1)} %get-tuple-element.64), channel_id=1, source_target_pairs={{0,16},{8,24},{16,32},{24,40},{32,48},{40,56},{48,0},{56,8},{64,80... | collective-permute-start | bytes 491528 | tf_op jit(solution)/shard_map/ppermute | solution.py:42
  102.7 13.4 %copy-start.11 = (bf16[320,256]{1,0:T(8,128)(2,1)}, bf16[320,256]{1,0:T(8,128)(2,1)S(1)}, u32[]{:S(2)}) copy-start(bf16[320,256]{1,0:T(8,128)(2,1)S(1)} %collective-permute-done.23.refs_10_) | copy-start | bytes 491524
  102.7 10.7 %collective-permute-start.20 = (bf16[320,256]{1,0:T(8,128)(2,1)S(1)}, bf16[320,256]{1,0:T(8,128)(2,1)S(1)}, u32[]{:S(2)}, u32[]{:S(2)}) collective-permute-start(bf16[320,256]{1,0:T(8,128)(2,1)S(1)} %get-tuple-element.65), channel_id=1, source_target_pairs={{0,32},{8,40},{16,48},{24,56},{32,0},{40,8},{48,16},{56,24},{64,96... | collective-permute-start | bytes 491528 | tf_op jit(solution)/shard_map/ppermute | solution.py:42
  105.5 10.5 %copy-start.12 = (bf16[320,256]{1,0:T(8,128)(2,1)}, bf16[320,256]{1,0:T(8,128)(2,1)S(1)}, u32[]{:S(2)}) copy-start(bf16[320,256]{1,0:T(8,128)(2,1)S(1)} %collective-permute-done.24.refs_11_) | copy-start | bytes 491524
  105.5 18.4 %copy-start.17 = (bf16[320,256]{1,0:T(8,128)(2,1)S(1)}, bf16[320,256]{1,0:T(8,128)(2,1)}, u32[]{:S(2)}) copy-start(bf16[320,256]{1,0:T(8,128)(2,1)} %get-tuple-element.76) | copy-start | bytes 491524
  105.5 9.6 %collective-permute-start.21 = (bf16[320,256]{1,0:T(8,128)(2,1)S(1)}, bf16[320,256]{1,0:T(8,128)(2,1)S(1)}, u32[]{:S(2)}, u32[]{:S(2)}) collective-permute-start(bf16[320,256]{1,0:T(8,128)(2,1)S(1)} %get-tuple-element.66), channel_id=1, source_target_pairs={{0,48},{8,56},{16,0},{24,8},{32,16},{40,24},{48,32},{56,40},{64,11... | collective-permute-start | bytes 491528 | tf_op jit(solution)/shard_map/ppermute | solution.py:42
  107.4 8.6 %copy-start.13 = (bf16[320,256]{1,0:T(8,128)(2,1)}, bf16[320,256]{1,0:T(8,128)(2,1)S(1)}, u32[]{:S(2)}) copy-start(bf16[320,256]{1,0:T(8,128)(2,1)S(1)} %collective-permute-done.25.refs_12_) | copy-start | bytes 491524
  108.3 16.3 %collective-permute-start.27 = (bf16[1280,256]{1,0:T(8,128)(2,1)}, bf16[1280,256]{1,0:T(8,128)(2,1)}, u32[]{:S(2)}, u32[]{:S(2)}) collective-permute-start(bf16[1280,256]{1,0:T(8,128)(2,1)} %pad_maximum_fusion.1), channel_id=1, source_target_pairs={{0,8},{8,0},{16,24},{24,16},{32,40},{40,32},{48,56},{56,48},{64,72... | collective-permute-start | bytes 1966088 | tf_op jit(solution)/shard_map/ppermute | solution.py:54
  111.5 13.1 %copy-start.14 = (bf16[320,256]{1,0:T(8,128)(2,1)}, bf16[320,256]{1,0:T(8,128)(2,1)S(1)}, u32[]{:S(2)}) copy-start(bf16[320,256]{1,0:T(8,128)(2,1)S(1)} %collective-permute-done.19.refs_6_) | copy-start | bytes 491524
  113.4 11.3 %copy-start.15 = (bf16[320,256]{1,0:T(8,128)(2,1)}, bf16[320,256]{1,0:T(8,128)(2,1)S(1)}, u32[]{:S(2)}) copy-start(bf16[320,256]{1,0:T(8,128)(2,1)S(1)} %collective-permute-done.20.refs_7_) | copy-start | bytes 491524
  115.1 9.6 %copy-start.16 = (bf16[320,256]{1,0:T(8,128)(2,1)}, bf16[320,256]{1,0:T(8,128)(2,1)S(1)}, u32[]{:S(2)}) copy-start(bf16[320,256]{1,0:T(8,128)(2,1)S(1)} %collective-permute-done.21.refs_8_) | copy-start | bytes 491524
  116.1 8.6 %collective-permute-start.26 = (bf16[1280,256]{1,0:T(8,128)(2,1)}, bf16[1280,256]{1,0:T(8,128)(2,1)}, u32[]{:S(2)}, u32[]{:S(2)}) collective-permute-start(bf16[1280,256]{1,0:T(8,128)(2,1)} %pad_maximum_fusion), channel_id=1, source_target_pairs={{0,8},{8,0},{16,24},{24,16},{32,40},{40,32},{48,56},{56,48},{64,72... | collective-permute-start | bytes 1966088 | tf_op jit(solution)/shard_map/ppermute | solution.py:54
  124.7 1.1 copy-start.9

commit v3 on v2

--- a/solution.py
+++ b/solution.py
@@ -285,17 +285,20 @@
     order = [(0, 0), (3, 0), (1, 0), (0, 1), (3, 1), (2, 0), (1, 1), (2, 1)]
     features = jnp.stack([feature(dx, dy) for dx, dy in order]).astype(jnp.int32)
     chunks = tokens.reshape(16, CHUNKS, W, 1024)
+    early, late = (chunks[:, j].reshape(ROWS, 1024) for j in range(CHUNKS))
     tables = []
     for j in range(CHUNKS):
         positions = old_mine[:, None] * FINE + j * W + jnp.arange(W, dtype=jnp.int32)[None, :]
-        tables.append((send_info, *angle_tables(positions.reshape(-1))))
-    early, late = (chunks[:, j].reshape(ROWS, 1024) for j in range(CHUNKS))
+        tables += angle_tables(positions.reshape(-1))
+    old_flat = old_map.reshape(-1)
 
     left = shift_x(early, 1)
     right = shift_x(early, -1)
     across = swap_y(early)
     late_across = swap_y(after(late, early))
-    left, right, across = together(left, right, across)
+    left, right, across, send_info, attend_info, old_flat, *tables = together(
+        left, right, across, send_info, attend_info, old_flat, *tables
+    )
     left_across = shift_x(across, 1)
     far = shift_x(right, -1)
     right_across = swap_y(right)
@@ -310,26 +313,29 @@
     late_right, far_across, total = together(late_right, far_across, total)
     late_far = shift_x(late_right, -1)
     late_right_across = swap_y(late_right)
-    sent = project(features[7:], [(far_across,)], weights, total, tables[0], joint=True)
+    sent = project(features[7:], [(far_across,)], weights, total, (send_info, *tables[:2]), joint=True)
     partner = shift_ctx(sent[4], 1, 0)
-    late_left, late_far, late_right_across, partner = together(late_left, late_far, late_right_across, partner)
+    late_across, late_left = together(late_across, late_left, sent[0])[:2]
     late_left_across = shift_x(late_across, 1)
+    blocks = [(late,), (late_left,), (late_right,), (late_across,)]
+    total = project(features[:4], blocks, weights)
+    late_far, late_right_across, total = together(late_far, late_right_across, total)
     late_far_across = shift_x(late_right_across, -1)
+    partner = after(partner, late_right_across, late_far)
     early_parts = [
         jnp.concatenate([sent[dz], partner[:ROWS], partner[ROWS + dz * 4 * W : ROWS + (dz + 1) * 4 * W]], axis=0)
         for dz in range(4)
     ]
+    early_parts = list(together(*early_parts))
     early_parts[1:] = [shift_ctx(early_parts[dz], 0, dz) for dz in range(1, 4)]
-    blocks = [(late,), (late_left,), (late_right,), (late_across,)]
-    total = project(features[:4], blocks, weights)
-    late_far, late_right_across, total = together(late_far, late_right_across, total)
     total = project(features[5:7], [(late_far,), (late_right_across,)], weights, total)
     last = jnp.stack([features[4], features[7]])
-    sent = project(last, [(late_left_across,), (late_far_across,)], weights, total, tables[1])
+    tail = [(late_left_across,), (late_far_across,)]
+    sent = project(last, tail, weights, total, (send_info, *tables[2:]))
     early_other = swap_core(jnp.concatenate(early_parts, axis=0))
     late_parts = [sent[0]] + [shift_ctx(sent[r], *CHIPS[r]) for r in range(1, 8)]
     late_other = [swap_core(jnp.concatenate(late_parts[at : at + 4], axis=0)) for at in (0, 4)]
-    return attend(attend_info, old_map.reshape(-1), [*early_parts, early_other, *late_parts, *late_other])
+    return attend(attend_info, old_flat, [*early_parts, early_other, *late_parts, *late_other])
 
 
 def solution(mesh):

time: 154 us -> 143 us (0.929)
  waiting for transfers between devices: 32.1 us -> 19.9 us
  starting transfers between devices: 45.7 us -> 49.4 us
  local copies, waits for them, and re-layouts: 11.5 us -> 9.31 us
    ppermute x11, waiting for transfers between devices: 13.9 us -> 8.14 us  [shift_ctx(): return lax.ppermute(block, 'ctx', perm)]
    ppermute x4, waiting for transfers between devices: 9.23 us -> 4.12 us  [swap_y(): return lax.ppermute(block, 'tp', [(i, i ^ 1) for i in range(8)])]
    ppermute x10, waiting for transfers between devices: 8.95 us -> 5.92 us  [shift_x(): return lax.ppermute(block, 'tp', perm)]
    ppermute x3, starting transfers between devices: 10.3 us -> 12.9 us  [swap_core(): return lax.ppermute(block, 'ctx', [(i, i ^ 1) for i in range(16)])]
    ppermute x3, waiting for transfers between devices: 0.01 us -> 1.72 us  [swap_core(): return lax.ppermute(block, 'ctx', [(i, i ^ 1) for i in range(16)])]
    concatenate x2, other arithmetic: 1.79 us -> 0.09 us  [local(): jnp.concatenate(late_parts[at:at + 4], axis=0)]
    unnamed x44 -> x50, local copies, waits for them, and re-layouts: 7.86 us -> 6.62 us
  transfers between devices with their start and end apart: 28 -> 28, of which waited for: 7 -> 7; matrix products, arithmetic and copies ran while one was open for 7% -> 4% of each run, Pallas kernels for 17% -> 18%
where the time goes in v3:
time: 143 us; the launch traced here: 142 us
  Pallas kernels  53.8 us (38%)
  starting transfers between devices  49.4 us (35%)
  waiting for transfers between devices  19.9 us (14%)
  local copies, waits for them, and re-layouts  9.31 us (7%)
  between operations  5.17 us (4%)
  other arithmetic  4.56 us (3%)
    pallas_call x1, Pallas kernels, attend(): pl.pallas_call(attend_kernel, out_shape=jax.ShapeDtypeStruct((512, 512),...  27.8 us
    pallas_call x6, Pallas kernels, project(): pl.pallas_call(functools.partial(project_kernel, groups, acc is not None,...  26 us
    ppermute x11, starting transfers between devices, shift_ctx(): return lax.ppermute(block, 'ctx', perm)  21.1 us
    ppermute x3, starting transfers between devices, swap_core(): return lax.ppermute(block, 'ctx', [(i, i ^ 1) for i in range(16)])  12.9 us
    ppermute x10, starting transfers between devices, shift_x(): return lax.ppermute(block, 'tp', perm)  11.3 us
    ppermute x11, waiting for transfers between devices, shift_ctx(): return lax.ppermute(block, 'ctx', perm)  8.14 us
    unnamed x50, local copies, waits for them, and re-layouts  6.62 us
    ppermute x10, waiting for transfers between devices, shift_x(): return lax.ppermute(block, 'tp', perm)  5.92 us
  transfers between devices with their start and end apart: 28, of which 7 were waited for; matrix products, arithmetic and copies ran while one was open for 4% of the time, Pallas kernels for 18%

profile of v3, /device:TPU:1, one launch (start us, length us, event | category | flops | bytes accessed | tf_op | source)
XLA Modules:
  0.0 142.2 jit_solution(12816052335852253182)
XLA Ops:
  0.0 1.3 fusion.5
  1.3 2.2 %collective-permute-start.2 = (bf16[256,1024]{1,0:T(8,128)(2,1)S(1)}, bf16[256,1024]{1,0:T(8,128)(2,1)}, u32[]{:S(2)}, u32[]{:S(2)}) collective-permute-start(bf16[256,1024]{1,0:T(8,128)(2,1)S(1)} %bitcast.29), channel_id=1, source_target_pairs={{0,1},{1,0},{2,3},{3,2},{4,5},{5,4},{6,7},{7,6},{8,9},{9,8},{10,11... | collective-permute-start | bytes 1572872 | tf_op jit(solution)/shard_map/ppermute | solution.py:32
  3.5 2.5 %collective-permute-start.1 = (bf16[256,1024]{1,0:T(8,128)(2,1)S(1)}, bf16[256,1024]{1,0:T(8,128)(2,1)}, u32[]{:S(2)}, u32[]{:S(2)}) collective-permute-start(bf16[256,1024]{1,0:T(8,128)(2,1)S(1)} %bitcast.30), channel_id=1, source_target_pairs={{0,6},{1,7},{2,0},{3,1},{4,2},{5,3},{6,4},{7,5},{8,14},{9,15},{10,... | collective-permute-start | bytes 1572872 | tf_op jit(solution)/shard_map/ppermute | solution.py:28
  6.0 0.2 collective-permute-start.3
  6.2 0.6 fusion.7
  11.6 0.1 compare_reduce_fusion.1
  11.8 0.1 select_reduce_fusion.1
  11.9 0.1 compare_reduce_fusion
  12.0 0.1 select_reduce_fusion
  12.3 0.1 pad_add_fusion.refs_6_.refs_7_
  12.3 0.7 pad_add_fusion.1.info
  13.0 0.6 reshape.65.old_map
  13.6 0.1 convert_element_type.23
  13.7 0.1 convert_element_type.25
  13.7 1.0 fusion.4
  14.8 0.8 pad_maximum_fusion.9
  15.6 0.8 pad_maximum_fusion.7
  16.4 3.2 %collective-permute-done.refs_2_ = bf16[256,1024]{1,0:T(8,128)(2,1)} collective-permute-done((bf16[256,1024]{1,0:T(8,128)(2,1)S(1)}, bf16[256,1024]{1,0:T(8,128)(2,1)}, u32[]{:S(2)}, u32[]{:S(2)}) %collective-permute-start) | collective-permute-done | bytes 524320 | tf_op jit(solution)/shard_map/ppermute | solution.py:28
  19.5 2.7 %collective-permute-start.6 = (bf16[256,1024]{1,0:T(8,128)(2,1)}, bf16[256,1024]{1,0:T(8,128)(2,1)}, u32[]{:S(2)}, u32[]{:S(2)}) collective-permute-start(bf16[256,1024]{1,0:T(8,128)(2,1)} %collective-permute-done.1.refs_3_), channel_id=1, source_target_pairs={{0,6},{1,7},{2,0},{3,1},{4,2},{5,3},{6,4},{7,5},{8,14},{9,15},{10,... | collective-permute-start | bytes 1572872 | tf_op jit(solution)/shard_map/ppermute | solution.py:28
  22.2 0.1 pad_add_fusion.2.refs_0_
  22.3 0.2 collective-permute-start.8
  22.5 1.0 copy-done.4
  23.5 5.9 %project.6.refs_7_ = f32[256,768]{1,0:T(8,128)S(1)} custom-call(s32[4]{0:T(128)S(1)} %pad_add_fusion.2.refs_0_, bf16[256,1024]{1,0:T(8,128)(2,1)S(1)} %bitcast.32, bf16[256,1024]{1,0:T(8,128)(2,1)} %collective-permute-done.refs_2_, bf16[256,1024]{1,0:T(8,128)(2,1)} %collective-permute-done.1.refs_3_, bf16[256,1024]{1,0:T(8,128)(2,1)} %collective-permute-done.2.refs_4_, ...), custom_call_target="tpu_custom_call" | custom-call | tf_op jit(solution)/shard_map/project/pallas_call | solution.py:152
  29.5 0.1 collective-permute-start.4
  29.6 2.7 %collective-permute-done.5.refs_1_ = bf16[256,1024]{1,0:T(8,128)(2,1)} collective-permute-done((bf16[256,1024]{1,0:T(8,128)(2,1)}, bf16[256,1024]{1,0:T(8,128)(2,1)}, u32[]{:S(2)}, u32[]{:S(2)}) %collective-permute-start.5) | collective-permute-done | bytes 524320 | tf_op jit(solution)/shard_map/ppermute | solution.py:28
  32.3 0.1 pad_add_fusion.3.refs_0_
  32.4 0.9 collective-permute-start.12
  33.2 4.1 %collective-permute-done.8.refs_3_ = bf16[256,1024]{1,0:T(8,128)(2,1)} collective-permute-done((bf16[256,1024]{1,0:T(8,128)(2,1)}, bf16[256,1024]{1,0:T(8,128)(2,1)}, u32[]{:S(2)}, u32[]{:S(2)}) %collective-permute-start.8) | collective-permute-done | bytes 524320 | tf_op jit(solution)/shard_map/ppermute | solution.py:32
  37.4 5.1 %project.7.refs_5_ = f32[256,768]{1,0:T(8,128)S(1)} custom-call(s32[3]{0:T(128)S(1)} %pad_add_fusion.3.refs_0_, bf16[256,1024]{1,0:T(8,128)(2,1)} %collective-permute-done.5.refs_1_, bf16[256,1024]{1,0:T(8,128)(2,1)} %collective-permute-done.6.refs_2_, bf16[256,1024]{1,0:T(8,128)(2,1)} %collective-permute-done.8.refs_3_, bf16[8192,512]{1,0:T(8,128)(2,1)} %refs_3_.5, ...), custom_call_target="tpu_custom_call" | custom-call | tf_op jit(solution)/shard_map/project/pallas_call | solution.py:152
  42.4 0.9 copy-done.1
  43.3 1.6 %collective-permute-start.11 = (bf16[256,1024]{1,0:T(8,128)(2,1)}, bf16[256,1024]{1,0:T(8,128)(2,1)S(1)}, u32[]{:S(2)}, u32[]{:S(2)}) collective-permute-start(bf16[256,1024]{1,0:T(8,128)(2,1)} %collective-permute-done.4.refs_3_), channel_id=1, source_target_pairs={{0,1},{1,0},{2,3},{3,2},{4,5},{5,4},{6,7},{7,6},{8,9},{9,8},{10,11... | collective-permute-start | bytes 1572872 | tf_op jit(solution)/shard_map/ppermute | solution.py:32
  44.9 2.5 %collective-permute-start.10 = (bf16[256,1024]{1,0:T(8,128)(2,1)}, bf16[256,1024]{1,0:T(8,128)(2,1)}, u32[]{:S(2)}, u32[]{:S(2)}) collective-permute-start(bf16[256,1024]{1,0:T(8,128)(2,1)} %collective-permute-done.4.refs_3_), channel_id=1, source_target_pairs={{0,6},{1,7},{2,0},{3,1},{4,2},{5,3},{6,4},{7,5},{8,14},{9,15},{10,... | collective-permute-start | bytes 1572872 | tf_op jit(solution)/shard_map/ppermute | solution.py:28
  47.4 1.1 copy-done.2
  48.5 0.9 copy-done.6
  49.4 2.2 %project.8 = (bf16[320,256]{1,0:T(8,128)(2,1)S(1)}, bf16[320,256]{1,0:T(8,128)(2,1)S(1)}, bf16[320,256]{1,0:T(8,128)(2,1)S(1)}, bf16[320,256]{1,0:T(8,128)(2,1)S(1)}, bf16[512,256]{1,0:T(8,128)(2,1)S(1)}) custom-call(s32[1]{0:T(128)} %bitcast.9.refs_0_, bf16[256,1024]{1,0:T(8,128)(2,1)} %collective-permute-done.7.refs_1_, bf16[8192,512]{1,0:T(8,128)(2,1)} %refs_3_.5, ...), custom_call_target="tpu_custom_call" | custom-call | tf_op jit(solution)/shard_map/project/pallas_call | solution.py:152
  51.6 2.7 %collective-permute-start.9 = (bf16[512,256]{1,0:T(8,128)(2,1)S(1)}, bf16[512,256]{1,0:T(8,128)(2,1)S(1)}, u32[]{:S(2)}, u32[]{:S(2)}) collective-permute-start(bf16[512,256]{1,0:T(8,128)(2,1)S(1)} %get-tuple-element.64), channel_id=1, source_target_pairs={{0,64},{8,72},{16,80},{24,88},{32,96},{40,104},{48,112},{56,120},{... | collective-permute-start | bytes 786440 | tf_op jit(solution)/shard_map/ppermute | solution.py:42
  54.3 5.9 %project.9.refs_6_ = f32[256,768]{1,0:T(8,128)S(1)} custom-call(s32[4]{0:T(128)S(1)} %pad_add_fusion.2.refs_0_, bf16[256,1024]{1,0:T(8,128)(2,1)S(1)} %bitcast.28, bf16[256,1024]{1,0:T(8,128)(2,1)} %collective-permute-done.12.refs_2_, bf16[256,1024]{1,0:T(8,128)(2,1)} %collective-permute-done.4.refs_3_, bf16[256,1024]{1,0:T(8,128)(2,1)} %collective-permute-done.3.refs_4_, ...), custom_call_target="tpu_custom_call" | custom-call | tf_op jit(solution)/shard_map/project/pallas_call | solution.py:152
  60.3 2.7 %collective-permute-start.18 = (bf16[256,1024]{1,0:T(8,128)(2,1)S(1)}, bf16[256,1024]{1,0:T(8,128)(2,1)S(1)}, u32[]{:S(2)}, u32[]{:S(2)}) collective-permute-start(bf16[256,1024]{1,0:T(8,128)(2,1)S(1)} %collective-permute-done.11.refs_2_), channel_id=1, source_target_pairs={{0,6},{1,7},{2,0},{3,1},{4,2},{5,3},{6,4},{7,5},{8,14},{9,15},{10,... | collective-permute-start | bytes 1572872 | tf_op jit(solution)/shard_map/ppermute | solution.py:28
  63.2 1.7 %collective-permute-start.13 = (bf16[640,256]{1,0:T(8,128)(2,1)S(1)}, bf16[640,256]{1,0:T(8,128)(2,1)S(1)}, u32[]{:S(2)}, u32[]{:S(2)}) collective-permute-start(bf16[640,256]{1,0:T(8,128)(2,1)S(1)} %get-tuple-element.77), channel_id=1, source_target_pairs={{0,16},{8,24},{16,32},{24,40},{32,48},{40,56},{48,0},{56,8},{64,80... | collective-permute-start | bytes 983048 | tf_op jit(solution)/shard_map/ppermute | solution.py:42
  64.9 3.3 %collective-permute-start.14 = (bf16[640,256]{1,0:T(8,128)(2,1)S(1)}, bf16[640,256]{1,0:T(8,128)(2,1)S(1)}, u32[]{:S(2)}, u32[]{:S(2)}) collective-permute-start(bf16[640,256]{1,0:T(8,128)(2,1)S(1)} %get-tuple-element.78), channel_id=1, source_target_pairs={{0,32},{8,40},{16,48},{24,56},{32,0},{40,8},{48,16},{56,24},{64,96... | collective-permute-start | bytes 983048 | tf_op jit(solution)/shard_map/ppermute | solution.py:42
  68.2 0.7 collective-permute-start.15
  68.9 0.1 pad_add_fusion.4.refs_0_
  69.1 3.5 %project.10.refs_6_ = f32[256,768]{1,0:T(8,128)S(1)} custom-call(s32[2]{0:T(128)S(1)} %pad_add_fusion.5.refs_0_, bf16[256,1024]{1,0:T(8,128)(2,1)} %collective-permute-done.10.refs_1_, bf16[256,1024]{1,0:T(8,128)(2,1)S(1)} %collective-permute-done.11.refs_2_, bf16[8192,512]{1,0:T(8,128)(2,1)} %refs_3_.5, bf16[8192,128]{1,0:T(8,128)(2,1)S(1)} %copy-done, ...), custom_call_target="tpu_custom_call" | custom-call | tf_op jit(solution)/shard_map/project/pallas_call | solution.py:152
  72.6 3.4 %project.11 = (bf16[320,256]{1,0:T(8,128)(2,1)S(1)}, bf16[320,256]{1,0:T(8,128)(2,1)S(1)}, bf16[320,256]{1,0:T(8,128)(2,1)S(1)}, bf16[320,256]{1,0:T(8,128)(2,1)...) custom-call(s32[2]{0:T(128)S(1)} %pad_add_fusion.4.refs_0_, ...), custom_call_target="tpu_custom_call" | custom-call | tf_op jit(solution)/shard_map/project/pallas_call | solution.py:152
  76.1 0.8 collective-permute-start.19
  76.9 0.7 collective-permute-start.20
  77.6 1.8 %collective-permute-start.21 = (bf16[320,256]{1,0:T(8,128)(2,1)S(1)}, bf16[320,256]{1,0:T(8,128)(2,1)S(1)}, u32[]{:S(2)}, u32[]{:S(2)}) collective-permute-start(bf16[320,256]{1,0:T(8,128)(2,1)S(1)} %get-tuple-element.86), channel_id=1, source_target_pairs={{0,48},{8,56},{16,0},{24,8},{32,16},{40,24},{48,32},{56,40},{64,11... | collective-permute-start | bytes 491528 | tf_op jit(solution)/shard_map/ppermute | solution.py:42
  79.4 0.1 pad_maximum_fusion
  79.5 0.6 copy-done.11
  80.1 0.1 copy-done.12
  80.2 10.9 %collective-permute-start.16 = (bf16[2560,256]{1,0:T(8,128)(2,1)S(1)}, bf16[2560,256]{1,0:T(8,128)(2,1)S(1)}, u32[]{:S(2)}, u32[]{:S(2)}) collective-permute-start(bf16[2560,256]{1,0:T(8,128)(2,1)S(1)} %pad_maximum_fusion), channel_id=1, source_target_pairs={{0,8},{8,0},{16,24},{24,16},{32,40},{40,32},{48,56},{56,48},{64,72... | collective-permute-start | bytes 3932168 | tf_op jit(solution)/shard_map/ppermute | solution.py:54
  91.1 0.9 collective-permute-start.22
  91.9 3.0 %collective-permute-start.23 = (bf16[320,256]{1,0:T(8,128)(2,1)S(1)}, bf16[320,256]{1,0:T(8,128)(2,1)S(1)}, u32[]{:S(2)}, u32[]{:S(2)}) collective-permute-start(bf16[320,256]{1,0:T(8,128)(2,1)S(1)} %get-tuple-element.88), channel_id=1, source_target_pairs={{0,80},{8,88},{16,96},{24,104},{32,112},{40,120},{48,64},{56,72},{... | collective-permute-start | bytes 491528 | tf_op jit(solution)/shard_map/ppermute | solution.py:42
  94.9 2.4 %collective-permute-start.24 = (bf16[320,256]{1,0:T(8,128)(2,1)S(1)}, bf16[320,256]{1,0:T(8,128)(2,1)S(1)}, u32[]{:S(2)}, u32[]{:S(2)}) collective-permute-start(bf16[320,256]{1,0:T(8,128)(2,1)S(1)} %get-tuple-element.89), channel_id=1, source_target_pairs={{0,96},{8,104},{16,112},{24,120},{32,64},{40,72},{48,80},{56,88},{... | collective-permute-start | bytes 491528 | tf_op jit(solution)/shard_map/ppermute | solution.py:42
  97.3 3.1 %collective-permute-start.25 = (bf16[320,256]{1,0:T(8,128)(2,1)S(1)}, bf16[320,256]{1,0:T(8,128)(2,1)S(1)}, u32[]{:S(2)}, u32[]{:S(2)}) collective-permute-start(bf16[320,256]{1,0:T(8,128)(2,1)S(1)} %get-tuple-element.90), channel_id=1, source_target_pairs={{0,112},{8,120},{16,64},{24,72},{32,80},{40,88},{48,96},{56,104},{... | collective-permute-start | bytes 491528 | tf_op jit(solution)/shard_map/ppermute | solution.py:42
  100.5 1.2 collective-permute-start.26
  101.7 0.9 collective-permute-done.23.refs_10_
  102.6 4.7 %collective-permute-done.24.refs_11_ = bf16[320,256]{1,0:T(8,128)(2,1)S(1)} collective-permute-done((bf16[320,256]{1,0:T(8,128)(2,1)S(1)}, bf16[320,256]{1,0:T(8,128)(2,1)S(1)}, u32[]{:S(2)}, u32[]{:S(2)}) %collective-permute-start.24) | collective-permute-done | bytes 163872 | tf_op jit(solution)/shard_map/ppermute | solution.py:42
  107.3 2.5 %collective-permute-done.25.refs_12_ = bf16[320,256]{1,0:T(8,128)(2,1)S(1)} collective-permute-done((bf16[320,256]{1,0:T(8,128)(2,1)S(1)}, bf16[320,256]{1,0:T(8,128)(2,1)S(1)}, u32[]{:S(2)}, u32[]{:S(2)}) %collective-permute-start.25) | collective-permute-done | bytes 163872 | tf_op jit(solution)/shard_map/ppermute | solution.py:42
  109.9 0.9 collective-permute-start.27
  110.8 1.7 %collective-permute-done.27.refs_14_ = bf16[1280,256]{1,0:T(8,128)(2,1)S(1)} collective-permute-done((bf16[1280,256]{1,0:T(8,128)(2,1)S(1)}, bf16[1280,256]{1,0:T(8,128)(2,1)S(1)}, u32[]{:S(2)}, u32[]{:S(2)}) %collective-permute-start.27) | collective-permute-done | bytes 655392 | tf_op jit(solution)/shard_map/ppermute | solution.py:54
  112.5 0.8 copy-done.22
  113.3 1.1 copy-done.13
  114.4 27.8 %attend.1 = bf16[512,512]{1,0:T(8,128)(2,1)} custom-call(s32[19]{0:T(128)} %pad_add_fusion.1.info, s32[256]{0:T(256)} %reshape.65.old_map, bf16[640,256]{1,0:T(8,128)(2,1)} %copy-done.9, bf16[640,256]{1,0:T(8,128)(2,1)} %copy-done.10, bf16[640,256]{1,0:T(8,128)(2,1)} %copy-done.11, bf16[640,256]{1,0:T(8,128)(2,1)} %copy-done.12, ...), custom_call_target="tpu_custom_call" | custom-call | tf_op jit(solution)/shard_map/attend/pallas_call | solution.py:235
  (82 shorter events, 0.6 us)
Async XLA Ops:
  0.0 6.2 %copy-start.24 = (s32[16,16]{1,0:T(8,128)S(1)}, s32[16,16]{1,0:T(8,128)}, u32[]{:S(2)}) copy-start(s32[16,16]{1,0:T(8,128)} %param.8) | copy-start | bytes 3076
  0.0 11.5 %copy-start.23 = (s32[16,16]{1,0:T(8,128)S(1)}, s32[16,16]{1,0:T(8,128)}, u32[]{:S(2)}) copy-start(s32[16,16]{1,0:T(8,128)} %param.7) | copy-start | bytes 3076
  1.3 21.0 %copy-start.3 = (bf16[16,1,16,1024]{3,2,1,0:T(8,128)(2,1)}, bf16[16,1,16,1024]{3,2,1,0:T(8,128)(2,1)S(1)}, u32[]{:S(2)}) copy-start(bf16[16,1,16,1024]{3,2,1,0:T(8,128)(2,1)S(1)} %get-tuple-element.94) | copy-start | bytes 1572868
  1.3 21.1 %copy-start = (bf16[8192,128]{1,0:T(8,128)(2,1)S(1)}, bf16[8192,128]{1,0:T(8,128)(2,1)}, u32[]{:S(2)}) copy-start(bf16[8192,128]{1,0:T(8,128)(2,1)} %refs_4_.7) | copy-start | bytes 6291460
  1.3 15.0 %collective-permute-start.2 = (bf16[256,1024]{1,0:T(8,128)(2,1)S(1)}, bf16[256,1024]{1,0:T(8,128)(2,1)}, u32[]{:S(2)}, u32[]{:S(2)}) collective-permute-start(bf16[256,1024]{1,0:T(8,128)(2,1)S(1)} %bitcast.29), channel_id=1, source_target_pairs={{0,1},{1,0},{2,3},{3,2},{4,5},{5,4},{6,7},{7,6},{8,9},{9,8},{10,11... | collective-permute-start | bytes 1572872 | tf_op jit(solution)/shard_map/ppermute | solution.py:32
  3.5 12.8 %collective-permute-start.1 = (bf16[256,1024]{1,0:T(8,128)(2,1)S(1)}, bf16[256,1024]{1,0:T(8,128)(2,1)}, u32[]{:S(2)}, u32[]{:S(2)}) collective-permute-start(bf16[256,1024]{1,0:T(8,128)(2,1)S(1)} %bitcast.30), channel_id=1, source_target_pairs={{0,6},{1,7},{2,0},{3,1},{4,2},{5,3},{6,4},{7,5},{8,14},{9,15},{10,... | collective-permute-start | bytes 1572872 | tf_op jit(solution)/shard_map/ppermute | solution.py:28
  6.0 13.5 %collective-permute-start = (bf16[256,1024]{1,0:T(8,128)(2,1)S(1)}, bf16[256,1024]{1,0:T(8,128)(2,1)}, u32[]{:S(2)}, u32[]{:S(2)}) collective-permute-start(bf16[256,1024]{1,0:T(8,128)(2,1)S(1)} %bitcast.31), channel_id=1, source_target_pairs={{0,2},{1,3},{2,4},{3,5},{4,6},{5,7},{6,0},{7,1},{8,10},{9,11},{10,... | collective-permute-start | bytes 1572872 | tf_op jit(solution)/shard_map/ppermute | solution.py:28
  6.0 23.4 %collective-permute-start.3 = (bf16[256,1024]{1,0:T(8,128)(2,1)S(1)}, bf16[256,1024]{1,0:T(8,128)(2,1)}, u32[]{:S(2)}, u32[]{:S(2)}) collective-permute-start(bf16[256,1024]{1,0:T(8,128)(2,1)S(1)} %bitcast.25), channel_id=1, source_target_pairs={{0,1},{1,0},{2,3},{3,2},{4,5},{5,4},{6,7},{7,6},{8,9},{9,8},{10,11... | collective-permute-start | bytes 1572872 | tf_op jit(solution)/shard_map/ppermute | solution.py:32
  19.5 12.8 %collective-permute-start.5 = (bf16[256,1024]{1,0:T(8,128)(2,1)}, bf16[256,1024]{1,0:T(8,128)(2,1)}, u32[]{:S(2)}, u32[]{:S(2)}) collective-permute-start(bf16[256,1024]{1,0:T(8,128)(2,1)} %collective-permute-done.2.refs_4_), channel_id=1, source_target_pairs={{0,2},{1,3},{2,4},{3,5},{4,6},{5,7},{6,0},{7,1},{8,10},{9,11},{10,... | collective-permute-start | bytes 1572872 | tf_op jit(solution)/shard_map/ppermute | solution.py:28
  19.5 12.8 %collective-permute-start.6 = (bf16[256,1024]{1,0:T(8,128)(2,1)}, bf16[256,1024]{1,0:T(8,128)(2,1)}, u32[]{:S(2)}, u32[]{:S(2)}) collective-permute-start(bf16[256,1024]{1,0:T(8,128)(2,1)} %collective-permute-done.1.refs_3_), channel_id=1, source_target_pairs={{0,6},{1,7},{2,0},{3,1},{4,2},{5,3},{6,4},{7,5},{8,14},{9,15},{10,... | collective-permute-start | bytes 1572872 | tf_op jit(solution)/shard_map/ppermute | solution.py:28
  22.3 15.1 %collective-permute-start.8 = (bf16[256,1024]{1,0:T(8,128)(2,1)}, bf16[256,1024]{1,0:T(8,128)(2,1)}, u32[]{:S(2)}, u32[]{:S(2)}) collective-permute-start(bf16[256,1024]{1,0:T(8,128)(2,1)} %collective-permute-done.1.refs_3_), channel_id=1, source_target_pairs={{0,1},{1,0},{2,3},{3,2},{4,5},{5,4},{6,7},{7,6},{8,9},{9,8},{10,11... | collective-permute-start | bytes 1572872 | tf_op jit(solution)/shard_map/ppermute | solution.py:32
  22.5 1.0 copy-start.4
  29.5 13.9 %collective-permute-start.4 = (bf16[256,1024]{1,0:T(8,128)(2,1)S(1)}, bf16[256,1024]{1,0:T(8,128)(2,1)}, u32[]{:S(2)}, u32[]{:S(2)}) collective-permute-start(bf16[256,1024]{1,0:T(8,128)(2,1)S(1)} %bitcast.26), channel_id=1, source_target_pairs={{0,6},{1,7},{2,0},{3,1},{4,2},{5,3},{6,4},{7,5},{8,14},{9,15},{10,... | collective-permute-start | bytes 1572872 | tf_op jit(solution)/shard_map/ppermute | solution.py:28
  32.3 11.0 %collective-permute-start.7 = (bf16[256,1024]{1,0:T(8,128)(2,1)}, bf16[256,1024]{1,0:T(8,128)(2,1)}, u32[]{:S(2)}, u32[]{:S(2)}) collective-permute-start(bf16[256,1024]{1,0:T(8,128)(2,1)} %collective-permute-done.5.refs_1_), channel_id=1, source_target_pairs={{0,2},{1,3},{2,4},{3,5},{4,6},{5,7},{6,0},{7,1},{8,10},{9,11},{10,... | collective-permute-start | bytes 1572872 | tf_op jit(solution)/shard_map/ppermute | solution.py:28
  32.4 21.9 %collective-permute-start.12 = (bf16[256,1024]{1,0:T(8,128)(2,1)S(1)}, bf16[256,1024]{1,0:T(8,128)(2,1)}, u32[]{:S(2)}, u32[]{:S(2)}) collective-permute-start(bf16[256,1024]{1,0:T(8,128)(2,1)S(1)} %bitcast.27), channel_id=1, source_target_pairs={{0,2},{1,3},{2,4},{3,5},{4,6},{5,7},{6,0},{7,1},{8,10},{9,11},{10,... | collective-permute-start | bytes 1572872 | tf_op jit(solution)/shard_map/ppermute | solution.py:28
  42.4 0.9 copy-start.1
  43.3 16.9 %collective-permute-start.11 = (bf16[256,1024]{1,0:T(8,128)(2,1)}, bf16[256,1024]{1,0:T(8,128)(2,1)S(1)}, u32[]{:S(2)}, u32[]{:S(2)}) collective-permute-start(bf16[256,1024]{1,0:T(8,128)(2,1)} %collective-permute-done.4.refs_3_), channel_id=1, source_target_pairs={{0,1},{1,0},{2,3},{3,2},{4,5},{5,4},{6,7},{7,6},{8,9},{9,8},{10,11... | collective-permute-start | bytes 1572872 | tf_op jit(solution)/shard_map/ppermute | solution.py:32
  44.9 15.4 %collective-permute-start.10 = (bf16[256,1024]{1,0:T(8,128)(2,1)}, bf16[256,1024]{1,0:T(8,128)(2,1)}, u32[]{:S(2)}, u32[]{:S(2)}) collective-permute-start(bf16[256,1024]{1,0:T(8,128)(2,1)} %collective-permute-done.4.refs_3_), channel_id=1, source_target_pairs={{0,6},{1,7},{2,0},{3,1},{4,2},{5,3},{6,4},{7,5},{8,14},{9,15},{10,... | collective-permute-start | bytes 1572872 | tf_op jit(solution)/shard_map/ppermute | solution.py:28
  47.4 1.1 copy-start.2
  48.5 0.9 copy-start.6
  51.6 8.7 %collective-permute-start.9 = (bf16[512,256]{1,0:T(8,128)(2,1)S(1)}, bf16[512,256]{1,0:T(8,128)(2,1)S(1)}, u32[]{:S(2)}, u32[]{:S(2)}) collective-permute-start(bf16[512,256]{1,0:T(8,128)(2,1)S(1)} %get-tuple-element.64), channel_id=1, source_target_pairs={{0,64},{8,72},{16,80},{24,88},{32,96},{40,104},{48,112},{56,120},{... | collective-permute-start | bytes 786440 | tf_op jit(solution)/shard_map/ppermute | solution.py:42
  54.3 18.3 %collective-permute-start.17 = (bf16[256,1024]{1,0:T(8,128)(2,1)}, bf16[256,1024]{1,0:T(8,128)(2,1)S(1)}, u32[]{:S(2)}, u32[]{:S(2)}) collective-permute-start(bf16[256,1024]{1,0:T(8,128)(2,1)} %collective-permute-done.3.refs_4_), channel_id=1, source_target_pairs={{0,2},{1,3},{2,4},{3,5},{4,6},{5,7},{6,0},{7,1},{8,10},{9,11},{10,... | collective-permute-start | bytes 1572872 | tf_op jit(solution)/shard_map/ppermute | solution.py:28
  60.3 12.3 %collective-permute-start.18 = (bf16[256,1024]{1,0:T(8,128)(2,1)S(1)}, bf16[256,1024]{1,0:T(8,128)(2,1)S(1)}, u32[]{:S(2)}, u32[]{:S(2)}) collective-permute-start(bf16[256,1024]{1,0:T(8,128)(2,1)S(1)} %collective-permute-done.11.refs_2_), channel_id=1, source_target_pairs={{0,6},{1,7},{2,0},{3,1},{4,2},{5,3},{6,4},{7,5},{8,14},{9,15},{10,... | collective-permute-start | bytes 1572872 | tf_op jit(solution)/shard_map/ppermute | solution.py:28
  63.1 16.3 %copy-start.9 = (bf16[640,256]{1,0:T(8,128)(2,1)}, bf16[640,256]{1,0:T(8,128)(2,1)S(1)}, u32[]{:S(2)}) copy-start(bf16[640,256]{1,0:T(8,128)(2,1)S(1)} %pad_maximum_fusion.6.refs_0_) | copy-start | bytes 983044
  63.2 14.4 %collective-permute-start.13 = (bf16[640,256]{1,0:T(8,128)(2,1)S(1)}, bf16[640,256]{1,0:T(8,128)(2,1)S(1)}, u32[]{:S(2)}, u32[]{:S(2)}) collective-permute-start(bf16[640,256]{1,0:T(8,128)(2,1)S(1)} %get-tuple-element.77), channel_id=1, source_target_pairs={{0,16},{8,24},{16,32},{24,40},{32,48},{40,56},{48,0},{56,8},{64,80... | collective-permute-start | bytes 983048 | tf_op jit(solution)/shard_map/ppermute | solution.py:42
  64.9 14.5 %collective-permute-start.14 = (bf16[640,256]{1,0:T(8,128)(2,1)S(1)}, bf16[640,256]{1,0:T(8,128)(2,1)S(1)}, u32[]{:S(2)}, u32[]{:S(2)}) collective-permute-start(bf16[640,256]{1,0:T(8,128)(2,1)S(1)} %get-tuple-element.78), channel_id=1, source_target_pairs={{0,32},{8,40},{16,48},{24,56},{32,0},{40,8},{48,16},{56,24},{64,96... | collective-permute-start | bytes 983048 | tf_op jit(solution)/shard_map/ppermute | solution.py:42
  68.2 11.2 %collective-permute-start.15 = (bf16[640,256]{1,0:T(8,128)(2,1)S(1)}, bf16[640,256]{1,0:T(8,128)(2,1)S(1)}, u32[]{:S(2)}, u32[]{:S(2)}) collective-permute-start(bf16[640,256]{1,0:T(8,128)(2,1)S(1)} %get-tuple-element.79), channel_id=1, source_target_pairs={{0,48},{8,56},{16,0},{24,8},{32,16},{40,24},{48,32},{56,40},{64,11... | collective-permute-start | bytes 983048 | tf_op jit(solution)/shard_map/ppermute | solution.py:42
  69.1 3.5 %copy-start.7 = (f32[256,128]{1,0:T(8,128)S(1)}, f32[256,128]{1,0:T(8,128)}, u32[]{:S(2)}) copy-start(f32[256,128]{1,0:T(8,128)} %get-tuple-element.81.refs_8_) | copy-start | bytes 393220
  69.1 3.6 %copy-start.8 = (f32[256,128]{1,0:T(8,128)S(1)}, f32[256,128]{1,0:T(8,128)}, u32[]{:S(2)}) copy-start(f32[256,128]{1,0:T(8,128)} %get-tuple-element.82.refs_9_) | copy-start | bytes 393220
  76.1 24.4 %copy-start.5 = (bf16[320,256]{1,0:T(8,128)(2,1)}, bf16[320,256]{1,0:T(8,128)(2,1)S(1)}, u32[]{:S(2)}) copy-start(bf16[320,256]{1,0:T(8,128)(2,1)S(1)} %get-tuple-element.83.refs_5_) | copy-start | bytes 491524
  76.1 15.9 %collective-permute-start.19 = (bf16[320,256]{1,0:T(8,128)(2,1)S(1)}, bf16[320,256]{1,0:T(8,128)(2,1)S(1)}, u32[]{:S(2)}, u32[]{:S(2)}) collective-permute-start(bf16[320,256]{1,0:T(8,128)(2,1)S(1)} %get-tuple-element.84), channel_id=1, source_target_pairs={{0,16},{8,24},{16,32},{24,40},{32,48},{40,56},{48,0},{56,8},{64,80... | collective-permute-start | bytes 491528 | tf_op jit(solution)/shard_map/ppermute | solution.py:42
  76.9 18.1 %collective-permute-start.20 = (bf16[320,256]{1,0:T(8,128)(2,1)S(1)}, bf16[320,256]{1,0:T(8,128)(2,1)S(1)}, u32[]{:S(2)}, u32[]{:S(2)}) collective-permute-start(bf16[320,256]{1,0:T(8,128)(2,1)S(1)} %get-tuple-element.85), channel_id=1, source_target_pairs={{0,32},{8,40},{16,48},{24,56},{32,0},{40,8},{48,16},{56,24},{64,96... | collective-permute-start | bytes 491528 | tf_op jit(solution)/shard_map/ppermute | solution.py:42
  77.6 1.9 %copy-start.10 = (bf16[640,256]{1,0:T(8,128)(2,1)}, bf16[640,256]{1,0:T(8,128)(2,1)S(1)}, u32[]{:S(2)}) copy-start(bf16[640,256]{1,0:T(8,128)(2,1)S(1)} %collective-permute-done.13.refs_1_) | copy-start | bytes 983044
  77.6 19.7 %collective-permute-start.21 = (bf16[320,256]{1,0:T(8,128)(2,1)S(1)}, bf16[320,256]{1,0:T(8,128)(2,1)S(1)}, u32[]{:S(2)}, u32[]{:S(2)}) collective-permute-start(bf16[320,256]{1,0:T(8,128)(2,1)S(1)} %get-tuple-element.86), channel_id=1, source_target_pairs={{0,48},{8,56},{16,0},{24,8},{32,16},{40,24},{48,32},{56,40},{64,11... | collective-permute-start | bytes 491528 | tf_op jit(solution)/shard_map/ppermute | solution.py:42
  79.4 0.7 copy-start.11
  79.4 0.8 copy-start.12
  80.2 32.3 %collective-permute-start.16 = (bf16[2560,256]{1,0:T(8,128)(2,1)S(1)}, bf16[2560,256]{1,0:T(8,128)(2,1)S(1)}, u32[]{:S(2)}, u32[]{:S(2)}) collective-permute-start(bf16[2560,256]{1,0:T(8,128)(2,1)S(1)} %pad_maximum_fusion), channel_id=1, source_target_pairs={{0,8},{8,0},{16,24},{24,16},{32,40},{40,32},{48,56},{56,48},{64,72... | collective-permute-start | bytes 3932168 | tf_op jit(solution)/shard_map/ppermute | solution.py:54
  91.1 9.4 %collective-permute-start.22 = (bf16[320,256]{1,0:T(8,128)(2,1)S(1)}, bf16[320,256]{1,0:T(8,128)(2,1)S(1)}, u32[]{:S(2)}, u32[]{:S(2)}) collective-permute-start(bf16[320,256]{1,0:T(8,128)(2,1)S(1)} %get-tuple-element.87), channel_id=1, source_target_pairs={{0,64},{8,72},{16,80},{24,88},{32,96},{40,104},{48,112},{56,120},{... | collective-permute-start | bytes 491528 | tf_op jit(solution)/shard_map/ppermute | solution.py:42
  91.9 17.9 %copy-start.14 = (bf16[320,256]{1,0:T(8,128)(2,1)}, bf16[320,256]{1,0:T(8,128)(2,1)S(1)}, u32[]{:S(2)}) copy-start(bf16[320,256]{1,0:T(8,128)(2,1)S(1)} %collective-permute-done.19.refs_6_) | copy-start | bytes 491524
  91.9 10.6 %collective-permute-start.23 = (bf16[320,256]{1,0:T(8,128)(2,1)S(1)}, bf16[320,256]{1,0:T(8,128)(2,1)S(1)}, u32[]{:S(2)}, u32[]{:S(2)}) collective-permute-start(bf16[320,256]{1,0:T(8,128)(2,1)S(1)} %get-tuple-element.88), channel_id=1, source_target_pairs={{0,80},{8,88},{16,96},{24,104},{32,112},{40,120},{48,64},{56,72},{... | collective-permute-start | bytes 491528 | tf_op jit(solution)/shard_map/ppermute | solution.py:42
  94.9 14.9 %copy-start.15 = (bf16[320,256]{1,0:T(8,128)(2,1)}, bf16[320,256]{1,0:T(8,128)(2,1)S(1)}, u32[]{:S(2)}) copy-start(bf16[320,256]{1,0:T(8,128)(2,1)S(1)} %collective-permute-done.20.refs_7_) | copy-start | bytes 491524
  94.9 12.4 %collective-permute-start.24 = (bf16[320,256]{1,0:T(8,128)(2,1)S(1)}, bf16[320,256]{1,0:T(8,128)(2,1)S(1)}, u32[]{:S(2)}, u32[]{:S(2)}) collective-permute-start(bf16[320,256]{1,0:T(8,128)(2,1)S(1)} %get-tuple-element.89), channel_id=1, source_target_pairs={{0,96},{8,104},{16,112},{24,120},{32,64},{40,72},{48,80},{56,88},{... | collective-permute-start | bytes 491528 | tf_op jit(solution)/shard_map/ppermute | solution.py:42
  97.3 12.6 %copy-start.16 = (bf16[320,256]{1,0:T(8,128)(2,1)}, bf16[320,256]{1,0:T(8,128)(2,1)S(1)}, u32[]{:S(2)}) copy-start(bf16[320,256]{1,0:T(8,128)(2,1)S(1)} %collective-permute-done.21.refs_8_) | copy-start | bytes 491524
  97.3 12.5 %collective-permute-start.25 = (bf16[320,256]{1,0:T(8,128)(2,1)S(1)}, bf16[320,256]{1,0:T(8,128)(2,1)S(1)}, u32[]{:S(2)}, u32[]{:S(2)}) collective-permute-start(bf16[320,256]{1,0:T(8,128)(2,1)S(1)} %get-tuple-element.90), channel_id=1, source_target_pairs={{0,112},{8,120},{16,64},{24,72},{32,80},{40,88},{48,96},{56,104},{... | collective-permute-start | bytes 491528 | tf_op jit(solution)/shard_map/ppermute | solution.py:42
  100.5 12.0 %copy-start.17 = (bf16[320,256]{1,0:T(8,128)(2,1)}, bf16[320,256]{1,0:T(8,128)(2,1)S(1)}, u32[]{:S(2)}) copy-start(bf16[320,256]{1,0:T(8,128)(2,1)S(1)} %collective-permute-done.22.refs_9_) | copy-start | bytes 491524
  100.5 10.3 %collective-permute-start.26 = (bf16[1280,256]{1,0:T(8,128)(2,1)S(1)}, bf16[1280,256]{1,0:T(8,128)(2,1)S(1)}, u32[]{:S(2)}, u32[]{:S(2)}) collective-permute-start(bf16[1280,256]{1,0:T(8,128)(2,1)S(1)} %pad_maximum_fusion.1), channel_id=1, source_target_pairs={{0,8},{8,0},{16,24},{24,16},{32,40},{40,32},{48,56},{56,48},{64,72... | collective-permute-start | bytes 1966088 | tf_op jit(solution)/shard_map/ppermute | solution.py:54
  102.6 9.9 %copy-start.18 = (bf16[320,256]{1,0:T(8,128)(2,1)}, bf16[320,256]{1,0:T(8,128)(2,1)S(1)}, u32[]{:S(2)}) copy-start(bf16[320,256]{1,0:T(8,128)(2,1)S(1)} %collective-permute-done.23.refs_10_) | copy-start | bytes 491524
  107.3 5.2 %copy-start.19 = (bf16[320,256]{1,0:T(8,128)(2,1)}, bf16[320,256]{1,0:T(8,128)(2,1)S(1)}, u32[]{:S(2)}) copy-start(bf16[320,256]{1,0:T(8,128)(2,1)S(1)} %collective-permute-done.24.refs_11_) | copy-start | bytes 491524
  109.8 2.7 %copy-start.20 = (bf16[320,256]{1,0:T(8,128)(2,1)}, bf16[320,256]{1,0:T(8,128)(2,1)S(1)}, u32[]{:S(2)}) copy-start(bf16[320,256]{1,0:T(8,128)(2,1)S(1)} %collective-permute-done.25.refs_12_) | copy-start | bytes 491524
  109.9 2.6 %collective-permute-start.27 = (bf16[1280,256]{1,0:T(8,128)(2,1)S(1)}, bf16[1280,256]{1,0:T(8,128)(2,1)S(1)}, u32[]{:S(2)}, u32[]{:S(2)}) collective-permute-start(bf16[1280,256]{1,0:T(8,128)(2,1)S(1)} %pad_maximum_fusion.2), channel_id=1, source_target_pairs={{0,8},{8,0},{16,24},{24,16},{32,40},{40,32},{48,56},{56,48},{64,72... | collective-permute-start | bytes 1966088 | tf_op jit(solution)/shard_map/ppermute | solution.py:54
  110.8 1.8 %copy-start.21 = (bf16[1280,256]{1,0:T(8,128)(2,1)}, bf16[1280,256]{1,0:T(8,128)(2,1)S(1)}, u32[]{:S(2)}) copy-start(bf16[1280,256]{1,0:T(8,128)(2,1)S(1)} %collective-permute-done.26.refs_13_) | copy-start | bytes 1966084
  112.5 0.8 copy-start.22
  113.3 1.1 copy-start.13

commit v4 on v3

--- a/solution.py
+++ b/solution.py
@@ -88,8 +88,8 @@
         @pl.when(step == i)
         def add(i=i, parts=parts):
             block = parts[0][...] if len(parts) == 1 else jnp.concatenate([p[...] for p in parts], axis=0)
-            for lo, hi, w in ((0, 512, wq), (512, 640, wk), (640, 768, wv)):
-                value = dot(block, w[...])
+            for lo, hi, w in ((0, 512, wq[...]), (512, 768, jnp.concatenate([wk[...], wv[...]], axis=1))):
+                value = dot(block, w)
                 if i > 0:
                     value = value + acc[:, lo:hi]
                 elif has_acc:
@@ -295,24 +295,24 @@
     left = shift_x(early, 1)
     right = shift_x(early, -1)
     across = swap_y(early)
-    late_across = swap_y(after(late, early))
-    left, right, across, send_info, attend_info, old_flat, *tables = together(
-        left, right, across, send_info, attend_info, old_flat, *tables
+    late, left, right, across, send_info, attend_info, old_flat, *tables = together(
+        late, left, right, across, send_info, attend_info, old_flat, *tables
     )
     left_across = shift_x(across, 1)
     far = shift_x(right, -1)
     right_across = swap_y(right)
+    late_across = swap_y(late)
     total = project(features[:4], [(early,), (left,), (right,), (across,)], weights)
-    late_across, total = together(late_across, total)
-    late = after(late, total)
+    left_across, far, late = together(left_across, far, after(late, total))
     late_right = shift_x(late, -1)
-    left_across, far = together(left_across, far)
     far_across = shift_x(left_across, 1)
-    late_left = shift_x(after(late, left_across), 1)
+    right_across = after(right_across, late)
+    late_left = shift_x(after(late, right_across), 1)
     total = project(features[4:7], [(left_across,), (far,), (right_across,)], weights, total)
-    late_right, far_across, total = together(late_right, far_across, total)
+    late_right, late_across = together(late_right, late_across)
     late_far = shift_x(late_right, -1)
     late_right_across = swap_y(late_right)
+    far_across = after(far_across, late_right)
     sent = project(features[7:], [(far_across,)], weights, total, (send_info, *tables[:2]), joint=True)
     partner = shift_ctx(sent[4], 1, 0)
     late_across, late_left = together(late_across, late_left, sent[0])[:2]
@@ -321,14 +321,14 @@
     total = project(features[:4], blocks, weights)
     late_far, late_right_across, total = together(late_far, late_right_across, total)
     late_far_across = shift_x(late_right_across, -1)
-    partner = after(partner, late_right_across, late_far)
+    total = project(features[5:7], [(late_far,), (late_right_across,)], weights, total)
+    partner, total = together(partner, total)
     early_parts = [
         jnp.concatenate([sent[dz], partner[:ROWS], partner[ROWS + dz * 4 * W : ROWS + (dz + 1) * 4 * W]], axis=0)
         for dz in range(4)
     ]
     early_parts = list(together(*early_parts))
     early_parts[1:] = [shift_ctx(early_parts[dz], 0, dz) for dz in range(1, 4)]
-    total = project(features[5:7], [(late_far,), (late_right_across,)], weights, total)
     last = jnp.stack([features[4], features[7]])
     tail = [(late_left_across,), (late_far_across,)]
     sent = project(last, tail, weights, total, (send_info, *tables[2:]))

time: 143 us -> 144 us (level)
  waiting for transfers between devices: 19.9 us -> 22.1 us
  Pallas kernels: 53.8 us -> 52.2 us
    ppermute x4, waiting for transfers between devices: 4.12 us -> 9.37 us  [swap_y(): return lax.ppermute(block, 'tp', [(i, i ^ 1) for i in range(8)])]
    ppermute x10, waiting for transfers between devices: 5.92 us -> 2.94 us  [shift_x(): return lax.ppermute(block, 'tp', perm)]
    ppermute x3, starting transfers between devices: 12.9 us -> 10.4 us  [swap_core(): return lax.ppermute(block, 'ctx', [(i, i ^ 1) for i in range(16)])]
    ppermute x11, starting transfers between devices: 21.1 us -> 23.1 us  [shift_ctx(): return lax.ppermute(block, 'ctx', perm)]
    pallas_call x6, Pallas kernels: 26 us -> 24.4 us  [project(): pl.pallas_call(functools.partial(project_kernel, groups, acc is not None,...]
    unnamed x50 -> x54, local copies, waits for them, and re-layouts: 6.62 us -> 6.37 us
  transfers between devices with their start and end apart: 28 -> 28, of which waited for: 7 -> 8; matrix products, arithmetic and copies ran while one was open for 4% -> 4% of each run, Pallas kernels for 18% -> 17%
where the time goes in v4:
time: 144 us
  Pallas kernels  52.2 us (36%)
  starting transfers between devices  50.2 us (35%)
  waiting for transfers between devices  22.1 us (15%)
  local copies, waits for them, and re-layouts  9.18 us (6%)
  between operations  5.43 us (4%)
  other arithmetic  4.5 us (3%)
    pallas_call x1, Pallas kernels, attend(): pl.pallas_call(attend_kernel, out_shape=jax.ShapeDtypeStruct((512, 512),...  27.8 us
    pallas_call x6, Pallas kernels, project(): pl.pallas_call(functools.partial(project_kernel, groups, acc is not None,...  24.4 us
    ppermute x11, starting transfers between devices, shift_ctx(): return lax.ppermute(block, 'ctx', perm)  23.1 us
    ppermute x10, starting transfers between devices, shift_x(): return lax.ppermute(block, 'tp', perm)  12.2 us
    ppermute x3, starting transfers between devices, swap_core(): return lax.ppermute(block, 'ctx', [(i, i ^ 1) for i in range(16)])  10.4 us
    ppermute x4, waiting for transfers between devices, swap_y(): return lax.ppermute(block, 'tp', [(i, i ^ 1) for i in range(8)])  9.37 us
    ppermute x11, waiting for transfers between devices, shift_ctx(): return lax.ppermute(block, 'ctx', perm)  8.1 us
    unnamed x54, local copies, waits for them, and re-layouts  6.37 us
  transfers between devices with their start and end apart: 28, of which 8 were waited for; matrix products, arithmetic and copies ran while one was open for 4% of the time, Pallas kernels for 17%

profile of v4, /device:TPU:1, one launch (start us, length us, event | category | flops | bytes accessed | tf_op | source)
XLA Modules:
  0.0 143.6 jit_solution(5401819841859244516)
XLA Ops:
  0.0 1.3 fusion.5
  1.3 2.1 %collective-permute-start = (bf16[256,1024]{1,0:T(8,128)(2,1)S(1)}, bf16[256,1024]{1,0:T(8,128)(2,1)}, u32[]{:S(2)}, u32[]{:S(2)}) collective-permute-start(bf16[256,1024]{1,0:T(8,128)(2,1)S(1)} %bitcast.29), channel_id=1, source_target_pairs={{0,2},{1,3},{2,4},{3,5},{4,6},{5,7},{6,0},{7,1},{8,10},{9,11},{10,... | collective-permute-start | bytes 1572872 | tf_op jit(solution)/shard_map/ppermute | solution.py:28
  3.4 1.4 collective-permute-start.1
  4.8 1.4 collective-permute-start.2
  6.2 0.6 fusion.7
  11.9 0.1 compare_reduce_fusion.1
  12.0 0.1 select_reduce_fusion.1
  12.2 0.1 compare_reduce_fusion
  12.3 0.1 select_reduce_fusion
  12.7 0.6 pad_add_fusion.1.info
  13.3 0.7 reshape.65.old_map
  13.9 0.1 convert_element_type.25
  14.0 0.1 convert_element_type.23
  14.1 1.0 fusion.4
  15.1 0.8 pad_maximum_fusion.7
  15.9 0.9 pad_maximum_fusion.9
  16.7 0.3 collective-permute-done.2.refs_4_
  17.1 0.2 collective-permute-start.3
  17.2 2.5 %collective-permute-start.4 = (bf16[256,1024]{1,0:T(8,128)(2,1)}, bf16[256,1024]{1,0:T(8,128)(2,1)}, u32[]{:S(2)}, u32[]{:S(2)}) collective-permute-start(bf16[256,1024]{1,0:T(8,128)(2,1)} %collective-permute-done.1.refs_3_), channel_id=1, source_target_pairs={{0,6},{1,7},{2,0},{3,1},{4,2},{5,3},{6,4},{7,5},{8,14},{9,15},{10,... | collective-permute-start | bytes 1572872 | tf_op jit(solution)/shard_map/ppermute | solution.py:28
  19.7 0.1 pad_add_fusion.2.refs_0_
  19.8 1.5 %collective-permute-start.8 = (bf16[256,1024]{1,0:T(8,128)(2,1)}, bf16[256,1024]{1,0:T(8,128)(2,1)S(1)}, u32[]{:S(2)}, u32[]{:S(2)}) collective-permute-start(bf16[256,1024]{1,0:T(8,128)(2,1)} %collective-permute-done.1.refs_3_), channel_id=1, source_target_pairs={{0,1},{1,0},{2,3},{3,2},{4,5},{5,4},{6,7},{7,6},{8,9},{9,8},{10,11... | collective-permute-start | bytes 1572872 | tf_op jit(solution)/shard_map/ppermute | solution.py:32
  21.3 0.1 collective-permute-start.7
  21.4 1.0 copy-done.2
  22.4 5.5 %project.6.refs_7_ = f32[256,768]{1,0:T(8,128)S(1)} custom-call(s32[4]{0:T(128)S(1)} %pad_add_fusion.2.refs_0_, bf16[256,1024]{1,0:T(8,128)(2,1)S(1)} %bitcast.32, bf16[256,1024]{1,0:T(8,128)(2,1)} %collective-permute-done.refs_2_, bf16[256,1024]{1,0:T(8,128)(2,1)} %collective-permute-done.1.refs_3_, bf16[256,1024]{1,0:T(8,128)(2,1)} %collective-permute-done.2.refs_4_, ...), custom_call_target="tpu_custom_call" | custom-call | tf_op jit(solution)/shard_map/project/pallas_call | solution.py:152
  28.0 1.9 %collective-permute-done.3.refs_1_ = bf16[256,1024]{1,0:T(8,128)(2,1)} collective-permute-done((bf16[256,1024]{1,0:T(8,128)(2,1)}, bf16[256,1024]{1,0:T(8,128)(2,1)}, u32[]{:S(2)}, u32[]{:S(2)}) %collective-permute-start.3) | collective-permute-done | bytes 524320 | tf_op jit(solution)/shard_map/ppermute | solution.py:28
  29.8 2.4 %collective-permute-start.6 = (bf16[256,1024]{1,0:T(8,128)(2,1)S(1)}, bf16[256,1024]{1,0:T(8,128)(2,1)}, u32[]{:S(2)}, u32[]{:S(2)}) collective-permute-start(bf16[256,1024]{1,0:T(8,128)(2,1)S(1)} %bitcast.26), channel_id=1, source_target_pairs={{0,6},{1,7},{2,0},{3,1},{4,2},{5,3},{6,4},{7,5},{8,14},{9,15},{10,... | collective-permute-start | bytes 1572872 | tf_op jit(solution)/shard_map/ppermute | solution.py:28
  32.2 0.8 copy-done.7
  33.0 9.0 %collective-permute-done.7.refs_4_ = bf16[256,1024]{1,0:T(8,128)(2,1)S(1)} collective-permute-done((bf16[256,1024]{1,0:T(8,128)(2,1)S(1)}, bf16[256,1024]{1,0:T(8,128)(2,1)S(1)}, u32[]{:S(2)}, u32[]{:S(2)}) %collective-permute-start.7) | collective-permute-done | bytes 524320 | tf_op jit(solution)/shard_map/ppermute | solution.py:32
  42.1 0.8 copy-done.5
  42.8 0.7 collective-permute-start.10
  43.6 1.5 %collective-permute-start.11 = (bf16[256,1024]{1,0:T(8,128)(2,1)}, bf16[256,1024]{1,0:T(8,128)(2,1)}, u32[]{:S(2)}, u32[]{:S(2)}) collective-permute-start(bf16[256,1024]{1,0:T(8,128)(2,1)} %collective-permute-done.6.refs_3_), channel_id=1, source_target_pairs={{0,1},{1,0},{2,3},{3,2},{4,5},{5,4},{6,7},{7,6},{8,9},{9,8},{10,11... | collective-permute-start | bytes 1572872 | tf_op jit(solution)/shard_map/ppermute | solution.py:32
  45.1 1.0 copy-done.8
  46.2 4.6 %project.7.refs_5_ = f32[256,768]{1,0:T(8,128)S(1)} custom-call(s32[3]{0:T(128)S(1)} %pad_add_fusion.3.refs_0_, bf16[256,1024]{1,0:T(8,128)(2,1)} %collective-permute-done.3.refs_1_, bf16[256,1024]{1,0:T(8,128)(2,1)} %collective-permute-done.4.refs_2_, bf16[256,1024]{1,0:T(8,128)(2,1)S(1)} %copy-done.8, bf16[8192,512]{1,0:T(8,128)(2,1)} %refs_3_.5, ...), custom_call_target="tpu_custom_call" | custom-call | tf_op jit(solution)/shard_map/project/pallas_call | solution.py:152
  50.9 2.2 %project.8 = (bf16[320,256]{1,0:T(8,128)(2,1)S(1)}, bf16[320,256]{1,0:T(8,128)(2,1)S(1)}, bf16[320,256]{1,0:T(8,128)(2,1)S(1)}, bf16[320,256]{1,0:T(8,128)(2,1)S(1)}, bf16[512,256]{1,0:T(8,128)(2,1)S(1)}) custom-call(s32[1]{0:T(128)} %bitcast.10.refs_0_, bf16[256,1024]{1,0:T(8,128)(2,1)} %collective-permute-done.5.refs_1_, bf16[8192,512]{1,0:T(8,128)(2,1)} %refs_3_.5, ...), custom_call_target="tpu_custom_call" | custom-call | tf_op jit(solution)/shard_map/project/pallas_call | solution.py:152
  53.1 2.7 %collective-permute-start.9 = (bf16[512,256]{1,0:T(8,128)(2,1)S(1)}, bf16[512,256]{1,0:T(8,128)(2,1)S(1)}, u32[]{:S(2)}, u32[]{:S(2)}) collective-permute-start(bf16[512,256]{1,0:T(8,128)(2,1)S(1)} %get-tuple-element.66), channel_id=1, source_target_pairs={{0,64},{8,72},{16,80},{24,88},{32,96},{40,104},{48,112},{56,120},{... | collective-permute-start | bytes 786440 | tf_op jit(solution)/shard_map/ppermute | solution.py:42
  55.8 0.9 collective-permute-start.17
  56.8 5.4 %project.9.refs_6_ = f32[256,768]{1,0:T(8,128)S(1)} custom-call(s32[4]{0:T(128)S(1)} %pad_add_fusion.2.refs_0_, bf16[256,1024]{1,0:T(8,128)(2,1)S(1)} %bitcast.28, bf16[256,1024]{1,0:T(8,128)(2,1)} %collective-permute-done.12.refs_2_, bf16[256,1024]{1,0:T(8,128)(2,1)} %collective-permute-done.6.refs_3_, bf16[256,1024]{1,0:T(8,128)(2,1)S(1)} %copy-done.6, ...), custom_call_target="tpu_custom_call" | custom-call | tf_op jit(solution)/shard_map/project/pallas_call | solution.py:152
  62.2 3.4 %project.10.refs_6_ = f32[256,768]{1,0:T(8,128)S(1)} custom-call(s32[2]{0:T(128)S(1)} %pad_add_fusion.4.refs_0_, bf16[256,1024]{1,0:T(8,128)(2,1)} %collective-permute-done.10.refs_1_, bf16[256,1024]{1,0:T(8,128)(2,1)} %collective-permute-done.11.refs_2_, bf16[8192,512]{1,0:T(8,128)(2,1)} %refs_3_.5, bf16[8192,128]{1,0:T(8,128)(2,1)S(1)} %copy-done, ...), custom_call_target="tpu_custom_call" | custom-call | tf_op jit(solution)/shard_map/project/pallas_call | solution.py:152
  65.6 2.0 %collective-permute-start.18 = (bf16[256,1024]{1,0:T(8,128)(2,1)}, bf16[256,1024]{1,0:T(8,128)(2,1)S(1)}, u32[]{:S(2)}, u32[]{:S(2)}) collective-permute-start(bf16[256,1024]{1,0:T(8,128)(2,1)} %collective-permute-done.11.refs_2_), channel_id=1, source_target_pairs={{0,6},{1,7},{2,0},{3,1},{4,2},{5,3},{6,4},{7,5},{8,14},{9,15},{10,... | collective-permute-start | bytes 1572872 | tf_op jit(solution)/shard_map/ppermute | solution.py:28
  67.8 1.7 %collective-permute-start.13 = (bf16[640,256]{1,0:T(8,128)(2,1)S(1)}, bf16[640,256]{1,0:T(8,128)(2,1)S(1)}, u32[]{:S(2)}, u32[]{:S(2)}) collective-permute-start(bf16[640,256]{1,0:T(8,128)(2,1)S(1)} %get-tuple-element.79), channel_id=1, source_target_pairs={{0,16},{8,24},{16,32},{24,40},{32,48},{40,56},{48,0},{56,8},{64,80... | collective-permute-start | bytes 983048 | tf_op jit(solution)/shard_map/ppermute | solution.py:42
  69.5 3.3 %collective-permute-start.14 = (bf16[640,256]{1,0:T(8,128)(2,1)S(1)}, bf16[640,256]{1,0:T(8,128)(2,1)S(1)}, u32[]{:S(2)}, u32[]{:S(2)}) collective-permute-start(bf16[640,256]{1,0:T(8,128)(2,1)S(1)} %get-tuple-element.80), channel_id=1, source_target_pairs={{0,32},{8,40},{16,48},{24,56},{32,0},{40,8},{48,16},{56,24},{64,96... | collective-permute-start | bytes 983048 | tf_op jit(solution)/shard_map/ppermute | solution.py:42
  72.8 0.7 collective-permute-start.15
  73.6 1.1 collective-permute-done.18.refs_2_
  74.7 3.3 %project.11 = (bf16[320,256]{1,0:T(8,128)(2,1)S(1)}, bf16[320,256]{1,0:T(8,128)(2,1)S(1)}, bf16[320,256]{1,0:T(8,128)(2,1)S(1)}, bf16[320,256]{1,0:T(8,128)(2,1)...) custom-call(s32[2]{0:T(128)S(1)} %pad_add_fusion.5.refs_0_, ...), custom_call_target="tpu_custom_call" | custom-call | tf_op jit(solution)/shard_map/project/pallas_call | solution.py:152
  78.0 1.7 %collective-permute-start.19 = (bf16[320,256]{1,0:T(8,128)(2,1)S(1)}, bf16[320,256]{1,0:T(8,128)(2,1)S(1)}, u32[]{:S(2)}, u32[]{:S(2)}) collective-permute-start(bf16[320,256]{1,0:T(8,128)(2,1)S(1)} %get-tuple-element.86), channel_id=1, source_target_pairs={{0,16},{8,24},{16,32},{24,40},{32,48},{40,56},{48,0},{56,8},{64,80... | collective-permute-start | bytes 491528 | tf_op jit(solution)/shard_map/ppermute | solution.py:42
  79.7 3.3 %collective-permute-start.20 = (bf16[320,256]{1,0:T(8,128)(2,1)S(1)}, bf16[320,256]{1,0:T(8,128)(2,1)S(1)}, u32[]{:S(2)}, u32[]{:S(2)}) collective-permute-start(bf16[320,256]{1,0:T(8,128)(2,1)S(1)} %get-tuple-element.87), channel_id=1, source_target_pairs={{0,32},{8,40},{16,48},{24,56},{32,0},{40,8},{48,16},{56,24},{64,96... | collective-permute-start | bytes 491528 | tf_op jit(solution)/shard_map/ppermute | solution.py:42
  83.0 0.7 collective-permute-start.21
  83.7 0.1 pad_maximum_fusion
  83.8 0.6 copy-done.13
  84.4 0.1 copy-done.14
  84.6 8.4 %collective-permute-start.16 = (bf16[2560,256]{1,0:T(8,128)(2,1)S(1)}, bf16[2560,256]{1,0:T(8,128)(2,1)S(1)}, u32[]{:S(2)}, u32[]{:S(2)}) collective-permute-start(bf16[2560,256]{1,0:T(8,128)(2,1)S(1)} %pad_maximum_fusion), channel_id=1, source_target_pairs={{0,8},{8,0},{16,24},{24,16},{32,40},{40,32},{48,56},{56,48},{64,72... | collective-permute-start | bytes 3932168 | tf_op jit(solution)/shard_map/ppermute | solution.py:54
  93.0 1.8 %collective-permute-start.22 = (bf16[320,256]{1,0:T(8,128)(2,1)S(1)}, bf16[320,256]{1,0:T(8,128)(2,1)S(1)}, u32[]{:S(2)}, u32[]{:S(2)}) collective-permute-start(bf16[320,256]{1,0:T(8,128)(2,1)S(1)} %get-tuple-element.89), channel_id=1, source_target_pairs={{0,64},{8,72},{16,80},{24,88},{32,96},{40,104},{48,112},{56,120},{... | collective-permute-start | bytes 491528 | tf_op jit(solution)/shard_map/ppermute | solution.py:42
  94.8 1.6 %collective-permute-start.23 = (bf16[320,256]{1,0:T(8,128)(2,1)S(1)}, bf16[320,256]{1,0:T(8,128)(2,1)S(1)}, u32[]{:S(2)}, u32[]{:S(2)}) collective-permute-start(bf16[320,256]{1,0:T(8,128)(2,1)S(1)} %get-tuple-element.90), channel_id=1, source_target_pairs={{0,80},{8,88},{16,96},{24,104},{32,112},{40,120},{48,64},{56,72},{... | collective-permute-start | bytes 491528 | tf_op jit(solution)/shard_map/ppermute | solution.py:42
  96.4 3.6 %collective-permute-start.24 = (bf16[320,256]{1,0:T(8,128)(2,1)S(1)}, bf16[320,256]{1,0:T(8,128)(2,1)S(1)}, u32[]{:S(2)}, u32[]{:S(2)}) collective-permute-start(bf16[320,256]{1,0:T(8,128)(2,1)S(1)} %get-tuple-element.91), channel_id=1, source_target_pairs={{0,96},{8,104},{16,112},{24,120},{32,64},{40,72},{48,80},{56,88},{... | collective-permute-start | bytes 491528 | tf_op jit(solution)/shard_map/ppermute | solution.py:42
  100.0 1.9 %collective-permute-start.25 = (bf16[320,256]{1,0:T(8,128)(2,1)S(1)}, bf16[320,256]{1,0:T(8,128)(2,1)S(1)}, u32[]{:S(2)}, u32[]{:S(2)}) collective-permute-start(bf16[320,256]{1,0:T(8,128)(2,1)S(1)} %get-tuple-element.92), channel_id=1, source_target_pairs={{0,112},{8,120},{16,64},{24,72},{32,80},{40,88},{48,96},{56,104},{... | collective-permute-start | bytes 491528 | tf_op jit(solution)/shard_map/ppermute | solution.py:42
  102.0 1.2 collective-permute-start.26
  103.2 2.0 %collective-permute-done.23.refs_10_ = bf16[320,256]{1,0:T(8,128)(2,1)S(1)} collective-permute-done((bf16[320,256]{1,0:T(8,128)(2,1)S(1)}, bf16[320,256]{1,0:T(8,128)(2,1)S(1)}, u32[]{:S(2)}, u32[]{:S(2)}) %collective-permute-start.23) | collective-permute-done | bytes 163872 | tf_op jit(solution)/shard_map/ppermute | solution.py:42
  105.2 3.6 %collective-permute-done.24.refs_11_ = bf16[320,256]{1,0:T(8,128)(2,1)S(1)} collective-permute-done((bf16[320,256]{1,0:T(8,128)(2,1)S(1)}, bf16[320,256]{1,0:T(8,128)(2,1)S(1)}, u32[]{:S(2)}, u32[]{:S(2)}) %collective-permute-start.24) | collective-permute-done | bytes 163872 | tf_op jit(solution)/shard_map/ppermute | solution.py:42
  108.8 2.5 %collective-permute-done.25.refs_12_ = bf16[320,256]{1,0:T(8,128)(2,1)S(1)} collective-permute-done((bf16[320,256]{1,0:T(8,128)(2,1)S(1)}, bf16[320,256]{1,0:T(8,128)(2,1)S(1)}, u32[]{:S(2)}, u32[]{:S(2)}) %collective-permute-start.25) | collective-permute-done | bytes 163872 | tf_op jit(solution)/shard_map/ppermute | solution.py:42
  111.4 0.9 collective-permute-start.27
  112.2 1.7 %collective-permute-done.27.refs_14_ = bf16[1280,256]{1,0:T(8,128)(2,1)S(1)} collective-permute-done((bf16[1280,256]{1,0:T(8,128)(2,1)S(1)}, bf16[1280,256]{1,0:T(8,128)(2,1)S(1)}, u32[]{:S(2)}, u32[]{:S(2)}) %collective-permute-start.27) | collective-permute-done | bytes 655392 | tf_op jit(solution)/shard_map/ppermute | solution.py:54
  114.0 0.8 copy-done.24
  114.8 1.1 copy-done.15
  115.9 27.8 %attend.1 = bf16[512,512]{1,0:T(8,128)(2,1)} custom-call(s32[19]{0:T(128)} %pad_add_fusion.1.info, s32[256]{0:T(256)} %reshape.65.old_map, bf16[640,256]{1,0:T(8,128)(2,1)} %copy-done.11, bf16[640,256]{1,0:T(8,128)(2,1)} %copy-done.12, bf16[640,256]{1,0:T(8,128)(2,1)} %copy-done.13, bf16[640,256]{1,0:T(8,128)(2,1)} %copy-done.14, ...), custom_call_target="tpu_custom_call" | custom-call | tf_op jit(solution)/shard_map/attend/pallas_call | solution.py:235
  (86 shorter events, 0.8 us)
Async XLA Ops:
  0.0 6.2 %copy-start.26 = (s32[16,16]{1,0:T(8,128)S(1)}, s32[16,16]{1,0:T(8,128)}, u32[]{:S(2)}) copy-start(s32[16,16]{1,0:T(8,128)} %param.8) | copy-start | bytes 3076
  0.0 11.9 %copy-start.25 = (s32[16,16]{1,0:T(8,128)S(1)}, s32[16,16]{1,0:T(8,128)}, u32[]{:S(2)}) copy-start(s32[16,16]{1,0:T(8,128)} %param.7) | copy-start | bytes 3076
  1.3 20.0 %copy-start.1 = (bf16[16,1,16,1024]{3,2,1,0:T(8,128)(2,1)}, bf16[16,1,16,1024]{3,2,1,0:T(8,128)(2,1)S(1)}, u32[]{:S(2)}) copy-start(bf16[16,1,16,1024]{3,2,1,0:T(8,128)(2,1)S(1)} %get-tuple-element.95) | copy-start | bytes 1572868
  1.3 20.0 %copy-start = (bf16[8192,128]{1,0:T(8,128)(2,1)S(1)}, bf16[8192,128]{1,0:T(8,128)(2,1)}, u32[]{:S(2)}) copy-start(bf16[8192,128]{1,0:T(8,128)(2,1)} %refs_4_.7) | copy-start | bytes 6291460
  1.3 15.4 %collective-permute-start = (bf16[256,1024]{1,0:T(8,128)(2,1)S(1)}, bf16[256,1024]{1,0:T(8,128)(2,1)}, u32[]{:S(2)}, u32[]{:S(2)}) collective-permute-start(bf16[256,1024]{1,0:T(8,128)(2,1)S(1)} %bitcast.29), channel_id=1, source_target_pairs={{0,2},{1,3},{2,4},{3,5},{4,6},{5,7},{6,0},{7,1},{8,10},{9,11},{10,... | collective-permute-start | bytes 1572872 | tf_op jit(solution)/shard_map/ppermute | solution.py:28
  3.4 13.3 %collective-permute-start.1 = (bf16[256,1024]{1,0:T(8,128)(2,1)S(1)}, bf16[256,1024]{1,0:T(8,128)(2,1)}, u32[]{:S(2)}, u32[]{:S(2)}) collective-permute-start(bf16[256,1024]{1,0:T(8,128)(2,1)S(1)} %bitcast.30), channel_id=1, source_target_pairs={{0,6},{1,7},{2,0},{3,1},{4,2},{5,3},{6,4},{7,5},{8,14},{9,15},{10,... | collective-permute-start | bytes 1572872 | tf_op jit(solution)/shard_map/ppermute | solution.py:28
  4.8 12.3 %collective-permute-start.2 = (bf16[256,1024]{1,0:T(8,128)(2,1)S(1)}, bf16[256,1024]{1,0:T(8,128)(2,1)}, u32[]{:S(2)}, u32[]{:S(2)}) collective-permute-start(bf16[256,1024]{1,0:T(8,128)(2,1)S(1)} %bitcast.31), channel_id=1, source_target_pairs={{0,1},{1,0},{2,3},{3,2},{4,5},{5,4},{6,7},{7,6},{8,9},{9,8},{10,11... | collective-permute-start | bytes 1572872 | tf_op jit(solution)/shard_map/ppermute | solution.py:32
  17.1 12.8 %collective-permute-start.3 = (bf16[256,1024]{1,0:T(8,128)(2,1)}, bf16[256,1024]{1,0:T(8,128)(2,1)}, u32[]{:S(2)}, u32[]{:S(2)}) collective-permute-start(bf16[256,1024]{1,0:T(8,128)(2,1)} %collective-permute-done.2.refs_4_), channel_id=1, source_target_pairs={{0,2},{1,3},{2,4},{3,5},{4,6},{5,7},{6,0},{7,1},{8,10},{9,11},{10,... | collective-permute-start | bytes 1572872 | tf_op jit(solution)/shard_map/ppermute | solution.py:28
  17.2 12.6 %collective-permute-start.4 = (bf16[256,1024]{1,0:T(8,128)(2,1)}, bf16[256,1024]{1,0:T(8,128)(2,1)}, u32[]{:S(2)}, u32[]{:S(2)}) collective-permute-start(bf16[256,1024]{1,0:T(8,128)(2,1)} %collective-permute-done.1.refs_3_), channel_id=1, source_target_pairs={{0,6},{1,7},{2,0},{3,1},{4,2},{5,3},{6,4},{7,5},{8,14},{9,15},{10,... | collective-permute-start | bytes 1572872 | tf_op jit(solution)/shard_map/ppermute | solution.py:28
  19.8 12.4 %collective-permute-start.8 = (bf16[256,1024]{1,0:T(8,128)(2,1)}, bf16[256,1024]{1,0:T(8,128)(2,1)S(1)}, u32[]{:S(2)}, u32[]{:S(2)}) collective-permute-start(bf16[256,1024]{1,0:T(8,128)(2,1)} %collective-permute-done.1.refs_3_), channel_id=1, source_target_pairs={{0,1},{1,0},{2,3},{3,2},{4,5},{5,4},{6,7},{7,6},{8,9},{9,8},{10,11... | collective-permute-start | bytes 1572872 | tf_op jit(solution)/shard_map/ppermute | solution.py:32
  21.3 20.8 %collective-permute-start.7 = (bf16[256,1024]{1,0:T(8,128)(2,1)S(1)}, bf16[256,1024]{1,0:T(8,128)(2,1)S(1)}, u32[]{:S(2)}, u32[]{:S(2)}) collective-permute-start(bf16[256,1024]{1,0:T(8,128)(2,1)S(1)} %bitcast.25), channel_id=1, source_target_pairs={{0,1},{1,0},{2,3},{3,2},{4,5},{5,4},{6,7},{7,6},{8,9},{9,8},{10,11... | collective-permute-start | bytes 1572872 | tf_op jit(solution)/shard_map/ppermute | solution.py:32
  21.4 1.0 copy-start.2
  29.8 12.2 %collective-permute-start.6 = (bf16[256,1024]{1,0:T(8,128)(2,1)S(1)}, bf16[256,1024]{1,0:T(8,128)(2,1)}, u32[]{:S(2)}, u32[]{:S(2)}) collective-permute-start(bf16[256,1024]{1,0:T(8,128)(2,1)S(1)} %bitcast.26), channel_id=1, source_target_pairs={{0,6},{1,7},{2,0},{3,1},{4,2},{5,3},{6,4},{7,5},{8,14},{9,15},{10,... | collective-permute-start | bytes 1572872 | tf_op jit(solution)/shard_map/ppermute | solution.py:28
  32.2 18.6 %collective-permute-start.5 = (bf16[256,1024]{1,0:T(8,128)(2,1)}, bf16[256,1024]{1,0:T(8,128)(2,1)}, u32[]{:S(2)}, u32[]{:S(2)}) collective-permute-start(bf16[256,1024]{1,0:T(8,128)(2,1)} %collective-permute-done.3.refs_1_), channel_id=1, source_target_pairs={{0,2},{1,3},{2,4},{3,5},{4,6},{5,7},{6,0},{7,1},{8,10},{9,11},{10,... | collective-permute-start | bytes 1572872 | tf_op jit(solution)/shard_map/ppermute | solution.py:28
  32.2 0.8 copy-start.7
  33.0 22.8 %collective-permute-start.12 = (bf16[256,1024]{1,0:T(8,128)(2,1)S(1)}, bf16[256,1024]{1,0:T(8,128)(2,1)}, u32[]{:S(2)}, u32[]{:S(2)}) collective-permute-start(bf16[256,1024]{1,0:T(8,128)(2,1)S(1)} %bitcast.27), channel_id=1, source_target_pairs={{0,2},{1,3},{2,4},{3,5},{4,6},{5,7},{6,0},{7,1},{8,10},{9,11},{10,... | collective-permute-start | bytes 1572872 | tf_op jit(solution)/shard_map/ppermute | solution.py:28
  42.0 0.8 copy-start.5
  42.8 19.3 %collective-permute-start.10 = (bf16[256,1024]{1,0:T(8,128)(2,1)}, bf16[256,1024]{1,0:T(8,128)(2,1)}, u32[]{:S(2)}, u32[]{:S(2)}) collective-permute-start(bf16[256,1024]{1,0:T(8,128)(2,1)} %collective-permute-done.6.refs_3_), channel_id=1, source_target_pairs={{0,6},{1,7},{2,0},{3,1},{4,2},{5,3},{6,4},{7,5},{8,14},{9,15},{10,... | collective-permute-start | bytes 1572872 | tf_op jit(solution)/shard_map/ppermute | solution.py:28
  43.6 18.6 %collective-permute-start.11 = (bf16[256,1024]{1,0:T(8,128)(2,1)}, bf16[256,1024]{1,0:T(8,128)(2,1)}, u32[]{:S(2)}, u32[]{:S(2)}) collective-permute-start(bf16[256,1024]{1,0:T(8,128)(2,1)} %collective-permute-done.6.refs_3_), channel_id=1, source_target_pairs={{0,1},{1,0},{2,3},{3,2},{4,5},{5,4},{6,7},{7,6},{8,9},{9,8},{10,11... | collective-permute-start | bytes 1572872 | tf_op jit(solution)/shard_map/ppermute | solution.py:32
  45.1 1.0 copy-start.8
  46.2 4.7 %copy-start.4 = (f32[256,128]{1,0:T(8,128)S(1)}, f32[256,128]{1,0:T(8,128)}, u32[]{:S(2)}) copy-start(f32[256,128]{1,0:T(8,128)} %get-tuple-element.64.refs_8_) | copy-start | bytes 393220
  50.8 5.0 %copy-start.6 = (bf16[256,1024]{1,0:T(8,128)(2,1)S(1)}, bf16[256,1024]{1,0:T(8,128)(2,1)}, u32[]{:S(2)}) copy-start(bf16[256,1024]{1,0:T(8,128)(2,1)} %copy-done.5) | copy-start | bytes 1572868
  53.1 12.5 %collective-permute-start.9 = (bf16[512,256]{1,0:T(8,128)(2,1)S(1)}, bf16[512,256]{1,0:T(8,128)(2,1)S(1)}, u32[]{:S(2)}, u32[]{:S(2)}) collective-permute-start(bf16[512,256]{1,0:T(8,128)(2,1)S(1)} %get-tuple-element.66), channel_id=1, source_target_pairs={{0,64},{8,72},{16,80},{24,88},{32,96},{40,104},{48,112},{56,120},{... | collective-permute-start | bytes 786440 | tf_op jit(solution)/shard_map/ppermute | solution.py:42
  55.8 17.8 %collective-permute-start.17 = (bf16[256,1024]{1,0:T(8,128)(2,1)S(1)}, bf16[256,1024]{1,0:T(8,128)(2,1)S(1)}, u32[]{:S(2)}, u32[]{:S(2)}) collective-permute-start(bf16[256,1024]{1,0:T(8,128)(2,1)S(1)} %copy-done.6), channel_id=1, source_target_pairs={{0,2},{1,3},{2,4},{3,5},{4,6},{5,7},{6,0},{7,1},{8,10},{9,11},{10,... | collective-permute-start | bytes 1572872 | tf_op jit(solution)/shard_map/ppermute | solution.py:28
  65.6 9.1 %copy-start.9 = (f32[256,128]{1,0:T(8,128)S(1)}, f32[256,128]{1,0:T(8,128)}, u32[]{:S(2)}) copy-start(f32[256,128]{1,0:T(8,128)} %get-tuple-element.83.refs_8_) | copy-start | bytes 393220
  65.6 9.0 %copy-start.10 = (f32[256,128]{1,0:T(8,128)S(1)}, f32[256,128]{1,0:T(8,128)}, u32[]{:S(2)}) copy-start(f32[256,128]{1,0:T(8,128)} %get-tuple-element.84.refs_9_) | copy-start | bytes 393220
  65.6 9.0 %collective-permute-start.18 = (bf16[256,1024]{1,0:T(8,128)(2,1)}, bf16[256,1024]{1,0:T(8,128)(2,1)S(1)}, u32[]{:S(2)}, u32[]{:S(2)}) collective-permute-start(bf16[256,1024]{1,0:T(8,128)(2,1)} %collective-permute-done.11.refs_2_), channel_id=1, source_target_pairs={{0,6},{1,7},{2,0},{3,1},{4,2},{5,3},{6,4},{7,5},{8,14},{9,15},{10,... | collective-permute-start | bytes 1572872 | tf_op jit(solution)/shard_map/ppermute | solution.py:28
  67.7 16.0 %copy-start.11 = (bf16[640,256]{1,0:T(8,128)(2,1)}, bf16[640,256]{1,0:T(8,128)(2,1)S(1)}, u32[]{:S(2)}) copy-start(bf16[640,256]{1,0:T(8,128)(2,1)S(1)} %pad_maximum_fusion.6.refs_0_) | copy-start | bytes 983044
  67.8 15.2 %collective-permute-start.13 = (bf16[640,256]{1,0:T(8,128)(2,1)S(1)}, bf16[640,256]{1,0:T(8,128)(2,1)S(1)}, u32[]{:S(2)}, u32[]{:S(2)}) collective-permute-start(bf16[640,256]{1,0:T(8,128)(2,1)S(1)} %get-tuple-element.79), channel_id=1, source_target_pairs={{0,16},{8,24},{16,32},{24,40},{32,48},{40,56},{48,0},{56,8},{64,80... | collective-permute-start | bytes 983048 | tf_op jit(solution)/shard_map/ppermute | solution.py:42
  69.5 14.2 %collective-permute-start.14 = (bf16[640,256]{1,0:T(8,128)(2,1)S(1)}, bf16[640,256]{1,0:T(8,128)(2,1)S(1)}, u32[]{:S(2)}, u32[]{:S(2)}) collective-permute-start(bf16[640,256]{1,0:T(8,128)(2,1)S(1)} %get-tuple-element.80), channel_id=1, source_target_pairs={{0,32},{8,40},{16,48},{24,56},{32,0},{40,8},{48,16},{56,24},{64,96... | collective-permute-start | bytes 983048 | tf_op jit(solution)/shard_map/ppermute | solution.py:42
  72.8 10.9 %collective-permute-start.15 = (bf16[640,256]{1,0:T(8,128)(2,1)S(1)}, bf16[640,256]{1,0:T(8,128)(2,1)S(1)}, u32[]{:S(2)}, u32[]{:S(2)}) collective-permute-start(bf16[640,256]{1,0:T(8,128)(2,1)S(1)} %get-tuple-element.81), channel_id=1, source_target_pairs={{0,48},{8,56},{16,0},{24,8},{32,16},{40,24},{48,32},{56,40},{64,11... | collective-permute-start | bytes 983048 | tf_op jit(solution)/shard_map/ppermute | solution.py:42
  78.0 24.0 %copy-start.3 = (bf16[320,256]{1,0:T(8,128)(2,1)}, bf16[320,256]{1,0:T(8,128)(2,1)S(1)}, u32[]{:S(2)}) copy-start(bf16[320,256]{1,0:T(8,128)(2,1)S(1)} %get-tuple-element.85.refs_5_) | copy-start | bytes 491524
  78.0 16.8 %collective-permute-start.19 = (bf16[320,256]{1,0:T(8,128)(2,1)S(1)}, bf16[320,256]{1,0:T(8,128)(2,1)S(1)}, u32[]{:S(2)}, u32[]{:S(2)}) collective-permute-start(bf16[320,256]{1,0:T(8,128)(2,1)S(1)} %get-tuple-element.86), channel_id=1, source_target_pairs={{0,16},{8,24},{16,32},{24,40},{32,48},{40,56},{48,0},{56,8},{64,80... | collective-permute-start | bytes 491528 | tf_op jit(solution)/shard_map/ppermute | solution.py:42
  79.7 16.7 %collective-permute-start.20 = (bf16[320,256]{1,0:T(8,128)(2,1)S(1)}, bf16[320,256]{1,0:T(8,128)(2,1)S(1)}, u32[]{:S(2)}, u32[]{:S(2)}) collective-permute-start(bf16[320,256]{1,0:T(8,128)(2,1)S(1)} %get-tuple-element.87), channel_id=1, source_target_pairs={{0,32},{8,40},{16,48},{24,56},{32,0},{40,8},{48,16},{56,24},{64,96... | collective-permute-start | bytes 491528 | tf_op jit(solution)/shard_map/ppermute | solution.py:42
  83.0 0.9 copy-start.12
  83.0 17.1 %collective-permute-start.21 = (bf16[320,256]{1,0:T(8,128)(2,1)S(1)}, bf16[320,256]{1,0:T(8,128)(2,1)S(1)}, u32[]{:S(2)}, u32[]{:S(2)}) collective-permute-start(bf16[320,256]{1,0:T(8,128)(2,1)S(1)} %get-tuple-element.88), channel_id=1, source_target_pairs={{0,48},{8,56},{16,0},{24,8},{32,16},{40,24},{48,32},{56,40},{64,11... | collective-permute-start | bytes 491528 | tf_op jit(solution)/shard_map/ppermute | solution.py:42
  83.7 0.7 copy-start.13
  83.7 0.8 copy-start.14
  84.6 29.4 %collective-permute-start.16 = (bf16[2560,256]{1,0:T(8,128)(2,1)S(1)}, bf16[2560,256]{1,0:T(8,128)(2,1)S(1)}, u32[]{:S(2)}, u32[]{:S(2)}) collective-permute-start(bf16[2560,256]{1,0:T(8,128)(2,1)S(1)} %pad_maximum_fusion), channel_id=1, source_target_pairs={{0,8},{8,0},{16,24},{24,16},{32,40},{40,32},{48,56},{56,48},{64,72... | collective-permute-start | bytes 3932168 | tf_op jit(solution)/shard_map/ppermute | solution.py:54
  93.0 9.0 %collective-permute-start.22 = (bf16[320,256]{1,0:T(8,128)(2,1)S(1)}, bf16[320,256]{1,0:T(8,128)(2,1)S(1)}, u32[]{:S(2)}, u32[]{:S(2)}) collective-permute-start(bf16[320,256]{1,0:T(8,128)(2,1)S(1)} %get-tuple-element.89), channel_id=1, source_target_pairs={{0,64},{8,72},{16,80},{24,88},{32,96},{40,104},{48,112},{56,120},{... | collective-permute-start | bytes 491528 | tf_op jit(solution)/shard_map/ppermute | solution.py:42
  94.8 16.6 %copy-start.16 = (bf16[320,256]{1,0:T(8,128)(2,1)}, bf16[320,256]{1,0:T(8,128)(2,1)S(1)}, u32[]{:S(2)}) copy-start(bf16[320,256]{1,0:T(8,128)(2,1)S(1)} %collective-permute-done.19.refs_6_) | copy-start | bytes 491524
  94.8 10.5 %collective-permute-start.23 = (bf16[320,256]{1,0:T(8,128)(2,1)S(1)}, bf16[320,256]{1,0:T(8,128)(2,1)S(1)}, u32[]{:S(2)}, u32[]{:S(2)}) collective-permute-start(bf16[320,256]{1,0:T(8,128)(2,1)S(1)} %get-tuple-element.90), channel_id=1, source_target_pairs={{0,80},{8,88},{16,96},{24,104},{32,112},{40,120},{48,64},{56,72},{... | collective-permute-start | bytes 491528 | tf_op jit(solution)/shard_map/ppermute | solution.py:42
  96.4 14.9 %copy-start.17 = (bf16[320,256]{1,0:T(8,128)(2,1)}, bf16[320,256]{1,0:T(8,128)(2,1)S(1)}, u32[]{:S(2)}) copy-start(bf16[320,256]{1,0:T(8,128)(2,1)S(1)} %collective-permute-done.20.refs_7_) | copy-start | bytes 491524
  96.4 12.4 %collective-permute-start.24 = (bf16[320,256]{1,0:T(8,128)(2,1)S(1)}, bf16[320,256]{1,0:T(8,128)(2,1)S(1)}, u32[]{:S(2)}, u32[]{:S(2)}) collective-permute-start(bf16[320,256]{1,0:T(8,128)(2,1)S(1)} %get-tuple-element.91), channel_id=1, source_target_pairs={{0,96},{8,104},{16,112},{24,120},{32,64},{40,72},{48,80},{56,88},{... | collective-permute-start | bytes 491528 | tf_op jit(solution)/shard_map/ppermute | solution.py:42
  100.0 11.3 %copy-start.18 = (bf16[320,256]{1,0:T(8,128)(2,1)}, bf16[320,256]{1,0:T(8,128)(2,1)S(1)}, u32[]{:S(2)}) copy-start(bf16[320,256]{1,0:T(8,128)(2,1)S(1)} %collective-permute-done.21.refs_8_) | copy-start | bytes 491524
  100.0 11.3 %collective-permute-start.25 = (bf16[320,256]{1,0:T(8,128)(2,1)S(1)}, bf16[320,256]{1,0:T(8,128)(2,1)S(1)}, u32[]{:S(2)}, u32[]{:S(2)}) collective-permute-start(bf16[320,256]{1,0:T(8,128)(2,1)S(1)} %get-tuple-element.92), channel_id=1, source_target_pairs={{0,112},{8,120},{16,64},{24,72},{32,80},{40,88},{48,96},{56,104},{... | collective-permute-start | bytes 491528 | tf_op jit(solution)/shard_map/ppermute | solution.py:42
  102.0 12.0 %copy-start.19 = (bf16[320,256]{1,0:T(8,128)(2,1)}, bf16[320,256]{1,0:T(8,128)(2,1)S(1)}, u32[]{:S(2)}) copy-start(bf16[320,256]{1,0:T(8,128)(2,1)S(1)} %collective-permute-done.22.refs_9_) | copy-start | bytes 491524
  102.0 10.2 %collective-permute-start.26 = (bf16[1280,256]{1,0:T(8,128)(2,1)S(1)}, bf16[1280,256]{1,0:T(8,128)(2,1)S(1)}, u32[]{:S(2)}, u32[]{:S(2)}) collective-permute-start(bf16[1280,256]{1,0:T(8,128)(2,1)S(1)} %pad_maximum_fusion.1), channel_id=1, source_target_pairs={{0,8},{8,0},{16,24},{24,16},{32,40},{40,32},{48,56},{56,48},{64,72... | collective-permute-start | bytes 1966088 | tf_op jit(solution)/shard_map/ppermute | solution.py:54
  105.2 8.7 %copy-start.20 = (bf16[320,256]{1,0:T(8,128)(2,1)}, bf16[320,256]{1,0:T(8,128)(2,1)S(1)}, u32[]{:S(2)}) copy-start(bf16[320,256]{1,0:T(8,128)(2,1)S(1)} %collective-permute-done.23.refs_10_) | copy-start | bytes 491524
  108.8 5.2 %copy-start.21 = (bf16[320,256]{1,0:T(8,128)(2,1)}, bf16[320,256]{1,0:T(8,128)(2,1)S(1)}, u32[]{:S(2)}) copy-start(bf16[320,256]{1,0:T(8,128)(2,1)S(1)} %collective-permute-done.24.refs_11_) | copy-start | bytes 491524
  111.3 2.7 %copy-start.22 = (bf16[320,256]{1,0:T(8,128)(2,1)}, bf16[320,256]{1,0:T(8,128)(2,1)S(1)}, u32[]{:S(2)}) copy-start(bf16[320,256]{1,0:T(8,128)(2,1)S(1)} %collective-permute-done.25.refs_12_) | copy-start | bytes 491524
  111.4 2.6 %collective-permute-start.27 = (bf16[1280,256]{1,0:T(8,128)(2,1)S(1)}, bf16[1280,256]{1,0:T(8,128)(2,1)S(1)}, u32[]{:S(2)}, u32[]{:S(2)}) collective-permute-start(bf16[1280,256]{1,0:T(8,128)(2,1)S(1)} %pad_maximum_fusion.2), channel_id=1, source_target_pairs={{0,8},{8,0},{16,24},{24,16},{32,40},{40,32},{48,56},{56,48},{64,72... | collective-permute-start | bytes 1966088 | tf_op jit(solution)/shard_map/ppermute | solution.py:54
  112.2 1.8 %copy-start.23 = (bf16[1280,256]{1,0:T(8,128)(2,1)}, bf16[1280,256]{1,0:T(8,128)(2,1)S(1)}, u32[]{:S(2)}) copy-start(bf16[1280,256]{1,0:T(8,128)(2,1)S(1)} %collective-permute-done.26.refs_13_) | copy-start | bytes 1966084
  113.9 0.8 copy-start.24
  114.8 1.1 copy-start.15

commit v5 on v4

--- a/solution.py
+++ b/solution.py
@@ -11,6 +11,7 @@
 HEAD = 128
 THETA = 500000.0
 SCALE = HEAD ** -0.5
+LOG2E = math.log2(math.e)
 FINE = 32
 CHUNKS = 2
 W = FINE // CHUNKS
@@ -60,6 +61,17 @@
 
 def dot_t(a, b):
     return lax.dot_general(a, b, (((1,), (1,)), ((), ())), preferred_element_type=jnp.float32)
+
+
+def fold(block, combine):
+    result = block[:, :HEAD]
+    for at in range(HEAD, block.shape[1], HEAD):
+        result = combine(result, block[:, at : at + HEAD])
+    return result
+
+
+def less(block, lanes):
+    return jnp.concatenate([block[:, at : at + HEAD] - lanes for at in range(0, block.shape[1], HEAD)], axis=1)
 
 
 def project_kernel(groups, has_acc, last, joint, *refs):
@@ -160,6 +172,7 @@
         ),
         out_shape=out_shape,
         compiler_params=pltpu.CompilerParams(vmem_limit_bytes=48 * 2**20),
+        cost_estimate=pl.CostEstimate(flops=1, bytes_accessed=1, transcendentals=0),
         name="project",
     )(features, *operands)
 
@@ -204,15 +217,12 @@
                 visible = lax.broadcasted_iota(jnp.int32, (1024, KB), 1) + start <= row
                 scores = jnp.where(visible, scores, -1e30)
             old = top[...]
-            new = jnp.maximum(old, jnp.max(scores, axis=-1, keepdims=True))
-            factor = jnp.exp((old - new) * SCALE)
-            weights = jnp.exp((scores - new[:, :1]) * SCALE)
+            new = jnp.maximum(old, jnp.max(fold(scores, jnp.maximum), axis=-1, keepdims=True))
+            factor = jnp.exp2((old - new) * (SCALE * LOG2E))
+            weights = jnp.exp2(less(scores, new) * (SCALE * LOG2E))
             if masked:
                 weights = jnp.where(visible, weights, 0.0)
-            sums = total[...] * factor
-            for i in range(KB // HEAD):
-                sums = sums + weights[:, i * HEAD : (i + 1) * HEAD]
-            total[...] = sums
+            total[...] = total[...] * factor + fold(weights, jnp.add)
             accum[...] = accum[...] * factor + dot(
                 weights.astype(jnp.bfloat16), values[pl.ds(start, KB), :]
             )
@@ -309,7 +319,7 @@
     right_across = after(right_across, late)
     late_left = shift_x(after(late, right_across), 1)
     total = project(features[4:7], [(left_across,), (far,), (right_across,)], weights, total)
-    late_right, late_across = together(late_right, late_across)
+    late_right, late_across, total = together(late_right, late_across, total)
     late_far = shift_x(late_right, -1)
     late_right_across = swap_y(late_right)
     far_across = after(far_across, late_right)
@@ -321,19 +331,21 @@
     total = project(features[:4], blocks, weights)
     late_far, late_right_across, total = together(late_far, late_right_across, total)
     late_far_across = shift_x(late_right_across, -1)
-    total = project(features[5:7], [(late_far,), (late_right_across,)], weights, total)
-    partner, total = together(partner, total)
     early_parts = [
         jnp.concatenate([sent[dz], partner[:ROWS], partner[ROWS + dz * 4 * W : ROWS + (dz + 1) * 4 * W]], axis=0)
         for dz in range(4)
     ]
-    early_parts = list(together(*early_parts))
+    *early_parts, total = together(*early_parts, total)
+    total = project(features[5:7], [(late_far,), (late_right_across,)], weights, total)
     early_parts[1:] = [shift_ctx(early_parts[dz], 0, dz) for dz in range(1, 4)]
     last = jnp.stack([features[4], features[7]])
     tail = [(late_left_across,), (late_far_across,)]
     sent = project(last, tail, weights, total, (send_info, *tables[2:]))
     early_other = swap_core(jnp.concatenate(early_parts, axis=0))
-    late_parts = [sent[0]] + [shift_ctx(sent[r], *CHIPS[r]) for r in range(1, 8)]
+    sent = list(sent)
+    late_parts = [shift_ctx(sent[r], *CHIPS[r]) for r in range(4, 8)]
+    early_parts[1], late_parts[0], *sent[:4] = together(early_parts[1], late_parts[0], *sent[:4])
+    late_parts = [sent[0]] + [shift_ctx(sent[r], *CHIPS[r]) for r in range(1, 4)] + late_parts
     late_other = [swap_core(jnp.concatenate(late_parts[at : at + 4], axis=0)) for at in (0, 4)]
     return attend(attend_info, old_flat, [*early_parts, early_other, *late_parts, *late_other])
 

time: 144 us -> 130 us (0.903)
  Pallas kernels: 52.2 us -> 45 us
  waiting for transfers between devices: 22.1 us -> 17.5 us
  starting transfers between devices: 50.2 us -> 47.4 us
    pallas_call x1, Pallas kernels: 27.8 us -> 20.4 us  [attend(): pl.pallas_call(attend_kernel, out_shape=jax.ShapeDtypeStruct((512, 512),...]
    ppermute x4, waiting for transfers between devices: 9.37 us -> 4.49 us  [swap_y(): return lax.ppermute(block, 'tp', [(i, i ^ 1) for i in range(8)])]
    ppermute x10, waiting for transfers between devices: 2.94 us -> 4.73 us  [shift_x(): return lax.ppermute(block, 'tp', perm)]
    ppermute x3, starting transfers between devices: 10.4 us -> 8.87 us  [swap_core(): return lax.ppermute(block, 'ctx', [(i, i ^ 1) for i in range(16)])]
    ppermute x11, waiting for transfers between devices: 8.1 us -> 6.55 us  [shift_ctx(): return lax.ppermute(block, 'ctx', perm)]
    ppermute x11, starting transfers between devices: 23.1 us -> 21.6 us  [shift_ctx(): return lax.ppermute(block, 'ctx', perm)]
    unnamed x54 -> x50, local copies, waits for them, and re-layouts: 6.37 us -> 6.56 us
  transfers between devices with their start and end apart: 28 -> 28, of which waited for: 8 -> 9; matrix products, arithmetic and copies ran while one was open for 4% -> 5% of each run, Pallas kernels for 17% -> 19%
where the time goes in v5:
time: 130 us; the launch traced here: 129 us
  starting transfers between devices  47.4 us (36%)
  Pallas kernels  45 us (35%)
  waiting for transfers between devices  17.5 us (13%)
  local copies, waits for them, and re-layouts  9.38 us (7%)
  between operations  5.18 us (4%)
  other arithmetic  4.52 us (3%)
    pallas_call x6, Pallas kernels, project(): pl.pallas_call(functools.partial(project_kernel, groups, acc is not None,...  24.5 us
    ppermute x11, starting transfers between devices, shift_ctx(): return lax.ppermute(block, 'ctx', perm)  21.6 us
    pallas_call x1, Pallas kernels, attend(): pl.pallas_call(attend_kernel, out_shape=jax.ShapeDtypeStruct((512, 512),...  20.4 us
    ppermute x10, starting transfers between devices, shift_x(): return lax.ppermute(block, 'tp', perm)  12.5 us
    ppermute x3, starting transfers between devices, swap_core(): return lax.ppermute(block, 'ctx', [(i, i ^ 1) for i in range(16)])  8.87 us
    unnamed x50, local copies, waits for them, and re-layouts  6.56 us
    ppermute x11, waiting for transfers between devices, shift_ctx(): return lax.ppermute(block, 'ctx', perm)  6.55 us
    ppermute x10, waiting for transfers between devices, shift_x(): return lax.ppermute(block, 'tp', perm)  4.73 us
  transfers between devices with their start and end apart: 28, of which 9 were waited for; matrix products, arithmetic and copies ran while one was open for 5% of the time, Pallas kernels for 19%

profile of v5, /device:TPU:1, one launch (start us, length us, event | category | flops | bytes accessed | tf_op | source)
XLA Modules:
  0.0 129.0 jit_solution(3081254325412352482)
XLA Ops:
  0.0 1.3 %fusion.5 = (bf16[16,1,16,1024]{3,2,1,0:T(8,128)(2,1)S(1)}, bf16[16,1,16,1024]{3,2,1,0:T(8,128)(2,1)S(1)}) fusion(bf16[16,2,16,1024]{3,2,1,0:T(8,128)(2,1)} %bitcast.33), kind=kLoop, calls=%fused_computation.37 | loop fusion | bytes 2097152 | tf_op jit(solution)/shard_map/slice | solution.py:298
  1.3 2.1 %collective-permute-start = (bf16[256,1024]{1,0:T(8,128)(2,1)S(1)}, bf16[256,1024]{1,0:T(8,128)(2,1)}, u32[]{:S(2)}, u32[]{:S(2)}) collective-permute-start(bf16[256,1024]{1,0:T(8,128)(2,1)S(1)} %bitcast.29), channel_id=1, source_target_pairs={{0,2},{1,3},{2,4},{3,5},{4,6},{5,7},{6,0},{7,1},{8,10},{9,11},{10,... | collective-permute-start | bytes 1572872 | tf_op jit(solution)/shard_map/ppermute | solution.py:29
  3.4 1.4 %collective-permute-start.1 = (bf16[256,1024]{1,0:T(8,128)(2,1)S(1)}, bf16[256,1024]{1,0:T(8,128)(2,1)}, u32[]{:S(2)}, u32[]{:S(2)}) collective-permute-start(bf16[256,1024]{1,0:T(8,128)(2,1)S(1)} %bitcast.30), channel_id=1, source_target_pairs={{0,6},{1,7},{2,0},{3,1},{4,2},{5,3},{6,4},{7,5},{8,14},{9,15},{10,... | collective-permute-start | bytes 1572872 | tf_op jit(solution)/shard_map/ppermute | solution.py:29
  4.8 1.4 %collective-permute-start.2 = (bf16[256,1024]{1,0:T(8,128)(2,1)S(1)}, bf16[256,1024]{1,0:T(8,128)(2,1)}, u32[]{:S(2)}, u32[]{:S(2)}) collective-permute-start(bf16[256,1024]{1,0:T(8,128)(2,1)S(1)} %bitcast.31), channel_id=1, source_target_pairs={{0,1},{1,0},{2,3},{3,2},{4,5},{5,4},{6,7},{7,6},{8,9},{9,8},{10,11... | collective-permute-start | bytes 1572872 | tf_op jit(solution)/shard_map/ppermute | solution.py:33
  6.2 0.6 fusion.7
  11.7 0.1 compare_reduce_fusion.1
  11.8 0.1 select_reduce_fusion.1
  11.9 0.1 compare_reduce_fusion
  12.1 0.1 select_reduce_fusion
  12.4 0.6 pad_add_fusion.1.info
  13.0 0.7 reshape.65.old_map
  13.7 0.1 convert_element_type.25
  13.8 0.1 convert_element_type.23
  13.9 1.0 fusion.4
  14.9 0.8 pad_maximum_fusion.7
  15.6 0.9 pad_maximum_fusion.9
  16.5 0.5 collective-permute-done.2.refs_4_
  17.1 0.2 collective-permute-start.3
  17.2 2.5 %collective-permute-start.4 = (bf16[256,1024]{1,0:T(8,128)(2,1)}, bf16[256,1024]{1,0:T(8,128)(2,1)}, u32[]{:S(2)}, u32[]{:S(2)}) collective-permute-start(bf16[256,1024]{1,0:T(8,128)(2,1)} %collective-permute-done.1.refs_3_), channel_id=1, source_target_pairs={{0,6},{1,7},{2,0},{3,1},{4,2},{5,3},{6,4},{7,5},{8,14},{9,15},{10,... | collective-permute-start | bytes 1572872 | tf_op jit(solution)/shard_map/ppermute | solution.py:29
  19.7 1.4 %collective-permute-start.8 = (bf16[256,1024]{1,0:T(8,128)(2,1)}, bf16[256,1024]{1,0:T(8,128)(2,1)}, u32[]{:S(2)}, u32[]{:S(2)}) collective-permute-start(bf16[256,1024]{1,0:T(8,128)(2,1)} %collective-permute-done.1.refs_3_), channel_id=1, source_target_pairs={{0,1},{1,0},{2,3},{3,2},{4,5},{5,4},{6,7},{7,6},{8,9},{9,8},{10,11... | collective-permute-start | bytes 1572872 | tf_op jit(solution)/shard_map/ppermute | solution.py:33
  21.2 0.1 pad_add_fusion.2.refs_0_
  21.3 1.0 copy-done.4
  22.3 5.5 %project.6.refs_7_ = f32[256,768]{1,0:T(8,128)S(1)} custom-call(s32[4]{0:T(128)S(1)} %pad_add_fusion.2.refs_0_, bf16[256,1024]{1,0:T(8,128)(2,1)S(1)} %bitcast.32, bf16[256,1024]{1,0:T(8,128)(2,1)} %collective-permute-done.refs_2_, bf16[256,1024]{1,0:T(8,128)(2,1)} %collective-permute-done.1.refs_3_, bf16[256,1024]{1,0:T(8,128)(2,1)} %collective-permute-done.2.refs_4_, ...), custom_call_target="tpu_custom_call" | custom-call | flops 1 | bytes 1 | tf_op jit(solution)/shard_map/project/pallas_call | solution.py:164
  27.9 1.9 %collective-permute-done.3.refs_1_ = bf16[256,1024]{1,0:T(8,128)(2,1)} collective-permute-done((bf16[256,1024]{1,0:T(8,128)(2,1)}, bf16[256,1024]{1,0:T(8,128)(2,1)}, u32[]{:S(2)}, u32[]{:S(2)}) %collective-permute-start.3) | collective-permute-done | bytes 524320 | tf_op jit(solution)/shard_map/ppermute | solution.py:29
  29.8 2.4 %collective-permute-start.6 = (bf16[256,1024]{1,0:T(8,128)(2,1)S(1)}, bf16[256,1024]{1,0:T(8,128)(2,1)}, u32[]{:S(2)}, u32[]{:S(2)}) collective-permute-start(bf16[256,1024]{1,0:T(8,128)(2,1)S(1)} %bitcast.26), channel_id=1, source_target_pairs={{0,6},{1,7},{2,0},{3,1},{4,2},{5,3},{6,4},{7,5},{8,14},{9,15},{10,... | collective-permute-start | bytes 1572872 | tf_op jit(solution)/shard_map/ppermute | solution.py:29
  32.3 0.1 pad_add_fusion.3.refs_0_
  32.3 4.8 %project.7.refs_5_ = f32[256,768]{1,0:T(8,128)S(1)} custom-call(s32[3]{0:T(128)S(1)} %pad_add_fusion.3.refs_0_, bf16[256,1024]{1,0:T(8,128)(2,1)} %collective-permute-done.3.refs_1_, bf16[256,1024]{1,0:T(8,128)(2,1)} %collective-permute-done.4.refs_2_, bf16[256,1024]{1,0:T(8,128)(2,1)} %collective-permute-done.8.refs_3_, bf16[8192,512]{1,0:T(8,128)(2,1)} %refs_3_.5, ...), custom_call_target="tpu_custom_call" | custom-call | flops 1 | bytes 1 | tf_op jit(solution)/shard_map/project/pallas_call | solution.py:164
  37.2 0.9 copy-done.1
  38.0 3.9 %collective-permute-done.7.refs_4_ = bf16[256,1024]{1,0:T(8,128)(2,1)} collective-permute-done((bf16[256,1024]{1,0:T(8,128)(2,1)S(1)}, bf16[256,1024]{1,0:T(8,128)(2,1)}, u32[]{:S(2)}, u32[]{:S(2)}) %collective-permute-start.7) | collective-permute-done | bytes 524320 | tf_op jit(solution)/shard_map/ppermute | solution.py:33
  42.0 1.6 %collective-permute-start.10 = (bf16[256,1024]{1,0:T(8,128)(2,1)}, bf16[256,1024]{1,0:T(8,128)(2,1)}, u32[]{:S(2)}, u32[]{:S(2)}) collective-permute-start(bf16[256,1024]{1,0:T(8,128)(2,1)} %collective-permute-done.6.refs_3_), channel_id=1, source_target_pairs={{0,6},{1,7},{2,0},{3,1},{4,2},{5,3},{6,4},{7,5},{8,14},{9,15},{10,... | collective-permute-start | bytes 1572872 | tf_op jit(solution)/shard_map/ppermute | solution.py:29
  43.6 1.5 %collective-permute-start.11 = (bf16[256,1024]{1,0:T(8,128)(2,1)}, bf16[256,1024]{1,0:T(8,128)(2,1)S(1)}, u32[]{:S(2)}, u32[]{:S(2)}) collective-permute-start(bf16[256,1024]{1,0:T(8,128)(2,1)} %collective-permute-done.6.refs_3_), channel_id=1, source_target_pairs={{0,1},{1,0},{2,3},{3,2},{4,5},{5,4},{6,7},{7,6},{8,9},{9,8},{10,11... | collective-permute-start | bytes 1572872 | tf_op jit(solution)/shard_map/ppermute | solution.py:33
  45.1 1.1 copy-done.2
  46.2 0.9 copy-done.6
  47.1 2.1 %project.8 = (bf16[320,256]{1,0:T(8,128)(2,1)S(1)}, bf16[320,256]{1,0:T(8,128)(2,1)S(1)}, bf16[320,256]{1,0:T(8,128)(2,1)S(1)}, bf16[320,256]{1,0:T(8,128)(2,1)S(1)}, bf16[512,256]{1,0:T(8,128)(2,1)S(1)}) custom-call(s32[1]{0:T(128)} %bitcast.10.refs_0_, bf16[256,1024]{1,0:T(8,128)(2,1)} %collective-permute-done.5.refs_1_, bf16[8192,512]{1,0:T(8,128)(2,1)} %refs_3_.5, ...), custom_call_target="tpu_custom_call" | custom-call | flops 1 | bytes 1 | tf_op jit(solution)/shard_map/project/pallas_call | solution.py:164
  49.2 2.7 %collective-permute-start.9 = (bf16[512,256]{1,0:T(8,128)(2,1)S(1)}, bf16[512,256]{1,0:T(8,128)(2,1)S(1)}, u32[]{:S(2)}, u32[]{:S(2)}) collective-permute-start(bf16[512,256]{1,0:T(8,128)(2,1)S(1)} %get-tuple-element.73), channel_id=1, source_target_pairs={{0,64},{8,72},{16,80},{24,88},{32,96},{40,104},{48,112},{56,120},{... | collective-permute-start | bytes 786440 | tf_op jit(solution)/shard_map/ppermute | solution.py:43
  51.9 2.8 %collective-permute-done.12.refs_2_ = bf16[256,1024]{1,0:T(8,128)(2,1)} collective-permute-done((bf16[256,1024]{1,0:T(8,128)(2,1)S(1)}, bf16[256,1024]{1,0:T(8,128)(2,1)}, u32[]{:S(2)}, u32[]{:S(2)}) %collective-permute-start.12) | collective-permute-done | bytes 524320 | tf_op jit(solution)/shard_map/ppermute | solution.py:29
  54.7 5.5 %project.9.refs_6_ = f32[256,768]{1,0:T(8,128)S(1)} custom-call(s32[4]{0:T(128)S(1)} %pad_add_fusion.2.refs_0_, bf16[256,1024]{1,0:T(8,128)(2,1)S(1)} %bitcast.28, bf16[256,1024]{1,0:T(8,128)(2,1)} %collective-permute-done.12.refs_2_, bf16[256,1024]{1,0:T(8,128)(2,1)} %collective-permute-done.6.refs_3_, bf16[256,1024]{1,0:T(8,128)(2,1)} %collective-permute-done.7.refs_4_, ...), custom_call_target="tpu_custom_call" | custom-call | flops 1 | bytes 1 | tf_op jit(solution)/shard_map/project/pallas_call | solution.py:164
  60.3 0.3 collective-permute-done.9
  60.6 2.4 %collective-permute-start.15 = (bf16[256,1024]{1,0:T(8,128)(2,1)S(1)}, bf16[256,1024]{1,0:T(8,128)(2,1)S(1)}, u32[]{:S(2)}, u32[]{:S(2)}) collective-permute-start(bf16[256,1024]{1,0:T(8,128)(2,1)S(1)} %collective-permute-done.11.refs_2_), channel_id=1, source_target_pairs={{0,6},{1,7},{2,0},{3,1},{4,2},{5,3},{6,4},{7,5},{8,14},{9,15},{10,... | collective-permute-start | bytes 1572872 | tf_op jit(solution)/shard_map/ppermute | solution.py:29
  63.2 1.9 %collective-permute-start.13 = (bf16[640,256]{1,0:T(8,128)(2,1)S(1)}, bf16[640,256]{1,0:T(8,128)(2,1)S(1)}, u32[]{:S(2)}, u32[]{:S(2)}) collective-permute-start(bf16[640,256]{1,0:T(8,128)(2,1)S(1)} %get-tuple-element.83), channel_id=1, source_target_pairs={{0,16},{8,24},{16,32},{24,40},{32,48},{40,56},{48,0},{56,8},{64,80... | collective-permute-start | bytes 983048 | tf_op jit(solution)/shard_map/ppermute | solution.py:43
  65.1 3.3 %collective-permute-start.17 = (bf16[640,256]{1,0:T(8,128)(2,1)S(1)}, bf16[640,256]{1,0:T(8,128)(2,1)S(1)}, u32[]{:S(2)}, u32[]{:S(2)}) collective-permute-start(bf16[640,256]{1,0:T(8,128)(2,1)S(1)} %get-tuple-element.95), channel_id=1, source_target_pairs={{0,32},{8,40},{16,48},{24,56},{32,0},{40,8},{48,16},{56,24},{64,96... | collective-permute-start | bytes 983048 | tf_op jit(solution)/shard_map/ppermute | solution.py:43
  68.4 0.7 collective-permute-start.18
  69.1 0.1 pad_add_fusion.4.refs_0_
  69.3 3.2 %project.10.refs_6_ = f32[256,768]{1,0:T(8,128)S(1)} custom-call(s32[2]{0:T(128)S(1)} %pad_add_fusion.5.refs_0_, bf16[256,1024]{1,0:T(8,128)(2,1)} %collective-permute-done.10.refs_1_, bf16[256,1024]{1,0:T(8,128)(2,1)S(1)} %collective-permute-done.11.refs_2_, bf16[8192,512]{1,0:T(8,128)(2,1)} %refs_3_.5, bf16[8192,128]{1,0:T(8,128)(2,1)S(1)} %copy-done, ...), custom_call_target="tpu_custom_call" | custom-call | flops 1 | bytes 1 | tf_op jit(solution)/shard_map/project/pallas_call | solution.py:164
  72.6 3.3 %project.11 = (bf16[320,256]{1,0:T(8,128)(2,1)S(1)}, bf16[320,256]{1,0:T(8,128)(2,1)S(1)}, bf16[320,256]{1,0:T(8,128)(2,1)S(1)}, bf16[320,256]{1,0:T(8,128)(2,1)...) custom-call(s32[2]{0:T(128)S(1)} %pad_add_fusion.4.refs_0_, ...), custom_call_target="tpu_custom_call" | custom-call | flops 1 | bytes 1 | tf_op jit(solution)/shard_map/project/pallas_call | solution.py:164
  75.9 3.0 %collective-permute-start.16 = (bf16[320,256]{1,0:T(8,128)(2,1)S(1)}, bf16[320,256]{1,0:T(8,128)(2,1)S(1)}, u32[]{:S(2)}, u32[]{:S(2)}) collective-permute-start(bf16[320,256]{1,0:T(8,128)(2,1)S(1)} %get-tuple-element.89), channel_id=1, source_target_pairs={{0,64},{8,72},{16,80},{24,88},{32,96},{40,104},{48,112},{56,120},{... | collective-permute-start | bytes 491528 | tf_op jit(solution)/shard_map/ppermute | solution.py:43
  78.9 0.5 collective-permute-start.23
  79.4 3.8 %collective-permute-start.24 = (bf16[320,256]{1,0:T(8,128)(2,1)S(1)}, bf16[320,256]{1,0:T(8,128)(2,1)S(1)}, u32[]{:S(2)}, u32[]{:S(2)}) collective-permute-start(bf16[320,256]{1,0:T(8,128)(2,1)S(1)} %get-tuple-element.103), channel_id=1, source_target_pairs={{0,96},{8,104},{16,112},{24,120},{32,64},{40,72},{48,80},{56,88},{... | collective-permute-start | bytes 491528 | tf_op jit(solution)/shard_map/ppermute | solution.py:43
  83.3 1.2 collective-permute-start.25
  84.5 0.1 pad_maximum_fusion
  84.6 0.6 copy-done.12
  85.3 6.8 %collective-permute-start.19 = (bf16[2560,256]{1,0:T(8,128)(2,1)S(1)}, bf16[2560,256]{1,0:T(8,128)(2,1)S(1)}, u32[]{:S(2)}, u32[]{:S(2)}) collective-permute-start(bf16[2560,256]{1,0:T(8,128)(2,1)S(1)} %pad_maximum_fusion), channel_id=1, source_target_pairs={{0,8},{8,0},{16,24},{24,16},{32,40},{40,32},{48,56},{56,48},{64,72... | collective-permute-start | bytes 3932168 | tf_op jit(solution)/shard_map/ppermute | solution.py:55
  92.1 0.4 collective-permute-start.20
  92.4 2.0 %collective-permute-start.21 = (bf16[320,256]{1,0:T(8,128)(2,1)S(1)}, bf16[320,256]{1,0:T(8,128)(2,1)S(1)}, u32[]{:S(2)}, u32[]{:S(2)}) collective-permute-start(bf16[320,256]{1,0:T(8,128)(2,1)S(1)} %get-tuple-element.99), channel_id=1, source_target_pairs={{0,32},{8,40},{16,48},{24,56},{32,0},{40,8},{48,16},{56,24},{64,96... | collective-permute-start | bytes 491528 | tf_op jit(solution)/shard_map/ppermute | solution.py:43
  94.5 1.9 %collective-permute-start.22 = (bf16[320,256]{1,0:T(8,128)(2,1)S(1)}, bf16[320,256]{1,0:T(8,128)(2,1)S(1)}, u32[]{:S(2)}, u32[]{:S(2)}) collective-permute-start(bf16[320,256]{1,0:T(8,128)(2,1)S(1)} %get-tuple-element.100), channel_id=1, source_target_pairs={{0,48},{8,56},{16,0},{24,8},{32,16},{40,24},{48,32},{56,40},{64,11... | collective-permute-start | bytes 491528 | tf_op jit(solution)/shard_map/ppermute | solution.py:43
  96.5 1.4 %collective-permute-start.27 = (bf16[1280,256]{1,0:T(8,128)(2,1)S(1)}, bf16[1280,256]{1,0:T(8,128)(2,1)S(1)}, u32[]{:S(2)}, u32[]{:S(2)}) collective-permute-start(bf16[1280,256]{1,0:T(8,128)(2,1)S(1)} %pad_maximum_fusion.2), channel_id=1, source_target_pairs={{0,8},{8,0},{16,24},{24,16},{32,40},{40,32},{48,56},{56,48},{64,72... | collective-permute-start | bytes 1966088 | tf_op jit(solution)/shard_map/ppermute | solution.py:55
  97.9 1.4 %collective-permute-done.20.refs_6_ = bf16[320,256]{1,0:T(8,128)(2,1)S(1)} collective-permute-done((bf16[320,256]{1,0:T(8,128)(2,1)S(1)}, bf16[320,256]{1,0:T(8,128)(2,1)S(1)}, u32[]{:S(2)}, u32[]{:S(2)}) %collective-permute-start.20) | collective-permute-done | bytes 163872 | tf_op jit(solution)/shard_map/ppermute | solution.py:43
  99.3 3.0 %collective-permute-done.21.refs_7_ = bf16[320,256]{1,0:T(8,128)(2,1)S(1)} collective-permute-done((bf16[320,256]{1,0:T(8,128)(2,1)S(1)}, bf16[320,256]{1,0:T(8,128)(2,1)S(1)}, u32[]{:S(2)}, u32[]{:S(2)}) %collective-permute-start.21) | collective-permute-done | bytes 163872 | tf_op jit(solution)/shard_map/ppermute | solution.py:43
  102.3 1.8 %collective-permute-done.22.refs_8_ = bf16[320,256]{1,0:T(8,128)(2,1)S(1)} collective-permute-done((bf16[320,256]{1,0:T(8,128)(2,1)S(1)}, bf16[320,256]{1,0:T(8,128)(2,1)S(1)}, u32[]{:S(2)}, u32[]{:S(2)}) %collective-permute-start.22) | collective-permute-done | bytes 163872 | tf_op jit(solution)/shard_map/ppermute | solution.py:43
  104.2 0.6 collective-permute-start.26
  104.8 1.7 %collective-permute-done.26.refs_13_ = bf16[1280,256]{1,0:T(8,128)(2,1)S(1)} collective-permute-done((bf16[1280,256]{1,0:T(8,128)(2,1)S(1)}, bf16[1280,256]{1,0:T(8,128)(2,1)S(1)}, u32[]{:S(2)}, u32[]{:S(2)}) %collective-permute-start.26) | collective-permute-done | bytes 655392 | tf_op jit(solution)/shard_map/ppermute | solution.py:55
  106.6 0.8 copy-done.22
  107.4 1.1 copy-done.13
  108.5 20.4 %attend.1 = bf16[512,512]{1,0:T(8,128)(2,1)} custom-call(s32[19]{0:T(128)} %pad_add_fusion.1.info, s32[256]{0:T(256)} %reshape.65.old_map, bf16[640,256]{1,0:T(8,128)(2,1)} %copy-done.9, bf16[640,256]{1,0:T(8,128)(2,1)} %copy-done.10, bf16[640,256]{1,0:T(8,128)(2,1)} %copy-done.11, bf16[640,256]{1,0:T(8,128)(2,1)} %copy-done.12, ...), custom_call_target="tpu_custom_call" | custom-call | tf_op jit(solution)/shard_map/attend/pallas_call | solution.py:245
  (82 shorter events, 0.7 us)
Async XLA Ops:
  0.0 6.2 %copy-start.24 = (s32[16,16]{1,0:T(8,128)S(1)}, s32[16,16]{1,0:T(8,128)}, u32[]{:S(2)}) copy-start(s32[16,16]{1,0:T(8,128)} %param.8) | copy-start | bytes 3076
  0.0 11.6 %copy-start.23 = (s32[16,16]{1,0:T(8,128)S(1)}, s32[16,16]{1,0:T(8,128)}, u32[]{:S(2)}) copy-start(s32[16,16]{1,0:T(8,128)} %param.7) | copy-start | bytes 3076
  1.3 19.9 %copy-start.3 = (bf16[16,1,16,1024]{3,2,1,0:T(8,128)(2,1)}, bf16[16,1,16,1024]{3,2,1,0:T(8,128)(2,1)S(1)}, u32[]{:S(2)}) copy-start(bf16[16,1,16,1024]{3,2,1,0:T(8,128)(2,1)S(1)} %get-tuple-element.107) | copy-start | bytes 1572868
  1.3 20.0 %copy-start = (bf16[8192,128]{1,0:T(8,128)(2,1)S(1)}, bf16[8192,128]{1,0:T(8,128)(2,1)}, u32[]{:S(2)}) copy-start(bf16[8192,128]{1,0:T(8,128)(2,1)} %refs_4_.7) | copy-start | bytes 6291460
  1.3 15.2 %collective-permute-start = (bf16[256,1024]{1,0:T(8,128)(2,1)S(1)}, bf16[256,1024]{1,0:T(8,128)(2,1)}, u32[]{:S(2)}, u32[]{:S(2)}) collective-permute-start(bf16[256,1024]{1,0:T(8,128)(2,1)S(1)} %bitcast.29), channel_id=1, source_target_pairs={{0,2},{1,3},{2,4},{3,5},{4,6},{5,7},{6,0},{7,1},{8,10},{9,11},{10,... | collective-permute-start | bytes 1572872 | tf_op jit(solution)/shard_map/ppermute | solution.py:29
  3.4 13.1 %collective-permute-start.1 = (bf16[256,1024]{1,0:T(8,128)(2,1)S(1)}, bf16[256,1024]{1,0:T(8,128)(2,1)}, u32[]{:S(2)}, u32[]{:S(2)}) collective-permute-start(bf16[256,1024]{1,0:T(8,128)(2,1)S(1)} %bitcast.30), channel_id=1, source_target_pairs={{0,6},{1,7},{2,0},{3,1},{4,2},{5,3},{6,4},{7,5},{8,14},{9,15},{10,... | collective-permute-start | bytes 1572872 | tf_op jit(solution)/shard_map/ppermute | solution.py:29
  4.8 12.3 %collective-permute-start.2 = (bf16[256,1024]{1,0:T(8,128)(2,1)S(1)}, bf16[256,1024]{1,0:T(8,128)(2,1)}, u32[]{:S(2)}, u32[]{:S(2)}) collective-permute-start(bf16[256,1024]{1,0:T(8,128)(2,1)S(1)} %bitcast.31), channel_id=1, source_target_pairs={{0,1},{1,0},{2,3},{3,2},{4,5},{5,4},{6,7},{7,6},{8,9},{9,8},{10,11... | collective-permute-start | bytes 1572872 | tf_op jit(solution)/shard_map/ppermute | solution.py:33
  17.1 12.8 %collective-permute-start.3 = (bf16[256,1024]{1,0:T(8,128)(2,1)}, bf16[256,1024]{1,0:T(8,128)(2,1)}, u32[]{:S(2)}, u32[]{:S(2)}) collective-permute-start(bf16[256,1024]{1,0:T(8,128)(2,1)} %collective-permute-done.2.refs_4_), channel_id=1, source_target_pairs={{0,2},{1,3},{2,4},{3,5},{4,6},{5,7},{6,0},{7,1},{8,10},{9,11},{10,... | collective-permute-start | bytes 1572872 | tf_op jit(solution)/shard_map/ppermute | solution.py:29
  17.2 12.6 %collective-permute-start.4 = (bf16[256,1024]{1,0:T(8,128)(2,1)}, bf16[256,1024]{1,0:T(8,128)(2,1)}, u32[]{:S(2)}, u32[]{:S(2)}) collective-permute-start(bf16[256,1024]{1,0:T(8,128)(2,1)} %collective-permute-done.1.refs_3_), channel_id=1, source_target_pairs={{0,6},{1,7},{2,0},{3,1},{4,2},{5,3},{6,4},{7,5},{8,14},{9,15},{10,... | collective-permute-start | bytes 1572872 | tf_op jit(solution)/shard_map/ppermute | solution.py:29
  19.7 12.5 %collective-permute-start.8 = (bf16[256,1024]{1,0:T(8,128)(2,1)}, bf16[256,1024]{1,0:T(8,128)(2,1)}, u32[]{:S(2)}, u32[]{:S(2)}) collective-permute-start(bf16[256,1024]{1,0:T(8,128)(2,1)} %collective-permute-done.1.refs_3_), channel_id=1, source_target_pairs={{0,1},{1,0},{2,3},{3,2},{4,5},{5,4},{6,7},{7,6},{8,9},{9,8},{10,11... | collective-permute-start | bytes 1572872 | tf_op jit(solution)/shard_map/ppermute | solution.py:33
  21.3 20.7 %collective-permute-start.7 = (bf16[256,1024]{1,0:T(8,128)(2,1)S(1)}, bf16[256,1024]{1,0:T(8,128)(2,1)}, u32[]{:S(2)}, u32[]{:S(2)}) collective-permute-start(bf16[256,1024]{1,0:T(8,128)(2,1)S(1)} %bitcast.25), channel_id=1, source_target_pairs={{0,1},{1,0},{2,3},{3,2},{4,5},{5,4},{6,7},{7,6},{8,9},{9,8},{10,11... | collective-permute-start | bytes 1572872 | tf_op jit(solution)/shard_map/ppermute | solution.py:33
  21.3 1.0 copy-start.4
  29.8 12.2 %collective-permute-start.6 = (bf16[256,1024]{1,0:T(8,128)(2,1)S(1)}, bf16[256,1024]{1,0:T(8,128)(2,1)}, u32[]{:S(2)}, u32[]{:S(2)}) collective-permute-start(bf16[256,1024]{1,0:T(8,128)(2,1)S(1)} %bitcast.26), channel_id=1, source_target_pairs={{0,6},{1,7},{2,0},{3,1},{4,2},{5,3},{6,4},{7,5},{8,14},{9,15},{10,... | collective-permute-start | bytes 1572872 | tf_op jit(solution)/shard_map/ppermute | solution.py:29
  32.2 12.8 %collective-permute-start.5 = (bf16[256,1024]{1,0:T(8,128)(2,1)}, bf16[256,1024]{1,0:T(8,128)(2,1)}, u32[]{:S(2)}, u32[]{:S(2)}) collective-permute-start(bf16[256,1024]{1,0:T(8,128)(2,1)} %collective-permute-done.3.refs_1_), channel_id=1, source_target_pairs={{0,2},{1,3},{2,4},{3,5},{4,6},{5,7},{6,0},{7,1},{8,10},{9,11},{10,... | collective-permute-start | bytes 1572872 | tf_op jit(solution)/shard_map/ppermute | solution.py:29
  32.2 22.5 %collective-permute-start.12 = (bf16[256,1024]{1,0:T(8,128)(2,1)S(1)}, bf16[256,1024]{1,0:T(8,128)(2,1)}, u32[]{:S(2)}, u32[]{:S(2)}) collective-permute-start(bf16[256,1024]{1,0:T(8,128)(2,1)S(1)} %bitcast.27), channel_id=1, source_target_pairs={{0,2},{1,3},{2,4},{3,5},{4,6},{5,7},{6,0},{7,1},{8,10},{9,11},{10,... | collective-permute-start | bytes 1572872 | tf_op jit(solution)/shard_map/ppermute | solution.py:29
  37.1 0.9 copy-start.1
  42.0 18.7 %collective-permute-start.10 = (bf16[256,1024]{1,0:T(8,128)(2,1)}, bf16[256,1024]{1,0:T(8,128)(2,1)}, u32[]{:S(2)}, u32[]{:S(2)}) collective-permute-start(bf16[256,1024]{1,0:T(8,128)(2,1)} %collective-permute-done.6.refs_3_), channel_id=1, source_target_pairs={{0,6},{1,7},{2,0},{3,1},{4,2},{5,3},{6,4},{7,5},{8,14},{9,15},{10,... | collective-permute-start | bytes 1572872 | tf_op jit(solution)/shard_map/ppermute | solution.py:29
  43.6 17.1 %collective-permute-start.11 = (bf16[256,1024]{1,0:T(8,128)(2,1)}, bf16[256,1024]{1,0:T(8,128)(2,1)S(1)}, u32[]{:S(2)}, u32[]{:S(2)}) collective-permute-start(bf16[256,1024]{1,0:T(8,128)(2,1)} %collective-permute-done.6.refs_3_), channel_id=1, source_target_pairs={{0,1},{1,0},{2,3},{3,2},{4,5},{5,4},{6,7},{7,6},{8,9},{9,8},{10,11... | collective-permute-start | bytes 1572872 | tf_op jit(solution)/shard_map/ppermute | solution.py:33
  45.0 1.1 copy-start.2
  46.2 0.9 copy-start.6
  49.2 11.3 %collective-permute-start.9 = (bf16[512,256]{1,0:T(8,128)(2,1)S(1)}, bf16[512,256]{1,0:T(8,128)(2,1)S(1)}, u32[]{:S(2)}, u32[]{:S(2)}) collective-permute-start(bf16[512,256]{1,0:T(8,128)(2,1)S(1)} %get-tuple-element.73), channel_id=1, source_target_pairs={{0,64},{8,72},{16,80},{24,88},{32,96},{40,104},{48,112},{56,120},{... | collective-permute-start | bytes 786440 | tf_op jit(solution)/shard_map/ppermute | solution.py:43
  54.7 17.8 %collective-permute-start.14 = (bf16[256,1024]{1,0:T(8,128)(2,1)}, bf16[256,1024]{1,0:T(8,128)(2,1)S(1)}, u32[]{:S(2)}, u32[]{:S(2)}) collective-permute-start(bf16[256,1024]{1,0:T(8,128)(2,1)} %collective-permute-done.7.refs_4_), channel_id=1, source_target_pairs={{0,2},{1,3},{2,4},{3,5},{4,6},{5,7},{6,0},{7,1},{8,10},{9,11},{10,... | collective-permute-start | bytes 1572872 | tf_op jit(solution)/shard_map/ppermute | solution.py:29
  60.6 11.9 %collective-permute-start.15 = (bf16[256,1024]{1,0:T(8,128)(2,1)S(1)}, bf16[256,1024]{1,0:T(8,128)(2,1)S(1)}, u32[]{:S(2)}, u32[]{:S(2)}) collective-permute-start(bf16[256,1024]{1,0:T(8,128)(2,1)S(1)} %collective-permute-done.11.refs_2_), channel_id=1, source_target_pairs={{0,6},{1,7},{2,0},{3,1},{4,2},{5,3},{6,4},{7,5},{8,14},{9,15},{10,... | collective-permute-start | bytes 1572872 | tf_op jit(solution)/shard_map/ppermute | solution.py:29
  63.1 21.4 %copy-start.9 = (bf16[640,256]{1,0:T(8,128)(2,1)}, bf16[640,256]{1,0:T(8,128)(2,1)S(1)}, u32[]{:S(2)}) copy-start(bf16[640,256]{1,0:T(8,128)(2,1)S(1)} %pad_maximum_fusion.6.refs_0_) | copy-start | bytes 983044
  63.2 16.2 %collective-permute-start.13 = (bf16[640,256]{1,0:T(8,128)(2,1)S(1)}, bf16[640,256]{1,0:T(8,128)(2,1)S(1)}, u32[]{:S(2)}, u32[]{:S(2)}) collective-permute-start(bf16[640,256]{1,0:T(8,128)(2,1)S(1)} %get-tuple-element.83), channel_id=1, source_target_pairs={{0,16},{8,24},{16,32},{24,40},{32,48},{40,56},{48,0},{56,8},{64,80... | collective-permute-start | bytes 983048 | tf_op jit(solution)/shard_map/ppermute | solution.py:43
  65.1 18.2 %collective-permute-start.17 = (bf16[640,256]{1,0:T(8,128)(2,1)S(1)}, bf16[640,256]{1,0:T(8,128)(2,1)S(1)}, u32[]{:S(2)}, u32[]{:S(2)}) collective-permute-start(bf16[640,256]{1,0:T(8,128)(2,1)S(1)} %get-tuple-element.95), channel_id=1, source_target_pairs={{0,32},{8,40},{16,48},{24,56},{32,0},{40,8},{48,16},{56,24},{64,96... | collective-permute-start | bytes 983048 | tf_op jit(solution)/shard_map/ppermute | solution.py:43
  68.4 16.1 %collective-permute-start.18 = (bf16[640,256]{1,0:T(8,128)(2,1)S(1)}, bf16[640,256]{1,0:T(8,128)(2,1)S(1)}, u32[]{:S(2)}, u32[]{:S(2)}) collective-permute-start(bf16[640,256]{1,0:T(8,128)(2,1)S(1)} %get-tuple-element.96), channel_id=1, source_target_pairs={{0,48},{8,56},{16,0},{24,8},{32,16},{40,24},{48,32},{56,40},{64,11... | collective-permute-start | bytes 983048 | tf_op jit(solution)/shard_map/ppermute | solution.py:43
  69.3 3.3 %copy-start.7 = (f32[256,128]{1,0:T(8,128)S(1)}, f32[256,128]{1,0:T(8,128)}, u32[]{:S(2)}) copy-start(f32[256,128]{1,0:T(8,128)} %get-tuple-element.87.refs_8_) | copy-start | bytes 393220
  69.3 3.3 %copy-start.8 = (f32[256,128]{1,0:T(8,128)S(1)}, f32[256,128]{1,0:T(8,128)}, u32[]{:S(2)}) copy-start(f32[256,128]{1,0:T(8,128)} %get-tuple-element.88.refs_9_) | copy-start | bytes 393220
  75.9 28.2 %copy-start.5 = (bf16[320,256]{1,0:T(8,128)(2,1)}, bf16[320,256]{1,0:T(8,128)(2,1)S(1)}, u32[]{:S(2)}) copy-start(bf16[320,256]{1,0:T(8,128)(2,1)S(1)} %get-tuple-element.97.refs_5_) | copy-start | bytes 491524
  75.9 16.2 %collective-permute-start.16 = (bf16[320,256]{1,0:T(8,128)(2,1)S(1)}, bf16[320,256]{1,0:T(8,128)(2,1)S(1)}, u32[]{:S(2)}, u32[]{:S(2)}) collective-permute-start(bf16[320,256]{1,0:T(8,128)(2,1)S(1)} %get-tuple-element.89), channel_id=1, source_target_pairs={{0,64},{8,72},{16,80},{24,88},{32,96},{40,104},{48,112},{56,120},{... | collective-permute-start | bytes 491528 | tf_op jit(solution)/shard_map/ppermute | solution.py:43
  78.9 13.5 %collective-permute-start.23 = (bf16[320,256]{1,0:T(8,128)(2,1)S(1)}, bf16[320,256]{1,0:T(8,128)(2,1)S(1)}, u32[]{:S(2)}, u32[]{:S(2)}) collective-permute-start(bf16[320,256]{1,0:T(8,128)(2,1)S(1)} %get-tuple-element.102), channel_id=1, source_target_pairs={{0,80},{8,88},{16,96},{24,104},{32,112},{40,120},{48,64},{56,72},{... | collective-permute-start | bytes 491528 | tf_op jit(solution)/shard_map/ppermute | solution.py:43
  79.4 5.2 %copy-start.10 = (bf16[640,256]{1,0:T(8,128)(2,1)}, bf16[640,256]{1,0:T(8,128)(2,1)S(1)}, u32[]{:S(2)}) copy-start(bf16[640,256]{1,0:T(8,128)(2,1)S(1)} %collective-permute-done.13.refs_1_) | copy-start | bytes 983044
  79.4 15.0 %collective-permute-start.24 = (bf16[320,256]{1,0:T(8,128)(2,1)S(1)}, bf16[320,256]{1,0:T(8,128)(2,1)S(1)}, u32[]{:S(2)}, u32[]{:S(2)}) collective-permute-start(bf16[320,256]{1,0:T(8,128)(2,1)S(1)} %get-tuple-element.103), channel_id=1, source_target_pairs={{0,96},{8,104},{16,112},{24,120},{32,64},{40,72},{48,80},{56,88},{... | collective-permute-start | bytes 491528 | tf_op jit(solution)/shard_map/ppermute | solution.py:43
  83.3 1.4 %copy-start.11 = (bf16[640,256]{1,0:T(8,128)(2,1)}, bf16[640,256]{1,0:T(8,128)(2,1)S(1)}, u32[]{:S(2)}) copy-start(bf16[640,256]{1,0:T(8,128)(2,1)S(1)} %collective-permute-done.17.refs_2_) | copy-start | bytes 983044
  83.3 13.1 %collective-permute-start.25 = (bf16[320,256]{1,0:T(8,128)(2,1)S(1)}, bf16[320,256]{1,0:T(8,128)(2,1)S(1)}, u32[]{:S(2)}, u32[]{:S(2)}) collective-permute-start(bf16[320,256]{1,0:T(8,128)(2,1)S(1)} %get-tuple-element.104), channel_id=1, source_target_pairs={{0,112},{8,120},{16,64},{24,72},{32,80},{40,88},{48,96},{56,104},{... | collective-permute-start | bytes 491528 | tf_op jit(solution)/shard_map/ppermute | solution.py:43
  84.5 0.7 copy-start.12
  85.3 21.3 %collective-permute-start.19 = (bf16[2560,256]{1,0:T(8,128)(2,1)S(1)}, bf16[2560,256]{1,0:T(8,128)(2,1)S(1)}, u32[]{:S(2)}, u32[]{:S(2)}) collective-permute-start(bf16[2560,256]{1,0:T(8,128)(2,1)S(1)} %pad_maximum_fusion), channel_id=1, source_target_pairs={{0,8},{8,0},{16,24},{24,16},{32,40},{40,32},{48,56},{56,48},{64,72... | collective-permute-start | bytes 3932168 | tf_op jit(solution)/shard_map/ppermute | solution.py:55
  92.1 12.1 %copy-start.14 = (bf16[320,256]{1,0:T(8,128)(2,1)}, bf16[320,256]{1,0:T(8,128)(2,1)S(1)}, u32[]{:S(2)}) copy-start(bf16[320,256]{1,0:T(8,128)(2,1)S(1)} %collective-permute-done.16.refs_9_) | copy-start | bytes 491524
  92.1 7.2 %collective-permute-start.20 = (bf16[320,256]{1,0:T(8,128)(2,1)S(1)}, bf16[320,256]{1,0:T(8,128)(2,1)S(1)}, u32[]{:S(2)}, u32[]{:S(2)}) collective-permute-start(bf16[320,256]{1,0:T(8,128)(2,1)S(1)} %get-tuple-element.98), channel_id=1, source_target_pairs={{0,16},{8,24},{16,32},{24,40},{32,48},{40,56},{48,0},{56,8},{64,80... | collective-permute-start | bytes 491528 | tf_op jit(solution)/shard_map/ppermute | solution.py:43
  92.4 11.7 %copy-start.15 = (bf16[320,256]{1,0:T(8,128)(2,1)}, bf16[320,256]{1,0:T(8,128)(2,1)S(1)}, u32[]{:S(2)}) copy-start(bf16[320,256]{1,0:T(8,128)(2,1)S(1)} %collective-permute-done.23.refs_10_) | copy-start | bytes 491524
  92.4 9.9 %collective-permute-start.21 = (bf16[320,256]{1,0:T(8,128)(2,1)S(1)}, bf16[320,256]{1,0:T(8,128)(2,1)S(1)}, u32[]{:S(2)}, u32[]{:S(2)}) collective-permute-start(bf16[320,256]{1,0:T(8,128)(2,1)S(1)} %get-tuple-element.99), channel_id=1, source_target_pairs={{0,32},{8,40},{16,48},{24,56},{32,0},{40,8},{48,16},{56,24},{64,96... | collective-permute-start | bytes 491528 | tf_op jit(solution)/shard_map/ppermute | solution.py:43
  94.5 9.7 %copy-start.16 = (bf16[320,256]{1,0:T(8,128)(2,1)}, bf16[320,256]{1,0:T(8,128)(2,1)S(1)}, u32[]{:S(2)}) copy-start(bf16[320,256]{1,0:T(8,128)(2,1)S(1)} %collective-permute-done.24.refs_11_) | copy-start | bytes 491524
  94.5 9.6 %collective-permute-start.22 = (bf16[320,256]{1,0:T(8,128)(2,1)S(1)}, bf16[320,256]{1,0:T(8,128)(2,1)S(1)}, u32[]{:S(2)}, u32[]{:S(2)}) collective-permute-start(bf16[320,256]{1,0:T(8,128)(2,1)S(1)} %get-tuple-element.100), channel_id=1, source_target_pairs={{0,48},{8,56},{16,0},{24,8},{32,16},{40,24},{48,32},{56,40},{64,11... | collective-permute-start | bytes 491528 | tf_op jit(solution)/shard_map/ppermute | solution.py:43
  96.4 7.8 %copy-start.17 = (bf16[320,256]{1,0:T(8,128)(2,1)}, bf16[320,256]{1,0:T(8,128)(2,1)S(1)}, u32[]{:S(2)}) copy-start(bf16[320,256]{1,0:T(8,128)(2,1)S(1)} %collective-permute-done.25.refs_12_) | copy-start | bytes 491524
  96.5 8.4 %collective-permute-start.27 = (bf16[1280,256]{1,0:T(8,128)(2,1)S(1)}, bf16[1280,256]{1,0:T(8,128)(2,1)S(1)}, u32[]{:S(2)}, u32[]{:S(2)}) collective-permute-start(bf16[1280,256]{1,0:T(8,128)(2,1)S(1)} %pad_maximum_fusion.2), channel_id=1, source_target_pairs={{0,8},{8,0},{16,24},{24,16},{32,40},{40,32},{48,56},{56,48},{64,72... | collective-permute-start | bytes 1966088 | tf_op jit(solution)/shard_map/ppermute | solution.py:55
  99.3 7.3 %copy-start.18 = (bf16[320,256]{1,0:T(8,128)(2,1)}, bf16[320,256]{1,0:T(8,128)(2,1)S(1)}, u32[]{:S(2)}) copy-start(bf16[320,256]{1,0:T(8,128)(2,1)S(1)} %collective-permute-done.20.refs_6_) | copy-start | bytes 491524
  102.3 4.3 %copy-start.19 = (bf16[320,256]{1,0:T(8,128)(2,1)}, bf16[320,256]{1,0:T(8,128)(2,1)S(1)}, u32[]{:S(2)}) copy-start(bf16[320,256]{1,0:T(8,128)(2,1)S(1)} %collective-permute-done.21.refs_7_) | copy-start | bytes 491524
  104.1 2.5 %copy-start.20 = (bf16[320,256]{1,0:T(8,128)(2,1)}, bf16[320,256]{1,0:T(8,128)(2,1)S(1)}, u32[]{:S(2)}) copy-start(bf16[320,256]{1,0:T(8,128)(2,1)S(1)} %collective-permute-done.22.refs_8_) | copy-start | bytes 491524
  104.2 2.4 %collective-permute-start.26 = (bf16[1280,256]{1,0:T(8,128)(2,1)S(1)}, bf16[1280,256]{1,0:T(8,128)(2,1)S(1)}, u32[]{:S(2)}, u32[]{:S(2)}) collective-permute-start(bf16[1280,256]{1,0:T(8,128)(2,1)S(1)} %pad_maximum_fusion.1), channel_id=1, source_target_pairs={{0,8},{8,0},{16,24},{24,16},{32,40},{40,32},{48,56},{56,48},{64,72... | collective-permute-start | bytes 1966088 | tf_op jit(solution)/shard_map/ppermute | solution.py:55
  104.8 1.7 %copy-start.21 = (bf16[1280,256]{1,0:T(8,128)(2,1)}, bf16[1280,256]{1,0:T(8,128)(2,1)S(1)}, u32[]{:S(2)}) copy-start(bf16[1280,256]{1,0:T(8,128)(2,1)S(1)} %collective-permute-done.27.refs_14_) | copy-start | bytes 1966084
  106.6 0.8 copy-start.22
  107.4 1.1 copy-start.13

commit v6 on v5

--- a/solution.py
+++ b/solution.py
@@ -20,6 +20,7 @@
 KB = 512
 VMEM = pl.BlockSpec(memory_space=pltpu.VMEM)
 SMEM = pl.BlockSpec(memory_space=pltpu.SMEM)
+ANY = pl.BlockSpec(memory_space=pl.ANY)
 
 CHIPS = [(dh, dz) for dh in range(2) for dz in range(4)]
 
@@ -74,107 +75,101 @@
     return jnp.concatenate([block[:, at : at + HEAD] - lanes for at in range(0, block.shape[1], HEAD)], axis=1)
 
 
-def project_kernel(groups, has_acc, last, joint, *refs):
-    features, refs = refs[0], refs[1:]
-    blocks, at = [], 0
-    for n in groups:
-        blocks.append(refs[at : at + n])
-        at += n
-    wq, wk, wv = refs[at : at + 3]
-    at += 3
+def project_kernel(count, has_acc, last, joint, features, *refs):
+    blocks, (wq, wk, wv), refs = refs[:count], refs[count : count + 3], refs[count + 3 :]
     acc_in = None
     if has_acc:
-        acc_in = refs[at]
-        at += 1
+        acc_in, refs = refs[0], refs[1:]
     if last:
-        info, cosine, sine = refs[at : at + 3]
-        at += 3
-        outs = refs[at:-2]
-        acc, heads = refs[-2:]
+        info, cosine, sine = refs[:3]
+        held, held_sems, acc, heads, packed, packed_sems = refs[-6:]
+        outs = refs[3:-6]
     else:
-        out, acc = refs[at : at + 2]
-    step = pl.program_id(0)
-
-    for i, parts in enumerate(blocks):
-
-        @pl.when(step == i)
-        def add(i=i, parts=parts):
-            block = parts[0][...] if len(parts) == 1 else jnp.concatenate([p[...] for p in parts], axis=0)
-            for lo, hi, w in ((0, 512, wq[...]), (512, 768, jnp.concatenate([wk[...], wv[...]], axis=1))):
-                value = dot(block, w)
-                if i > 0:
-                    value = value + acc[:, lo:hi]
-                elif has_acc:
-                    value = value + acc_in[:, lo:hi]
-                acc[:, lo:hi] = value
-
-    @pl.when(step == len(blocks) - 1)
-    def finish():
-        if not last:
-            out[...] = acc[...]
-            return
-        cos, sin = cosine[...], sine[...]
-
-        def rotated(lo):
-            vector = acc[:, lo : lo + HEAD]
-            return (vector * cos + pltpu.roll(vector, HEAD // 2, 1) * sin).astype(jnp.bfloat16)
-
-        for h in range(4):
-            heads[:, h * HEAD : (h + 1) * HEAD] = rotated(h * HEAD)
-        key = rotated(512)
-        value = acc[:, 640:768].astype(jnp.bfloat16)
-        me = info[0]
-        high, z = me // 8, lax.rem(me // 2, 4)
-        for payload in outs:
-            payload[0:ROWS, 0:HEAD] = key
-            payload[0:ROWS, HEAD : 2 * HEAD] = value
-        for r, (dh, dz) in enumerate(CHIPS):
-            to, base = (outs[4], dz * 4 * W) if joint and dh else (outs[r], 0)
+        acc, held, held_sems = refs
+    copies = [pltpu.make_async_copy(blocks[i], held.at[i], held_sems.at[i]) for i in range(count)]
+    for copy in copies:
+        copy.start()
+    for i, copy in enumerate(copies):
+        copy.wait()
+        rows = pl.ds(pl.multiple_of(features[i] * 1024, 1024), 1024)
+        block = held[i]
+        for lo, hi in ((0, 512), (512, 768)):
+            w = wq[rows, :] if lo == 0 else jnp.concatenate([wk[rows, :], wv[rows, :]], axis=1)
+            value = dot(block, w)
+            if i > 0:
+                value = value + acc[:, lo:hi]
+            elif has_acc:
+                value = value + acc_in[:, lo:hi]
+            acc[:, lo:hi] = value
+    if not last:
+        return
+    cos, sin = cosine[...], sine[...]
+
+    def rotated(lo):
+        vector = acc[:, lo : lo + HEAD]
+        return (vector * cos + pltpu.roll(vector, HEAD // 2, 1) * sin).astype(jnp.bfloat16)
+
+    for h in range(4):
+        heads[:, h * HEAD : (h + 1) * HEAD] = rotated(h * HEAD)
+    key = rotated(512)
+    value = acc[:, 640:768].astype(jnp.bfloat16)
+    me = info[0]
+    high, z = me // 8, lax.rem(me // 2, 4)
+    starts = [sum(out.shape[0] for out in outs[:r]) for r in range(len(outs))]
+    sends = []
+    for r, out in enumerate(outs):
+        base = starts[r]
+        packed[base : base + ROWS, 0:HEAD] = key
+        packed[base : base + ROWS, HEAD : 2 * HEAD] = value
+        chips = CHIPS[4:] if joint and r == 4 else CHIPS[r : r + 1]
+        for n, (dh, dz) in enumerate(chips):
             chip = lax.rem(high + dh, 2) * 8 + lax.rem(z + dz, 4) * 2
             for core in range(2):
-                k = info[1 + chip + core]
-                rows = pl.ds(pl.multiple_of(k * W, W), W)
+                rows = pl.ds(pl.multiple_of(info[1 + chip + core] * W, W), W)
                 for half in range(2):
-                    at = ROWS + base + (core * 2 + half) * W
-                    to[at : at + W, :] = heads[rows, half * 256 : half * 256 + 256]
+                    at = base + ROWS + (n * 4 + core * 2 + half) * W
+                    packed[at : at + W, :] = heads[rows, half * 256 : half * 256 + 256]
+        send = pltpu.make_async_copy(packed.at[base : base + out.shape[0]], out, packed_sems.at[r])
+        send.start()
+        sends.append(send)
+    for send in sends:
+        send.wait()
 
 
 def project(features, blocks, weights, acc=None, tables=None, joint=False):
-    groups = [len(b) for b in blocks]
-    flat = [p for b in blocks for p in b]
-    whole = lambda shape: pl.BlockSpec(shape, lambda i, f: (0,) * len(shape))
+    count = len(blocks)
     last = tables is not None
-    specs = [whole(p.shape) for p in flat]
-    specs += [pl.BlockSpec((1024, w.shape[1]), lambda i, f: (f[i], 0)) for w in weights]
-    operands = flat + list(weights)
+    specs = [SMEM] + [ANY] * count + [VMEM] * 3
+    operands = [features, *blocks, *weights]
     if acc is not None:
-        specs.append(whole(acc.shape))
+        specs.append(VMEM)
         operands.append(acc)
-    scratch = [pltpu.VMEM((ROWS, 768), jnp.float32)]
+    scratch = [pltpu.VMEM((count, ROWS, 1024), jnp.bfloat16), pltpu.SemaphoreType.DMA((count,))]
     if last:
-        specs += [SMEM, whole((ROWS, HEAD)), whole((ROWS, HEAD))]
+        specs += [SMEM, VMEM, VMEM]
         operands += list(tables)
         sizes = [PAYLOAD] * 4 + [2 * ROWS] if joint else [PAYLOAD] * 8
         out_shape = [jax.ShapeDtypeStruct((n, 256), jnp.bfloat16) for n in sizes]
-        out_specs = [whole((n, 256)) for n in sizes]
-        scratch.append(pltpu.VMEM((ROWS, 512), jnp.bfloat16))
+        out_specs = [ANY] * len(sizes)
+        scratch += [
+            pltpu.VMEM((ROWS, 768), jnp.float32),
+            pltpu.VMEM((ROWS, 512), jnp.bfloat16),
+            pltpu.VMEM((sum(sizes), 256), jnp.bfloat16),
+            pltpu.SemaphoreType.DMA((len(sizes),)),
+        ]
     else:
         out_shape = jax.ShapeDtypeStruct((ROWS, 768), jnp.float32)
-        out_specs = whole((ROWS, 768))
+        out_specs = VMEM
     return pl.pallas_call(
-        functools.partial(project_kernel, groups, acc is not None, last, joint),
-        grid_spec=pltpu.PrefetchScalarGridSpec(
-            num_scalar_prefetch=1,
-            grid=(len(blocks),),
-            in_specs=specs,
-            out_specs=out_specs,
-            scratch_shapes=scratch,
-        ),
+        functools.partial(project_kernel, count, acc is not None, last, joint),
+        in_specs=specs,
+        out_specs=out_specs,
         out_shape=out_shape,
-        compiler_params=pltpu.CompilerParams(vmem_limit_bytes=48 * 2**20),
+        scratch_shapes=scratch,
+        compiler_params=pltpu.CompilerParams(vmem_limit_bytes=32 * 2**20),
         cost_estimate=pl.CostEstimate(flops=1, bytes_accessed=1, transcendentals=0),
         name="project",
-    )(features, *operands)
+    )(*operands)
 
 
 def attend_kernel(info, old_map, *refs):
@@ -312,34 +307,34 @@
     far = shift_x(right, -1)
     right_across = swap_y(right)
     late_across = swap_y(late)
-    total = project(features[:4], [(early,), (left,), (right,), (across,)], weights)
+    total = project(features[:4], [early, left, right, across], weights)
     left_across, far, late = together(left_across, far, after(late, total))
     late_right = shift_x(late, -1)
     far_across = shift_x(left_across, 1)
     right_across = after(right_across, late)
-    late_left = shift_x(after(late, right_across), 1)
-    total = project(features[4:7], [(left_across,), (far,), (right_across,)], weights, total)
-    late_right, late_across, total = together(late_right, late_across, total)
+    total = project(features[4:7], [left_across, far, right_across], weights, total)
+    late_right, total = together(late_right, total)
     late_far = shift_x(late_right, -1)
     late_right_across = swap_y(late_right)
     far_across = after(far_across, late_right)
-    sent = project(features[7:], [(far_across,)], weights, total, (send_info, *tables[:2]), joint=True)
+    late_left = shift_x(after(late, far_across), 1)
+    sent = project(features[7:], [far_across], weights, total, (send_info, *tables[:2]), joint=True)
     partner = shift_ctx(sent[4], 1, 0)
     late_across, late_left = together(late_across, late_left, sent[0])[:2]
     late_left_across = shift_x(late_across, 1)
-    blocks = [(late,), (late_left,), (late_right,), (late_across,)]
-    total = project(features[:4], blocks, weights)
-    late_far, late_right_across, total = together(late_far, late_right_across, total)
+    total = project(features[:4], [late, late_left, late_right, late_across], weights)
+    late_far, late_right_across = together(late_far, late_right_across)
     late_far_across = shift_x(late_right_across, -1)
+    partner, total = together(partner, total)
     early_parts = [
         jnp.concatenate([sent[dz], partner[:ROWS], partner[ROWS + dz * 4 * W : ROWS + (dz + 1) * 4 * W]], axis=0)
         for dz in range(4)
     ]
     *early_parts, total = together(*early_parts, total)
-    total = project(features[5:7], [(late_far,), (late_right_across,)], weights, total)
+    total = project(features[5:7], [late_far, late_right_across], weights, total)
     early_parts[1:] = [shift_ctx(early_parts[dz], 0, dz) for dz in range(1, 4)]
     last = jnp.stack([features[4], features[7]])
-    tail = [(late_left_across,), (late_far_across,)]
+    tail = [late_left_across, late_far_across]
     sent = project(last, tail, weights, total, (send_info, *tables[2:]))
     early_other = swap_core(jnp.concatenate(early_parts, axis=0))
     sent = list(sent)

time: 130 us -> 135 us (1.038)
  local copies, waits for them, and re-layouts: 9.38 us -> 24.3 us
  waiting for transfers between devices: 17.5 us -> 9.65 us
  Pallas kernels: 45 us -> 41.7 us
  starting transfers between devices: 47.4 us -> 49.4 us
    unnamed x50 -> x64, local copies, waits for them, and re-layouts: 6.56 us -> 21.5 us
    ppermute x10, waiting for transfers between devices: 4.73 us -> 0.04 us  [shift_x(): return lax.ppermute(block, 'tp', perm)]
    ppermute x4, waiting for transfers between devices: 4.49 us -> 0.44 us  [swap_y(): return lax.ppermute(block, 'tp', [(i, i ^ 1) for i in range(8)])]
    pallas_call x6, Pallas kernels: 24.5 us -> 21.3 us  [project(): pl.pallas_call(functools.partial(project_kernel, count, acc is not None,...]
    ppermute x3, starting transfers between devices: 8.87 us -> 10.7 us  [swap_core(): return lax.ppermute(block, 'ctx', [(i, i ^ 1) for i in range(16)])]
  transfers between devices with their start and end apart: 28 -> 28, of which waited for: 9 -> 5; matrix products, arithmetic and copies ran while one was open for 5% -> 4% of each run, Pallas kernels for 19% -> 16%
where the time goes in v6:
time: 135 us
  starting transfers between devices  49.4 us (37%)
  Pallas kernels  41.7 us (31%)
  local copies, waits for them, and re-layouts  24.3 us (18%)
  waiting for transfers between devices  9.65 us (7%)
  between operations  5.37 us (4%)
  other arithmetic  4.51 us (3%)
    unnamed x64, local copies, waits for them, and re-layouts  21.5 us
    pallas_call x6, Pallas kernels, project(): pl.pallas_call(functools.partial(project_kernel, count, acc is not None,...  21.3 us
    ppermute x11, starting transfers between devices, shift_ctx(): return lax.ppermute(block, 'ctx', perm)  20.9 us
    pallas_call x1, Pallas kernels, attend(): pl.pallas_call(attend_kernel, out_shape=jax.ShapeDtypeStruct((512, 512),...  20.4 us
    ppermute x10, starting transfers between devices, shift_x(): return lax.ppermute(block, 'tp', perm)  12.1 us
    ppermute x3, starting transfers between devices, swap_core(): return lax.ppermute(block, 'ctx', [(i, i ^ 1) for i in range(16)])  10.7 us
    ppermute x11, waiting for transfers between devices, shift_ctx(): return lax.ppermute(block, 'ctx', perm)  7.44 us
    ppermute x4, starting transfers between devices, swap_y(): return lax.ppermute(block, 'tp', [(i, i ^ 1) for i in range(8)])  5.59 us
  transfers between devices with their start and end apart: 28, of which 5 were waited for; matrix products, arithmetic and copies ran while one was open for 4% of the time, Pallas kernels for 16%

profile of v6, /device:TPU:1, one launch (start us, length us, event | category | flops | bytes accessed | tf_op | source)
XLA Modules:
  0.0 134.9 jit_solution(10224479411013982392)
XLA Ops:
  0.0 1.3 fusion.5
  1.3 2.1 %collective-permute-start = (bf16[256,1024]{1,0:T(8,128)(2,1)S(1)}, bf16[256,1024]{1,0:T(8,128)(2,1)}, u32[]{:S(2)}, u32[]{:S(2)}) collective-permute-start(bf16[256,1024]{1,0:T(8,128)(2,1)S(1)} %bitcast.29), channel_id=1, source_target_pairs={{0,2},{1,3},{2,4},{3,5},{4,6},{5,7},{6,0},{7,1},{8,10},{9,11},{10,... | collective-permute-start | bytes 1572872 | tf_op jit(solution)/shard_map/ppermute | solution.py:30
  3.4 1.4 %collective-permute-start.1 = (bf16[256,1024]{1,0:T(8,128)(2,1)S(1)}, bf16[256,1024]{1,0:T(8,128)(2,1)}, u32[]{:S(2)}, u32[]{:S(2)}) collective-permute-start(bf16[256,1024]{1,0:T(8,128)(2,1)S(1)} %bitcast.30), channel_id=1, source_target_pairs={{0,6},{1,7},{2,0},{3,1},{4,2},{5,3},{6,4},{7,5},{8,14},{9,15},{10,... | collective-permute-start | bytes 1572872 | tf_op jit(solution)/shard_map/ppermute | solution.py:30
  4.8 1.4 %collective-permute-start.2 = (bf16[256,1024]{1,0:T(8,128)(2,1)S(1)}, bf16[256,1024]{1,0:T(8,128)(2,1)}, u32[]{:S(2)}, u32[]{:S(2)}) collective-permute-start(bf16[256,1024]{1,0:T(8,128)(2,1)S(1)} %bitcast.31), channel_id=1, source_target_pairs={{0,1},{1,0},{2,3},{3,2},{4,5},{5,4},{6,7},{7,6},{8,9},{9,8},{10,11... | collective-permute-start | bytes 1572872 | tf_op jit(solution)/shard_map/ppermute | solution.py:34
  6.2 0.6 fusion.7
  11.8 0.1 compare_reduce_fusion.1
  12.0 0.1 select_reduce_fusion.1
  12.1 0.1 compare_reduce_fusion
  12.2 0.1 select_reduce_fusion
  12.6 0.6 pad_add_fusion.1.info
  13.2 0.7 reshape.65.old_map
  13.8 0.1 convert_element_type.25
  14.0 1.0 fusion.4
  15.0 0.8 pad_maximum_fusion.7
  15.8 0.8 pad_maximum_fusion.9
  16.6 0.4 collective-permute-done.2.refs_3_
  17.1 0.2 collective-permute-start.3
  17.2 2.5 %collective-permute-start.4 = (bf16[256,1024]{1,0:T(8,128)(2,1)}, bf16[256,1024]{1,0:T(8,128)(2,1)}, u32[]{:S(2)}, u32[]{:S(2)}) collective-permute-start(bf16[256,1024]{1,0:T(8,128)(2,1)} %collective-permute-done.1.refs_2_), channel_id=1, source_target_pairs={{0,6},{1,7},{2,0},{3,1},{4,2},{5,3},{6,4},{7,5},{8,14},{9,15},{10,... | collective-permute-start | bytes 1572872 | tf_op jit(solution)/shard_map/ppermute | solution.py:30
  19.8 1.5 %collective-permute-start.7 = (bf16[256,1024]{1,0:T(8,128)(2,1)}, bf16[256,1024]{1,0:T(8,128)(2,1)}, u32[]{:S(2)}, u32[]{:S(2)}) collective-permute-start(bf16[256,1024]{1,0:T(8,128)(2,1)} %collective-permute-done.1.refs_2_), channel_id=1, source_target_pairs={{0,1},{1,0},{2,3},{3,2},{4,5},{5,4},{6,7},{7,6},{8,9},{9,8},{10,11... | collective-permute-start | bytes 1572872 | tf_op jit(solution)/shard_map/ppermute | solution.py:34
  21.3 3.4 %copy-done = bf16[8192,512]{1,0:T(8,128)(2,1)S(1)} copy-done((bf16[8192,512]{1,0:T(8,128)(2,1)S(1)}, bf16[8192,512]{1,0:T(8,128)(2,1)}, u32[]{:S(2)}) %copy-start) | copy-done | bytes 8388632
  24.7 1.6 %copy-done.5 = bf16[8192,128]{1,0:T(8,128)(2,1)S(1)} copy-done((bf16[8192,128]{1,0:T(8,128)(2,1)S(1)}, bf16[8192,128]{1,0:T(8,128)(2,1)}, u32[]{:S(2)}) %copy-start.5) | copy-done | bytes 2097176
  26.3 1.0 copy-done.11
  27.3 3.5 %project.6.refs_6_ = f32[256,768]{1,0:T(8,128)S(1)} custom-call(s32[4]{0:T(128)S(1)} %pad_add_fusion.2.features, bf16[256,1024]{1,0:T(8,128)(2,1)S(1)} %bitcast.32, bf16[256,1024]{1,0:T(8,128)(2,1)} %collective-permute-done.refs_1_, bf16[256,1024]{1,0:T(8,128)(2,1)} %collective-permute-done.1.refs_2_, bf16[256,1024]{1,0:T(8,128)(2,1)} %collective-permute-done.2.refs_3_, ...), custom_call_target="tpu_custom_call" | custom-call | flops 1 | bytes 1 | tf_op jit(solution)/shard_map/project/pallas_call | solution.py:163
  30.9 1.3 collective-permute-start.6
  32.2 0.2 collective-permute-start.5
  32.5 1.3 collective-permute-start.9
  33.8 3.4 %copy-done.1 = bf16[8192,512]{1,0:T(8,128)(2,1)S(1)} copy-done((bf16[8192,512]{1,0:T(8,128)(2,1)S(1)}, bf16[8192,512]{1,0:T(8,128)(2,1)}, u32[]{:S(2)}) %copy-start.1) | copy-done | bytes 8388632
  37.2 1.6 %copy-done.6 = bf16[8192,128]{1,0:T(8,128)(2,1)S(1)} copy-done((bf16[8192,128]{1,0:T(8,128)(2,1)S(1)}, bf16[8192,128]{1,0:T(8,128)(2,1)}, u32[]{:S(2)}) %copy-start.6) | copy-done | bytes 2097176
  38.7 3.8 %project.7.refs_4_ = f32[256,768]{1,0:T(8,128)S(1)} custom-call(s32[3]{0:T(128)S(1)} %pad_add_fusion.3.features, bf16[256,1024]{1,0:T(8,128)(2,1)} %collective-permute-done.3.refs_0_, bf16[256,1024]{1,0:T(8,128)(2,1)} %collective-permute-done.4.refs_1_, bf16[256,1024]{1,0:T(8,128)(2,1)} %collective-permute-done.7.refs_2_, bf16[8192,512]{1,0:T(8,128)(2,1)S(1)} %copy-done.1, ...), custom_call_target="tpu_custom_call" | custom-call | flops 1 | bytes 1 | tf_op jit(solution)/shard_map/project/pallas_call | solution.py:163
  42.5 0.9 copy-done.8
  43.5 2.7 %collective-permute-start.13 = (bf16[256,1024]{1,0:T(8,128)(2,1)}, bf16[256,1024]{1,0:T(8,128)(2,1)}, u32[]{:S(2)}, u32[]{:S(2)}) collective-permute-start(bf16[256,1024]{1,0:T(8,128)(2,1)} %collective-permute-done.6.refs_2_), channel_id=1, source_target_pairs={{0,6},{1,7},{2,0},{3,1},{4,2},{5,3},{6,4},{7,5},{8,14},{9,15},{10,... | collective-permute-start | bytes 1572872 | tf_op jit(solution)/shard_map/ppermute | solution.py:30
  46.2 1.4 %collective-permute-start.14 = (bf16[256,1024]{1,0:T(8,128)(2,1)}, bf16[256,1024]{1,0:T(8,128)(2,1)S(1)}, u32[]{:S(2)}, u32[]{:S(2)}) collective-permute-start(bf16[256,1024]{1,0:T(8,128)(2,1)} %collective-permute-done.6.refs_2_), channel_id=1, source_target_pairs={{0,1},{1,0},{2,3},{3,2},{4,5},{5,4},{6,7},{7,6},{8,9},{9,8},{10,11... | collective-permute-start | bytes 1572872 | tf_op jit(solution)/shard_map/ppermute | solution.py:34
  47.7 3.4 %copy-done.2 = bf16[8192,512]{1,0:T(8,128)(2,1)S(1)} copy-done((bf16[8192,512]{1,0:T(8,128)(2,1)S(1)}, bf16[8192,512]{1,0:T(8,128)(2,1)}, u32[]{:S(2)}) %copy-start.2) | copy-done | bytes 8388632
  51.0 1.6 %copy-done.7 = bf16[8192,128]{1,0:T(8,128)(2,1)S(1)} copy-done((bf16[8192,128]{1,0:T(8,128)(2,1)S(1)}, bf16[8192,128]{1,0:T(8,128)(2,1)}, u32[]{:S(2)}) %copy-start.7) | copy-done | bytes 2097176
  52.6 1.1 copy-done.9
  53.8 0.9 copy-done.13
  54.7 3.5 %project.8 = (bf16[320,256]{1,0:T(8,128)(2,1)S(1)}, bf16[320,256]{1,0:T(8,128)(2,1)S(1)}, bf16[320,256]{1,0:T(8,128)(2,1)S(1)}, bf16[320,256]{1,0:T(8,128)(2,1)S(1)}, bf16[512,256]{1,0:T(8,128)(2,1)S(1)}) custom-call(s32[1]{0:T(128)} %bitcast.10.features, bf16[256,1024]{1,0:T(8,128)(2,1)} %collective-permute-done.5.refs_0_, bf16[8192,512]{1,0:T(8,128)(2,1)S(1)} %copy-done.2, ...), custom_call_target="tpu_custom_call" | custom-call | flops 1 | bytes 1 | tf_op jit(solution)/shard_map/project/pallas_call | solution.py:163
  58.2 2.7 %collective-permute-start.8 = (bf16[512,256]{1,0:T(8,128)(2,1)S(1)}, bf16[512,256]{1,0:T(8,128)(2,1)S(1)}, u32[]{:S(2)}, u32[]{:S(2)}) collective-permute-start(bf16[512,256]{1,0:T(8,128)(2,1)S(1)} %get-tuple-element.73), channel_id=1, source_target_pairs={{0,64},{8,72},{16,80},{24,88},{32,96},{40,104},{48,112},{56,120},{... | collective-permute-start | bytes 786440 | tf_op jit(solution)/shard_map/ppermute | solution.py:44
  60.9 3.5 %project.9.refs_5_ = f32[256,768]{1,0:T(8,128)S(1)} custom-call(s32[4]{0:T(128)S(1)} %pad_add_fusion.2.features, bf16[256,1024]{1,0:T(8,128)(2,1)S(1)} %bitcast.28, bf16[256,1024]{1,0:T(8,128)(2,1)} %collective-permute-done.10.refs_1_, bf16[256,1024]{1,0:T(8,128)(2,1)} %collective-permute-done.6.refs_2_, bf16[256,1024]{1,0:T(8,128)(2,1)} %collective-permute-done.9.refs_3_, ...), custom_call_target="tpu_custom_call" | custom-call | flops 1 | bytes 1 | tf_op jit(solution)/shard_map/project/pallas_call | solution.py:163
  64.5 1.1 collective-permute-done.8
  65.6 1.7 %collective-permute-start.15 = (bf16[256,1024]{1,0:T(8,128)(2,1)S(1)}, bf16[256,1024]{1,0:T(8,128)(2,1)S(1)}, u32[]{:S(2)}, u32[]{:S(2)}) collective-permute-start(bf16[256,1024]{1,0:T(8,128)(2,1)S(1)} %collective-permute-done.14.refs_1_), channel_id=1, source_target_pairs={{0,6},{1,7},{2,0},{3,1},{4,2},{5,3},{6,4},{7,5},{8,14},{9,15},{10,... | collective-permute-start | bytes 1572872 | tf_op jit(solution)/shard_map/ppermute | solution.py:30
  67.4 1.7 %collective-permute-start.11 = (bf16[640,256]{1,0:T(8,128)(2,1)S(1)}, bf16[640,256]{1,0:T(8,128)(2,1)S(1)}, u32[]{:S(2)}, u32[]{:S(2)}) collective-permute-start(bf16[640,256]{1,0:T(8,128)(2,1)S(1)} %get-tuple-element.83), channel_id=1, source_target_pairs={{0,16},{8,24},{16,32},{24,40},{32,48},{40,56},{48,0},{56,8},{64,80... | collective-permute-start | bytes 983048 | tf_op jit(solution)/shard_map/ppermute | solution.py:44
  69.1 3.3 %collective-permute-start.17 = (bf16[640,256]{1,0:T(8,128)(2,1)S(1)}, bf16[640,256]{1,0:T(8,128)(2,1)S(1)}, u32[]{:S(2)}, u32[]{:S(2)}) collective-permute-start(bf16[640,256]{1,0:T(8,128)(2,1)S(1)} %get-tuple-element.95), channel_id=1, source_target_pairs={{0,32},{8,40},{16,48},{24,56},{32,0},{40,8},{48,16},{56,24},{64,96... | collective-permute-start | bytes 983048 | tf_op jit(solution)/shard_map/ppermute | solution.py:44
  72.4 0.7 collective-permute-start.18
  73.3 2.9 %project.10.refs_5_ = f32[256,768]{1,0:T(8,128)S(1)} custom-call(s32[2]{0:T(128)S(1)} %pad_add_fusion.5.features, bf16[256,1024]{1,0:T(8,128)(2,1)} %collective-permute-done.13.refs_0_, bf16[256,1024]{1,0:T(8,128)(2,1)S(1)} %collective-permute-done.14.refs_1_, bf16[8192,512]{1,0:T(8,128)(2,1)S(1)} %copy-done.3, bf16[8192,128]{1,0:T(8,128)(2,1)S(1)} %copy-done.4, ...), custom_call_target="tpu_custom_call" | custom-call | flops 1 | bytes 1 | tf_op jit(solution)/shard_map/project/pallas_call | solution.py:163
  76.3 4.0 %project.11 = (bf16[320,256]{1,0:T(8,128)(2,1)S(1)}, bf16[320,256]{1,0:T(8,128)(2,1)S(1)}, bf16[320,256]{1,0:T(8,128)(2,1)S(1)}, bf16[320,256]{1,0:T(8,128)(2,1)...) custom-call(s32[2]{0:T(128)S(1)} %pad_add_fusion.4.features, ...), custom_call_target="tpu_custom_call" | custom-call | flops 1 | bytes 1 | tf_op jit(solution)/shard_map/project/pallas_call | solution.py:163
  80.3 1.0 collective-permute-start.16
  81.2 2.5 %collective-permute-start.23 = (bf16[320,256]{1,0:T(8,128)(2,1)S(1)}, bf16[320,256]{1,0:T(8,128)(2,1)S(1)}, u32[]{:S(2)}, u32[]{:S(2)}) collective-permute-start(bf16[320,256]{1,0:T(8,128)(2,1)S(1)} %get-tuple-element.102), channel_id=1, source_target_pairs={{0,80},{8,88},{16,96},{24,104},{32,112},{40,120},{48,64},{56,72},{... | collective-permute-start | bytes 491528 | tf_op jit(solution)/shard_map/ppermute | solution.py:44
  83.8 3.7 %collective-permute-start.24 = (bf16[320,256]{1,0:T(8,128)(2,1)S(1)}, bf16[320,256]{1,0:T(8,128)(2,1)S(1)}, u32[]{:S(2)}, u32[]{:S(2)}) collective-permute-start(bf16[320,256]{1,0:T(8,128)(2,1)S(1)} %get-tuple-element.103), channel_id=1, source_target_pairs={{0,96},{8,104},{16,112},{24,120},{32,64},{40,72},{48,80},{56,88},{... | collective-permute-start | bytes 491528 | tf_op jit(solution)/shard_map/ppermute | solution.py:44
  87.5 1.3 collective-permute-start.25
  88.8 0.1 pad_maximum_fusion
  88.9 0.6 copy-done.19
  89.5 8.1 %collective-permute-start.19 = (bf16[2560,256]{1,0:T(8,128)(2,1)S(1)}, bf16[2560,256]{1,0:T(8,128)(2,1)S(1)}, u32[]{:S(2)}, u32[]{:S(2)}) collective-permute-start(bf16[2560,256]{1,0:T(8,128)(2,1)S(1)} %pad_maximum_fusion), channel_id=1, source_target_pairs={{0,8},{8,0},{16,24},{24,16},{32,40},{40,32},{48,56},{56,48},{64,72... | collective-permute-start | bytes 3932168 | tf_op jit(solution)/shard_map/ppermute | solution.py:56
  97.6 0.7 collective-permute-start.20
  98.4 1.3 collective-permute-start.21
  99.6 2.0 %collective-permute-start.22 = (bf16[320,256]{1,0:T(8,128)(2,1)S(1)}, bf16[320,256]{1,0:T(8,128)(2,1)S(1)}, u32[]{:S(2)}, u32[]{:S(2)}) collective-permute-start(bf16[320,256]{1,0:T(8,128)(2,1)S(1)} %get-tuple-element.100), channel_id=1, source_target_pairs={{0,48},{8,56},{16,0},{24,8},{32,16},{40,24},{48,32},{56,40},{64,11... | collective-permute-start | bytes 491528 | tf_op jit(solution)/shard_map/ppermute | solution.py:44
  101.7 2.1 %collective-permute-start.27 = (bf16[1280,256]{1,0:T(8,128)(2,1)S(1)}, bf16[1280,256]{1,0:T(8,128)(2,1)S(1)}, u32[]{:S(2)}, u32[]{:S(2)}) collective-permute-start(bf16[1280,256]{1,0:T(8,128)(2,1)S(1)} %pad_maximum_fusion.2), channel_id=1, source_target_pairs={{0,8},{8,0},{16,24},{24,16},{32,40},{40,32},{48,56},{56,48},{64,72... | collective-permute-start | bytes 1966088 | tf_op jit(solution)/shard_map/ppermute | solution.py:56
  103.8 4.3 %collective-permute-done.20.refs_6_ = bf16[320,256]{1,0:T(8,128)(2,1)S(1)} collective-permute-done((bf16[320,256]{1,0:T(8,128)(2,1)S(1)}, bf16[320,256]{1,0:T(8,128)(2,1)S(1)}, u32[]{:S(2)}, u32[]{:S(2)}) %collective-permute-start.20) | collective-permute-done | bytes 163872 | tf_op jit(solution)/shard_map/ppermute | solution.py:44
  108.1 2.0 %collective-permute-done.22.refs_8_ = bf16[320,256]{1,0:T(8,128)(2,1)S(1)} collective-permute-done((bf16[320,256]{1,0:T(8,128)(2,1)S(1)}, bf16[320,256]{1,0:T(8,128)(2,1)S(1)}, u32[]{:S(2)}, u32[]{:S(2)}) %collective-permute-start.22) | collective-permute-done | bytes 163872 | tf_op jit(solution)/shard_map/ppermute | solution.py:44
  110.2 0.6 collective-permute-start.26
  110.8 1.7 %collective-permute-done.26.refs_13_ = bf16[1280,256]{1,0:T(8,128)(2,1)S(1)} collective-permute-done((bf16[1280,256]{1,0:T(8,128)(2,1)S(1)}, bf16[1280,256]{1,0:T(8,128)(2,1)S(1)}, u32[]{:S(2)}, u32[]{:S(2)}) %collective-permute-start.26) | collective-permute-done | bytes 655392 | tf_op jit(solution)/shard_map/ppermute | solution.py:56
  112.5 0.8 copy-done.29
  113.3 1.1 copy-done.20
  114.4 20.4 %attend.1 = bf16[512,512]{1,0:T(8,128)(2,1)} custom-call(s32[19]{0:T(128)} %pad_add_fusion.1.info, s32[256]{0:T(256)} %reshape.65.old_map, bf16[640,256]{1,0:T(8,128)(2,1)} %copy-done.16, bf16[640,256]{1,0:T(8,128)(2,1)} %copy-done.17, bf16[640,256]{1,0:T(8,128)(2,1)} %copy-done.18, bf16[640,256]{1,0:T(8,128)(2,1)} %copy-done.19, ...), custom_call_target="tpu_custom_call" | custom-call | tf_op jit(solution)/shard_map/attend/pallas_call | solution.py:240
  (96 shorter events, 1.0 us)
Async XLA Ops:
  0.0 6.2 %copy-start.31 = (s32[16,16]{1,0:T(8,128)S(1)}, s32[16,16]{1,0:T(8,128)}, u32[]{:S(2)}) copy-start(s32[16,16]{1,0:T(8,128)} %param.8) | copy-start | bytes 3076
  0.0 11.8 %copy-start.30 = (s32[16,16]{1,0:T(8,128)S(1)}, s32[16,16]{1,0:T(8,128)}, u32[]{:S(2)}) copy-start(s32[16,16]{1,0:T(8,128)} %param.7) | copy-start | bytes 3076
  1.3 18.5 %copy-start.10 = (bf16[16,1,16,1024]{3,2,1,0:T(8,128)(2,1)}, bf16[16,1,16,1024]{3,2,1,0:T(8,128)(2,1)S(1)}, u32[]{:S(2)}) copy-start(bf16[16,1,16,1024]{3,2,1,0:T(8,128)(2,1)S(1)} %get-tuple-element.107) | copy-start | bytes 1572868
  1.3 19.9 %copy-start.4 = (bf16[8192,128]{1,0:T(8,128)(2,1)S(1)}, bf16[8192,128]{1,0:T(8,128)(2,1)}, u32[]{:S(2)}) copy-start(bf16[8192,128]{1,0:T(8,128)(2,1)} %refs_3_.7) | copy-start | bytes 6291460
  1.3 15.3 %collective-permute-start = (bf16[256,1024]{1,0:T(8,128)(2,1)S(1)}, bf16[256,1024]{1,0:T(8,128)(2,1)}, u32[]{:S(2)}, u32[]{:S(2)}) collective-permute-start(bf16[256,1024]{1,0:T(8,128)(2,1)S(1)} %bitcast.29), channel_id=1, source_target_pairs={{0,2},{1,3},{2,4},{3,5},{4,6},{5,7},{6,0},{7,1},{8,10},{9,11},{10,... | collective-permute-start | bytes 1572872 | tf_op jit(solution)/shard_map/ppermute | solution.py:30
  3.4 13.2 %collective-permute-start.1 = (bf16[256,1024]{1,0:T(8,128)(2,1)S(1)}, bf16[256,1024]{1,0:T(8,128)(2,1)}, u32[]{:S(2)}, u32[]{:S(2)}) collective-permute-start(bf16[256,1024]{1,0:T(8,128)(2,1)S(1)} %bitcast.30), channel_id=1, source_target_pairs={{0,6},{1,7},{2,0},{3,1},{4,2},{5,3},{6,4},{7,5},{8,14},{9,15},{10,... | collective-permute-start | bytes 1572872 | tf_op jit(solution)/shard_map/ppermute | solution.py:30
  4.8 12.3 %collective-permute-start.2 = (bf16[256,1024]{1,0:T(8,128)(2,1)S(1)}, bf16[256,1024]{1,0:T(8,128)(2,1)}, u32[]{:S(2)}, u32[]{:S(2)}) collective-permute-start(bf16[256,1024]{1,0:T(8,128)(2,1)S(1)} %bitcast.31), channel_id=1, source_target_pairs={{0,1},{1,0},{2,3},{3,2},{4,5},{5,4},{6,7},{7,6},{8,9},{9,8},{10,11... | collective-permute-start | bytes 1572872 | tf_op jit(solution)/shard_map/ppermute | solution.py:34
  17.1 13.8 %collective-permute-start.3 = (bf16[256,1024]{1,0:T(8,128)(2,1)}, bf16[256,1024]{1,0:T(8,128)(2,1)}, u32[]{:S(2)}, u32[]{:S(2)}) collective-permute-start(bf16[256,1024]{1,0:T(8,128)(2,1)} %collective-permute-done.2.refs_3_), channel_id=1, source_target_pairs={{0,2},{1,3},{2,4},{3,5},{4,6},{5,7},{6,0},{7,1},{8,10},{9,11},{10,... | collective-permute-start | bytes 1572872 | tf_op jit(solution)/shard_map/ppermute | solution.py:30
  17.2 13.6 %collective-permute-start.4 = (bf16[256,1024]{1,0:T(8,128)(2,1)}, bf16[256,1024]{1,0:T(8,128)(2,1)}, u32[]{:S(2)}, u32[]{:S(2)}) collective-permute-start(bf16[256,1024]{1,0:T(8,128)(2,1)} %collective-permute-done.1.refs_2_), channel_id=1, source_target_pairs={{0,6},{1,7},{2,0},{3,1},{4,2},{5,3},{6,4},{7,5},{8,14},{9,15},{10,... | collective-permute-start | bytes 1572872 | tf_op jit(solution)/shard_map/ppermute | solution.py:30
  19.8 14.0 %collective-permute-start.7 = (bf16[256,1024]{1,0:T(8,128)(2,1)}, bf16[256,1024]{1,0:T(8,128)(2,1)}, u32[]{:S(2)}, u32[]{:S(2)}) collective-permute-start(bf16[256,1024]{1,0:T(8,128)(2,1)} %collective-permute-done.1.refs_2_), channel_id=1, source_target_pairs={{0,1},{1,0},{2,3},{3,2},{4,5},{5,4},{6,7},{7,6},{8,9},{9,8},{10,11... | collective-permute-start | bytes 1572872 | tf_op jit(solution)/shard_map/ppermute | solution.py:34
  21.3 3.4 %copy-start = (bf16[8192,512]{1,0:T(8,128)(2,1)S(1)}, bf16[8192,512]{1,0:T(8,128)(2,1)}, u32[]{:S(2)}) copy-start(bf16[8192,512]{1,0:T(8,128)(2,1)} %refs_2_.5) | copy-start | bytes 25165828
  24.7 1.6 %copy-start.5 = (bf16[8192,128]{1,0:T(8,128)(2,1)S(1)}, bf16[8192,128]{1,0:T(8,128)(2,1)}, u32[]{:S(2)}) copy-start(bf16[8192,128]{1,0:T(8,128)(2,1)} %refs_4_.9) | copy-start | bytes 6291460
  26.3 1.0 copy-start.11
  30.9 12.6 %collective-permute-start.6 = (bf16[256,1024]{1,0:T(8,128)(2,1)S(1)}, bf16[256,1024]{1,0:T(8,128)(2,1)}, u32[]{:S(2)}, u32[]{:S(2)}) collective-permute-start(bf16[256,1024]{1,0:T(8,128)(2,1)S(1)} %bitcast.25), channel_id=1, source_target_pairs={{0,6},{1,7},{2,0},{3,1},{4,2},{5,3},{6,4},{7,5},{8,14},{9,15},{10,... | collective-permute-start | bytes 1572872 | tf_op jit(solution)/shard_map/ppermute | solution.py:30
  32.2 11.3 %collective-permute-start.5 = (bf16[256,1024]{1,0:T(8,128)(2,1)}, bf16[256,1024]{1,0:T(8,128)(2,1)}, u32[]{:S(2)}, u32[]{:S(2)}) collective-permute-start(bf16[256,1024]{1,0:T(8,128)(2,1)} %collective-permute-done.3.refs_0_), channel_id=1, source_target_pairs={{0,2},{1,3},{2,4},{3,5},{4,6},{5,7},{6,0},{7,1},{8,10},{9,11},{10,... | collective-permute-start | bytes 1572872 | tf_op jit(solution)/shard_map/ppermute | solution.py:30
  32.5 28.4 %collective-permute-start.9 = (bf16[256,1024]{1,0:T(8,128)(2,1)S(1)}, bf16[256,1024]{1,0:T(8,128)(2,1)}, u32[]{:S(2)}, u32[]{:S(2)}) collective-permute-start(bf16[256,1024]{1,0:T(8,128)(2,1)S(1)} %bitcast.26), channel_id=1, source_target_pairs={{0,1},{1,0},{2,3},{3,2},{4,5},{5,4},{6,7},{7,6},{8,9},{9,8},{10,11... | collective-permute-start | bytes 1572872 | tf_op jit(solution)/shard_map/ppermute | solution.py:34
  33.8 3.4 %copy-start.1 = (bf16[8192,512]{1,0:T(8,128)(2,1)S(1)}, bf16[8192,512]{1,0:T(8,128)(2,1)}, u32[]{:S(2)}) copy-start(bf16[8192,512]{1,0:T(8,128)(2,1)} %refs_2_.5) | copy-start | bytes 25165828
  37.2 1.6 %copy-start.6 = (bf16[8192,128]{1,0:T(8,128)(2,1)S(1)}, bf16[8192,128]{1,0:T(8,128)(2,1)}, u32[]{:S(2)}) copy-start(bf16[8192,128]{1,0:T(8,128)(2,1)} %refs_4_.9) | copy-start | bytes 6291460
  42.5 0.9 copy-start.8
  43.5 17.4 %collective-permute-start.10 = (bf16[256,1024]{1,0:T(8,128)(2,1)S(1)}, bf16[256,1024]{1,0:T(8,128)(2,1)}, u32[]{:S(2)}, u32[]{:S(2)}) collective-permute-start(bf16[256,1024]{1,0:T(8,128)(2,1)S(1)} %bitcast.27), channel_id=1, source_target_pairs={{0,2},{1,3},{2,4},{3,5},{4,6},{5,7},{6,0},{7,1},{8,10},{9,11},{10,... | collective-permute-start | bytes 1572872 | tf_op jit(solution)/shard_map/ppermute | solution.py:30
  43.5 22.1 %collective-permute-start.13 = (bf16[256,1024]{1,0:T(8,128)(2,1)}, bf16[256,1024]{1,0:T(8,128)(2,1)}, u32[]{:S(2)}, u32[]{:S(2)}) collective-permute-start(bf16[256,1024]{1,0:T(8,128)(2,1)} %collective-permute-done.6.refs_2_), channel_id=1, source_target_pairs={{0,6},{1,7},{2,0},{3,1},{4,2},{5,3},{6,4},{7,5},{8,14},{9,15},{10,... | collective-permute-start | bytes 1572872 | tf_op jit(solution)/shard_map/ppermute | solution.py:30
  46.2 19.3 %collective-permute-start.14 = (bf16[256,1024]{1,0:T(8,128)(2,1)}, bf16[256,1024]{1,0:T(8,128)(2,1)S(1)}, u32[]{:S(2)}, u32[]{:S(2)}) collective-permute-start(bf16[256,1024]{1,0:T(8,128)(2,1)} %collective-permute-done.6.refs_2_), channel_id=1, source_target_pairs={{0,1},{1,0},{2,3},{3,2},{4,5},{5,4},{6,7},{7,6},{8,9},{9,8},{10,11... | collective-permute-start | bytes 1572872 | tf_op jit(solution)/shard_map/ppermute | solution.py:34
  47.7 3.4 %copy-start.2 = (bf16[8192,512]{1,0:T(8,128)(2,1)S(1)}, bf16[8192,512]{1,0:T(8,128)(2,1)}, u32[]{:S(2)}) copy-start(bf16[8192,512]{1,0:T(8,128)(2,1)} %refs_2_.5) | copy-start | bytes 25165828
  51.0 1.6 %copy-start.7 = (bf16[8192,128]{1,0:T(8,128)(2,1)S(1)}, bf16[8192,128]{1,0:T(8,128)(2,1)}, u32[]{:S(2)}) copy-start(bf16[8192,128]{1,0:T(8,128)(2,1)} %refs_4_.9) | copy-start | bytes 6291460
  52.6 1.1 copy-start.9
  53.8 0.9 copy-start.13
  54.7 6.2 %copy-start.3 = (bf16[8192,512]{1,0:T(8,128)(2,1)S(1)}, bf16[8192,512]{1,0:T(8,128)(2,1)}, u32[]{:S(2)}) copy-start(bf16[8192,512]{1,0:T(8,128)(2,1)} %refs_2_.5) | copy-start | bytes 25165828
  58.2 7.3 %collective-permute-start.8 = (bf16[512,256]{1,0:T(8,128)(2,1)S(1)}, bf16[512,256]{1,0:T(8,128)(2,1)S(1)}, u32[]{:S(2)}, u32[]{:S(2)}) collective-permute-start(bf16[512,256]{1,0:T(8,128)(2,1)S(1)} %get-tuple-element.73), channel_id=1, source_target_pairs={{0,64},{8,72},{16,80},{24,88},{32,96},{40,104},{48,112},{56,120},{... | collective-permute-start | bytes 786440 | tf_op jit(solution)/shard_map/ppermute | solution.py:44
  60.9 15.3 %collective-permute-start.12 = (bf16[256,1024]{1,0:T(8,128)(2,1)}, bf16[256,1024]{1,0:T(8,128)(2,1)S(1)}, u32[]{:S(2)}, u32[]{:S(2)}) collective-permute-start(bf16[256,1024]{1,0:T(8,128)(2,1)} %collective-permute-done.9.refs_3_), channel_id=1, source_target_pairs={{0,2},{1,3},{2,4},{3,5},{4,6},{5,7},{6,0},{7,1},{8,10},{9,11},{10,... | collective-permute-start | bytes 1572872 | tf_op jit(solution)/shard_map/ppermute | solution.py:30
  65.6 10.7 %collective-permute-start.15 = (bf16[256,1024]{1,0:T(8,128)(2,1)S(1)}, bf16[256,1024]{1,0:T(8,128)(2,1)S(1)}, u32[]{:S(2)}, u32[]{:S(2)}) collective-permute-start(bf16[256,1024]{1,0:T(8,128)(2,1)S(1)} %collective-permute-done.14.refs_1_), channel_id=1, source_target_pairs={{0,6},{1,7},{2,0},{3,1},{4,2},{5,3},{6,4},{7,5},{8,14},{9,15},{10,... | collective-permute-start | bytes 1572872 | tf_op jit(solution)/shard_map/ppermute | solution.py:30
  67.3 21.5 %copy-start.16 = (bf16[640,256]{1,0:T(8,128)(2,1)}, bf16[640,256]{1,0:T(8,128)(2,1)S(1)}, u32[]{:S(2)}) copy-start(bf16[640,256]{1,0:T(8,128)(2,1)S(1)} %pad_maximum_fusion.6.refs_0_) | copy-start | bytes 983044
  67.4 16.4 %collective-permute-start.11 = (bf16[640,256]{1,0:T(8,128)(2,1)S(1)}, bf16[640,256]{1,0:T(8,128)(2,1)S(1)}, u32[]{:S(2)}, u32[]{:S(2)}) collective-permute-start(bf16[640,256]{1,0:T(8,128)(2,1)S(1)} %get-tuple-element.83), channel_id=1, source_target_pairs={{0,16},{8,24},{16,32},{24,40},{32,48},{40,56},{48,0},{56,8},{64,80... | collective-permute-start | bytes 983048 | tf_op jit(solution)/shard_map/ppermute | solution.py:44
  69.1 18.4 %collective-permute-start.17 = (bf16[640,256]{1,0:T(8,128)(2,1)S(1)}, bf16[640,256]{1,0:T(8,128)(2,1)S(1)}, u32[]{:S(2)}, u32[]{:S(2)}) collective-permute-start(bf16[640,256]{1,0:T(8,128)(2,1)S(1)} %get-tuple-element.95), channel_id=1, source_target_pairs={{0,32},{8,40},{16,48},{24,56},{32,0},{40,8},{48,16},{56,24},{64,96... | collective-permute-start | bytes 983048 | tf_op jit(solution)/shard_map/ppermute | solution.py:44
  72.4 16.4 %collective-permute-start.18 = (bf16[640,256]{1,0:T(8,128)(2,1)S(1)}, bf16[640,256]{1,0:T(8,128)(2,1)S(1)}, u32[]{:S(2)}, u32[]{:S(2)}) collective-permute-start(bf16[640,256]{1,0:T(8,128)(2,1)S(1)} %get-tuple-element.96), channel_id=1, source_target_pairs={{0,48},{8,56},{16,0},{24,8},{32,16},{40,24},{48,32},{56,40},{64,11... | collective-permute-start | bytes 983048 | tf_op jit(solution)/shard_map/ppermute | solution.py:44
  73.3 3.0 %copy-start.14 = (f32[256,128]{1,0:T(8,128)S(1)}, f32[256,128]{1,0:T(8,128)}, u32[]{:S(2)}) copy-start(f32[256,128]{1,0:T(8,128)} %get-tuple-element.87.refs_7_) | copy-start | bytes 393220
  73.3 3.0 %copy-start.15 = (f32[256,128]{1,0:T(8,128)S(1)}, f32[256,128]{1,0:T(8,128)}, u32[]{:S(2)}) copy-start(f32[256,128]{1,0:T(8,128)} %get-tuple-element.88.refs_8_) | copy-start | bytes 393220
  80.2 29.9 %copy-start.12 = (bf16[320,256]{1,0:T(8,128)(2,1)}, bf16[320,256]{1,0:T(8,128)(2,1)S(1)}, u32[]{:S(2)}) copy-start(bf16[320,256]{1,0:T(8,128)(2,1)S(1)} %get-tuple-element.97.refs_5_) | copy-start | bytes 491524
  80.3 17.4 %collective-permute-start.16 = (bf16[320,256]{1,0:T(8,128)(2,1)S(1)}, bf16[320,256]{1,0:T(8,128)(2,1)S(1)}, u32[]{:S(2)}, u32[]{:S(2)}) collective-permute-start(bf16[320,256]{1,0:T(8,128)(2,1)S(1)} %get-tuple-element.89), channel_id=1, source_target_pairs={{0,64},{8,72},{16,80},{24,88},{32,96},{40,104},{48,112},{56,120},{... | collective-permute-start | bytes 491528 | tf_op jit(solution)/shard_map/ppermute | solution.py:44
  81.2 17.1 %collective-permute-start.23 = (bf16[320,256]{1,0:T(8,128)(2,1)S(1)}, bf16[320,256]{1,0:T(8,128)(2,1)S(1)}, u32[]{:S(2)}, u32[]{:S(2)}) collective-permute-start(bf16[320,256]{1,0:T(8,128)(2,1)S(1)} %get-tuple-element.102), channel_id=1, source_target_pairs={{0,80},{8,88},{16,96},{24,104},{32,112},{40,120},{48,64},{56,72},{... | collective-permute-start | bytes 491528 | tf_op jit(solution)/shard_map/ppermute | solution.py:44
  83.8 5.1 %copy-start.17 = (bf16[640,256]{1,0:T(8,128)(2,1)}, bf16[640,256]{1,0:T(8,128)(2,1)S(1)}, u32[]{:S(2)}) copy-start(bf16[640,256]{1,0:T(8,128)(2,1)S(1)} %collective-permute-done.11.refs_1_) | copy-start | bytes 983044
  83.8 15.9 %collective-permute-start.24 = (bf16[320,256]{1,0:T(8,128)(2,1)S(1)}, bf16[320,256]{1,0:T(8,128)(2,1)S(1)}, u32[]{:S(2)}, u32[]{:S(2)}) collective-permute-start(bf16[320,256]{1,0:T(8,128)(2,1)S(1)} %get-tuple-element.103), channel_id=1, source_target_pairs={{0,96},{8,104},{16,112},{24,120},{32,64},{40,72},{48,80},{56,88},{... | collective-permute-start | bytes 491528 | tf_op jit(solution)/shard_map/ppermute | solution.py:44
  87.5 1.4 %copy-start.18 = (bf16[640,256]{1,0:T(8,128)(2,1)}, bf16[640,256]{1,0:T(8,128)(2,1)S(1)}, u32[]{:S(2)}) copy-start(bf16[640,256]{1,0:T(8,128)(2,1)S(1)} %collective-permute-done.17.refs_2_) | copy-start | bytes 983044
  87.5 14.1 %collective-permute-start.25 = (bf16[320,256]{1,0:T(8,128)(2,1)S(1)}, bf16[320,256]{1,0:T(8,128)(2,1)S(1)}, u32[]{:S(2)}, u32[]{:S(2)}) collective-permute-start(bf16[320,256]{1,0:T(8,128)(2,1)S(1)} %get-tuple-element.104), channel_id=1, source_target_pairs={{0,112},{8,120},{16,64},{24,72},{32,80},{40,88},{48,96},{56,104},{... | collective-permute-start | bytes 491528 | tf_op jit(solution)/shard_map/ppermute | solution.py:44
  88.8 0.7 copy-start.19
  89.5 23.0 %collective-permute-start.19 = (bf16[2560,256]{1,0:T(8,128)(2,1)S(1)}, bf16[2560,256]{1,0:T(8,128)(2,1)S(1)}, u32[]{:S(2)}, u32[]{:S(2)}) collective-permute-start(bf16[2560,256]{1,0:T(8,128)(2,1)S(1)} %pad_maximum_fusion), channel_id=1, source_target_pairs={{0,8},{8,0},{16,24},{24,16},{32,40},{40,32},{48,56},{56,48},{64,72... | collective-permute-start | bytes 3932168 | tf_op jit(solution)/shard_map/ppermute | solution.py:56
  97.6 12.5 %copy-start.21 = (bf16[320,256]{1,0:T(8,128)(2,1)}, bf16[320,256]{1,0:T(8,128)(2,1)S(1)}, u32[]{:S(2)}) copy-start(bf16[320,256]{1,0:T(8,128)(2,1)S(1)} %collective-permute-done.16.refs_9_) | copy-start | bytes 491524
  97.6 10.5 %collective-permute-start.20 = (bf16[320,256]{1,0:T(8,128)(2,1)S(1)}, bf16[320,256]{1,0:T(8,128)(2,1)S(1)}, u32[]{:S(2)}, u32[]{:S(2)}) collective-permute-start(bf16[320,256]{1,0:T(8,128)(2,1)S(1)} %get-tuple-element.98), channel_id=1, source_target_pairs={{0,16},{8,24},{16,32},{24,40},{32,48},{40,56},{48,0},{56,8},{64,80... | collective-permute-start | bytes 491528 | tf_op jit(solution)/shard_map/ppermute | solution.py:44
  98.4 11.8 %copy-start.22 = (bf16[320,256]{1,0:T(8,128)(2,1)}, bf16[320,256]{1,0:T(8,128)(2,1)S(1)}, u32[]{:S(2)}) copy-start(bf16[320,256]{1,0:T(8,128)(2,1)S(1)} %collective-permute-done.23.refs_10_) | copy-start | bytes 491524
  98.4 9.7 %collective-permute-start.21 = (bf16[320,256]{1,0:T(8,128)(2,1)S(1)}, bf16[320,256]{1,0:T(8,128)(2,1)S(1)}, u32[]{:S(2)}, u32[]{:S(2)}) collective-permute-start(bf16[320,256]{1,0:T(8,128)(2,1)S(1)} %get-tuple-element.99), channel_id=1, source_target_pairs={{0,32},{8,40},{16,48},{24,56},{32,0},{40,8},{48,16},{56,24},{64,96... | collective-permute-start | bytes 491528 | tf_op jit(solution)/shard_map/ppermute | solution.py:44
  99.6 10.6 %copy-start.23 = (bf16[320,256]{1,0:T(8,128)(2,1)}, bf16[320,256]{1,0:T(8,128)(2,1)S(1)}, u32[]{:S(2)}) copy-start(bf16[320,256]{1,0:T(8,128)(2,1)S(1)} %collective-permute-done.24.refs_11_) | copy-start | bytes 491524
  99.6 10.5 %collective-permute-start.22 = (bf16[320,256]{1,0:T(8,128)(2,1)S(1)}, bf16[320,256]{1,0:T(8,128)(2,1)S(1)}, u32[]{:S(2)}, u32[]{:S(2)}) collective-permute-start(bf16[320,256]{1,0:T(8,128)(2,1)S(1)} %get-tuple-element.100), channel_id=1, source_target_pairs={{0,48},{8,56},{16,0},{24,8},{32,16},{40,24},{48,32},{56,40},{64,11... | collective-permute-start | bytes 491528 | tf_op jit(solution)/shard_map/ppermute | solution.py:44
  101.6 8.6 %copy-start.24 = (bf16[320,256]{1,0:T(8,128)(2,1)}, bf16[320,256]{1,0:T(8,128)(2,1)S(1)}, u32[]{:S(2)}) copy-start(bf16[320,256]{1,0:T(8,128)(2,1)S(1)} %collective-permute-done.25.refs_12_) | copy-start | bytes 491524
  101.7 9.1 %collective-permute-start.27 = (bf16[1280,256]{1,0:T(8,128)(2,1)S(1)}, bf16[1280,256]{1,0:T(8,128)(2,1)S(1)}, u32[]{:S(2)}, u32[]{:S(2)}) collective-permute-start(bf16[1280,256]{1,0:T(8,128)(2,1)S(1)} %pad_maximum_fusion.2), channel_id=1, source_target_pairs={{0,8},{8,0},{16,24},{24,16},{32,40},{40,32},{48,56},{56,48},{64,72... | collective-permute-start | bytes 1966088 | tf_op jit(solution)/shard_map/ppermute | solution.py:56
  108.1 4.4 %copy-start.25 = (bf16[320,256]{1,0:T(8,128)(2,1)}, bf16[320,256]{1,0:T(8,128)(2,1)S(1)}, u32[]{:S(2)}) copy-start(bf16[320,256]{1,0:T(8,128)(2,1)S(1)} %collective-permute-done.20.refs_6_) | copy-start | bytes 491524
  108.1 4.4 %copy-start.26 = (bf16[320,256]{1,0:T(8,128)(2,1)}, bf16[320,256]{1,0:T(8,128)(2,1)S(1)}, u32[]{:S(2)}) copy-start(bf16[320,256]{1,0:T(8,128)(2,1)S(1)} %collective-permute-done.21.refs_7_) | copy-start | bytes 491524
  110.1 2.4 %copy-start.27 = (bf16[320,256]{1,0:T(8,128)(2,1)}, bf16[320,256]{1,0:T(8,128)(2,1)S(1)}, u32[]{:S(2)}) copy-start(bf16[320,256]{1,0:T(8,128)(2,1)S(1)} %collective-permute-done.22.refs_8_) | copy-start | bytes 491524
  110.2 2.3 %collective-permute-start.26 = (bf16[1280,256]{1,0:T(8,128)(2,1)S(1)}, bf16[1280,256]{1,0:T(8,128)(2,1)S(1)}, u32[]{:S(2)}, u32[]{:S(2)}) collective-permute-start(bf16[1280,256]{1,0:T(8,128)(2,1)S(1)} %pad_maximum_fusion.1), channel_id=1, source_target_pairs={{0,8},{8,0},{16,24},{24,16},{32,40},{40,32},{48,56},{56,48},{64,72... | collective-permute-start | bytes 1966088 | tf_op jit(solution)/shard_map/ppermute | solution.py:56
  110.8 1.7 %copy-start.28 = (bf16[1280,256]{1,0:T(8,128)(2,1)}, bf16[1280,256]{1,0:T(8,128)(2,1)S(1)}, u32[]{:S(2)}) copy-start(bf16[1280,256]{1,0:T(8,128)(2,1)S(1)} %collective-permute-done.27.refs_14_) | copy-start | bytes 1966084
  112.5 0.9 copy-start.29
  113.3 1.1 copy-start.20

commit v7 on v6

--- a/solution.py
+++ b/solution.py
@@ -20,7 +20,7 @@
 KB = 512
 VMEM = pl.BlockSpec(memory_space=pltpu.VMEM)
 SMEM = pl.BlockSpec(memory_space=pltpu.SMEM)
-ANY = pl.BlockSpec(memory_space=pl.ANY)
+HBM = pl.BlockSpec(memory_space=pltpu.HBM)
 
 CHIPS = [(dh, dz) for dh in range(2) for dz in range(4)]
 
@@ -76,7 +76,7 @@
 
 
 def project_kernel(count, has_acc, last, joint, features, *refs):
-    blocks, (wq, wk, wv), refs = refs[:count], refs[count : count + 3], refs[count + 3 :]
+    blocks, weights, refs = refs[:count], refs[count], refs[count + 1 :]
     acc_in = None
     if has_acc:
         acc_in, refs = refs[0], refs[1:]
@@ -93,14 +93,12 @@
         copy.wait()
         rows = pl.ds(pl.multiple_of(features[i] * 1024, 1024), 1024)
         block = held[i]
-        for lo, hi in ((0, 512), (512, 768)):
-            w = wq[rows, :] if lo == 0 else jnp.concatenate([wk[rows, :], wv[rows, :]], axis=1)
-            value = dot(block, w)
-            if i > 0:
-                value = value + acc[:, lo:hi]
-            elif has_acc:
-                value = value + acc_in[:, lo:hi]
-            acc[:, lo:hi] = value
+        value = dot(block, weights[rows, :])
+        if i > 0:
+            value = value + acc[...]
+        elif has_acc:
+            value = value + acc_in[...]
+        acc[...] = value
     if not last:
         return
     cos, sin = cosine[...], sine[...]
@@ -139,8 +137,8 @@
 def project(features, blocks, weights, acc=None, tables=None, joint=False):
     count = len(blocks)
     last = tables is not None
-    specs = [SMEM] + [ANY] * count + [VMEM] * 3
-    operands = [features, *blocks, *weights]
+    specs = [SMEM] + [HBM] * count + [VMEM]
+    operands = [features, *blocks, weights]
     if acc is not None:
         specs.append(VMEM)
         operands.append(acc)
@@ -150,7 +148,7 @@
         operands += list(tables)
         sizes = [PAYLOAD] * 4 + [2 * ROWS] if joint else [PAYLOAD] * 8
         out_shape = [jax.ShapeDtypeStruct((n, 256), jnp.bfloat16) for n in sizes]
-        out_specs = [ANY] * len(sizes)
+        out_specs = [HBM] * len(sizes)
         scratch += [
             pltpu.VMEM((ROWS, 768), jnp.float32),
             pltpu.VMEM((ROWS, 512), jnp.bfloat16),
@@ -173,19 +171,24 @@
 
 
 def attend_kernel(info, old_map, *refs):
-    packed, packed_other, late, late_other = refs[:4], refs[4], refs[5:13], refs[13:15]
-    out, query, keys, values, top, total, accum = refs[15:]
+    packed, packed_other, late, late_source = refs[:4], refs[4], refs[5:13], refs[13:15]
+    out, query, keys, values, top, total, accum, late_other, sems = refs[15:]
+    copies = [pltpu.make_async_copy(late_source[i], late_other.at[i], sems.at[i]) for i in range(2)]
+    for copy in copies:
+        copy.start()
     me = info[0]
     high, z, core = me // 8, lax.rem(me // 2, 4), lax.rem(me, 2)
-    for r, (dh, dz) in enumerate(CHIPS):
-        for swapped in range(2):
+    for swapped in range(2):
+        for r, (dh, dz) in enumerate(CHIPS):
+            if swapped and r % 4 == 0:
+                copies[r // 4].wait()
             source = lax.rem(high + dh, 2) * 8 + lax.rem(z + 4 - dz, 4) * 2 + lax.rem(core + swapped, 2)
             slot = info[3 + source]
             for j in range(CHUNKS):
                 if j == 0:
                     ref, base = (packed_other, (dz * 2 + dh) * PAYLOAD) if swapped else (packed[dz], dh * PAYLOAD)
                 else:
-                    ref, base = (late_other[r // 4], (r % 4) * PAYLOAD) if swapped else (late[r], 0)
+                    ref, base = (late_other.at[r // 4], (r % 4) * PAYLOAD) if swapped else (late[r], 0)
                 for k in range(16):
                     at = pl.ds(pl.multiple_of(old_map[source * 16 + k] * FINE + j * W, W), W)
                     rows = slice(base + k * W, base + (k + 1) * W)
@@ -240,7 +243,7 @@
     return pl.pallas_call(
         attend_kernel,
         out_shape=jax.ShapeDtypeStruct((512, 512), jnp.bfloat16),
-        in_specs=[SMEM, SMEM] + [VMEM] * len(parts),
+        in_specs=[SMEM, SMEM] + [VMEM] * (len(parts) - 2) + [HBM] * 2,
         out_specs=VMEM,
         scratch_shapes=[
             pltpu.VMEM((2048, HEAD), jnp.bfloat16),
@@ -249,6 +252,8 @@
             pltpu.VMEM((1024, HEAD), jnp.float32),
             pltpu.VMEM((1024, HEAD), jnp.float32),
             pltpu.VMEM((1024, HEAD), jnp.float32),
+            pltpu.VMEM((2, 4 * PAYLOAD, 256), jnp.bfloat16),
+            pltpu.SemaphoreType.DMA((2,)),
         ],
         compiler_params=pltpu.CompilerParams(vmem_limit_bytes=56 * 2**20),
         name="attend",
@@ -283,7 +288,7 @@
 def local(tokens, old_map, new_map, w_query, key_projection_weight, value_projection_weight):
     me = lax.axis_index("ctx").astype(jnp.int32)
     place = lax.axis_index("tp").astype(jnp.int32)
-    weights = (w_query, key_projection_weight, value_projection_weight)
+    weights = jnp.concatenate([w_query, key_projection_weight, value_projection_weight], axis=1)
     send_info, attend_info, old_mine = routing(old_map, new_map, me)
     x, y = place // 2, place % 2
     feature = lambda dx, dy: ((x + dx) % 4) * 2 + (y + dy) % 2
@@ -300,8 +305,8 @@
     left = shift_x(early, 1)
     right = shift_x(early, -1)
     across = swap_y(early)
-    late, left, right, across, send_info, attend_info, old_flat, *tables = together(
-        late, left, right, across, send_info, attend_info, old_flat, *tables
+    weights, late, left, right, across, send_info, attend_info, old_flat, *tables = together(
+        weights, late, left, right, across, send_info, attend_info, old_flat, *tables
     )
     left_across = shift_x(across, 1)
     far = shift_x(right, -1)

time: 135 us -> 146 us (1.081)
  other arithmetic: 4.51 us -> 14.4 us
  waiting for transfers between devices: 9.65 us -> 11.7 us
  starting transfers between devices: 49.4 us -> 47.5 us
    concatenate x0 -> x1, other arithmetic: none -> 10.5 us  [local(): jnp.concatenate([w_query, key_projection_weight, value_projection_weight]...]
    ppermute x10, waiting for transfers between devices: 0.04 us -> 4.85 us  [shift_x(): return lax.ppermute(block, 'tp', perm)]
    ppermute x4, starting transfers between devices: 5.59 us -> 2.75 us  [swap_y(): return lax.ppermute(block, 'tp', [(i, i ^ 1) for i in range(8)])]
    ppermute x11, waiting for transfers between devices: 7.44 us -> 5.12 us  [shift_ctx(): return lax.ppermute(block, 'ctx', perm)]
    pallas_call x6, Pallas kernels: 21.3 us -> 19.4 us  [project(): pl.pallas_call(functools.partial(project_kernel, count, acc is not None,...]
    unnamed x64 -> x50, local copies, waits for them, and re-layouts: 21.5 us -> 22.1 us
  transfers between devices with their start and end apart: 28 -> 28, of which waited for: 5 -> 6; matrix products, arithmetic and copies ran while one was open for 4% -> 11% of each run, Pallas kernels for 16% -> 13%
where the time goes in v7:
time: 146 us; the launch traced here: 145 us
  starting transfers between devices  47.5 us (33%)
  Pallas kernels  40.9 us (28%)
  local copies, waits for them, and re-layouts  24.9 us (17%)
  other arithmetic  14.4 us (10%)
  waiting for transfers between devices  11.7 us (8%)
  between operations  5.65 us (4%)
    unnamed x50, local copies, waits for them, and re-layouts  22.1 us
    pallas_call x1, Pallas kernels, attend(): pl.pallas_call(attend_kernel, out_shape=jax.ShapeDtypeStruct((512, 512),...  21.5 us
    ppermute x11, starting transfers between devices, shift_ctx(): return lax.ppermute(block, 'ctx', perm)  21.2 us
    pallas_call x6, Pallas kernels, project(): pl.pallas_call(functools.partial(project_kernel, count, acc is not None,...  19.4 us
    ppermute x10, starting transfers between devices, shift_x(): return lax.ppermute(block, 'tp', perm)  13 us
    ppermute x3, starting transfers between devices, swap_core(): return lax.ppermute(block, 'ctx', [(i, i ^ 1) for i in range(16)])  10.6 us
    concatenate x1, other arithmetic, local(): jnp.concatenate([w_query, key_projection_weight, value_projection_weight]...  10.5 us
    ppermute x11, waiting for transfers between devices, shift_ctx(): return lax.ppermute(block, 'ctx', perm)  5.12 us
  transfers between devices with their start and end apart: 28, of which 6 were waited for; matrix products, arithmetic and copies ran while one was open for 11% of the time, Pallas kernels for 13%

profile of v7, /device:TPU:1, one launch (start us, length us, event | category | flops | bytes accessed | tf_op | source)
XLA Modules:
  0.0 145.0 jit_solution(10709832993940941242)
XLA Ops:
  0.0 1.3 fusion.5
  1.3 2.2 %collective-permute-start.2 = (bf16[256,1024]{1,0:T(8,128)(2,1)S(1)}, bf16[256,1024]{1,0:T(8,128)(2,1)S(1)}, u32[]{:S(2)}, u32[]{:S(2)}) collective-permute-start(bf16[256,1024]{1,0:T(8,128)(2,1)S(1)} %bitcast.29), channel_id=1, source_target_pairs={{0,1},{1,0},{2,3},{3,2},{4,5},{5,4},{6,7},{7,6},{8,9},{9,8},{10,11... | collective-permute-start | bytes 1572872 | tf_op jit(solution)/shard_map/ppermute | solution.py:34
  3.5 2.5 %collective-permute-start.1 = (bf16[256,1024]{1,0:T(8,128)(2,1)S(1)}, bf16[256,1024]{1,0:T(8,128)(2,1)S(1)}, u32[]{:S(2)}, u32[]{:S(2)}) collective-permute-start(bf16[256,1024]{1,0:T(8,128)(2,1)S(1)} %bitcast.30), channel_id=1, source_target_pairs={{0,6},{1,7},{2,0},{3,1},{4,2},{5,3},{6,4},{7,5},{8,14},{9,15},{10,... | collective-permute-start | bytes 1572872 | tf_op jit(solution)/shard_map/ppermute | solution.py:30
  6.0 0.6 fusion.7
  11.8 0.1 compare_reduce_fusion.1
  11.9 0.1 select_reduce_fusion.1
  12.0 0.1 compare_reduce_fusion
  12.2 0.1 select_reduce_fusion
  12.4 0.1 pad_add_fusion.refs_3_.refs_4_
  12.5 10.5 %pad_maximum_fusion.refs_4_.refs_3_.refs_1_.refs_2_ = bf16[8192,768]{1,0:T(8,128)(2,1)} fusion(bf16[8192,128]{1,0:T(8,128)(2,1)} %param.11, bf16[8192,128]{1,0:T(8,128)(2,1)} %param.10, bf16[8192,512]{1,0:T(8,128)(2,1)} %param.9), kind=kLoop, calls=%fused_computation | loop fusion | flops 37748736 | bytes 25165824 | tf_op jit(solution)/shard_map/concatenate | solution.py:291
  23.0 0.7 pad_add_fusion.1.info
  23.7 0.7 reshape.65.old_map
  24.4 0.1 convert_element_type.23
  24.4 0.1 convert_element_type.25
  24.5 1.0 fusion.4
  25.5 0.8 pad_maximum_fusion.10
  26.3 0.1 pad_maximum_fusion.8
  26.5 0.8 copy-done.6
  27.3 0.2 collective-permute-start.3
  27.5 2.5 %collective-permute-start.4 = (bf16[256,1024]{1,0:T(8,128)(2,1)S(1)}, bf16[256,1024]{1,0:T(8,128)(2,1)}, u32[]{:S(2)}, u32[]{:S(2)}) collective-permute-start(bf16[256,1024]{1,0:T(8,128)(2,1)S(1)} %collective-permute-done.1.refs_2_), channel_id=1, source_target_pairs={{0,6},{1,7},{2,0},{3,1},{4,2},{5,3},{6,4},{7,5},{8,14},{9,15},{10,... | collective-permute-start | bytes 1572872 | tf_op jit(solution)/shard_map/ppermute | solution.py:30
  30.0 0.1 pad_add_fusion.2.features
  30.0 0.2 collective-permute-start.7
  30.2 4.6 %copy-done = bf16[8192,768]{1,0:T(8,128)(2,1)S(1)} copy-done((bf16[8192,768]{1,0:T(8,128)(2,1)S(1)}, bf16[8192,768]{1,0:T(8,128)(2,1)}, u32[]{:S(2)}) %copy-start) | copy-done | bytes 12582936
  34.8 1.0 copy-done.7
  35.8 3.6 %project.6.refs_4_ = f32[256,768]{1,0:T(8,128)S(1)} custom-call(s32[4]{0:T(128)S(1)} %pad_add_fusion.2.features, bf16[256,1024]{1,0:T(8,128)(2,1)S(1)} %bitcast.32, bf16[256,1024]{1,0:T(8,128)(2,1)S(1)} %copy-done.7, bf16[256,1024]{1,0:T(8,128)(2,1)S(1)} %collective-permute-done.1.refs_2_, bf16[256,1024]{1,0:T(8,128)(2,1)S(1)} %collective-permute-done.2.refs_3_, ...), custom_call_target="tpu_custom_call" | custom-call | flops 1 | bytes 1 | tf_op jit(solution)/shard_map/project/pallas_call | solution.py:161
  39.4 1.3 collective-permute-done.3.refs_0_
  40.8 2.4 %collective-permute-start.6 = (bf16[256,1024]{1,0:T(8,128)(2,1)S(1)}, bf16[256,1024]{1,0:T(8,128)(2,1)}, u32[]{:S(2)}, u32[]{:S(2)}) collective-permute-start(bf16[256,1024]{1,0:T(8,128)(2,1)S(1)} %bitcast.25), channel_id=1, source_target_pairs={{0,6},{1,7},{2,0},{3,1},{4,2},{5,3},{6,4},{7,5},{8,14},{9,15},{10,... | collective-permute-start | bytes 1572872 | tf_op jit(solution)/shard_map/ppermute | solution.py:30
  43.2 0.1 pad_add_fusion.3.features
  43.2 0.2 collective-permute-start.9
  43.4 4.6 %copy-done.1 = bf16[8192,768]{1,0:T(8,128)(2,1)S(1)} copy-done((bf16[8192,768]{1,0:T(8,128)(2,1)S(1)}, bf16[8192,768]{1,0:T(8,128)(2,1)}, u32[]{:S(2)}) %copy-start.1) | copy-done | bytes 12582936
  48.0 3.8 %project.7.refs_2_ = f32[256,768]{1,0:T(8,128)S(1)} custom-call(s32[3]{0:T(128)S(1)} %pad_add_fusion.3.features, bf16[256,1024]{1,0:T(8,128)(2,1)} %collective-permute-done.3.refs_0_, bf16[256,1024]{1,0:T(8,128)(2,1)} %collective-permute-done.4.refs_1_, bf16[256,1024]{1,0:T(8,128)(2,1)} %collective-permute-done.7.refs_2_, bf16[8192,768]{1,0:T(8,128)(2,1)S(1)} %copy-done.1, ...), custom_call_target="tpu_custom_call" | custom-call | flops 1 | bytes 1 | tf_op jit(solution)/shard_map/project/pallas_call | solution.py:161
  51.8 0.3 collective-permute-done.6.refs_2_
  52.1 3.1 %collective-permute-done.5.refs_0_ = bf16[256,1024]{1,0:T(8,128)(2,1)S(1)} collective-permute-done((bf16[256,1024]{1,0:T(8,128)(2,1)}, bf16[256,1024]{1,0:T(8,128)(2,1)S(1)}, u32[]{:S(2)}, u32[]{:S(2)}) %collective-permute-start.5) | collective-permute-done | bytes 524320 | tf_op jit(solution)/shard_map/ppermute | solution.py:30
  55.3 0.2 collective-permute-start.14
  55.5 2.7 %collective-permute-start.13 = (bf16[256,1024]{1,0:T(8,128)(2,1)}, bf16[256,1024]{1,0:T(8,128)(2,1)S(1)}, u32[]{:S(2)}, u32[]{:S(2)}) collective-permute-start(bf16[256,1024]{1,0:T(8,128)(2,1)} %collective-permute-done.6.refs_2_), channel_id=1, source_target_pairs={{0,6},{1,7},{2,0},{3,1},{4,2},{5,3},{6,4},{7,5},{8,14},{9,15},{10,... | collective-permute-start | bytes 1572872 | tf_op jit(solution)/shard_map/ppermute | solution.py:30
  58.1 4.6 %copy-done.2 = bf16[8192,768]{1,0:T(8,128)(2,1)S(1)} copy-done((bf16[8192,768]{1,0:T(8,128)(2,1)S(1)}, bf16[8192,768]{1,0:T(8,128)(2,1)}, u32[]{:S(2)}) %copy-start.2) | copy-done | bytes 12582936
  62.7 2.3 %project.8 = (bf16[320,256]{1,0:T(8,128)(2,1)S(1)}, bf16[320,256]{1,0:T(8,128)(2,1)S(1)}, bf16[320,256]{1,0:T(8,128)(2,1)S(1)}, bf16[320,256]{1,0:T(8,128)(2,1)S(1)}, bf16[512,256]{1,0:T(8,128)(2,1)S(1)}) custom-call(s32[1]{0:T(128)} %bitcast.10.features, bf16[256,1024]{1,0:T(8,128)(2,1)S(1)} %collective-permute-done.5.refs_0_, ...), custom_call_target="tpu_custom_call" | custom-call | flops 1 | bytes 1 | tf_op jit(solution)/shard_map/project/pallas_call | solution.py:161
  65.0 3.0 %collective-permute-start.8 = (bf16[512,256]{1,0:T(8,128)(2,1)S(1)}, bf16[512,256]{1,0:T(8,128)(2,1)S(1)}, u32[]{:S(2)}, u32[]{:S(2)}) collective-permute-start(bf16[512,256]{1,0:T(8,128)(2,1)S(1)} %get-tuple-element.75), channel_id=1, source_target_pairs={{0,64},{8,72},{16,80},{24,88},{32,96},{40,104},{48,112},{56,120},{... | collective-permute-start | bytes 786440 | tf_op jit(solution)/shard_map/ppermute | solution.py:44
  68.0 4.6 %copy-done.3 = bf16[8192,768]{1,0:T(8,128)(2,1)S(1)} copy-done((bf16[8192,768]{1,0:T(8,128)(2,1)S(1)}, bf16[8192,768]{1,0:T(8,128)(2,1)}, u32[]{:S(2)}) %copy-start.3) | copy-done | bytes 12582936
  72.6 3.8 %project.9.refs_3_ = f32[256,768]{1,0:T(8,128)S(1)} custom-call(s32[4]{0:T(128)S(1)} %pad_add_fusion.2.features, bf16[256,1024]{1,0:T(8,128)(2,1)S(1)} %bitcast.28, bf16[256,1024]{1,0:T(8,128)(2,1)} %collective-permute-done.10.refs_1_, bf16[256,1024]{1,0:T(8,128)(2,1)} %collective-permute-done.6.refs_2_, bf16[256,1024]{1,0:T(8,128)(2,1)} %collective-permute-done.9.refs_3_, ...), custom_call_target="tpu_custom_call" | custom-call | flops 1 | bytes 1 | tf_op jit(solution)/shard_map/project/pallas_call | solution.py:161
  76.4 2.7 %collective-permute-start.15 = (bf16[256,1024]{1,0:T(8,128)(2,1)S(1)}, bf16[256,1024]{1,0:T(8,128)(2,1)S(1)}, u32[]{:S(2)}, u32[]{:S(2)}) collective-permute-start(bf16[256,1024]{1,0:T(8,128)(2,1)S(1)} %collective-permute-done.14.refs_1_), channel_id=1, source_target_pairs={{0,6},{1,7},{2,0},{3,1},{4,2},{5,3},{6,4},{7,5},{8,14},{9,15},{10,... | collective-permute-start | bytes 1572872 | tf_op jit(solution)/shard_map/ppermute | solution.py:30
  79.3 1.7 %collective-permute-start.11 = (bf16[640,256]{1,0:T(8,128)(2,1)S(1)}, bf16[640,256]{1,0:T(8,128)(2,1)S(1)}, u32[]{:S(2)}, u32[]{:S(2)}) collective-permute-start(bf16[640,256]{1,0:T(8,128)(2,1)S(1)} %get-tuple-element.85), channel_id=1, source_target_pairs={{0,16},{8,24},{16,32},{24,40},{32,48},{40,56},{48,0},{56,8},{64,80... | collective-permute-start | bytes 983048 | tf_op jit(solution)/shard_map/ppermute | solution.py:44
  81.0 3.3 %collective-permute-start.17 = (bf16[640,256]{1,0:T(8,128)(2,1)S(1)}, bf16[640,256]{1,0:T(8,128)(2,1)S(1)}, u32[]{:S(2)}, u32[]{:S(2)}) collective-permute-start(bf16[640,256]{1,0:T(8,128)(2,1)S(1)} %get-tuple-element.97), channel_id=1, source_target_pairs={{0,32},{8,40},{16,48},{24,56},{32,0},{40,8},{48,16},{56,24},{64,96... | collective-permute-start | bytes 983048 | tf_op jit(solution)/shard_map/ppermute | solution.py:44
  84.3 0.7 collective-permute-start.18
  85.1 0.1 pad_add_fusion.5.features
  85.2 2.0 %project.10.refs_3_ = f32[256,768]{1,0:T(8,128)S(1)} custom-call(s32[2]{0:T(128)S(1)} %pad_add_fusion.5.features, bf16[256,1024]{1,0:T(8,128)(2,1)S(1)} %collective-permute-done.13.refs_0_, bf16[256,1024]{1,0:T(8,128)(2,1)S(1)} %collective-permute-done.14.refs_1_, bf16[8192,768]{1,0:T(8,128)(2,1)S(1)} %copy-done.4, f32[256,768]{1,0:T(8,128)S(1)} %project.9.refs_3_), custom_call_target="tpu_custom_call" | custom-call | flops 1 | bytes 1 | tf_op jit(solution)/shard_map/project/pallas_call | solution.py:161
  87.2 4.0 %project.11 = (bf16[320,256]{1,0:T(8,128)(2,1)S(1)}, bf16[320,256]{1,0:T(8,128)(2,1)S(1)}, bf16[320,256]{1,0:T(8,128)(2,1)S(1)}, bf16[320,256]{1,0:T(8,128)(2,1)...) custom-call(s32[2]{0:T(128)S(1)} %pad_add_fusion.4.features, ...), custom_call_target="tpu_custom_call" | custom-call | flops 1 | bytes 1 | tf_op jit(solution)/shard_map/project/pallas_call | solution.py:161
  91.2 1.1 collective-permute-start.16
  92.3 2.4 %collective-permute-start.23 = (bf16[320,256]{1,0:T(8,128)(2,1)S(1)}, bf16[320,256]{1,0:T(8,128)(2,1)S(1)}, u32[]{:S(2)}, u32[]{:S(2)}) collective-permute-start(bf16[320,256]{1,0:T(8,128)(2,1)S(1)} %get-tuple-element.104), channel_id=1, source_target_pairs={{0,80},{8,88},{16,96},{24,104},{32,112},{40,120},{48,64},{56,72},{... | collective-permute-start | bytes 491528 | tf_op jit(solution)/shard_map/ppermute | solution.py:44
  94.8 3.2 %collective-permute-start.24 = (bf16[320,256]{1,0:T(8,128)(2,1)S(1)}, bf16[320,256]{1,0:T(8,128)(2,1)S(1)}, u32[]{:S(2)}, u32[]{:S(2)}) collective-permute-start(bf16[320,256]{1,0:T(8,128)(2,1)S(1)} %get-tuple-element.105), channel_id=1, source_target_pairs={{0,96},{8,104},{16,112},{24,120},{32,64},{40,72},{48,80},{56,88},{... | collective-permute-start | bytes 491528 | tf_op jit(solution)/shard_map/ppermute | solution.py:44
  98.0 2.2 %collective-permute-start.25 = (bf16[320,256]{1,0:T(8,128)(2,1)S(1)}, bf16[320,256]{1,0:T(8,128)(2,1)S(1)}, u32[]{:S(2)}, u32[]{:S(2)}) collective-permute-start(bf16[320,256]{1,0:T(8,128)(2,1)S(1)} %get-tuple-element.106), channel_id=1, source_target_pairs={{0,112},{8,120},{16,64},{24,72},{32,80},{40,88},{48,96},{56,104},{... | collective-permute-start | bytes 491528 | tf_op jit(solution)/shard_map/ppermute | solution.py:44
  100.2 0.1 pad_maximum_fusion.1
  100.3 7.2 %collective-permute-start.19 = (bf16[2560,256]{1,0:T(8,128)(2,1)S(1)}, bf16[2560,256]{1,0:T(8,128)(2,1)S(1)}, u32[]{:S(2)}, u32[]{:S(2)}) collective-permute-start(bf16[2560,256]{1,0:T(8,128)(2,1)S(1)} %pad_maximum_fusion.1), channel_id=1, source_target_pairs={{0,8},{8,0},{16,24},{24,16},{32,40},{40,32},{48,56},{56,48},{64,72... | collective-permute-start | bytes 3932168 | tf_op jit(solution)/shard_map/ppermute | solution.py:56
  107.5 0.8 collective-permute-start.20
  108.2 0.8 collective-permute-start.21
  109.1 1.9 %collective-permute-start.22 = (bf16[320,256]{1,0:T(8,128)(2,1)S(1)}, bf16[320,256]{1,0:T(8,128)(2,1)S(1)}, u32[]{:S(2)}, u32[]{:S(2)}) collective-permute-start(bf16[320,256]{1,0:T(8,128)(2,1)S(1)} %get-tuple-element.102), channel_id=1, source_target_pairs={{0,48},{8,56},{16,0},{24,8},{32,16},{40,24},{48,32},{56,40},{64,11... | collective-permute-start | bytes 491528 | tf_op jit(solution)/shard_map/ppermute | solution.py:44
  111.1 2.1 %collective-permute-start.27 = (bf16[1280,256]{1,0:T(8,128)(2,1)S(1)}, bf16[1280,256]{1,0:T(8,128)(2,1)S(1)}, u32[]{:S(2)}, u32[]{:S(2)}) collective-permute-start(bf16[1280,256]{1,0:T(8,128)(2,1)S(1)} %pad_maximum_fusion.3), channel_id=1, source_target_pairs={{0,8},{8,0},{16,24},{24,16},{32,40},{40,32},{48,56},{56,48},{64,72... | collective-permute-start | bytes 1966088 | tf_op jit(solution)/shard_map/ppermute | solution.py:56
  113.2 4.8 %collective-permute-done.20.refs_6_ = bf16[320,256]{1,0:T(8,128)(2,1)S(1)} collective-permute-done((bf16[320,256]{1,0:T(8,128)(2,1)S(1)}, bf16[320,256]{1,0:T(8,128)(2,1)S(1)}, u32[]{:S(2)}, u32[]{:S(2)}) %collective-permute-start.20) | collective-permute-done | bytes 163872 | tf_op jit(solution)/shard_map/ppermute | solution.py:44
  118.0 0.3 collective-permute-done.22.refs_8_
  118.4 1.3 collective-permute-start.26
  119.6 1.7 %collective-permute-done.26.refs_13_ = bf16[1280,256]{1,0:T(8,128)(2,1)S(1)} collective-permute-done((bf16[1280,256]{1,0:T(8,128)(2,1)S(1)}, bf16[1280,256]{1,0:T(8,128)(2,1)S(1)}, u32[]{:S(2)}, u32[]{:S(2)}) %collective-permute-start.26) | collective-permute-done | bytes 655392 | tf_op jit(solution)/shard_map/ppermute | solution.py:56
  121.4 0.8 copy-done.22
  122.2 1.1 copy-done.13
  123.3 21.5 %attend.1 = bf16[512,512]{1,0:T(8,128)(2,1)} custom-call(s32[19]{0:T(128)} %pad_add_fusion.1.info, s32[256]{0:T(256)} %reshape.65.old_map, bf16[640,256]{1,0:T(8,128)(2,1)} %copy-done.9, bf16[640,256]{1,0:T(8,128)(2,1)} %copy-done.10, bf16[640,256]{1,0:T(8,128)(2,1)} %copy-done.11, bf16[640,256]{1,0:T(8,128)(2,1)} %copy-done.12, ...), custom_call_target="tpu_custom_call" | custom-call | tf_op jit(solution)/shard_map/attend/pallas_call | solution.py:243
  (83 shorter events, 0.6 us)
Async XLA Ops:
  0.0 6.0 %copy-start.24 = (s32[16,16]{1,0:T(8,128)S(1)}, s32[16,16]{1,0:T(8,128)}, u32[]{:S(2)}) copy-start(s32[16,16]{1,0:T(8,128)} %param.8) | copy-start | bytes 3076
  0.0 11.7 %copy-start.23 = (s32[16,16]{1,0:T(8,128)S(1)}, s32[16,16]{1,0:T(8,128)}, u32[]{:S(2)}) copy-start(s32[16,16]{1,0:T(8,128)} %param.7) | copy-start | bytes 3076
  1.3 25.1 %collective-permute-start.2 = (bf16[256,1024]{1,0:T(8,128)(2,1)S(1)}, bf16[256,1024]{1,0:T(8,128)(2,1)S(1)}, u32[]{:S(2)}, u32[]{:S(2)}) collective-permute-start(bf16[256,1024]{1,0:T(8,128)(2,1)S(1)} %bitcast.29), channel_id=1, source_target_pairs={{0,1},{1,0},{2,3},{3,2},{4,5},{5,4},{6,7},{7,6},{8,9},{9,8},{10,11... | collective-permute-start | bytes 1572872 | tf_op jit(solution)/shard_map/ppermute | solution.py:34
  3.5 22.9 %collective-permute-start.1 = (bf16[256,1024]{1,0:T(8,128)(2,1)S(1)}, bf16[256,1024]{1,0:T(8,128)(2,1)S(1)}, u32[]{:S(2)}, u32[]{:S(2)}) collective-permute-start(bf16[256,1024]{1,0:T(8,128)(2,1)S(1)} %bitcast.30), channel_id=1, source_target_pairs={{0,6},{1,7},{2,0},{3,1},{4,2},{5,3},{6,4},{7,5},{8,14},{9,15},{10,... | collective-permute-start | bytes 1572872 | tf_op jit(solution)/shard_map/ppermute | solution.py:30
  6.0 20.5 %collective-permute-start = (bf16[256,1024]{1,0:T(8,128)(2,1)S(1)}, bf16[256,1024]{1,0:T(8,128)(2,1)S(1)}, u32[]{:S(2)}, u32[]{:S(2)}) collective-permute-start(bf16[256,1024]{1,0:T(8,128)(2,1)S(1)} %bitcast.31), channel_id=1, source_target_pairs={{0,2},{1,3},{2,4},{3,5},{4,6},{5,7},{6,0},{7,1},{8,10},{9,11},{10,... | collective-permute-start | bytes 1572872 | tf_op jit(solution)/shard_map/ppermute | solution.py:30
  26.5 0.8 copy-start.6
  27.3 13.5 %collective-permute-start.3 = (bf16[256,1024]{1,0:T(8,128)(2,1)S(1)}, bf16[256,1024]{1,0:T(8,128)(2,1)}, u32[]{:S(2)}, u32[]{:S(2)}) collective-permute-start(bf16[256,1024]{1,0:T(8,128)(2,1)S(1)} %collective-permute-done.2.refs_3_), channel_id=1, source_target_pairs={{0,2},{1,3},{2,4},{3,5},{4,6},{5,7},{6,0},{7,1},{8,10},{9,11},{10,... | collective-permute-start | bytes 1572872 | tf_op jit(solution)/shard_map/ppermute | solution.py:30
  27.5 13.3 %collective-permute-start.4 = (bf16[256,1024]{1,0:T(8,128)(2,1)S(1)}, bf16[256,1024]{1,0:T(8,128)(2,1)}, u32[]{:S(2)}, u32[]{:S(2)}) collective-permute-start(bf16[256,1024]{1,0:T(8,128)(2,1)S(1)} %collective-permute-done.1.refs_2_), channel_id=1, source_target_pairs={{0,6},{1,7},{2,0},{3,1},{4,2},{5,3},{6,4},{7,5},{8,14},{9,15},{10,... | collective-permute-start | bytes 1572872 | tf_op jit(solution)/shard_map/ppermute | solution.py:30
  30.0 13.4 %collective-permute-start.7 = (bf16[256,1024]{1,0:T(8,128)(2,1)S(1)}, bf16[256,1024]{1,0:T(8,128)(2,1)}, u32[]{:S(2)}, u32[]{:S(2)}) collective-permute-start(bf16[256,1024]{1,0:T(8,128)(2,1)S(1)} %collective-permute-done.1.refs_2_), channel_id=1, source_target_pairs={{0,1},{1,0},{2,3},{3,2},{4,5},{5,4},{6,7},{7,6},{8,9},{9,8},{10,11... | collective-permute-start | bytes 1572872 | tf_op jit(solution)/shard_map/ppermute | solution.py:34
  30.2 4.6 %copy-start = (bf16[8192,768]{1,0:T(8,128)(2,1)S(1)}, bf16[8192,768]{1,0:T(8,128)(2,1)}, u32[]{:S(2)}) copy-start(bf16[8192,768]{1,0:T(8,128)(2,1)} %pad_maximum_fusion.refs_4_.refs_3_.refs_1_.refs_2_) | copy-start | bytes 37748740
  34.8 1.0 copy-start.7
  40.8 11.4 %collective-permute-start.6 = (bf16[256,1024]{1,0:T(8,128)(2,1)S(1)}, bf16[256,1024]{1,0:T(8,128)(2,1)}, u32[]{:S(2)}, u32[]{:S(2)}) collective-permute-start(bf16[256,1024]{1,0:T(8,128)(2,1)S(1)} %bitcast.25), channel_id=1, source_target_pairs={{0,6},{1,7},{2,0},{3,1},{4,2},{5,3},{6,4},{7,5},{8,14},{9,15},{10,... | collective-permute-start | bytes 1572872 | tf_op jit(solution)/shard_map/ppermute | solution.py:30
  43.2 12.1 %collective-permute-start.5 = (bf16[256,1024]{1,0:T(8,128)(2,1)}, bf16[256,1024]{1,0:T(8,128)(2,1)S(1)}, u32[]{:S(2)}, u32[]{:S(2)}) collective-permute-start(bf16[256,1024]{1,0:T(8,128)(2,1)} %collective-permute-done.3.refs_0_), channel_id=1, source_target_pairs={{0,2},{1,3},{2,4},{3,5},{4,6},{5,7},{6,0},{7,1},{8,10},{9,11},{10,... | collective-permute-start | bytes 1572872 | tf_op jit(solution)/shard_map/ppermute | solution.py:30
  43.2 24.7 %collective-permute-start.9 = (bf16[256,1024]{1,0:T(8,128)(2,1)S(1)}, bf16[256,1024]{1,0:T(8,128)(2,1)}, u32[]{:S(2)}, u32[]{:S(2)}) collective-permute-start(bf16[256,1024]{1,0:T(8,128)(2,1)S(1)} %bitcast.26), channel_id=1, source_target_pairs={{0,1},{1,0},{2,3},{3,2},{4,5},{5,4},{6,7},{7,6},{8,9},{9,8},{10,11... | collective-permute-start | bytes 1572872 | tf_op jit(solution)/shard_map/ppermute | solution.py:34
  43.4 4.6 %copy-start.1 = (bf16[8192,768]{1,0:T(8,128)(2,1)S(1)}, bf16[8192,768]{1,0:T(8,128)(2,1)}, u32[]{:S(2)}) copy-start(bf16[8192,768]{1,0:T(8,128)(2,1)} %pad_maximum_fusion.refs_4_.refs_3_.refs_1_.refs_2_) | copy-start | bytes 37748740
  55.3 12.7 %collective-permute-start.10 = (bf16[256,1024]{1,0:T(8,128)(2,1)S(1)}, bf16[256,1024]{1,0:T(8,128)(2,1)}, u32[]{:S(2)}, u32[]{:S(2)}) collective-permute-start(bf16[256,1024]{1,0:T(8,128)(2,1)S(1)} %bitcast.27), channel_id=1, source_target_pairs={{0,2},{1,3},{2,4},{3,5},{4,6},{5,7},{6,0},{7,1},{8,10},{9,11},{10,... | collective-permute-start | bytes 1572872 | tf_op jit(solution)/shard_map/ppermute | solution.py:30
  55.3 21.1 %collective-permute-start.14 = (bf16[256,1024]{1,0:T(8,128)(2,1)}, bf16[256,1024]{1,0:T(8,128)(2,1)S(1)}, u32[]{:S(2)}, u32[]{:S(2)}) collective-permute-start(bf16[256,1024]{1,0:T(8,128)(2,1)} %collective-permute-done.6.refs_2_), channel_id=1, source_target_pairs={{0,1},{1,0},{2,3},{3,2},{4,5},{5,4},{6,7},{7,6},{8,9},{9,8},{10,11... | collective-permute-start | bytes 1572872 | tf_op jit(solution)/shard_map/ppermute | solution.py:34
  55.5 21.0 %collective-permute-start.13 = (bf16[256,1024]{1,0:T(8,128)(2,1)}, bf16[256,1024]{1,0:T(8,128)(2,1)S(1)}, u32[]{:S(2)}, u32[]{:S(2)}) collective-permute-start(bf16[256,1024]{1,0:T(8,128)(2,1)} %collective-permute-done.6.refs_2_), channel_id=1, source_target_pairs={{0,6},{1,7},{2,0},{3,1},{4,2},{5,3},{6,4},{7,5},{8,14},{9,15},{10,... | collective-permute-start | bytes 1572872 | tf_op jit(solution)/shard_map/ppermute | solution.py:30
  58.1 4.6 %copy-start.2 = (bf16[8192,768]{1,0:T(8,128)(2,1)S(1)}, bf16[8192,768]{1,0:T(8,128)(2,1)}, u32[]{:S(2)}) copy-start(bf16[8192,768]{1,0:T(8,128)(2,1)} %pad_maximum_fusion.refs_4_.refs_3_.refs_1_.refs_2_) | copy-start | bytes 37748740
  65.0 11.4 %collective-permute-start.8 = (bf16[512,256]{1,0:T(8,128)(2,1)S(1)}, bf16[512,256]{1,0:T(8,128)(2,1)S(1)}, u32[]{:S(2)}, u32[]{:S(2)}) collective-permute-start(bf16[512,256]{1,0:T(8,128)(2,1)S(1)} %get-tuple-element.75), channel_id=1, source_target_pairs={{0,64},{8,72},{16,80},{24,88},{32,96},{40,104},{48,112},{56,120},{... | collective-permute-start | bytes 786440 | tf_op jit(solution)/shard_map/ppermute | solution.py:44
  68.0 19.2 %collective-permute-start.12 = (bf16[256,1024]{1,0:T(8,128)(2,1)}, bf16[256,1024]{1,0:T(8,128)(2,1)S(1)}, u32[]{:S(2)}, u32[]{:S(2)}) collective-permute-start(bf16[256,1024]{1,0:T(8,128)(2,1)} %collective-permute-done.9.refs_3_), channel_id=1, source_target_pairs={{0,2},{1,3},{2,4},{3,5},{4,6},{5,7},{6,0},{7,1},{8,10},{9,11},{10,... | collective-permute-start | bytes 1572872 | tf_op jit(solution)/shard_map/ppermute | solution.py:30
  68.0 4.6 %copy-start.3 = (bf16[8192,768]{1,0:T(8,128)(2,1)S(1)}, bf16[8192,768]{1,0:T(8,128)(2,1)}, u32[]{:S(2)}) copy-start(bf16[8192,768]{1,0:T(8,128)(2,1)} %pad_maximum_fusion.refs_4_.refs_3_.refs_1_.refs_2_) | copy-start | bytes 37748740
  72.6 12.6 %copy-start.4 = (bf16[8192,768]{1,0:T(8,128)(2,1)S(1)}, bf16[8192,768]{1,0:T(8,128)(2,1)}, u32[]{:S(2)}) copy-start(bf16[8192,768]{1,0:T(8,128)(2,1)} %pad_maximum_fusion.refs_4_.refs_3_.refs_1_.refs_2_) | copy-start | bytes 37748740
  76.4 10.8 %collective-permute-start.15 = (bf16[256,1024]{1,0:T(8,128)(2,1)S(1)}, bf16[256,1024]{1,0:T(8,128)(2,1)S(1)}, u32[]{:S(2)}, u32[]{:S(2)}) collective-permute-start(bf16[256,1024]{1,0:T(8,128)(2,1)S(1)} %collective-permute-done.14.refs_1_), channel_id=1, source_target_pairs={{0,6},{1,7},{2,0},{3,1},{4,2},{5,3},{6,4},{7,5},{8,14},{9,15},{10,... | collective-permute-start | bytes 1572872 | tf_op jit(solution)/shard_map/ppermute | solution.py:30
  79.2 21.0 %copy-start.9 = (bf16[640,256]{1,0:T(8,128)(2,1)}, bf16[640,256]{1,0:T(8,128)(2,1)S(1)}, u32[]{:S(2)}) copy-start(bf16[640,256]{1,0:T(8,128)(2,1)S(1)} %pad_maximum_fusion.7.refs_0_) | copy-start | bytes 983044
  79.3 15.4 %collective-permute-start.11 = (bf16[640,256]{1,0:T(8,128)(2,1)S(1)}, bf16[640,256]{1,0:T(8,128)(2,1)S(1)}, u32[]{:S(2)}, u32[]{:S(2)}) collective-permute-start(bf16[640,256]{1,0:T(8,128)(2,1)S(1)} %get-tuple-element.85), channel_id=1, source_target_pairs={{0,16},{8,24},{16,32},{24,40},{32,48},{40,56},{48,0},{56,8},{64,80... | collective-permute-start | bytes 983048 | tf_op jit(solution)/shard_map/ppermute | solution.py:44
  81.0 17.0 %collective-permute-start.17 = (bf16[640,256]{1,0:T(8,128)(2,1)S(1)}, bf16[640,256]{1,0:T(8,128)(2,1)S(1)}, u32[]{:S(2)}, u32[]{:S(2)}) collective-permute-start(bf16[640,256]{1,0:T(8,128)(2,1)S(1)} %get-tuple-element.97), channel_id=1, source_target_pairs={{0,32},{8,40},{16,48},{24,56},{32,0},{40,8},{48,16},{56,24},{64,96... | collective-permute-start | bytes 983048 | tf_op jit(solution)/shard_map/ppermute | solution.py:44
  84.3 15.8 %collective-permute-start.18 = (bf16[640,256]{1,0:T(8,128)(2,1)S(1)}, bf16[640,256]{1,0:T(8,128)(2,1)S(1)}, u32[]{:S(2)}, u32[]{:S(2)}) collective-permute-start(bf16[640,256]{1,0:T(8,128)(2,1)S(1)} %get-tuple-element.98), channel_id=1, source_target_pairs={{0,48},{8,56},{16,0},{24,8},{32,16},{40,24},{48,32},{56,40},{64,11... | collective-permute-start | bytes 983048 | tf_op jit(solution)/shard_map/ppermute | solution.py:44
  85.2 2.0 %copy-start.8 = (f32[256,128]{1,0:T(8,128)S(1)}, f32[256,128]{1,0:T(8,128)}, u32[]{:S(2)}) copy-start(f32[256,128]{1,0:T(8,128)} %get-tuple-element.90.refs_6_) | copy-start | bytes 393220
  91.2 27.1 %copy-start.5 = (bf16[320,256]{1,0:T(8,128)(2,1)}, bf16[320,256]{1,0:T(8,128)(2,1)S(1)}, u32[]{:S(2)}) copy-start(bf16[320,256]{1,0:T(8,128)(2,1)S(1)} %get-tuple-element.99.refs_5_) | copy-start | bytes 491524
  91.2 16.2 %collective-permute-start.16 = (bf16[320,256]{1,0:T(8,128)(2,1)S(1)}, bf16[320,256]{1,0:T(8,128)(2,1)S(1)}, u32[]{:S(2)}, u32[]{:S(2)}) collective-permute-start(bf16[320,256]{1,0:T(8,128)(2,1)S(1)} %get-tuple-element.91), channel_id=1, source_target_pairs={{0,64},{8,72},{16,80},{24,88},{32,96},{40,104},{48,112},{56,120},{... | collective-permute-start | bytes 491528 | tf_op jit(solution)/shard_map/ppermute | solution.py:44
  92.3 15.9 %collective-permute-start.23 = (bf16[320,256]{1,0:T(8,128)(2,1)S(1)}, bf16[320,256]{1,0:T(8,128)(2,1)S(1)}, u32[]{:S(2)}, u32[]{:S(2)}) collective-permute-start(bf16[320,256]{1,0:T(8,128)(2,1)S(1)} %get-tuple-element.104), channel_id=1, source_target_pairs={{0,80},{8,88},{16,96},{24,104},{32,112},{40,120},{48,64},{56,72},{... | collective-permute-start | bytes 491528 | tf_op jit(solution)/shard_map/ppermute | solution.py:44
  94.8 23.6 %copy-start.10 = (bf16[640,256]{1,0:T(8,128)(2,1)}, bf16[640,256]{1,0:T(8,128)(2,1)S(1)}, u32[]{:S(2)}) copy-start(bf16[640,256]{1,0:T(8,128)(2,1)S(1)} %collective-permute-done.11.refs_1_) | copy-start | bytes 983044
  94.8 14.3 %collective-permute-start.24 = (bf16[320,256]{1,0:T(8,128)(2,1)S(1)}, bf16[320,256]{1,0:T(8,128)(2,1)S(1)}, u32[]{:S(2)}, u32[]{:S(2)}) collective-permute-start(bf16[320,256]{1,0:T(8,128)(2,1)S(1)} %get-tuple-element.105), channel_id=1, source_target_pairs={{0,96},{8,104},{16,112},{24,120},{32,64},{40,72},{48,80},{56,88},{... | collective-permute-start | bytes 491528 | tf_op jit(solution)/shard_map/ppermute | solution.py:44
  98.0 20.4 %copy-start.11 = (bf16[640,256]{1,0:T(8,128)(2,1)}, bf16[640,256]{1,0:T(8,128)(2,1)S(1)}, u32[]{:S(2)}) copy-start(bf16[640,256]{1,0:T(8,128)(2,1)S(1)} %collective-permute-done.17.refs_2_) | copy-start | bytes 983044
  98.0 13.0 %collective-permute-start.25 = (bf16[320,256]{1,0:T(8,128)(2,1)S(1)}, bf16[320,256]{1,0:T(8,128)(2,1)S(1)}, u32[]{:S(2)}, u32[]{:S(2)}) collective-permute-start(bf16[320,256]{1,0:T(8,128)(2,1)S(1)} %get-tuple-element.106), channel_id=1, source_target_pairs={{0,112},{8,120},{16,64},{24,72},{32,80},{40,88},{48,96},{56,104},{... | collective-permute-start | bytes 491528 | tf_op jit(solution)/shard_map/ppermute | solution.py:44
  100.2 18.2 %copy-start.12 = (bf16[640,256]{1,0:T(8,128)(2,1)}, bf16[640,256]{1,0:T(8,128)(2,1)S(1)}, u32[]{:S(2)}) copy-start(bf16[640,256]{1,0:T(8,128)(2,1)S(1)} %collective-permute-done.18.refs_3_) | copy-start | bytes 983044
  100.3 21.1 %collective-permute-start.19 = (bf16[2560,256]{1,0:T(8,128)(2,1)S(1)}, bf16[2560,256]{1,0:T(8,128)(2,1)S(1)}, u32[]{:S(2)}, u32[]{:S(2)}) collective-permute-start(bf16[2560,256]{1,0:T(8,128)(2,1)S(1)} %pad_maximum_fusion.1), channel_id=1, source_target_pairs={{0,8},{8,0},{16,24},{24,16},{32,40},{40,32},{48,56},{56,48},{64,72... | collective-permute-start | bytes 3932168 | tf_op jit(solution)/shard_map/ppermute | solution.py:56
  107.5 13.9 %copy-start.14 = (bf16[320,256]{1,0:T(8,128)(2,1)}, bf16[320,256]{1,0:T(8,128)(2,1)S(1)}, u32[]{:S(2)}) copy-start(bf16[320,256]{1,0:T(8,128)(2,1)S(1)} %collective-permute-done.16.refs_9_) | copy-start | bytes 491524
  107.5 10.5 %collective-permute-start.20 = (bf16[320,256]{1,0:T(8,128)(2,1)S(1)}, bf16[320,256]{1,0:T(8,128)(2,1)S(1)}, u32[]{:S(2)}, u32[]{:S(2)}) collective-permute-start(bf16[320,256]{1,0:T(8,128)(2,1)S(1)} %get-tuple-element.100), channel_id=1, source_target_pairs={{0,16},{8,24},{16,32},{24,40},{32,48},{40,56},{48,0},{56,8},{64,80... | collective-permute-start | bytes 491528 | tf_op jit(solution)/shard_map/ppermute | solution.py:44
  108.2 13.1 %copy-start.15 = (bf16[320,256]{1,0:T(8,128)(2,1)}, bf16[320,256]{1,0:T(8,128)(2,1)S(1)}, u32[]{:S(2)}) copy-start(bf16[320,256]{1,0:T(8,128)(2,1)S(1)} %collective-permute-done.23.refs_10_) | copy-start | bytes 491524
  108.2 9.7 %collective-permute-start.21 = (bf16[320,256]{1,0:T(8,128)(2,1)S(1)}, bf16[320,256]{1,0:T(8,128)(2,1)S(1)}, u32[]{:S(2)}, u32[]{:S(2)}) collective-permute-start(bf16[320,256]{1,0:T(8,128)(2,1)S(1)} %get-tuple-element.101), channel_id=1, source_target_pairs={{0,32},{8,40},{16,48},{24,56},{32,0},{40,8},{48,16},{56,24},{64,96... | collective-permute-start | bytes 491528 | tf_op jit(solution)/shard_map/ppermute | solution.py:44
  109.1 12.3 %copy-start.16 = (bf16[320,256]{1,0:T(8,128)(2,1)}, bf16[320,256]{1,0:T(8,128)(2,1)S(1)}, u32[]{:S(2)}) copy-start(bf16[320,256]{1,0:T(8,128)(2,1)S(1)} %collective-permute-done.24.refs_11_) | copy-start | bytes 491524
  109.1 9.2 %collective-permute-start.22 = (bf16[320,256]{1,0:T(8,128)(2,1)S(1)}, bf16[320,256]{1,0:T(8,128)(2,1)S(1)}, u32[]{:S(2)}, u32[]{:S(2)}) collective-permute-start(bf16[320,256]{1,0:T(8,128)(2,1)S(1)} %get-tuple-element.102), channel_id=1, source_target_pairs={{0,48},{8,56},{16,0},{24,8},{32,16},{40,24},{48,32},{56,40},{64,11... | collective-permute-start | bytes 491528 | tf_op jit(solution)/shard_map/ppermute | solution.py:44
  111.0 10.3 %copy-start.17 = (bf16[320,256]{1,0:T(8,128)(2,1)}, bf16[320,256]{1,0:T(8,128)(2,1)S(1)}, u32[]{:S(2)}) copy-start(bf16[320,256]{1,0:T(8,128)(2,1)S(1)} %collective-permute-done.25.refs_12_) | copy-start | bytes 491524
  111.1 8.5 %collective-permute-start.27 = (bf16[1280,256]{1,0:T(8,128)(2,1)S(1)}, bf16[1280,256]{1,0:T(8,128)(2,1)S(1)}, u32[]{:S(2)}, u32[]{:S(2)}) collective-permute-start(bf16[1280,256]{1,0:T(8,128)(2,1)S(1)} %pad_maximum_fusion.3), channel_id=1, source_target_pairs={{0,8},{8,0},{16,24},{24,16},{32,40},{40,32},{48,56},{56,48},{64,72... | collective-permute-start | bytes 1966088 | tf_op jit(solution)/shard_map/ppermute | solution.py:56
  118.0 3.4 %copy-start.18 = (bf16[320,256]{1,0:T(8,128)(2,1)}, bf16[320,256]{1,0:T(8,128)(2,1)S(1)}, u32[]{:S(2)}) copy-start(bf16[320,256]{1,0:T(8,128)(2,1)S(1)} %collective-permute-done.20.refs_6_) | copy-start | bytes 491524
  118.0 3.4 %copy-start.19 = (bf16[320,256]{1,0:T(8,128)(2,1)}, bf16[320,256]{1,0:T(8,128)(2,1)S(1)}, u32[]{:S(2)}) copy-start(bf16[320,256]{1,0:T(8,128)(2,1)S(1)} %collective-permute-done.21.refs_7_) | copy-start | bytes 491524
  118.3 3.1 %copy-start.20 = (bf16[320,256]{1,0:T(8,128)(2,1)}, bf16[320,256]{1,0:T(8,128)(2,1)S(1)}, u32[]{:S(2)}) copy-start(bf16[320,256]{1,0:T(8,128)(2,1)S(1)} %collective-permute-done.22.refs_8_) | copy-start | bytes 491524
  118.4 3.0 %collective-permute-start.26 = (bf16[1280,256]{1,0:T(8,128)(2,1)S(1)}, bf16[1280,256]{1,0:T(8,128)(2,1)S(1)}, u32[]{:S(2)}, u32[]{:S(2)}) collective-permute-start(bf16[1280,256]{1,0:T(8,128)(2,1)S(1)} %pad_maximum_fusion.2), channel_id=1, source_target_pairs={{0,8},{8,0},{16,24},{24,16},{32,40},{40,32},{48,56},{56,48},{64,72... | collective-permute-start | bytes 1966088 | tf_op jit(solution)/shard_map/ppermute | solution.py:56
  119.6 1.8 %copy-start.21 = (bf16[1280,256]{1,0:T(8,128)(2,1)}, bf16[1280,256]{1,0:T(8,128)(2,1)S(1)}, u32[]{:S(2)}) copy-start(bf16[1280,256]{1,0:T(8,128)(2,1)S(1)} %collective-permute-done.27.refs_14_) | copy-start | bytes 1966084
  121.4 0.8 copy-start.22
  122.2 1.1 copy-start.13

commit v8 on v7

--- a/solution.py
+++ b/solution.py
@@ -76,24 +76,29 @@
 
 
 def project_kernel(count, has_acc, last, joint, features, *refs):
-    blocks, weights, refs = refs[:count], refs[count], refs[count + 1 :]
+    blocks, weights, refs = refs[:count], refs[count : count + 3], refs[count + 3 :]
     acc_in = None
     if has_acc:
         acc_in, refs = refs[0], refs[1:]
     if last:
         info, cosine, sine = refs[:3]
-        held, held_sems, acc, heads, packed, packed_sems = refs[-6:]
-        outs = refs[3:-6]
+        held, joined, held_sems, acc, heads, packed, packed_sems = refs[-7:]
+        outs = refs[3:-7]
     else:
-        acc, held, held_sems = refs
-    copies = [pltpu.make_async_copy(blocks[i], held.at[i], held_sems.at[i]) for i in range(count)]
-    for copy in copies:
-        copy.start()
-    for i, copy in enumerate(copies):
-        copy.wait()
+        acc, held, joined, held_sems = refs
+    copies = []
+    for i in range(count):
         rows = pl.ds(pl.multiple_of(features[i] * 1024, 1024), 1024)
-        block = held[i]
-        value = dot(block, weights[rows, :])
+        pairs = [(blocks[i], held.at[i])]
+        for w, lo in zip(weights, (0, 512, 640)):
+            pairs.append((w.at[rows, :], joined.at[i, :, lo : lo + w.shape[1]]))
+        copies.append([pltpu.make_async_copy(a, b, held_sems.at[i, n]) for n, (a, b) in enumerate(pairs)])
+        for copy in copies[i]:
+            copy.start()
+    for i in range(count):
+        for copy in copies[i]:
+            copy.wait()
+        value = dot(held[i], joined[i])
         if i > 0:
             value = value + acc[...]
         elif has_acc:
@@ -137,12 +142,16 @@
 def project(features, blocks, weights, acc=None, tables=None, joint=False):
     count = len(blocks)
     last = tables is not None
-    specs = [SMEM] + [HBM] * count + [VMEM]
-    operands = [features, *blocks, weights]
+    specs = [SMEM] + [HBM] * (count + 3)
+    operands = [features, *blocks, *weights]
     if acc is not None:
         specs.append(VMEM)
         operands.append(acc)
-    scratch = [pltpu.VMEM((count, ROWS, 1024), jnp.bfloat16), pltpu.SemaphoreType.DMA((count,))]
+    scratch = [
+        pltpu.VMEM((count, ROWS, 1024), jnp.bfloat16),
+        pltpu.VMEM((count, 1024, 768), jnp.bfloat16),
+        pltpu.SemaphoreType.DMA((count, 4)),
+    ]
     if last:
         specs += [SMEM, VMEM, VMEM]
         operands += list(tables)
@@ -164,7 +173,7 @@
         out_specs=out_specs,
         out_shape=out_shape,
         scratch_shapes=scratch,
-        compiler_params=pltpu.CompilerParams(vmem_limit_bytes=32 * 2**20),
+        compiler_params=pltpu.CompilerParams(vmem_limit_bytes=58 * 2**20),
         cost_estimate=pl.CostEstimate(flops=1, bytes_accessed=1, transcendentals=0),
         name="project",
     )(*operands)
@@ -288,7 +297,7 @@
 def local(tokens, old_map, new_map, w_query, key_projection_weight, value_projection_weight):
     me = lax.axis_index("ctx").astype(jnp.int32)
     place = lax.axis_index("tp").astype(jnp.int32)
-    weights = jnp.concatenate([w_query, key_projection_weight, value_projection_weight], axis=1)
+    weights = (w_query, key_projection_weight, value_projection_weight)
     send_info, attend_info, old_mine = routing(old_map, new_map, me)
     x, y = place // 2, place % 2
     feature = lambda dx, dy: ((x + dx) % 4) * 2 + (y + dy) % 2
@@ -305,8 +314,8 @@
     left = shift_x(early, 1)
     right = shift_x(early, -1)
     across = swap_y(early)
-    weights, late, left, right, across, send_info, attend_info, old_flat, *tables = together(
-        weights, late, left, right, across, send_info, attend_info, old_flat, *tables
+    late, left, right, across, send_info, attend_info, old_flat, *tables = together(
+        late, left, right, across, send_info, attend_info, old_flat, *tables
     )
     left_across = shift_x(across, 1)
     far = shift_x(right, -1)

time: 146 us -> 138 us (0.945)
  local copies, waits for them, and re-layouts: 24.9 us -> 7.08 us
  Pallas kernels: 40.9 us -> 54.2 us
  other arithmetic: 14.4 us -> 7.28 us
  waiting for transfers between devices: 11.7 us -> 14.8 us
    unnamed x50 -> x74, local copies, waits for them, and re-layouts: 22.1 us -> 4.39 us
    pallas_call x6, Pallas kernels: 19.4 us -> 32.7 us  [project(): pl.pallas_call(functools.partial(project_kernel, count, acc is not None,...]
    concatenate x1 -> x0, other arithmetic: 10.5 us -> none  [local(): jnp.concatenate([w_query, key_projection_weight, value_projection_weight]...]
    ppermute x10, waiting for transfers between devices: 4.85 us -> 7.59 us  [shift_x(): return lax.ppermute(block, 'tp', perm)]
    another operation x3, other arithmetic: 0.23 us -> 1.79 us  [local(): jnp.stack([feature(dx, dy) for dx, dy in order]).astype(jnp.int32)]
  transfers between devices with their start and end apart: 28 -> 28, of which waited for: 6 -> 9; matrix products, arithmetic and copies ran while one was open for 11% -> 6% of each run, Pallas kernels for 13% -> 24%
where the time goes in v8:
time: 138 us; the launch traced here: 137 us
  Pallas kernels  54.2 us (39%)
  starting transfers between devices  48.1 us (35%)
  waiting for transfers between devices  14.8 us (11%)
  other arithmetic  7.28 us (5%)
  local copies, waits for them, and re-layouts  7.08 us (5%)
  between operations  5.7 us (4%)
    pallas_call x6, Pallas kernels, project(): pl.pallas_call(functools.partial(project_kernel, count, acc is not None,...  32.7 us
    pallas_call x1, Pallas kernels, attend(): pl.pallas_call(attend_kernel, out_shape=jax.ShapeDtypeStruct((512, 512),...  21.5 us
    ppermute x11, starting transfers between devices, shift_ctx(): return lax.ppermute(block, 'ctx', perm)  20.9 us
    ppermute x10, starting transfers between devices, shift_x(): return lax.ppermute(block, 'tp', perm)  13.5 us
    ppermute x3, starting transfers between devices, swap_core(): return lax.ppermute(block, 'ctx', [(i, i ^ 1) for i in range(16)])  10.6 us
    ppermute x10, waiting for transfers between devices, shift_x(): return lax.ppermute(block, 'tp', perm)  7.59 us
    ppermute x11, waiting for transfers between devices, shift_ctx(): return lax.ppermute(block, 'ctx', perm)  5.51 us
    unnamed x74, local copies, waits for them, and re-layouts  4.39 us
  transfers between devices with their start and end apart: 28, of which 9 were waited for; matrix products, arithmetic and copies ran while one was open for 6% of the time, Pallas kernels for 24%

profile of v8, /device:TPU:1, one launch (start us, length us, event | category | flops | bytes accessed | tf_op | source)
XLA Modules:
  0.0 137.2 jit_solution(8039331109083200884)
XLA Ops:
  0.0 1.3 fusion.5
  1.3 2.1 %collective-permute-start = (bf16[256,1024]{1,0:T(8,128)(2,1)S(1)}, bf16[256,1024]{1,0:T(8,128)(2,1)S(1)}, u32[]{:S(2)}, u32[]{:S(2)}) collective-permute-start(bf16[256,1024]{1,0:T(8,128)(2,1)S(1)} %bitcast.29), channel_id=1, source_target_pairs={{0,2},{1,3},{2,4},{3,5},{4,6},{5,7},{6,0},{7,1},{8,10},{9,11},{10,... | collective-permute-start | bytes 1572872 | tf_op jit(solution)/shard_map/ppermute | solution.py:30
  3.4 1.3 collective-permute-start.1
  4.8 1.4 %collective-permute-start.2 = (bf16[256,1024]{1,0:T(8,128)(2,1)S(1)}, bf16[256,1024]{1,0:T(8,128)(2,1)S(1)}, u32[]{:S(2)}, u32[]{:S(2)}) collective-permute-start(bf16[256,1024]{1,0:T(8,128)(2,1)S(1)} %bitcast.31), channel_id=1, source_target_pairs={{0,1},{1,0},{2,3},{3,2},{4,5},{5,4},{6,7},{7,6},{8,9},{9,8},{10,11... | collective-permute-start | bytes 1572872 | tf_op jit(solution)/shard_map/ppermute | solution.py:34
  6.2 0.6 fusion.7
  11.9 0.1 compare_reduce_fusion.1
  12.0 0.1 select_reduce_fusion.1
  12.1 0.1 compare_reduce_fusion
  12.3 0.1 select_reduce_fusion
  12.6 0.7 pad_add_fusion.refs_5_.refs_6_
  13.2 0.6 pad_add_fusion.1.info
  13.8 0.6 reshape.65.old_map
  14.4 0.1 convert_element_type.25
  14.6 1.0 fusion.4
  15.6 0.9 pad_maximum_fusion.7
  16.5 0.8 pad_maximum_fusion.9
  17.4 2.7 %collective-permute-start.4 = (bf16[256,1024]{1,0:T(8,128)(2,1)S(1)}, bf16[256,1024]{1,0:T(8,128)(2,1)}, u32[]{:S(2)}, u32[]{:S(2)}) collective-permute-start(bf16[256,1024]{1,0:T(8,128)(2,1)S(1)} %collective-permute-done.1.refs_2_), channel_id=1, source_target_pairs={{0,6},{1,7},{2,0},{3,1},{4,2},{5,3},{6,4},{7,5},{8,14},{9,15},{10,... | collective-permute-start | bytes 1572872 | tf_op jit(solution)/shard_map/ppermute | solution.py:30
  20.1 0.6 pad_add_fusion.2.features
  20.7 1.0 collective-permute-start.7
  21.7 6.0 %project.6.refs_6_ = f32[256,768]{1,0:T(8,128)} custom-call(s32[4]{0:T(128)} %pad_add_fusion.2.features, bf16[256,1024]{1,0:T(8,128)(2,1)} %bitcast.32, bf16[256,1024]{1,0:T(8,128)(2,1)} %copy-done.19, bf16[256,1024]{1,0:T(8,128)(2,1)} %copy-done.18, bf16[256,1024]{1,0:T(8,128)(2,1)} %copy-done.20, bf16[8192,512]{1,0:T(8,128)(2,1)} %refs_2_.5, ...), custom_call_target="tpu_custom_call" | custom-call | flops 1 | bytes 1 | tf_op jit(solution)/shard_map/project/pallas_call | solution.py:170
  27.7 2.6 %collective-permute-done.3.refs_0_ = bf16[256,1024]{1,0:T(8,128)(2,1)S(1)} collective-permute-done((bf16[256,1024]{1,0:T(8,128)(2,1)S(1)}, bf16[256,1024]{1,0:T(8,128)(2,1)S(1)}, u32[]{:S(2)}, u32[]{:S(2)}) %collective-permute-start.3) | collective-permute-done | bytes 524320 | tf_op jit(solution)/shard_map/ppermute | solution.py:30
  30.3 2.5 %collective-permute-start.6 = (bf16[256,1024]{1,0:T(8,128)(2,1)S(1)}, bf16[256,1024]{1,0:T(8,128)(2,1)S(1)}, u32[]{:S(2)}, u32[]{:S(2)}) collective-permute-start(bf16[256,1024]{1,0:T(8,128)(2,1)S(1)} %bitcast.25), channel_id=1, source_target_pairs={{0,6},{1,7},{2,0},{3,1},{4,2},{5,3},{6,4},{7,5},{8,14},{9,15},{10,... | collective-permute-start | bytes 1572872 | tf_op jit(solution)/shard_map/ppermute | solution.py:30
  32.8 0.7 pad_add_fusion.3.features
  33.5 0.5 collective-permute-start.9
  34.0 5.9 %project.7.refs_4_ = f32[256,768]{1,0:T(8,128)} custom-call(s32[3]{0:T(128)} %pad_add_fusion.3.features, bf16[256,1024]{1,0:T(8,128)(2,1)} %copy-done.21, bf16[256,1024]{1,0:T(8,128)(2,1)} %collective-permute-done.4.refs_1_, bf16[256,1024]{1,0:T(8,128)(2,1)} %collective-permute-done.7.refs_2_, bf16[8192,512]{1,0:T(8,128)(2,1)} %refs_2_.5, ...), custom_call_target="tpu_custom_call" | custom-call | flops 1 | bytes 1 | tf_op jit(solution)/shard_map/project/pallas_call | solution.py:170
  39.9 1.2 collective-permute-done.6.refs_2_
  41.1 3.1 %collective-permute-done.5.refs_0_ = bf16[256,1024]{1,0:T(8,128)(2,1)S(1)} collective-permute-done((bf16[256,1024]{1,0:T(8,128)(2,1)S(1)}, bf16[256,1024]{1,0:T(8,128)(2,1)S(1)}, u32[]{:S(2)}, u32[]{:S(2)}) %collective-permute-start.5) | collective-permute-done | bytes 524320 | tf_op jit(solution)/shard_map/ppermute | solution.py:30
  44.2 2.7 %collective-permute-start.13 = (bf16[256,1024]{1,0:T(8,128)(2,1)S(1)}, bf16[256,1024]{1,0:T(8,128)(2,1)S(1)}, u32[]{:S(2)}, u32[]{:S(2)}) collective-permute-start(bf16[256,1024]{1,0:T(8,128)(2,1)S(1)} %collective-permute-done.6.refs_2_), channel_id=1, source_target_pairs={{0,6},{1,7},{2,0},{3,1},{4,2},{5,3},{6,4},{7,5},{8,14},{9,15},{10,... | collective-permute-start | bytes 1572872 | tf_op jit(solution)/shard_map/ppermute | solution.py:30
  46.9 0.1 collective-permute-start.14
  47.0 4.5 %project.8 = (bf16[320,256]{1,0:T(8,128)(2,1)}, bf16[320,256]{1,0:T(8,128)(2,1)}, bf16[320,256]{1,0:T(8,128)(2,1)}, bf16[320,256]{1,0:T(8,128)(2,1)}, bf16[512,256]{1,0:T(8,128)(2,1)}) custom-call(s32[1]{0:T(128)} %bitcast.10.features, bf16[256,1024]{1,0:T(8,128)(2,1)} %copy-done.17, bf16[8192,512]{1,0:T(8,128)(2,1)} %refs_2_.5, bf16[8192,128]{1,0:T(8,128)(2,1)} %refs_3_.7, ...), custom_call_target="tpu_custom_call" | custom-call | flops 1 | bytes 1 | tf_op jit(solution)/shard_map/project/pallas_call | solution.py:170
  51.5 2.7 %collective-permute-start.8 = (bf16[512,256]{1,0:T(8,128)(2,1)}, bf16[512,256]{1,0:T(8,128)(2,1)S(1)}, u32[]{:S(2)}, u32[]{:S(2)}) collective-permute-start(bf16[512,256]{1,0:T(8,128)(2,1)} %get-tuple-element.73), channel_id=1, source_target_pairs={{0,64},{8,72},{16,80},{24,88},{32,96},{40,104},{48,112},{56,120},{... | collective-permute-start | bytes 786440 | tf_op jit(solution)/shard_map/ppermute | solution.py:44
  54.2 0.6 collective-permute-done.10.refs_1_
  54.9 0.2 copy-done.22
  55.0 6.1 %project.9.refs_5_ = f32[256,768]{1,0:T(8,128)} custom-call(s32[4]{0:T(128)} %pad_add_fusion.2.features, bf16[256,1024]{1,0:T(8,128)(2,1)} %bitcast.28, bf16[256,1024]{1,0:T(8,128)(2,1)} %collective-permute-done.10.refs_1_, bf16[256,1024]{1,0:T(8,128)(2,1)} %copy-done.23, bf16[256,1024]{1,0:T(8,128)(2,1)} %copy-done.22, bf16[8192,512]{1,0:T(8,128)(2,1)} %refs_2_.5, ...), custom_call_target="tpu_custom_call" | custom-call | flops 1 | bytes 1 | tf_op jit(solution)/shard_map/project/pallas_call | solution.py:170
  61.1 0.5 collective-permute-done.8
  61.7 2.1 %collective-permute-start.15 = (bf16[256,1024]{1,0:T(8,128)(2,1)S(1)}, bf16[256,1024]{1,0:T(8,128)(2,1)S(1)}, u32[]{:S(2)}, u32[]{:S(2)}) collective-permute-start(bf16[256,1024]{1,0:T(8,128)(2,1)S(1)} %collective-permute-done.14.refs_1_), channel_id=1, source_target_pairs={{0,6},{1,7},{2,0},{3,1},{4,2},{5,3},{6,4},{7,5},{8,14},{9,15},{10,... | collective-permute-start | bytes 1572872 | tf_op jit(solution)/shard_map/ppermute | solution.py:30
  64.0 1.7 %collective-permute-start.11 = (bf16[640,256]{1,0:T(8,128)(2,1)S(1)}, bf16[640,256]{1,0:T(8,128)(2,1)S(1)}, u32[]{:S(2)}, u32[]{:S(2)}) collective-permute-start(bf16[640,256]{1,0:T(8,128)(2,1)S(1)} %get-tuple-element.83), channel_id=1, source_target_pairs={{0,16},{8,24},{16,32},{24,40},{32,48},{40,56},{48,0},{56,8},{64,80... | collective-permute-start | bytes 983048 | tf_op jit(solution)/shard_map/ppermute | solution.py:44
  65.7 3.3 %collective-permute-start.17 = (bf16[640,256]{1,0:T(8,128)(2,1)S(1)}, bf16[640,256]{1,0:T(8,128)(2,1)S(1)}, u32[]{:S(2)}, u32[]{:S(2)}) collective-permute-start(bf16[640,256]{1,0:T(8,128)(2,1)S(1)} %get-tuple-element.95), channel_id=1, source_target_pairs={{0,32},{8,40},{16,48},{24,56},{32,0},{40,8},{48,16},{56,24},{64,96... | collective-permute-start | bytes 983048 | tf_op jit(solution)/shard_map/ppermute | solution.py:44
  69.0 0.7 collective-permute-start.18
  69.8 0.6 pad_add_fusion.4.features
  70.3 0.6 pad_add_fusion.5.features
  70.9 4.9 %project.10.refs_5_ = f32[256,768]{1,0:T(8,128)} custom-call(s32[2]{0:T(128)} %pad_add_fusion.5.features, bf16[256,1024]{1,0:T(8,128)(2,1)} %copy-done.25, bf16[256,1024]{1,0:T(8,128)(2,1)} %copy-done.24, bf16[8192,512]{1,0:T(8,128)(2,1)} %refs_2_.5, bf16[8192,128]{1,0:T(8,128)(2,1)} %refs_3_.7, bf16[8192,128]{1,0:T(8,128)(2,1)} %refs_4_.9, ...), custom_call_target="tpu_custom_call" | custom-call | flops 1 | bytes 1 | tf_op jit(solution)/shard_map/project/pallas_call | solution.py:170
  75.9 0.8 copy-done.26
  76.7 0.8 copy-done.27
  77.5 5.3 %project.11 = (bf16[320,256]{1,0:T(8,128)(2,1)}, bf16[320,256]{1,0:T(8,128)(2,1)}, bf16[320,256]{1,0:T(8,128)(2,1)}, bf16[320,256]{1,0:T(8,128)(2,1)}, bf16[320,...) custom-call(s32[2]{0:T(128)} %pad_add_fusion.4.features, ...), custom_call_target="tpu_custom_call" | custom-call | flops 1 | bytes 1 | tf_op jit(solution)/shard_map/project/pallas_call | solution.py:170
  82.8 1.7 %collective-permute-start.16 = (bf16[320,256]{1,0:T(8,128)(2,1)}, bf16[320,256]{1,0:T(8,128)(2,1)S(1)}, u32[]{:S(2)}, u32[]{:S(2)}) collective-permute-start(bf16[320,256]{1,0:T(8,128)(2,1)} %get-tuple-element.89), channel_id=1, source_target_pairs={{0,64},{8,72},{16,80},{24,88},{32,96},{40,104},{48,112},{56,120},{... | collective-permute-start | bytes 491528 | tf_op jit(solution)/shard_map/ppermute | solution.py:44
  84.5 1.8 %collective-permute-start.23 = (bf16[320,256]{1,0:T(8,128)(2,1)}, bf16[320,256]{1,0:T(8,128)(2,1)S(1)}, u32[]{:S(2)}, u32[]{:S(2)}) collective-permute-start(bf16[320,256]{1,0:T(8,128)(2,1)} %get-tuple-element.102), channel_id=1, source_target_pairs={{0,80},{8,88},{16,96},{24,104},{32,112},{40,120},{48,64},{56,72},{... | collective-permute-start | bytes 491528 | tf_op jit(solution)/shard_map/ppermute | solution.py:44
  86.3 1.8 %collective-permute-start.24 = (bf16[320,256]{1,0:T(8,128)(2,1)}, bf16[320,256]{1,0:T(8,128)(2,1)S(1)}, u32[]{:S(2)}, u32[]{:S(2)}) collective-permute-start(bf16[320,256]{1,0:T(8,128)(2,1)} %get-tuple-element.103), channel_id=1, source_target_pairs={{0,96},{8,104},{16,112},{24,120},{32,64},{40,72},{48,80},{56,88},{... | collective-permute-start | bytes 491528 | tf_op jit(solution)/shard_map/ppermute | solution.py:44
  88.2 2.5 %collective-permute-start.25 = (bf16[320,256]{1,0:T(8,128)(2,1)}, bf16[320,256]{1,0:T(8,128)(2,1)S(1)}, u32[]{:S(2)}, u32[]{:S(2)}) collective-permute-start(bf16[320,256]{1,0:T(8,128)(2,1)} %get-tuple-element.104), channel_id=1, source_target_pairs={{0,112},{8,120},{16,64},{24,72},{32,80},{40,88},{48,96},{56,104},{... | collective-permute-start | bytes 491528 | tf_op jit(solution)/shard_map/ppermute | solution.py:44
  90.7 0.1 pad_maximum_fusion
  90.8 0.6 copy-done.5
  91.4 8.1 %collective-permute-start.19 = (bf16[2560,256]{1,0:T(8,128)(2,1)S(1)}, bf16[2560,256]{1,0:T(8,128)(2,1)S(1)}, u32[]{:S(2)}, u32[]{:S(2)}) collective-permute-start(bf16[2560,256]{1,0:T(8,128)(2,1)S(1)} %pad_maximum_fusion), channel_id=1, source_target_pairs={{0,8},{8,0},{16,24},{24,16},{32,40},{40,32},{48,56},{56,48},{64,72... | collective-permute-start | bytes 3932168 | tf_op jit(solution)/shard_map/ppermute | solution.py:56
  99.5 0.1 collective-permute-start.20
  99.7 2.5 %collective-permute-start.21 = (bf16[320,256]{1,0:T(8,128)(2,1)S(1)}, bf16[320,256]{1,0:T(8,128)(2,1)S(1)}, u32[]{:S(2)}, u32[]{:S(2)}) collective-permute-start(bf16[320,256]{1,0:T(8,128)(2,1)S(1)} %copy-done.35), channel_id=1, source_target_pairs={{0,32},{8,40},{16,48},{24,56},{32,0},{40,8},{48,16},{56,24},{64,96... | collective-permute-start | bytes 491528 | tf_op jit(solution)/shard_map/ppermute | solution.py:44
  102.1 2.0 %collective-permute-start.22 = (bf16[320,256]{1,0:T(8,128)(2,1)S(1)}, bf16[320,256]{1,0:T(8,128)(2,1)S(1)}, u32[]{:S(2)}, u32[]{:S(2)}) collective-permute-start(bf16[320,256]{1,0:T(8,128)(2,1)S(1)} %copy-done.34), channel_id=1, source_target_pairs={{0,48},{8,56},{16,0},{24,8},{32,16},{40,24},{48,32},{56,40},{64,11... | collective-permute-start | bytes 491528 | tf_op jit(solution)/shard_map/ppermute | solution.py:44
  104.2 1.3 collective-permute-start.27
  105.5 1.3 collective-permute-done.20.refs_6_
  106.8 3.1 %collective-permute-done.21.refs_7_ = bf16[320,256]{1,0:T(8,128)(2,1)S(1)} collective-permute-done((bf16[320,256]{1,0:T(8,128)(2,1)S(1)}, bf16[320,256]{1,0:T(8,128)(2,1)S(1)}, u32[]{:S(2)}, u32[]{:S(2)}) %collective-permute-start.21) | collective-permute-done | bytes 163872 | tf_op jit(solution)/shard_map/ppermute | solution.py:44
  109.9 0.6 collective-permute-done.22.refs_8_
  110.6 1.2 collective-permute-start.26
  111.8 1.7 %collective-permute-done.26.refs_13_ = bf16[1280,256]{1,0:T(8,128)(2,1)S(1)} collective-permute-done((bf16[1280,256]{1,0:T(8,128)(2,1)S(1)}, bf16[1280,256]{1,0:T(8,128)(2,1)S(1)}, u32[]{:S(2)}, u32[]{:S(2)}) %collective-permute-start.26) | collective-permute-done | bytes 655392 | tf_op jit(solution)/shard_map/ppermute | solution.py:56
  113.6 0.8 copy-done.16
  114.4 1.1 copy-done.6
  115.5 21.5 %attend.1 = bf16[512,512]{1,0:T(8,128)(2,1)} custom-call(s32[19]{0:T(128)} %pad_add_fusion.1.info, s32[256]{0:T(256)} %reshape.65.old_map, bf16[640,256]{1,0:T(8,128)(2,1)} %copy-done, bf16[640,256]{1,0:T(8,128)(2,1)} %copy-done.3, bf16[640,256]{1,0:T(8,128)(2,1)} %copy-done.4, bf16[640,256]{1,0:T(8,128)(2,1)} %copy-done.5, bf16[2560,256]{1,0:T(8,128)(2,1)} %copy-done.6, ...), custom_call_target="tpu_custom_call" | custom-call | tf_op jit(solution)/shard_map/attend/pallas_call | solution.py:252
  (106 shorter events, 0.7 us)
Async XLA Ops:
  0.0 6.2 %copy-start.33 = (s32[16,16]{1,0:T(8,128)S(1)}, s32[16,16]{1,0:T(8,128)}, u32[]{:S(2)}) copy-start(s32[16,16]{1,0:T(8,128)} %param.8) | copy-start | bytes 3076
  0.0 11.8 %copy-start.32 = (s32[16,16]{1,0:T(8,128)S(1)}, s32[16,16]{1,0:T(8,128)}, u32[]{:S(2)}) copy-start(s32[16,16]{1,0:T(8,128)} %param.7) | copy-start | bytes 3076
  1.3 20.3 %copy-start.2 = (bf16[16,1,16,1024]{3,2,1,0:T(8,128)(2,1)}, bf16[16,1,16,1024]{3,2,1,0:T(8,128)(2,1)S(1)}, u32[]{:S(2)}) copy-start(bf16[16,1,16,1024]{3,2,1,0:T(8,128)(2,1)S(1)} %get-tuple-element.107) | copy-start | bytes 1572868
  1.3 42.9 %copy-start.1 = (bf16[16,1,16,1024]{3,2,1,0:T(8,128)(2,1)}, bf16[16,1,16,1024]{3,2,1,0:T(8,128)(2,1)S(1)}, u32[]{:S(2)}) copy-start(bf16[16,1,16,1024]{3,2,1,0:T(8,128)(2,1)S(1)} %get-tuple-element.108) | copy-start | bytes 1572868
  1.3 16.0 %collective-permute-start = (bf16[256,1024]{1,0:T(8,128)(2,1)S(1)}, bf16[256,1024]{1,0:T(8,128)(2,1)S(1)}, u32[]{:S(2)}, u32[]{:S(2)}) collective-permute-start(bf16[256,1024]{1,0:T(8,128)(2,1)S(1)} %bitcast.29), channel_id=1, source_target_pairs={{0,2},{1,3},{2,4},{3,5},{4,6},{5,7},{6,0},{7,1},{8,10},{9,11},{10,... | collective-permute-start | bytes 1572872 | tf_op jit(solution)/shard_map/ppermute | solution.py:30
  3.4 13.9 %collective-permute-start.1 = (bf16[256,1024]{1,0:T(8,128)(2,1)S(1)}, bf16[256,1024]{1,0:T(8,128)(2,1)S(1)}, u32[]{:S(2)}, u32[]{:S(2)}) collective-permute-start(bf16[256,1024]{1,0:T(8,128)(2,1)S(1)} %bitcast.30), channel_id=1, source_target_pairs={{0,6},{1,7},{2,0},{3,1},{4,2},{5,3},{6,4},{7,5},{8,14},{9,15},{10,... | collective-permute-start | bytes 1572872 | tf_op jit(solution)/shard_map/ppermute | solution.py:30
  4.8 12.5 %collective-permute-start.2 = (bf16[256,1024]{1,0:T(8,128)(2,1)S(1)}, bf16[256,1024]{1,0:T(8,128)(2,1)S(1)}, u32[]{:S(2)}, u32[]{:S(2)}) collective-permute-start(bf16[256,1024]{1,0:T(8,128)(2,1)S(1)} %bitcast.31), channel_id=1, source_target_pairs={{0,1},{1,0},{2,3},{3,2},{4,5},{5,4},{6,7},{7,6},{8,9},{9,8},{10,11... | collective-permute-start | bytes 1572872 | tf_op jit(solution)/shard_map/ppermute | solution.py:34
  17.3 4.4 %copy-start.19 = (bf16[256,1024]{1,0:T(8,128)(2,1)}, bf16[256,1024]{1,0:T(8,128)(2,1)S(1)}, u32[]{:S(2)}) copy-start(bf16[256,1024]{1,0:T(8,128)(2,1)S(1)} %collective-permute-done.refs_1_) | copy-start | bytes 1572868
  17.3 4.3 %copy-start.18 = (bf16[256,1024]{1,0:T(8,128)(2,1)}, bf16[256,1024]{1,0:T(8,128)(2,1)S(1)}, u32[]{:S(2)}) copy-start(bf16[256,1024]{1,0:T(8,128)(2,1)S(1)} %collective-permute-done.1.refs_2_) | copy-start | bytes 1572868
  17.3 4.3 %copy-start.20 = (bf16[256,1024]{1,0:T(8,128)(2,1)}, bf16[256,1024]{1,0:T(8,128)(2,1)S(1)}, u32[]{:S(2)}) copy-start(bf16[256,1024]{1,0:T(8,128)(2,1)S(1)} %collective-permute-done.2.refs_3_) | copy-start | bytes 1572868
  17.3 13.0 %collective-permute-start.3 = (bf16[256,1024]{1,0:T(8,128)(2,1)S(1)}, bf16[256,1024]{1,0:T(8,128)(2,1)S(1)}, u32[]{:S(2)}, u32[]{:S(2)}) collective-permute-start(bf16[256,1024]{1,0:T(8,128)(2,1)S(1)} %collective-permute-done.2.refs_3_), channel_id=1, source_target_pairs={{0,2},{1,3},{2,4},{3,5},{4,6},{5,7},{6,0},{7,1},{8,10},{9,11},{10,... | collective-permute-start | bytes 1572872 | tf_op jit(solution)/shard_map/ppermute | solution.py:30
  17.4 12.9 %collective-permute-start.4 = (bf16[256,1024]{1,0:T(8,128)(2,1)S(1)}, bf16[256,1024]{1,0:T(8,128)(2,1)}, u32[]{:S(2)}, u32[]{:S(2)}) collective-permute-start(bf16[256,1024]{1,0:T(8,128)(2,1)S(1)} %collective-permute-done.1.refs_2_), channel_id=1, source_target_pairs={{0,6},{1,7},{2,0},{3,1},{4,2},{5,3},{6,4},{7,5},{8,14},{9,15},{10,... | collective-permute-start | bytes 1572872 | tf_op jit(solution)/shard_map/ppermute | solution.py:30
  20.7 13.3 %collective-permute-start.7 = (bf16[256,1024]{1,0:T(8,128)(2,1)S(1)}, bf16[256,1024]{1,0:T(8,128)(2,1)}, u32[]{:S(2)}, u32[]{:S(2)}) collective-permute-start(bf16[256,1024]{1,0:T(8,128)(2,1)S(1)} %collective-permute-done.1.refs_2_), channel_id=1, source_target_pairs={{0,1},{1,0},{2,3},{3,2},{4,5},{5,4},{6,7},{7,6},{8,9},{9,8},{10,11... | collective-permute-start | bytes 1572872 | tf_op jit(solution)/shard_map/ppermute | solution.py:34
  30.3 3.7 %copy-start.21 = (bf16[256,1024]{1,0:T(8,128)(2,1)}, bf16[256,1024]{1,0:T(8,128)(2,1)S(1)}, u32[]{:S(2)}) copy-start(bf16[256,1024]{1,0:T(8,128)(2,1)S(1)} %collective-permute-done.3.refs_0_) | copy-start | bytes 1572868
  30.3 10.8 %collective-permute-start.6 = (bf16[256,1024]{1,0:T(8,128)(2,1)S(1)}, bf16[256,1024]{1,0:T(8,128)(2,1)S(1)}, u32[]{:S(2)}, u32[]{:S(2)}) collective-permute-start(bf16[256,1024]{1,0:T(8,128)(2,1)S(1)} %bitcast.25), channel_id=1, source_target_pairs={{0,6},{1,7},{2,0},{3,1},{4,2},{5,3},{6,4},{7,5},{8,14},{9,15},{10,... | collective-permute-start | bytes 1572872 | tf_op jit(solution)/shard_map/ppermute | solution.py:30
  32.8 11.4 %collective-permute-start.5 = (bf16[256,1024]{1,0:T(8,128)(2,1)S(1)}, bf16[256,1024]{1,0:T(8,128)(2,1)S(1)}, u32[]{:S(2)}, u32[]{:S(2)}) collective-permute-start(bf16[256,1024]{1,0:T(8,128)(2,1)S(1)} %collective-permute-done.3.refs_0_), channel_id=1, source_target_pairs={{0,2},{1,3},{2,4},{3,5},{4,6},{5,7},{6,0},{7,1},{8,10},{9,11},{10,... | collective-permute-start | bytes 1572872 | tf_op jit(solution)/shard_map/ppermute | solution.py:30
  33.5 20.7 %collective-permute-start.9 = (bf16[256,1024]{1,0:T(8,128)(2,1)S(1)}, bf16[256,1024]{1,0:T(8,128)(2,1)S(1)}, u32[]{:S(2)}, u32[]{:S(2)}) collective-permute-start(bf16[256,1024]{1,0:T(8,128)(2,1)S(1)} %bitcast.26), channel_id=1, source_target_pairs={{0,1},{1,0},{2,3},{3,2},{4,5},{5,4},{6,7},{7,6},{8,9},{9,8},{10,11... | collective-permute-start | bytes 1572872 | tf_op jit(solution)/shard_map/ppermute | solution.py:34
  41.1 10.4 %copy-start.23 = (bf16[256,1024]{1,0:T(8,128)(2,1)}, bf16[256,1024]{1,0:T(8,128)(2,1)S(1)}, u32[]{:S(2)}) copy-start(bf16[256,1024]{1,0:T(8,128)(2,1)S(1)} %collective-permute-done.6.refs_2_) | copy-start | bytes 1572868
  44.2 2.8 %copy-start.17 = (bf16[256,1024]{1,0:T(8,128)(2,1)}, bf16[256,1024]{1,0:T(8,128)(2,1)S(1)}, u32[]{:S(2)}) copy-start(bf16[256,1024]{1,0:T(8,128)(2,1)S(1)} %collective-permute-done.5.refs_0_) | copy-start | bytes 1572868
  44.2 10.6 %collective-permute-start.10 = (bf16[256,1024]{1,0:T(8,128)(2,1)S(1)}, bf16[256,1024]{1,0:T(8,128)(2,1)}, u32[]{:S(2)}, u32[]{:S(2)}) collective-permute-start(bf16[256,1024]{1,0:T(8,128)(2,1)S(1)} %bitcast.27), channel_id=1, source_target_pairs={{0,2},{1,3},{2,4},{3,5},{4,6},{5,7},{6,0},{7,1},{8,10},{9,11},{10,... | collective-permute-start | bytes 1572872 | tf_op jit(solution)/shard_map/ppermute | solution.py:30
  44.2 17.4 %collective-permute-start.13 = (bf16[256,1024]{1,0:T(8,128)(2,1)S(1)}, bf16[256,1024]{1,0:T(8,128)(2,1)S(1)}, u32[]{:S(2)}, u32[]{:S(2)}) collective-permute-start(bf16[256,1024]{1,0:T(8,128)(2,1)S(1)} %collective-permute-done.6.refs_2_), channel_id=1, source_target_pairs={{0,6},{1,7},{2,0},{3,1},{4,2},{5,3},{6,4},{7,5},{8,14},{9,15},{10,... | collective-permute-start | bytes 1572872 | tf_op jit(solution)/shard_map/ppermute | solution.py:30
  46.9 14.8 %collective-permute-start.14 = (bf16[256,1024]{1,0:T(8,128)(2,1)S(1)}, bf16[256,1024]{1,0:T(8,128)(2,1)S(1)}, u32[]{:S(2)}, u32[]{:S(2)}) collective-permute-start(bf16[256,1024]{1,0:T(8,128)(2,1)S(1)} %collective-permute-done.6.refs_2_), channel_id=1, source_target_pairs={{0,1},{1,0},{2,3},{3,2},{4,5},{5,4},{6,7},{7,6},{8,9},{9,8},{10,11... | collective-permute-start | bytes 1572872 | tf_op jit(solution)/shard_map/ppermute | solution.py:34
  51.5 10.1 %collective-permute-start.8 = (bf16[512,256]{1,0:T(8,128)(2,1)}, bf16[512,256]{1,0:T(8,128)(2,1)S(1)}, u32[]{:S(2)}, u32[]{:S(2)}) collective-permute-start(bf16[512,256]{1,0:T(8,128)(2,1)} %get-tuple-element.73), channel_id=1, source_target_pairs={{0,64},{8,72},{16,80},{24,88},{32,96},{40,104},{48,112},{56,120},{... | collective-permute-start | bytes 786440 | tf_op jit(solution)/shard_map/ppermute | solution.py:44
  54.2 0.8 copy-start.22
  54.8 9.0 %copy-start.28 = (bf16[320,256]{1,0:T(8,128)(2,1)S(1)}, bf16[320,256]{1,0:T(8,128)(2,1)}, u32[]{:S(2)}) copy-start(bf16[320,256]{1,0:T(8,128)(2,1)} %get-tuple-element.72) | copy-start | bytes 491524
  54.8 21.0 %collective-permute-start.12 = (bf16[256,1024]{1,0:T(8,128)(2,1)S(1)}, bf16[256,1024]{1,0:T(8,128)(2,1)S(1)}, u32[]{:S(2)}, u32[]{:S(2)}) collective-permute-start(bf16[256,1024]{1,0:T(8,128)(2,1)S(1)} %collective-permute-done.9.refs_3_), channel_id=1, source_target_pairs={{0,2},{1,3},{2,4},{3,5},{4,6},{5,7},{6,0},{7,1},{8,10},{9,11},{10,... | collective-permute-start | bytes 1572872 | tf_op jit(solution)/shard_map/ppermute | solution.py:30
  61.1 2.8 %copy-start.29 = (bf16[320,256]{1,0:T(8,128)(2,1)S(1)}, bf16[320,256]{1,0:T(8,128)(2,1)}, u32[]{:S(2)}) copy-start(bf16[320,256]{1,0:T(8,128)(2,1)} %get-tuple-element.78) | copy-start | bytes 491524
  61.1 2.8 %copy-start.30 = (bf16[320,256]{1,0:T(8,128)(2,1)S(1)}, bf16[320,256]{1,0:T(8,128)(2,1)}, u32[]{:S(2)}) copy-start(bf16[320,256]{1,0:T(8,128)(2,1)} %get-tuple-element.79) | copy-start | bytes 491524
  61.1 2.8 %copy-start.31 = (bf16[320,256]{1,0:T(8,128)(2,1)S(1)}, bf16[320,256]{1,0:T(8,128)(2,1)}, u32[]{:S(2)}) copy-start(bf16[320,256]{1,0:T(8,128)(2,1)} %get-tuple-element.80) | copy-start | bytes 491524
  61.7 2.3 %copy-start.25 = (bf16[256,1024]{1,0:T(8,128)(2,1)}, bf16[256,1024]{1,0:T(8,128)(2,1)S(1)}, u32[]{:S(2)}) copy-start(bf16[256,1024]{1,0:T(8,128)(2,1)S(1)} %collective-permute-done.13.refs_0_) | copy-start | bytes 1572868
  61.7 2.3 %copy-start.24 = (bf16[256,1024]{1,0:T(8,128)(2,1)}, bf16[256,1024]{1,0:T(8,128)(2,1)S(1)}, u32[]{:S(2)}) copy-start(bf16[256,1024]{1,0:T(8,128)(2,1)S(1)} %collective-permute-done.14.refs_1_) | copy-start | bytes 1572868
  61.7 14.2 %collective-permute-start.15 = (bf16[256,1024]{1,0:T(8,128)(2,1)S(1)}, bf16[256,1024]{1,0:T(8,128)(2,1)S(1)}, u32[]{:S(2)}, u32[]{:S(2)}) collective-permute-start(bf16[256,1024]{1,0:T(8,128)(2,1)S(1)} %collective-permute-done.14.refs_1_), channel_id=1, source_target_pairs={{0,6},{1,7},{2,0},{3,1},{4,2},{5,3},{6,4},{7,5},{8,14},{9,15},{10,... | collective-permute-start | bytes 1572872 | tf_op jit(solution)/shard_map/ppermute | solution.py:30
  63.9 26.8 %copy-start = (bf16[640,256]{1,0:T(8,128)(2,1)}, bf16[640,256]{1,0:T(8,128)(2,1)S(1)}, u32[]{:S(2)}) copy-start(bf16[640,256]{1,0:T(8,128)(2,1)S(1)} %pad_maximum_fusion.6.refs_0_) | copy-start | bytes 983044
  64.0 22.3 %collective-permute-start.11 = (bf16[640,256]{1,0:T(8,128)(2,1)S(1)}, bf16[640,256]{1,0:T(8,128)(2,1)S(1)}, u32[]{:S(2)}, u32[]{:S(2)}) collective-permute-start(bf16[640,256]{1,0:T(8,128)(2,1)S(1)} %get-tuple-element.83), channel_id=1, source_target_pairs={{0,16},{8,24},{16,32},{24,40},{32,48},{40,56},{48,0},{56,8},{64,80... | collective-permute-start | bytes 983048 | tf_op jit(solution)/shard_map/ppermute | solution.py:44
  65.7 22.4 %collective-permute-start.17 = (bf16[640,256]{1,0:T(8,128)(2,1)S(1)}, bf16[640,256]{1,0:T(8,128)(2,1)S(1)}, u32[]{:S(2)}, u32[]{:S(2)}) collective-permute-start(bf16[640,256]{1,0:T(8,128)(2,1)S(1)} %get-tuple-element.95), channel_id=1, source_target_pairs={{0,32},{8,40},{16,48},{24,56},{32,0},{40,8},{48,16},{56,24},{64,96... | collective-permute-start | bytes 983048 | tf_op jit(solution)/shard_map/ppermute | solution.py:44
  69.0 21.7 %collective-permute-start.18 = (bf16[640,256]{1,0:T(8,128)(2,1)S(1)}, bf16[640,256]{1,0:T(8,128)(2,1)S(1)}, u32[]{:S(2)}, u32[]{:S(2)}) collective-permute-start(bf16[640,256]{1,0:T(8,128)(2,1)S(1)} %get-tuple-element.96), channel_id=1, source_target_pairs={{0,48},{8,56},{16,0},{24,8},{32,16},{40,24},{48,32},{56,40},{64,11... | collective-permute-start | bytes 983048 | tf_op jit(solution)/shard_map/ppermute | solution.py:44
  75.9 0.8 copy-start.26
  76.7 0.8 copy-start.27
  82.8 16.7 %collective-permute-start.16 = (bf16[320,256]{1,0:T(8,128)(2,1)}, bf16[320,256]{1,0:T(8,128)(2,1)S(1)}, u32[]{:S(2)}, u32[]{:S(2)}) collective-permute-start(bf16[320,256]{1,0:T(8,128)(2,1)} %get-tuple-element.89), channel_id=1, source_target_pairs={{0,64},{8,72},{16,80},{24,88},{32,96},{40,104},{48,112},{56,120},{... | collective-permute-start | bytes 491528 | tf_op jit(solution)/shard_map/ppermute | solution.py:44
  84.5 15.1 %collective-permute-start.23 = (bf16[320,256]{1,0:T(8,128)(2,1)}, bf16[320,256]{1,0:T(8,128)(2,1)S(1)}, u32[]{:S(2)}, u32[]{:S(2)}) collective-permute-start(bf16[320,256]{1,0:T(8,128)(2,1)} %get-tuple-element.102), channel_id=1, source_target_pairs={{0,80},{8,88},{16,96},{24,104},{32,112},{40,120},{48,64},{56,72},{... | collective-permute-start | bytes 491528 | tf_op jit(solution)/shard_map/ppermute | solution.py:44
  86.3 4.5 %copy-start.3 = (bf16[640,256]{1,0:T(8,128)(2,1)}, bf16[640,256]{1,0:T(8,128)(2,1)S(1)}, u32[]{:S(2)}) copy-start(bf16[640,256]{1,0:T(8,128)(2,1)S(1)} %collective-permute-done.11.refs_1_) | copy-start | bytes 983044
  86.3 15.8 %collective-permute-start.24 = (bf16[320,256]{1,0:T(8,128)(2,1)}, bf16[320,256]{1,0:T(8,128)(2,1)S(1)}, u32[]{:S(2)}, u32[]{:S(2)}) collective-permute-start(bf16[320,256]{1,0:T(8,128)(2,1)} %get-tuple-element.103), channel_id=1, source_target_pairs={{0,96},{8,104},{16,112},{24,120},{32,64},{40,72},{48,80},{56,88},{... | collective-permute-start | bytes 491528 | tf_op jit(solution)/shard_map/ppermute | solution.py:44
  88.1 2.7 %copy-start.4 = (bf16[640,256]{1,0:T(8,128)(2,1)}, bf16[640,256]{1,0:T(8,128)(2,1)S(1)}, u32[]{:S(2)}) copy-start(bf16[640,256]{1,0:T(8,128)(2,1)S(1)} %collective-permute-done.17.refs_2_) | copy-start | bytes 983044
  88.1 11.4 %copy-start.36 = (bf16[320,256]{1,0:T(8,128)(2,1)S(1)}, bf16[320,256]{1,0:T(8,128)(2,1)}, u32[]{:S(2)}) copy-start(bf16[320,256]{1,0:T(8,128)(2,1)} %get-tuple-element.98) | copy-start | bytes 491524
  88.1 11.5 %copy-start.35 = (bf16[320,256]{1,0:T(8,128)(2,1)S(1)}, bf16[320,256]{1,0:T(8,128)(2,1)}, u32[]{:S(2)}) copy-start(bf16[320,256]{1,0:T(8,128)(2,1)} %get-tuple-element.99) | copy-start | bytes 491524
  88.1 14.0 %copy-start.34 = (bf16[320,256]{1,0:T(8,128)(2,1)S(1)}, bf16[320,256]{1,0:T(8,128)(2,1)}, u32[]{:S(2)}) copy-start(bf16[320,256]{1,0:T(8,128)(2,1)} %get-tuple-element.100) | copy-start | bytes 491524
  88.2 16.0 %collective-permute-start.25 = (bf16[320,256]{1,0:T(8,128)(2,1)}, bf16[320,256]{1,0:T(8,128)(2,1)S(1)}, u32[]{:S(2)}, u32[]{:S(2)}) collective-permute-start(bf16[320,256]{1,0:T(8,128)(2,1)} %get-tuple-element.104), channel_id=1, source_target_pairs={{0,112},{8,120},{16,64},{24,72},{32,80},{40,88},{48,96},{56,104},{... | collective-permute-start | bytes 491528 | tf_op jit(solution)/shard_map/ppermute | solution.py:44
  91.4 19.1 %copy-start.7 = (bf16[320,256]{1,0:T(8,128)(2,1)S(1)}, bf16[320,256]{1,0:T(8,128)(2,1)}, u32[]{:S(2)}) copy-start(bf16[320,256]{1,0:T(8,128)(2,1)} %get-tuple-element.97.refs_5_) | copy-start | bytes 491524
  91.4 22.1 %collective-permute-start.19 = (bf16[2560,256]{1,0:T(8,128)(2,1)S(1)}, bf16[2560,256]{1,0:T(8,128)(2,1)S(1)}, u32[]{:S(2)}, u32[]{:S(2)}) collective-permute-start(bf16[2560,256]{1,0:T(8,128)(2,1)S(1)} %pad_maximum_fusion), channel_id=1, source_target_pairs={{0,8},{8,0},{16,24},{24,16},{32,40},{40,32},{48,56},{56,48},{64,72... | collective-permute-start | bytes 3932168 | tf_op jit(solution)/shard_map/ppermute | solution.py:56
  99.5 11.1 %copy-start.8 = (bf16[320,256]{1,0:T(8,128)(2,1)}, bf16[320,256]{1,0:T(8,128)(2,1)S(1)}, u32[]{:S(2)}) copy-start(bf16[320,256]{1,0:T(8,128)(2,1)S(1)} %collective-permute-done.16.refs_9_) | copy-start | bytes 491524
  99.5 7.3 %collective-permute-start.20 = (bf16[320,256]{1,0:T(8,128)(2,1)S(1)}, bf16[320,256]{1,0:T(8,128)(2,1)S(1)}, u32[]{:S(2)}, u32[]{:S(2)}) collective-permute-start(bf16[320,256]{1,0:T(8,128)(2,1)S(1)} %copy-done.36), channel_id=1, source_target_pairs={{0,16},{8,24},{16,32},{24,40},{32,48},{40,56},{48,0},{56,8},{64,80... | collective-permute-start | bytes 491528 | tf_op jit(solution)/shard_map/ppermute | solution.py:44
  99.7 10.9 %copy-start.9 = (bf16[320,256]{1,0:T(8,128)(2,1)}, bf16[320,256]{1,0:T(8,128)(2,1)S(1)}, u32[]{:S(2)}) copy-start(bf16[320,256]{1,0:T(8,128)(2,1)S(1)} %collective-permute-done.23.refs_10_) | copy-start | bytes 491524
  99.7 10.3 %collective-permute-start.21 = (bf16[320,256]{1,0:T(8,128)(2,1)S(1)}, bf16[320,256]{1,0:T(8,128)(2,1)S(1)}, u32[]{:S(2)}, u32[]{:S(2)}) collective-permute-start(bf16[320,256]{1,0:T(8,128)(2,1)S(1)} %copy-done.35), channel_id=1, source_target_pairs={{0,32},{8,40},{16,48},{24,56},{32,0},{40,8},{48,16},{56,24},{64,96... | collective-permute-start | bytes 491528 | tf_op jit(solution)/shard_map/ppermute | solution.py:44
  102.1 8.5 %copy-start.10 = (bf16[320,256]{1,0:T(8,128)(2,1)}, bf16[320,256]{1,0:T(8,128)(2,1)S(1)}, u32[]{:S(2)}) copy-start(bf16[320,256]{1,0:T(8,128)(2,1)S(1)} %collective-permute-done.24.refs_11_) | copy-start | bytes 491524
  102.1 8.4 %collective-permute-start.22 = (bf16[320,256]{1,0:T(8,128)(2,1)S(1)}, bf16[320,256]{1,0:T(8,128)(2,1)S(1)}, u32[]{:S(2)}, u32[]{:S(2)}) collective-permute-start(bf16[320,256]{1,0:T(8,128)(2,1)S(1)} %copy-done.34), channel_id=1, source_target_pairs={{0,48},{8,56},{16,0},{24,8},{32,16},{40,24},{48,32},{56,40},{64,11... | collective-permute-start | bytes 491528 | tf_op jit(solution)/shard_map/ppermute | solution.py:44
  104.1 6.5 %copy-start.11 = (bf16[320,256]{1,0:T(8,128)(2,1)}, bf16[320,256]{1,0:T(8,128)(2,1)S(1)}, u32[]{:S(2)}) copy-start(bf16[320,256]{1,0:T(8,128)(2,1)S(1)} %collective-permute-done.25.refs_12_) | copy-start | bytes 491524
  104.2 7.6 %collective-permute-start.27 = (bf16[1280,256]{1,0:T(8,128)(2,1)S(1)}, bf16[1280,256]{1,0:T(8,128)(2,1)S(1)}, u32[]{:S(2)}, u32[]{:S(2)}) collective-permute-start(bf16[1280,256]{1,0:T(8,128)(2,1)S(1)} %pad_maximum_fusion.2), channel_id=1, source_target_pairs={{0,8},{8,0},{16,24},{24,16},{32,40},{40,32},{48,56},{56,48},{64,72... | collective-permute-start | bytes 1966088 | tf_op jit(solution)/shard_map/ppermute | solution.py:56
  106.8 6.7 %copy-start.12 = (bf16[320,256]{1,0:T(8,128)(2,1)}, bf16[320,256]{1,0:T(8,128)(2,1)S(1)}, u32[]{:S(2)}) copy-start(bf16[320,256]{1,0:T(8,128)(2,1)S(1)} %collective-permute-done.20.refs_6_) | copy-start | bytes 491524
  109.9 3.6 %copy-start.13 = (bf16[320,256]{1,0:T(8,128)(2,1)}, bf16[320,256]{1,0:T(8,128)(2,1)S(1)}, u32[]{:S(2)}) copy-start(bf16[320,256]{1,0:T(8,128)(2,1)S(1)} %collective-permute-done.21.refs_7_) | copy-start | bytes 491524
  110.5 3.0 %copy-start.14 = (bf16[320,256]{1,0:T(8,128)(2,1)}, bf16[320,256]{1,0:T(8,128)(2,1)S(1)}, u32[]{:S(2)}) copy-start(bf16[320,256]{1,0:T(8,128)(2,1)S(1)} %collective-permute-done.22.refs_8_) | copy-start | bytes 491524
  110.6 2.9 %collective-permute-start.26 = (bf16[1280,256]{1,0:T(8,128)(2,1)S(1)}, bf16[1280,256]{1,0:T(8,128)(2,1)S(1)}, u32[]{:S(2)}, u32[]{:S(2)}) collective-permute-start(bf16[1280,256]{1,0:T(8,128)(2,1)S(1)} %pad_maximum_fusion.1), channel_id=1, source_target_pairs={{0,8},{8,0},{16,24},{24,16},{32,40},{40,32},{48,56},{56,48},{64,72... | collective-permute-start | bytes 1966088 | tf_op jit(solution)/shard_map/ppermute | solution.py:56
  111.8 1.7 %copy-start.15 = (bf16[1280,256]{1,0:T(8,128)(2,1)}, bf16[1280,256]{1,0:T(8,128)(2,1)S(1)}, u32[]{:S(2)}) copy-start(bf16[1280,256]{1,0:T(8,128)(2,1)S(1)} %collective-permute-done.27.refs_14_) | copy-start | bytes 1966084
  113.6 0.8 copy-start.16
  114.4 1.1 copy-start.6
  (1 other events, 0.7 us)

commit v9 on v5

--- a/solution.py
+++ b/solution.py
@@ -179,7 +179,7 @@
 
 def attend_kernel(info, old_map, *refs):
     packed, packed_other, late, late_other = refs[:4], refs[4], refs[5:13], refs[13:15]
-    out, query, keys, values, top, total, accum = refs[15:]
+    out, query, pairs, top, total, accum = refs[15:]
     me = info[0]
     high, z, core = me // 8, lax.rem(me // 2, 4), lax.rem(me, 2)
     for r, (dh, dz) in enumerate(CHIPS):
@@ -194,8 +194,7 @@
                 for k in range(16):
                     at = pl.ds(pl.multiple_of(old_map[source * 16 + k] * FINE + j * W, W), W)
                     rows = slice(base + k * W, base + (k + 1) * W)
-                    keys[at, :] = ref[rows, 0:HEAD]
-                    values[at, :] = ref[rows, HEAD : 2 * HEAD]
+                    pairs[at, :] = ref[rows, :]
                 for h in range(4):
                     at = pl.ds(pl.multiple_of(base + ROWS + (core * 2 + h // 2) * W, W), W)
                     to = (slot // 8) * 1024 + h * 256 + lax.rem(slot, 8) * FINE + j * W
@@ -211,7 +210,7 @@
 
         def absorb(block, masked, coarse=coarse, queries=queries):
             start = pl.multiple_of(block * KB, KB)
-            scores = dot_t(queries, keys[pl.ds(start, KB), :])
+            scores = dot_t(queries, pairs[pl.ds(start, KB), 0:HEAD])
             if masked:
                 row = lax.rem(lax.broadcasted_iota(jnp.int32, (1024, KB), 0), 256) + coarse * 256
                 visible = lax.broadcasted_iota(jnp.int32, (1024, KB), 1) + start <= row
@@ -224,7 +223,7 @@
                 weights = jnp.where(visible, weights, 0.0)
             total[...] = total[...] * factor + fold(weights, jnp.add)
             accum[...] = accum[...] * factor + dot(
-                weights.astype(jnp.bfloat16), values[pl.ds(start, KB), :]
+                weights.astype(jnp.bfloat16), pairs[pl.ds(start, KB), HEAD : 2 * HEAD]
             )
             top[...] = new
 
@@ -249,8 +248,7 @@
         out_specs=VMEM,
         scratch_shapes=[
             pltpu.VMEM((2048, HEAD), jnp.bfloat16),
-            pltpu.VMEM((8192, HEAD), jnp.bfloat16),
-            pltpu.VMEM((8192, HEAD), jnp.bfloat16),
+            pltpu.VMEM((8192, 2 * HEAD), jnp.bfloat16),
             pltpu.VMEM((1024, HEAD), jnp.float32),
             pltpu.VMEM((1024, HEAD), jnp.float32),
             pltpu.VMEM((1024, HEAD), jnp.float32),
@@ -327,8 +325,8 @@
     partner = shift_ctx(sent[4], 1, 0)
     late_across, late_left = together(late_across, late_left, sent[0])[:2]
     late_left_across = shift_x(late_across, 1)
-    blocks = [(late,), (late_left,), (late_right,), (late_across,)]
-    total = project(features[:4], blocks, weights)
+    blocks = [(late,), (late_right,), (late_across,)]
+    total = project(jnp.stack([features[0], features[2], features[3]]), blocks, weights)
     late_far, late_right_across, total = together(late_far, late_right_across, total)
     late_far_across = shift_x(late_right_across, -1)
     early_parts = [
@@ -336,7 +334,8 @@
         for dz in range(4)
     ]
     *early_parts, total = together(*early_parts, total)
-    total = project(features[5:7], [(late_far,), (late_right_across,)], weights, total)
+    blocks = [(late_left,), (late_far,), (late_right_across,)]
+    total = project(jnp.stack([features[1], features[5], features[6]]), blocks, weights, total)
     early_parts[1:] = [shift_ctx(early_parts[dz], 0, dz) for dz in range(1, 4)]
     last = jnp.stack([features[4], features[7]])
     tail = [(late_left_across,), (late_far_across,)]

time: 130 us -> 129 us (level)
  no operation moved by 1% of the time
where the time goes in v9:
time: 129 us; the launch traced here: 128 us
  starting transfers between devices  47.4 us (37%)
  Pallas kernels  45 us (35%)
  waiting for transfers between devices  17 us (13%)
  local copies, waits for them, and re-layouts  9.26 us (7%)
  between operations  5.16 us (4%)
  other arithmetic  4.63 us (4%)
    pallas_call x6, Pallas kernels, project(): pl.pallas_call(functools.partial(project_kernel, groups, acc is not None,...  25 us
    ppermute x11, starting transfers between devices, shift_ctx(): return lax.ppermute(block, 'ctx', perm)  21.7 us
    pallas_call x1, Pallas kernels, attend(): pl.pallas_call(attend_kernel, out_shape=jax.ShapeDtypeStruct((512, 512),...  20 us
    ppermute x10, starting transfers between devices, shift_x(): return lax.ppermute(block, 'tp', perm)  11.8 us
    ppermute x3, starting transfers between devices, swap_core(): return lax.ppermute(block, 'ctx', [(i, i ^ 1) for i in range(16)])  9.49 us
    unnamed x50, local copies, waits for them, and re-layouts  6.55 us
    ppermute x11, waiting for transfers between devices, shift_ctx(): return lax.ppermute(block, 'ctx', perm)  6.04 us
    ppermute x10, waiting for transfers between devices, shift_x(): return lax.ppermute(block, 'tp', perm)  4.65 us
  transfers between devices with their start and end apart: 28, of which 9 were waited for; matrix products, arithmetic and copies ran while one was open for 5% of the time, Pallas kernels for 19%

profile of v9, /device:TPU:1, one launch (start us, length us, event | category | flops | bytes accessed | tf_op | source)
XLA Modules:
  0.0 128.5 jit_solution(14860419013717823781)
XLA Ops:
  0.0 1.3 %fusion.5 = (bf16[16,1,16,1024]{3,2,1,0:T(8,128)(2,1)S(1)}, bf16[16,1,16,1024]{3,2,1,0:T(8,128)(2,1)S(1)}) fusion(bf16[16,2,16,1024]{3,2,1,0:T(8,128)(2,1)} %bitcast.33), kind=kLoop, calls=%fused_computation.38 | loop fusion | bytes 2097152 | tf_op jit(solution)/shard_map/slice | solution.py:296
  1.3 2.1 %collective-permute-start = (bf16[256,1024]{1,0:T(8,128)(2,1)S(1)}, bf16[256,1024]{1,0:T(8,128)(2,1)}, u32[]{:S(2)}, u32[]{:S(2)}) collective-permute-start(bf16[256,1024]{1,0:T(8,128)(2,1)S(1)} %bitcast.29), channel_id=1, source_target_pairs={{0,2},{1,3},{2,4},{3,5},{4,6},{5,7},{6,0},{7,1},{8,10},{9,11},{10,... | collective-permute-start | bytes 1572872 | tf_op jit(solution)/shard_map/ppermute | solution.py:29
  3.4 1.4 %collective-permute-start.1 = (bf16[256,1024]{1,0:T(8,128)(2,1)S(1)}, bf16[256,1024]{1,0:T(8,128)(2,1)}, u32[]{:S(2)}, u32[]{:S(2)}) collective-permute-start(bf16[256,1024]{1,0:T(8,128)(2,1)S(1)} %bitcast.30), channel_id=1, source_target_pairs={{0,6},{1,7},{2,0},{3,1},{4,2},{5,3},{6,4},{7,5},{8,14},{9,15},{10,... | collective-permute-start | bytes 1572872 | tf_op jit(solution)/shard_map/ppermute | solution.py:29
  4.8 1.4 %collective-permute-start.2 = (bf16[256,1024]{1,0:T(8,128)(2,1)S(1)}, bf16[256,1024]{1,0:T(8,128)(2,1)}, u32[]{:S(2)}, u32[]{:S(2)}) collective-permute-start(bf16[256,1024]{1,0:T(8,128)(2,1)S(1)} %bitcast.31), channel_id=1, source_target_pairs={{0,1},{1,0},{2,3},{3,2},{4,5},{5,4},{6,7},{7,6},{8,9},{9,8},{10,11... | collective-permute-start | bytes 1572872 | tf_op jit(solution)/shard_map/ppermute | solution.py:33
  6.2 0.6 fusion.7
  11.6 0.1 compare_reduce_fusion.1
  11.7 0.1 select_reduce_fusion.1
  11.8 0.1 compare_reduce_fusion
  12.0 0.1 select_reduce_fusion
  12.3 0.7 pad_add_fusion.1.info
  13.0 0.6 reshape.65.old_map
  13.6 0.1 convert_element_type.25
  13.7 0.1 convert_element_type.23
  13.8 1.0 fusion.4
  14.8 0.8 pad_maximum_fusion.7
  15.6 0.8 pad_maximum_fusion.9
  16.4 0.7 collective-permute-done.2.refs_4_
  17.1 0.2 collective-permute-start.3
  17.2 2.5 %collective-permute-start.4 = (bf16[256,1024]{1,0:T(8,128)(2,1)}, bf16[256,1024]{1,0:T(8,128)(2,1)}, u32[]{:S(2)}, u32[]{:S(2)}) collective-permute-start(bf16[256,1024]{1,0:T(8,128)(2,1)} %collective-permute-done.1.refs_3_), channel_id=1, source_target_pairs={{0,6},{1,7},{2,0},{3,1},{4,2},{5,3},{6,4},{7,5},{8,14},{9,15},{10,... | collective-permute-start | bytes 1572872 | tf_op jit(solution)/shard_map/ppermute | solution.py:29
  19.7 1.4 %collective-permute-start.8 = (bf16[256,1024]{1,0:T(8,128)(2,1)}, bf16[256,1024]{1,0:T(8,128)(2,1)}, u32[]{:S(2)}, u32[]{:S(2)}) collective-permute-start(bf16[256,1024]{1,0:T(8,128)(2,1)} %collective-permute-done.1.refs_3_), channel_id=1, source_target_pairs={{0,1},{1,0},{2,3},{3,2},{4,5},{5,4},{6,7},{7,6},{8,9},{9,8},{10,11... | collective-permute-start | bytes 1572872 | tf_op jit(solution)/shard_map/ppermute | solution.py:33
  21.2 0.1 pad_add_fusion.2.refs_0_
  21.3 1.0 copy-done.4
  22.3 5.5 %project.6.refs_7_ = f32[256,768]{1,0:T(8,128)S(1)} custom-call(s32[4]{0:T(128)S(1)} %pad_add_fusion.2.refs_0_, bf16[256,1024]{1,0:T(8,128)(2,1)S(1)} %bitcast.32, bf16[256,1024]{1,0:T(8,128)(2,1)} %collective-permute-done.refs_2_, bf16[256,1024]{1,0:T(8,128)(2,1)} %collective-permute-done.1.refs_3_, bf16[256,1024]{1,0:T(8,128)(2,1)} %collective-permute-done.2.refs_4_, ...), custom_call_target="tpu_custom_call" | custom-call | flops 1 | bytes 1 | tf_op jit(solution)/shard_map/project/pallas_call | solution.py:164
  27.9 1.9 %collective-permute-done.3.refs_1_ = bf16[256,1024]{1,0:T(8,128)(2,1)} collective-permute-done((bf16[256,1024]{1,0:T(8,128)(2,1)}, bf16[256,1024]{1,0:T(8,128)(2,1)}, u32[]{:S(2)}, u32[]{:S(2)}) %collective-permute-start.3) | collective-permute-done | bytes 524320 | tf_op jit(solution)/shard_map/ppermute | solution.py:29
  29.8 2.4 %collective-permute-start.6 = (bf16[256,1024]{1,0:T(8,128)(2,1)S(1)}, bf16[256,1024]{1,0:T(8,128)(2,1)}, u32[]{:S(2)}, u32[]{:S(2)}) collective-permute-start(bf16[256,1024]{1,0:T(8,128)(2,1)S(1)} %bitcast.26), channel_id=1, source_target_pairs={{0,6},{1,7},{2,0},{3,1},{4,2},{5,3},{6,4},{7,5},{8,14},{9,15},{10,... | collective-permute-start | bytes 1572872 | tf_op jit(solution)/shard_map/ppermute | solution.py:29
  32.3 0.1 add_add_fusion.refs_0_
  32.3 4.8 %project.7.refs_5_ = f32[256,768]{1,0:T(8,128)S(1)} custom-call(s32[3]{0:T(128)S(1)} %add_add_fusion.refs_0_, bf16[256,1024]{1,0:T(8,128)(2,1)} %collective-permute-done.3.refs_1_, bf16[256,1024]{1,0:T(8,128)(2,1)} %collective-permute-done.4.refs_2_, bf16[256,1024]{1,0:T(8,128)(2,1)} %collective-permute-done.8.refs_3_, bf16[8192,512]{1,0:T(8,128)(2,1)} %refs_3_.3, ...), custom_call_target="tpu_custom_call" | custom-call | flops 1 | bytes 1 | tf_op jit(solution)/shard_map/project/pallas_call | solution.py:164
  37.2 0.9 copy-done.1
  38.0 3.9 %collective-permute-done.7.refs_3_ = bf16[256,1024]{1,0:T(8,128)(2,1)} collective-permute-done((bf16[256,1024]{1,0:T(8,128)(2,1)S(1)}, bf16[256,1024]{1,0:T(8,128)(2,1)}, u32[]{:S(2)}, u32[]{:S(2)}) %collective-permute-start.7) | collective-permute-done | bytes 524320 | tf_op jit(solution)/shard_map/ppermute | solution.py:33
  42.0 1.6 %collective-permute-start.10 = (bf16[256,1024]{1,0:T(8,128)(2,1)}, bf16[256,1024]{1,0:T(8,128)(2,1)}, u32[]{:S(2)}, u32[]{:S(2)}) collective-permute-start(bf16[256,1024]{1,0:T(8,128)(2,1)} %collective-permute-done.6.refs_2_), channel_id=1, source_target_pairs={{0,6},{1,7},{2,0},{3,1},{4,2},{5,3},{6,4},{7,5},{8,14},{9,15},{10,... | collective-permute-start | bytes 1572872 | tf_op jit(solution)/shard_map/ppermute | solution.py:29
  43.6 1.5 %collective-permute-start.11 = (bf16[256,1024]{1,0:T(8,128)(2,1)}, bf16[256,1024]{1,0:T(8,128)(2,1)S(1)}, u32[]{:S(2)}, u32[]{:S(2)}) collective-permute-start(bf16[256,1024]{1,0:T(8,128)(2,1)} %collective-permute-done.6.refs_2_), channel_id=1, source_target_pairs={{0,1},{1,0},{2,3},{3,2},{4,5},{5,4},{6,7},{7,6},{8,9},{9,8},{10,11... | collective-permute-start | bytes 1572872 | tf_op jit(solution)/shard_map/ppermute | solution.py:33
  45.1 1.1 copy-done.2
  46.2 0.9 copy-done.6
  47.1 2.1 %project.8 = (bf16[320,256]{1,0:T(8,128)(2,1)S(1)}, bf16[320,256]{1,0:T(8,128)(2,1)S(1)}, bf16[320,256]{1,0:T(8,128)(2,1)S(1)}, bf16[320,256]{1,0:T(8,128)(2,1)S(1)}, bf16[512,256]{1,0:T(8,128)(2,1)S(1)}) custom-call(s32[1]{0:T(128)} %bitcast.10.refs_0_, bf16[256,1024]{1,0:T(8,128)(2,1)} %collective-permute-done.5.refs_1_, bf16[8192,512]{1,0:T(8,128)(2,1)} %refs_3_.3, ...), custom_call_target="tpu_custom_call" | custom-call | flops 1 | bytes 1 | tf_op jit(solution)/shard_map/project/pallas_call | solution.py:164
  49.2 2.7 %collective-permute-start.9 = (bf16[512,256]{1,0:T(8,128)(2,1)S(1)}, bf16[512,256]{1,0:T(8,128)(2,1)S(1)}, u32[]{:S(2)}, u32[]{:S(2)}) collective-permute-start(bf16[512,256]{1,0:T(8,128)(2,1)S(1)} %get-tuple-element.73), channel_id=1, source_target_pairs={{0,64},{8,72},{16,80},{24,88},{32,96},{40,104},{48,112},{56,120},{... | collective-permute-start | bytes 786440 | tf_op jit(solution)/shard_map/ppermute | solution.py:43
  51.9 0.1 pad_add_fusion.3.refs_0_
  52.0 2.7 %collective-permute-done.12.refs_1_ = bf16[256,1024]{1,0:T(8,128)(2,1)} collective-permute-done((bf16[256,1024]{1,0:T(8,128)(2,1)S(1)}, bf16[256,1024]{1,0:T(8,128)(2,1)}, u32[]{:S(2)}, u32[]{:S(2)}) %collective-permute-start.12) | collective-permute-done | bytes 524320 | tf_op jit(solution)/shard_map/ppermute | solution.py:29
  54.7 4.6 %project.9.refs_7_ = f32[256,768]{1,0:T(8,128)S(1)} custom-call(s32[3]{0:T(128)S(1)} %pad_add_fusion.3.refs_0_, bf16[256,1024]{1,0:T(8,128)(2,1)S(1)} %bitcast.28, bf16[256,1024]{1,0:T(8,128)(2,1)} %collective-permute-done.6.refs_2_, bf16[256,1024]{1,0:T(8,128)(2,1)} %collective-permute-done.7.refs_3_, bf16[8192,512]{1,0:T(8,128)(2,1)} %refs_3_.3, ...), custom_call_target="tpu_custom_call" | custom-call | flops 1 | bytes 1 | tf_op jit(solution)/shard_map/project/pallas_call | solution.py:164
  59.4 1.2 collective-permute-done.9
  60.6 1.7 %collective-permute-start.15 = (bf16[256,1024]{1,0:T(8,128)(2,1)S(1)}, bf16[256,1024]{1,0:T(8,128)(2,1)S(1)}, u32[]{:S(2)}, u32[]{:S(2)}) collective-permute-start(bf16[256,1024]{1,0:T(8,128)(2,1)S(1)} %collective-permute-done.11.refs_3_), channel_id=1, source_target_pairs={{0,6},{1,7},{2,0},{3,1},{4,2},{5,3},{6,4},{7,5},{8,14},{9,15},{10,... | collective-permute-start | bytes 1572872 | tf_op jit(solution)/shard_map/ppermute | solution.py:29
  62.5 1.9 %collective-permute-start.13 = (bf16[640,256]{1,0:T(8,128)(2,1)S(1)}, bf16[640,256]{1,0:T(8,128)(2,1)S(1)}, u32[]{:S(2)}, u32[]{:S(2)}) collective-permute-start(bf16[640,256]{1,0:T(8,128)(2,1)S(1)} %get-tuple-element.82), channel_id=1, source_target_pairs={{0,16},{8,24},{16,32},{24,40},{32,48},{40,56},{48,0},{56,8},{64,80... | collective-permute-start | bytes 983048 | tf_op jit(solution)/shard_map/ppermute | solution.py:43
  64.4 3.3 %collective-permute-start.17 = (bf16[640,256]{1,0:T(8,128)(2,1)S(1)}, bf16[640,256]{1,0:T(8,128)(2,1)S(1)}, u32[]{:S(2)}, u32[]{:S(2)}) collective-permute-start(bf16[640,256]{1,0:T(8,128)(2,1)S(1)} %get-tuple-element.95), channel_id=1, source_target_pairs={{0,32},{8,40},{16,48},{24,56},{32,0},{40,8},{48,16},{56,24},{64,96... | collective-permute-start | bytes 983048 | tf_op jit(solution)/shard_map/ppermute | solution.py:43
  67.7 0.7 collective-permute-start.18
  68.6 4.6 %project.10.refs_6_ = f32[256,768]{1,0:T(8,128)S(1)} custom-call(s32[3]{0:T(128)S(1)} %add_add_fusion.1.refs_0_, bf16[256,1024]{1,0:T(8,128)(2,1)} %collective-permute-done.12.refs_1_, bf16[256,1024]{1,0:T(8,128)(2,1)} %collective-permute-done.10.refs_2_, bf16[256,1024]{1,0:T(8,128)(2,1)S(1)} %collective-permute-done.11.refs_3_, bf16[8192,512]{1,0:T(8,128)(2,1)} %refs_3_.3, ...), custom_call_target="tpu_custom_call" | custom-call | flops 1 | bytes 1 | tf_op jit(solution)/shard_map/project/pallas_call | solution.py:164
  73.3 3.3 %project.11 = (bf16[320,256]{1,0:T(8,128)(2,1)S(1)}, bf16[320,256]{1,0:T(8,128)(2,1)S(1)}, bf16[320,256]{1,0:T(8,128)(2,1)S(1)}, bf16[320,256]{1,0:T(8,128)(2,1)...) custom-call(s32[2]{0:T(128)S(1)} %pad_add_fusion.4.refs_0_, ...), custom_call_target="tpu_custom_call" | custom-call | flops 1 | bytes 1 | tf_op jit(solution)/shard_map/project/pallas_call | solution.py:164
  76.6 3.0 %collective-permute-start.16 = (bf16[320,256]{1,0:T(8,128)(2,1)S(1)}, bf16[320,256]{1,0:T(8,128)(2,1)S(1)}, u32[]{:S(2)}, u32[]{:S(2)}) collective-permute-start(bf16[320,256]{1,0:T(8,128)(2,1)S(1)} %get-tuple-element.89), channel_id=1, source_target_pairs={{0,64},{8,72},{16,80},{24,88},{32,96},{40,104},{48,112},{56,120},{... | collective-permute-start | bytes 491528 | tf_op jit(solution)/shard_map/ppermute | solution.py:43
  79.6 0.5 collective-permute-start.23
  80.1 3.0 %collective-permute-start.24 = (bf16[320,256]{1,0:T(8,128)(2,1)S(1)}, bf16[320,256]{1,0:T(8,128)(2,1)S(1)}, u32[]{:S(2)}, u32[]{:S(2)}) collective-permute-start(bf16[320,256]{1,0:T(8,128)(2,1)S(1)} %get-tuple-element.103), channel_id=1, source_target_pairs={{0,96},{8,104},{16,112},{24,120},{32,64},{40,72},{48,80},{56,88},{... | collective-permute-start | bytes 491528 | tf_op jit(solution)/shard_map/ppermute | solution.py:43
  83.2 2.0 %collective-permute-start.25 = (bf16[320,256]{1,0:T(8,128)(2,1)S(1)}, bf16[320,256]{1,0:T(8,128)(2,1)S(1)}, u32[]{:S(2)}, u32[]{:S(2)}) collective-permute-start(bf16[320,256]{1,0:T(8,128)(2,1)S(1)} %get-tuple-element.104), channel_id=1, source_target_pairs={{0,112},{8,120},{16,64},{24,72},{32,80},{40,88},{48,96},{56,104},{... | collective-permute-start | bytes 491528 | tf_op jit(solution)/shard_map/ppermute | solution.py:43
  85.2 0.1 pad_maximum_fusion
  85.3 0.6 copy-done.12
  85.9 6.8 %collective-permute-start.19 = (bf16[2560,256]{1,0:T(8,128)(2,1)S(1)}, bf16[2560,256]{1,0:T(8,128)(2,1)S(1)}, u32[]{:S(2)}, u32[]{:S(2)}) collective-permute-start(bf16[2560,256]{1,0:T(8,128)(2,1)S(1)} %pad_maximum_fusion), channel_id=1, source_target_pairs={{0,8},{8,0},{16,24},{24,16},{32,40},{40,32},{48,56},{56,48},{64,72... | collective-permute-start | bytes 3932168 | tf_op jit(solution)/shard_map/ppermute | solution.py:55
  92.7 0.2 collective-permute-start.20
  92.9 2.4 %collective-permute-start.21 = (bf16[320,256]{1,0:T(8,128)(2,1)S(1)}, bf16[320,256]{1,0:T(8,128)(2,1)S(1)}, u32[]{:S(2)}, u32[]{:S(2)}) collective-permute-start(bf16[320,256]{1,0:T(8,128)(2,1)S(1)} %get-tuple-element.99), channel_id=1, source_target_pairs={{0,32},{8,40},{16,48},{24,56},{32,0},{40,8},{48,16},{56,24},{64,96... | collective-permute-start | bytes 491528 | tf_op jit(solution)/shard_map/ppermute | solution.py:43
  95.3 1.9 %collective-permute-start.22 = (bf16[320,256]{1,0:T(8,128)(2,1)S(1)}, bf16[320,256]{1,0:T(8,128)(2,1)S(1)}, u32[]{:S(2)}, u32[]{:S(2)}) collective-permute-start(bf16[320,256]{1,0:T(8,128)(2,1)S(1)} %get-tuple-element.100), channel_id=1, source_target_pairs={{0,48},{8,56},{16,0},{24,8},{32,16},{40,24},{48,32},{56,40},{64,11... | collective-permute-start | bytes 491528 | tf_op jit(solution)/shard_map/ppermute | solution.py:43
  97.2 1.4 %collective-permute-start.27 = (bf16[1280,256]{1,0:T(8,128)(2,1)S(1)}, bf16[1280,256]{1,0:T(8,128)(2,1)S(1)}, u32[]{:S(2)}, u32[]{:S(2)}) collective-permute-start(bf16[1280,256]{1,0:T(8,128)(2,1)S(1)} %pad_maximum_fusion.2), channel_id=1, source_target_pairs={{0,8},{8,0},{16,24},{24,16},{32,40},{40,32},{48,56},{56,48},{64,72... | collective-permute-start | bytes 1966088 | tf_op jit(solution)/shard_map/ppermute | solution.py:55
  98.7 1.2 collective-permute-done.20.refs_6_
  99.8 3.2 %collective-permute-done.21.refs_7_ = bf16[320,256]{1,0:T(8,128)(2,1)S(1)} collective-permute-done((bf16[320,256]{1,0:T(8,128)(2,1)S(1)}, bf16[320,256]{1,0:T(8,128)(2,1)S(1)}, u32[]{:S(2)}, u32[]{:S(2)}) %collective-permute-start.21) | collective-permute-done | bytes 163872 | tf_op jit(solution)/shard_map/ppermute | solution.py:43
  103.1 0.4 collective-permute-done.22.refs_8_
  103.6 1.3 collective-permute-start.26
  104.8 1.7 %collective-permute-done.26.refs_13_ = bf16[1280,256]{1,0:T(8,128)(2,1)S(1)} collective-permute-done((bf16[1280,256]{1,0:T(8,128)(2,1)S(1)}, bf16[1280,256]{1,0:T(8,128)(2,1)S(1)}, u32[]{:S(2)}, u32[]{:S(2)}) %collective-permute-start.26) | collective-permute-done | bytes 655392 | tf_op jit(solution)/shard_map/ppermute | solution.py:55
  106.6 0.8 copy-done.22
  107.4 1.1 copy-done.13
  108.5 20.0 %attend.1 = bf16[512,512]{1,0:T(8,128)(2,1)} custom-call(s32[19]{0:T(128)} %pad_add_fusion.1.info, s32[256]{0:T(256)} %reshape.65.old_map, bf16[640,256]{1,0:T(8,128)(2,1)} %copy-done.9, bf16[640,256]{1,0:T(8,128)(2,1)} %copy-done.10, bf16[640,256]{1,0:T(8,128)(2,1)} %copy-done.11, bf16[640,256]{1,0:T(8,128)(2,1)} %copy-done.12, ...), custom_call_target="tpu_custom_call" | custom-call | tf_op jit(solution)/shard_map/attend/pallas_call | solution.py:244
  (83 shorter events, 0.8 us)
Async XLA Ops:
  0.0 6.2 %copy-start.24 = (s32[16,16]{1,0:T(8,128)S(1)}, s32[16,16]{1,0:T(8,128)}, u32[]{:S(2)}) copy-start(s32[16,16]{1,0:T(8,128)} %param.8) | copy-start | bytes 3076
  0.0 11.6 %copy-start.23 = (s32[16,16]{1,0:T(8,128)S(1)}, s32[16,16]{1,0:T(8,128)}, u32[]{:S(2)}) copy-start(s32[16,16]{1,0:T(8,128)} %param.7) | copy-start | bytes 3076
  1.3 19.9 %copy-start.3 = (bf16[16,1,16,1024]{3,2,1,0:T(8,128)(2,1)}, bf16[16,1,16,1024]{3,2,1,0:T(8,128)(2,1)S(1)}, u32[]{:S(2)}) copy-start(bf16[16,1,16,1024]{3,2,1,0:T(8,128)(2,1)S(1)} %get-tuple-element.107) | copy-start | bytes 1572868
  1.3 20.0 %copy-start = (bf16[8192,128]{1,0:T(8,128)(2,1)S(1)}, bf16[8192,128]{1,0:T(8,128)(2,1)}, u32[]{:S(2)}) copy-start(bf16[8192,128]{1,0:T(8,128)(2,1)} %refs_4_.9) | copy-start | bytes 6291460
  1.3 15.1 %collective-permute-start = (bf16[256,1024]{1,0:T(8,128)(2,1)S(1)}, bf16[256,1024]{1,0:T(8,128)(2,1)}, u32[]{:S(2)}, u32[]{:S(2)}) collective-permute-start(bf16[256,1024]{1,0:T(8,128)(2,1)S(1)} %bitcast.29), channel_id=1, source_target_pairs={{0,2},{1,3},{2,4},{3,5},{4,6},{5,7},{6,0},{7,1},{8,10},{9,11},{10,... | collective-permute-start | bytes 1572872 | tf_op jit(solution)/shard_map/ppermute | solution.py:29
  3.4 12.9 %collective-permute-start.1 = (bf16[256,1024]{1,0:T(8,128)(2,1)S(1)}, bf16[256,1024]{1,0:T(8,128)(2,1)}, u32[]{:S(2)}, u32[]{:S(2)}) collective-permute-start(bf16[256,1024]{1,0:T(8,128)(2,1)S(1)} %bitcast.30), channel_id=1, source_target_pairs={{0,6},{1,7},{2,0},{3,1},{4,2},{5,3},{6,4},{7,5},{8,14},{9,15},{10,... | collective-permute-start | bytes 1572872 | tf_op jit(solution)/shard_map/ppermute | solution.py:29
  4.8 12.3 %collective-permute-start.2 = (bf16[256,1024]{1,0:T(8,128)(2,1)S(1)}, bf16[256,1024]{1,0:T(8,128)(2,1)}, u32[]{:S(2)}, u32[]{:S(2)}) collective-permute-start(bf16[256,1024]{1,0:T(8,128)(2,1)S(1)} %bitcast.31), channel_id=1, source_target_pairs={{0,1},{1,0},{2,3},{3,2},{4,5},{5,4},{6,7},{7,6},{8,9},{9,8},{10,11... | collective-permute-start | bytes 1572872 | tf_op jit(solution)/shard_map/ppermute | solution.py:33
  17.1 12.8 %collective-permute-start.3 = (bf16[256,1024]{1,0:T(8,128)(2,1)}, bf16[256,1024]{1,0:T(8,128)(2,1)}, u32[]{:S(2)}, u32[]{:S(2)}) collective-permute-start(bf16[256,1024]{1,0:T(8,128)(2,1)} %collective-permute-done.2.refs_4_), channel_id=1, source_target_pairs={{0,2},{1,3},{2,4},{3,5},{4,6},{5,7},{6,0},{7,1},{8,10},{9,11},{10,... | collective-permute-start | bytes 1572872 | tf_op jit(solution)/shard_map/ppermute | solution.py:29
  17.2 12.6 %collective-permute-start.4 = (bf16[256,1024]{1,0:T(8,128)(2,1)}, bf16[256,1024]{1,0:T(8,128)(2,1)}, u32[]{:S(2)}, u32[]{:S(2)}) collective-permute-start(bf16[256,1024]{1,0:T(8,128)(2,1)} %collective-permute-done.1.refs_3_), channel_id=1, source_target_pairs={{0,6},{1,7},{2,0},{3,1},{4,2},{5,3},{6,4},{7,5},{8,14},{9,15},{10,... | collective-permute-start | bytes 1572872 | tf_op jit(solution)/shard_map/ppermute | solution.py:29
  19.7 12.5 %collective-permute-start.8 = (bf16[256,1024]{1,0:T(8,128)(2,1)}, bf16[256,1024]{1,0:T(8,128)(2,1)}, u32[]{:S(2)}, u32[]{:S(2)}) collective-permute-start(bf16[256,1024]{1,0:T(8,128)(2,1)} %collective-permute-done.1.refs_3_), channel_id=1, source_target_pairs={{0,1},{1,0},{2,3},{3,2},{4,5},{5,4},{6,7},{7,6},{8,9},{9,8},{10,11... | collective-permute-start | bytes 1572872 | tf_op jit(solution)/shard_map/ppermute | solution.py:33
  21.3 20.7 %collective-permute-start.7 = (bf16[256,1024]{1,0:T(8,128)(2,1)S(1)}, bf16[256,1024]{1,0:T(8,128)(2,1)}, u32[]{:S(2)}, u32[]{:S(2)}) collective-permute-start(bf16[256,1024]{1,0:T(8,128)(2,1)S(1)} %bitcast.25), channel_id=1, source_target_pairs={{0,1},{1,0},{2,3},{3,2},{4,5},{5,4},{6,7},{7,6},{8,9},{9,8},{10,11... | collective-permute-start | bytes 1572872 | tf_op jit(solution)/shard_map/ppermute | solution.py:33
  21.3 1.0 copy-start.4
  29.8 12.2 %collective-permute-start.6 = (bf16[256,1024]{1,0:T(8,128)(2,1)S(1)}, bf16[256,1024]{1,0:T(8,128)(2,1)}, u32[]{:S(2)}, u32[]{:S(2)}) collective-permute-start(bf16[256,1024]{1,0:T(8,128)(2,1)S(1)} %bitcast.26), channel_id=1, source_target_pairs={{0,6},{1,7},{2,0},{3,1},{4,2},{5,3},{6,4},{7,5},{8,14},{9,15},{10,... | collective-permute-start | bytes 1572872 | tf_op jit(solution)/shard_map/ppermute | solution.py:29
  32.2 12.8 %collective-permute-start.5 = (bf16[256,1024]{1,0:T(8,128)(2,1)}, bf16[256,1024]{1,0:T(8,128)(2,1)}, u32[]{:S(2)}, u32[]{:S(2)}) collective-permute-start(bf16[256,1024]{1,0:T(8,128)(2,1)} %collective-permute-done.3.refs_1_), channel_id=1, source_target_pairs={{0,2},{1,3},{2,4},{3,5},{4,6},{5,7},{6,0},{7,1},{8,10},{9,11},{10,... | collective-permute-start | bytes 1572872 | tf_op jit(solution)/shard_map/ppermute | solution.py:29
  32.2 22.5 %collective-permute-start.12 = (bf16[256,1024]{1,0:T(8,128)(2,1)S(1)}, bf16[256,1024]{1,0:T(8,128)(2,1)}, u32[]{:S(2)}, u32[]{:S(2)}) collective-permute-start(bf16[256,1024]{1,0:T(8,128)(2,1)S(1)} %bitcast.27), channel_id=1, source_target_pairs={{0,2},{1,3},{2,4},{3,5},{4,6},{5,7},{6,0},{7,1},{8,10},{9,11},{10,... | collective-permute-start | bytes 1572872 | tf_op jit(solution)/shard_map/ppermute | solution.py:29
  37.1 0.9 copy-start.1
  42.0 18.7 %collective-permute-start.10 = (bf16[256,1024]{1,0:T(8,128)(2,1)}, bf16[256,1024]{1,0:T(8,128)(2,1)}, u32[]{:S(2)}, u32[]{:S(2)}) collective-permute-start(bf16[256,1024]{1,0:T(8,128)(2,1)} %collective-permute-done.6.refs_2_), channel_id=1, source_target_pairs={{0,6},{1,7},{2,0},{3,1},{4,2},{5,3},{6,4},{7,5},{8,14},{9,15},{10,... | collective-permute-start | bytes 1572872 | tf_op jit(solution)/shard_map/ppermute | solution.py:29
  43.6 17.1 %collective-permute-start.11 = (bf16[256,1024]{1,0:T(8,128)(2,1)}, bf16[256,1024]{1,0:T(8,128)(2,1)S(1)}, u32[]{:S(2)}, u32[]{:S(2)}) collective-permute-start(bf16[256,1024]{1,0:T(8,128)(2,1)} %collective-permute-done.6.refs_2_), channel_id=1, source_target_pairs={{0,1},{1,0},{2,3},{3,2},{4,5},{5,4},{6,7},{7,6},{8,9},{9,8},{10,11... | collective-permute-start | bytes 1572872 | tf_op jit(solution)/shard_map/ppermute | solution.py:33
  45.0 1.1 copy-start.2
  46.2 0.9 copy-start.6
  49.2 11.3 %collective-permute-start.9 = (bf16[512,256]{1,0:T(8,128)(2,1)S(1)}, bf16[512,256]{1,0:T(8,128)(2,1)S(1)}, u32[]{:S(2)}, u32[]{:S(2)}) collective-permute-start(bf16[512,256]{1,0:T(8,128)(2,1)S(1)} %get-tuple-element.73), channel_id=1, source_target_pairs={{0,64},{8,72},{16,80},{24,88},{32,96},{40,104},{48,112},{56,120},{... | collective-permute-start | bytes 786440 | tf_op jit(solution)/shard_map/ppermute | solution.py:43
  54.7 18.5 %collective-permute-start.14 = (bf16[256,1024]{1,0:T(8,128)(2,1)}, bf16[256,1024]{1,0:T(8,128)(2,1)S(1)}, u32[]{:S(2)}, u32[]{:S(2)}) collective-permute-start(bf16[256,1024]{1,0:T(8,128)(2,1)} %collective-permute-done.7.refs_3_), channel_id=1, source_target_pairs={{0,2},{1,3},{2,4},{3,5},{4,6},{5,7},{6,0},{7,1},{8,10},{9,11},{10,... | collective-permute-start | bytes 1572872 | tf_op jit(solution)/shard_map/ppermute | solution.py:29
  60.6 12.6 %collective-permute-start.15 = (bf16[256,1024]{1,0:T(8,128)(2,1)S(1)}, bf16[256,1024]{1,0:T(8,128)(2,1)S(1)}, u32[]{:S(2)}, u32[]{:S(2)}) collective-permute-start(bf16[256,1024]{1,0:T(8,128)(2,1)S(1)} %collective-permute-done.11.refs_3_), channel_id=1, source_target_pairs={{0,6},{1,7},{2,0},{3,1},{4,2},{5,3},{6,4},{7,5},{8,14},{9,15},{10,... | collective-permute-start | bytes 1572872 | tf_op jit(solution)/shard_map/ppermute | solution.py:29
  62.4 22.8 %copy-start.9 = (bf16[640,256]{1,0:T(8,128)(2,1)}, bf16[640,256]{1,0:T(8,128)(2,1)S(1)}, u32[]{:S(2)}) copy-start(bf16[640,256]{1,0:T(8,128)(2,1)S(1)} %pad_maximum_fusion.6.refs_0_) | copy-start | bytes 983044
  62.5 17.6 %collective-permute-start.13 = (bf16[640,256]{1,0:T(8,128)(2,1)S(1)}, bf16[640,256]{1,0:T(8,128)(2,1)S(1)}, u32[]{:S(2)}, u32[]{:S(2)}) collective-permute-start(bf16[640,256]{1,0:T(8,128)(2,1)S(1)} %get-tuple-element.82), channel_id=1, source_target_pairs={{0,16},{8,24},{16,32},{24,40},{32,48},{40,56},{48,0},{56,8},{64,80... | collective-permute-start | bytes 983048 | tf_op jit(solution)/shard_map/ppermute | solution.py:43
  64.4 18.8 %collective-permute-start.17 = (bf16[640,256]{1,0:T(8,128)(2,1)S(1)}, bf16[640,256]{1,0:T(8,128)(2,1)S(1)}, u32[]{:S(2)}, u32[]{:S(2)}) collective-permute-start(bf16[640,256]{1,0:T(8,128)(2,1)S(1)} %get-tuple-element.95), channel_id=1, source_target_pairs={{0,32},{8,40},{16,48},{24,56},{32,0},{40,8},{48,16},{56,24},{64,96... | collective-permute-start | bytes 983048 | tf_op jit(solution)/shard_map/ppermute | solution.py:43
  67.7 17.5 %collective-permute-start.18 = (bf16[640,256]{1,0:T(8,128)(2,1)S(1)}, bf16[640,256]{1,0:T(8,128)(2,1)S(1)}, u32[]{:S(2)}, u32[]{:S(2)}) collective-permute-start(bf16[640,256]{1,0:T(8,128)(2,1)S(1)} %get-tuple-element.96), channel_id=1, source_target_pairs={{0,48},{8,56},{16,0},{24,8},{32,16},{40,24},{48,32},{56,40},{64,11... | collective-permute-start | bytes 983048 | tf_op jit(solution)/shard_map/ppermute | solution.py:43
  68.6 4.7 %copy-start.7 = (f32[256,128]{1,0:T(8,128)S(1)}, f32[256,128]{1,0:T(8,128)}, u32[]{:S(2)}) copy-start(f32[256,128]{1,0:T(8,128)} %get-tuple-element.87.refs_8_) | copy-start | bytes 393220
  68.6 4.7 %copy-start.8 = (f32[256,128]{1,0:T(8,128)S(1)}, f32[256,128]{1,0:T(8,128)}, u32[]{:S(2)}) copy-start(f32[256,128]{1,0:T(8,128)} %get-tuple-element.88.refs_9_) | copy-start | bytes 393220
  76.6 26.9 %copy-start.5 = (bf16[320,256]{1,0:T(8,128)(2,1)}, bf16[320,256]{1,0:T(8,128)(2,1)S(1)}, u32[]{:S(2)}) copy-start(bf16[320,256]{1,0:T(8,128)(2,1)S(1)} %get-tuple-element.97.refs_5_) | copy-start | bytes 491524
  76.6 16.2 %collective-permute-start.16 = (bf16[320,256]{1,0:T(8,128)(2,1)S(1)}, bf16[320,256]{1,0:T(8,128)(2,1)S(1)}, u32[]{:S(2)}, u32[]{:S(2)}) collective-permute-start(bf16[320,256]{1,0:T(8,128)(2,1)S(1)} %get-tuple-element.89), channel_id=1, source_target_pairs={{0,64},{8,72},{16,80},{24,88},{32,96},{40,104},{48,112},{56,120},{... | collective-permute-start | bytes 491528 | tf_op jit(solution)/shard_map/ppermute | solution.py:43
  79.6 13.3 %collective-permute-start.23 = (bf16[320,256]{1,0:T(8,128)(2,1)S(1)}, bf16[320,256]{1,0:T(8,128)(2,1)S(1)}, u32[]{:S(2)}, u32[]{:S(2)}) collective-permute-start(bf16[320,256]{1,0:T(8,128)(2,1)S(1)} %get-tuple-element.102), channel_id=1, source_target_pairs={{0,80},{8,88},{16,96},{24,104},{32,112},{40,120},{48,64},{56,72},{... | collective-permute-start | bytes 491528 | tf_op jit(solution)/shard_map/ppermute | solution.py:43
  80.1 5.2 %copy-start.10 = (bf16[640,256]{1,0:T(8,128)(2,1)}, bf16[640,256]{1,0:T(8,128)(2,1)S(1)}, u32[]{:S(2)}) copy-start(bf16[640,256]{1,0:T(8,128)(2,1)S(1)} %collective-permute-done.13.refs_1_) | copy-start | bytes 983044
  80.1 15.1 %collective-permute-start.24 = (bf16[320,256]{1,0:T(8,128)(2,1)S(1)}, bf16[320,256]{1,0:T(8,128)(2,1)S(1)}, u32[]{:S(2)}, u32[]{:S(2)}) collective-permute-start(bf16[320,256]{1,0:T(8,128)(2,1)S(1)} %get-tuple-element.103), channel_id=1, source_target_pairs={{0,96},{8,104},{16,112},{24,120},{32,64},{40,72},{48,80},{56,88},{... | collective-permute-start | bytes 491528 | tf_op jit(solution)/shard_map/ppermute | solution.py:43
  83.2 2.1 %copy-start.11 = (bf16[640,256]{1,0:T(8,128)(2,1)}, bf16[640,256]{1,0:T(8,128)(2,1)S(1)}, u32[]{:S(2)}) copy-start(bf16[640,256]{1,0:T(8,128)(2,1)S(1)} %collective-permute-done.17.refs_2_) | copy-start | bytes 983044
  83.2 14.0 %collective-permute-start.25 = (bf16[320,256]{1,0:T(8,128)(2,1)S(1)}, bf16[320,256]{1,0:T(8,128)(2,1)S(1)}, u32[]{:S(2)}, u32[]{:S(2)}) collective-permute-start(bf16[320,256]{1,0:T(8,128)(2,1)S(1)} %get-tuple-element.104), channel_id=1, source_target_pairs={{0,112},{8,120},{16,64},{24,72},{32,80},{40,88},{48,96},{56,104},{... | collective-permute-start | bytes 491528 | tf_op jit(solution)/shard_map/ppermute | solution.py:43
  85.2 0.7 copy-start.12
  85.9 20.6 %collective-permute-start.19 = (bf16[2560,256]{1,0:T(8,128)(2,1)S(1)}, bf16[2560,256]{1,0:T(8,128)(2,1)S(1)}, u32[]{:S(2)}, u32[]{:S(2)}) collective-permute-start(bf16[2560,256]{1,0:T(8,128)(2,1)S(1)} %pad_maximum_fusion), channel_id=1, source_target_pairs={{0,8},{8,0},{16,24},{24,16},{32,40},{40,32},{48,56},{56,48},{64,72... | collective-permute-start | bytes 3932168 | tf_op jit(solution)/shard_map/ppermute | solution.py:55
  92.7 10.8 %copy-start.14 = (bf16[320,256]{1,0:T(8,128)(2,1)}, bf16[320,256]{1,0:T(8,128)(2,1)S(1)}, u32[]{:S(2)}) copy-start(bf16[320,256]{1,0:T(8,128)(2,1)S(1)} %collective-permute-done.16.refs_9_) | copy-start | bytes 491524
  92.7 7.1 %collective-permute-start.20 = (bf16[320,256]{1,0:T(8,128)(2,1)S(1)}, bf16[320,256]{1,0:T(8,128)(2,1)S(1)}, u32[]{:S(2)}, u32[]{:S(2)}) collective-permute-start(bf16[320,256]{1,0:T(8,128)(2,1)S(1)} %get-tuple-element.98), channel_id=1, source_target_pairs={{0,16},{8,24},{16,32},{24,40},{32,48},{40,56},{48,0},{56,8},{64,80... | collective-permute-start | bytes 491528 | tf_op jit(solution)/shard_map/ppermute | solution.py:43
  92.9 10.6 %copy-start.15 = (bf16[320,256]{1,0:T(8,128)(2,1)}, bf16[320,256]{1,0:T(8,128)(2,1)S(1)}, u32[]{:S(2)}) copy-start(bf16[320,256]{1,0:T(8,128)(2,1)S(1)} %collective-permute-done.23.refs_10_) | copy-start | bytes 491524
  92.9 10.2 %collective-permute-start.21 = (bf16[320,256]{1,0:T(8,128)(2,1)S(1)}, bf16[320,256]{1,0:T(8,128)(2,1)S(1)}, u32[]{:S(2)}, u32[]{:S(2)}) collective-permute-start(bf16[320,256]{1,0:T(8,128)(2,1)S(1)} %get-tuple-element.99), channel_id=1, source_target_pairs={{0,32},{8,40},{16,48},{24,56},{32,0},{40,8},{48,16},{56,24},{64,96... | collective-permute-start | bytes 491528 | tf_op jit(solution)/shard_map/ppermute | solution.py:43
  95.3 8.3 %copy-start.16 = (bf16[320,256]{1,0:T(8,128)(2,1)}, bf16[320,256]{1,0:T(8,128)(2,1)S(1)}, u32[]{:S(2)}) copy-start(bf16[320,256]{1,0:T(8,128)(2,1)S(1)} %collective-permute-done.24.refs_11_) | copy-start | bytes 491524
  95.3 8.2 %collective-permute-start.22 = (bf16[320,256]{1,0:T(8,128)(2,1)S(1)}, bf16[320,256]{1,0:T(8,128)(2,1)S(1)}, u32[]{:S(2)}, u32[]{:S(2)}) collective-permute-start(bf16[320,256]{1,0:T(8,128)(2,1)S(1)} %get-tuple-element.100), channel_id=1, source_target_pairs={{0,48},{8,56},{16,0},{24,8},{32,16},{40,24},{48,32},{56,40},{64,11... | collective-permute-start | bytes 491528 | tf_op jit(solution)/shard_map/ppermute | solution.py:43
  97.2 6.4 %copy-start.17 = (bf16[320,256]{1,0:T(8,128)(2,1)}, bf16[320,256]{1,0:T(8,128)(2,1)S(1)}, u32[]{:S(2)}) copy-start(bf16[320,256]{1,0:T(8,128)(2,1)S(1)} %collective-permute-done.25.refs_12_) | copy-start | bytes 491524
  97.2 7.6 %collective-permute-start.27 = (bf16[1280,256]{1,0:T(8,128)(2,1)S(1)}, bf16[1280,256]{1,0:T(8,128)(2,1)S(1)}, u32[]{:S(2)}, u32[]{:S(2)}) collective-permute-start(bf16[1280,256]{1,0:T(8,128)(2,1)S(1)} %pad_maximum_fusion.2), channel_id=1, source_target_pairs={{0,8},{8,0},{16,24},{24,16},{32,40},{40,32},{48,56},{56,48},{64,72... | collective-permute-start | bytes 1966088 | tf_op jit(solution)/shard_map/ppermute | solution.py:55
  99.8 6.7 %copy-start.18 = (bf16[320,256]{1,0:T(8,128)(2,1)}, bf16[320,256]{1,0:T(8,128)(2,1)S(1)}, u32[]{:S(2)}) copy-start(bf16[320,256]{1,0:T(8,128)(2,1)S(1)} %collective-permute-done.20.refs_6_) | copy-start | bytes 491524
  103.1 3.5 %copy-start.19 = (bf16[320,256]{1,0:T(8,128)(2,1)}, bf16[320,256]{1,0:T(8,128)(2,1)S(1)}, u32[]{:S(2)}) copy-start(bf16[320,256]{1,0:T(8,128)(2,1)S(1)} %collective-permute-done.21.refs_7_) | copy-start | bytes 491524
  103.5 3.1 %copy-start.20 = (bf16[320,256]{1,0:T(8,128)(2,1)}, bf16[320,256]{1,0:T(8,128)(2,1)S(1)}, u32[]{:S(2)}) copy-start(bf16[320,256]{1,0:T(8,128)(2,1)S(1)} %collective-permute-done.22.refs_8_) | copy-start | bytes 491524
  103.6 3.0 %collective-permute-start.26 = (bf16[1280,256]{1,0:T(8,128)(2,1)S(1)}, bf16[1280,256]{1,0:T(8,128)(2,1)S(1)}, u32[]{:S(2)}, u32[]{:S(2)}) collective-permute-start(bf16[1280,256]{1,0:T(8,128)(2,1)S(1)} %pad_maximum_fusion.1), channel_id=1, source_target_pairs={{0,8},{8,0},{16,24},{24,16},{32,40},{40,32},{48,56},{56,48},{64,72... | collective-permute-start | bytes 1966088 | tf_op jit(solution)/shard_map/ppermute | solution.py:55
  104.8 1.7 %copy-start.21 = (bf16[1280,256]{1,0:T(8,128)(2,1)}, bf16[1280,256]{1,0:T(8,128)(2,1)S(1)}, u32[]{:S(2)}) copy-start(bf16[1280,256]{1,0:T(8,128)(2,1)S(1)} %collective-permute-done.27.refs_14_) | copy-start | bytes 1966084
  106.6 0.8 copy-start.22
  107.4 1.1 copy-start.13

commit v10 on v9

--- a/solution.py
+++ b/solution.py
@@ -253,7 +253,7 @@
             pltpu.VMEM((1024, HEAD), jnp.float32),
             pltpu.VMEM((1024, HEAD), jnp.float32),
         ],
-        compiler_params=pltpu.CompilerParams(vmem_limit_bytes=56 * 2**20),
+        compiler_params=pltpu.CompilerParams(vmem_limit_bytes=62 * 2**20),
         name="attend",
     )(info, old_map, *parts)
 

time: 129 us -> 127 us (0.984)
  local copies, waits for them, and re-layouts: 9.26 us -> 7.44 us
    unnamed x50 -> x44, local copies, waits for them, and re-layouts: 6.55 us -> 4.67 us
  transfers between devices with their start and end apart: 28 -> 28, of which waited for: 9 -> 9; matrix products, arithmetic and copies ran while one was open for 5% -> 5% of each run, Pallas kernels for 19% -> 20%
where the time goes in v10:
time: 127 us
  starting transfers between devices  47.4 us (37%)
  Pallas kernels  45 us (35%)
  waiting for transfers between devices  16.8 us (13%)
  local copies, waits for them, and re-layouts  7.44 us (6%)
  between operations  5.42 us (4%)
  other arithmetic  4.59 us (4%)
    pallas_call x6, Pallas kernels, project(): pl.pallas_call(functools.partial(project_kernel, groups, acc is not None,...  25 us
    ppermute x11, starting transfers between devices, shift_ctx(): return lax.ppermute(block, 'ctx', perm)  21.7 us
    pallas_call x1, Pallas kernels, attend(): pl.pallas_call(attend_kernel, out_shape=jax.ShapeDtypeStruct((512, 512),...  20 us
    ppermute x10, starting transfers between devices, shift_x(): return lax.ppermute(block, 'tp', perm)  11.8 us
    ppermute x3, starting transfers between devices, swap_core(): return lax.ppermute(block, 'ctx', [(i, i ^ 1) for i in range(16)])  9.47 us
    ppermute x11, waiting for transfers between devices, shift_ctx(): return lax.ppermute(block, 'ctx', perm)  6.05 us
    unnamed x44, local copies, waits for them, and re-layouts  4.67 us
    ppermute x10, waiting for transfers between devices, shift_x(): return lax.ppermute(block, 'tp', perm)  4.65 us
  transfers between devices with their start and end apart: 28, of which 9 were waited for; matrix products, arithmetic and copies ran while one was open for 5% of the time, Pallas kernels for 20%

profile of v10, /device:TPU:1, one launch (start us, length us, event | category | flops | bytes accessed | tf_op | source)
XLA Modules:
  0.0 126.7 jit_solution(4056716164326403399)
XLA Ops:
  0.0 1.3 %fusion.5 = (bf16[16,1,16,1024]{3,2,1,0:T(8,128)(2,1)S(1)}, bf16[16,1,16,1024]{3,2,1,0:T(8,128)(2,1)S(1)}) fusion(bf16[16,2,16,1024]{3,2,1,0:T(8,128)(2,1)} %bitcast.33), kind=kLoop, calls=%fused_computation.38 | loop fusion | bytes 2097152 | tf_op jit(solution)/shard_map/slice | solution.py:296
  1.3 2.1 %collective-permute-start = (bf16[256,1024]{1,0:T(8,128)(2,1)S(1)}, bf16[256,1024]{1,0:T(8,128)(2,1)}, u32[]{:S(2)}, u32[]{:S(2)}) collective-permute-start(bf16[256,1024]{1,0:T(8,128)(2,1)S(1)} %bitcast.29), channel_id=1, source_target_pairs={{0,2},{1,3},{2,4},{3,5},{4,6},{5,7},{6,0},{7,1},{8,10},{9,11},{10,... | collective-permute-start | bytes 1572872 | tf_op jit(solution)/shard_map/ppermute | solution.py:29
  3.4 1.4 %collective-permute-start.1 = (bf16[256,1024]{1,0:T(8,128)(2,1)S(1)}, bf16[256,1024]{1,0:T(8,128)(2,1)}, u32[]{:S(2)}, u32[]{:S(2)}) collective-permute-start(bf16[256,1024]{1,0:T(8,128)(2,1)S(1)} %bitcast.30), channel_id=1, source_target_pairs={{0,6},{1,7},{2,0},{3,1},{4,2},{5,3},{6,4},{7,5},{8,14},{9,15},{10,... | collective-permute-start | bytes 1572872 | tf_op jit(solution)/shard_map/ppermute | solution.py:29
  4.8 1.4 %collective-permute-start.2 = (bf16[256,1024]{1,0:T(8,128)(2,1)S(1)}, bf16[256,1024]{1,0:T(8,128)(2,1)}, u32[]{:S(2)}, u32[]{:S(2)}) collective-permute-start(bf16[256,1024]{1,0:T(8,128)(2,1)S(1)} %bitcast.31), channel_id=1, source_target_pairs={{0,1},{1,0},{2,3},{3,2},{4,5},{5,4},{6,7},{7,6},{8,9},{9,8},{10,11... | collective-permute-start | bytes 1572872 | tf_op jit(solution)/shard_map/ppermute | solution.py:33
  6.2 0.6 fusion.7
  11.9 0.1 compare_reduce_fusion.1
  12.0 0.1 select_reduce_fusion.1
  12.1 0.1 compare_reduce_fusion
  12.3 0.1 select_reduce_fusion
  12.6 0.1 pad_add_fusion.refs_6_.refs_7_
  12.6 0.6 pad_add_fusion.1.info
  13.2 0.7 reshape.65.old_map
  13.9 0.1 convert_element_type.25
  13.9 0.1 convert_element_type.23
  14.0 1.0 fusion.4
  15.0 0.8 pad_maximum_fusion.7
  15.8 0.9 pad_maximum_fusion.9
  16.7 0.4 collective-permute-done.2.refs_4_
  17.1 0.2 collective-permute-start.3
  17.2 2.5 %collective-permute-start.4 = (bf16[256,1024]{1,0:T(8,128)(2,1)}, bf16[256,1024]{1,0:T(8,128)(2,1)}, u32[]{:S(2)}, u32[]{:S(2)}) collective-permute-start(bf16[256,1024]{1,0:T(8,128)(2,1)} %collective-permute-done.1.refs_3_), channel_id=1, source_target_pairs={{0,6},{1,7},{2,0},{3,1},{4,2},{5,3},{6,4},{7,5},{8,14},{9,15},{10,... | collective-permute-start | bytes 1572872 | tf_op jit(solution)/shard_map/ppermute | solution.py:29
  19.7 1.4 %collective-permute-start.8 = (bf16[256,1024]{1,0:T(8,128)(2,1)}, bf16[256,1024]{1,0:T(8,128)(2,1)}, u32[]{:S(2)}, u32[]{:S(2)}) collective-permute-start(bf16[256,1024]{1,0:T(8,128)(2,1)} %collective-permute-done.1.refs_3_), channel_id=1, source_target_pairs={{0,1},{1,0},{2,3},{3,2},{4,5},{5,4},{6,7},{7,6},{8,9},{9,8},{10,11... | collective-permute-start | bytes 1572872 | tf_op jit(solution)/shard_map/ppermute | solution.py:33
  21.2 0.1 pad_add_fusion.2.refs_0_
  21.3 1.0 copy-done.4
  22.3 5.5 %project.6.refs_7_ = f32[256,768]{1,0:T(8,128)S(1)} custom-call(s32[4]{0:T(128)S(1)} %pad_add_fusion.2.refs_0_, bf16[256,1024]{1,0:T(8,128)(2,1)S(1)} %bitcast.32, bf16[256,1024]{1,0:T(8,128)(2,1)} %collective-permute-done.refs_2_, bf16[256,1024]{1,0:T(8,128)(2,1)} %collective-permute-done.1.refs_3_, bf16[256,1024]{1,0:T(8,128)(2,1)} %collective-permute-done.2.refs_4_, ...), custom_call_target="tpu_custom_call" | custom-call | flops 1 | bytes 1 | tf_op jit(solution)/shard_map/project/pallas_call | solution.py:164
  27.9 1.9 %collective-permute-done.3.refs_1_ = bf16[256,1024]{1,0:T(8,128)(2,1)} collective-permute-done((bf16[256,1024]{1,0:T(8,128)(2,1)}, bf16[256,1024]{1,0:T(8,128)(2,1)}, u32[]{:S(2)}, u32[]{:S(2)}) %collective-permute-start.3) | collective-permute-done | bytes 524320 | tf_op jit(solution)/shard_map/ppermute | solution.py:29
  29.8 2.4 %collective-permute-start.6 = (bf16[256,1024]{1,0:T(8,128)(2,1)S(1)}, bf16[256,1024]{1,0:T(8,128)(2,1)}, u32[]{:S(2)}, u32[]{:S(2)}) collective-permute-start(bf16[256,1024]{1,0:T(8,128)(2,1)S(1)} %bitcast.26), channel_id=1, source_target_pairs={{0,6},{1,7},{2,0},{3,1},{4,2},{5,3},{6,4},{7,5},{8,14},{9,15},{10,... | collective-permute-start | bytes 1572872 | tf_op jit(solution)/shard_map/ppermute | solution.py:29
  32.3 0.1 add_add_fusion.refs_0_
  32.3 4.8 %project.7.refs_5_ = f32[256,768]{1,0:T(8,128)S(1)} custom-call(s32[3]{0:T(128)S(1)} %add_add_fusion.refs_0_, bf16[256,1024]{1,0:T(8,128)(2,1)} %collective-permute-done.3.refs_1_, bf16[256,1024]{1,0:T(8,128)(2,1)} %collective-permute-done.4.refs_2_, bf16[256,1024]{1,0:T(8,128)(2,1)} %collective-permute-done.8.refs_3_, bf16[8192,512]{1,0:T(8,128)(2,1)} %refs_3_.3, ...), custom_call_target="tpu_custom_call" | custom-call | flops 1 | bytes 1 | tf_op jit(solution)/shard_map/project/pallas_call | solution.py:164
  37.2 0.9 copy-done.1
  38.0 3.9 %collective-permute-done.7.refs_3_ = bf16[256,1024]{1,0:T(8,128)(2,1)} collective-permute-done((bf16[256,1024]{1,0:T(8,128)(2,1)S(1)}, bf16[256,1024]{1,0:T(8,128)(2,1)}, u32[]{:S(2)}, u32[]{:S(2)}) %collective-permute-start.7) | collective-permute-done | bytes 524320 | tf_op jit(solution)/shard_map/ppermute | solution.py:33
  42.0 1.6 %collective-permute-start.10 = (bf16[256,1024]{1,0:T(8,128)(2,1)}, bf16[256,1024]{1,0:T(8,128)(2,1)}, u32[]{:S(2)}, u32[]{:S(2)}) collective-permute-start(bf16[256,1024]{1,0:T(8,128)(2,1)} %collective-permute-done.6.refs_2_), channel_id=1, source_target_pairs={{0,6},{1,7},{2,0},{3,1},{4,2},{5,3},{6,4},{7,5},{8,14},{9,15},{10,... | collective-permute-start | bytes 1572872 | tf_op jit(solution)/shard_map/ppermute | solution.py:29
  43.6 1.5 %collective-permute-start.11 = (bf16[256,1024]{1,0:T(8,128)(2,1)}, bf16[256,1024]{1,0:T(8,128)(2,1)S(1)}, u32[]{:S(2)}, u32[]{:S(2)}) collective-permute-start(bf16[256,1024]{1,0:T(8,128)(2,1)} %collective-permute-done.6.refs_2_), channel_id=1, source_target_pairs={{0,1},{1,0},{2,3},{3,2},{4,5},{5,4},{6,7},{7,6},{8,9},{9,8},{10,11... | collective-permute-start | bytes 1572872 | tf_op jit(solution)/shard_map/ppermute | solution.py:33
  45.1 1.1 copy-done.2
  46.2 0.9 copy-done.6
  47.1 2.1 %project.8 = (bf16[320,256]{1,0:T(8,128)(2,1)S(1)}, bf16[320,256]{1,0:T(8,128)(2,1)S(1)}, bf16[320,256]{1,0:T(8,128)(2,1)S(1)}, bf16[320,256]{1,0:T(8,128)(2,1)S(1)}, bf16[512,256]{1,0:T(8,128)(2,1)S(1)}) custom-call(s32[1]{0:T(128)} %bitcast.10.refs_0_, bf16[256,1024]{1,0:T(8,128)(2,1)} %collective-permute-done.5.refs_1_, bf16[8192,512]{1,0:T(8,128)(2,1)} %refs_3_.3, ...), custom_call_target="tpu_custom_call" | custom-call | flops 1 | bytes 1 | tf_op jit(solution)/shard_map/project/pallas_call | solution.py:164
  49.2 2.7 %collective-permute-start.9 = (bf16[512,256]{1,0:T(8,128)(2,1)S(1)}, bf16[512,256]{1,0:T(8,128)(2,1)S(1)}, u32[]{:S(2)}, u32[]{:S(2)}) collective-permute-start(bf16[512,256]{1,0:T(8,128)(2,1)S(1)} %get-tuple-element.73), channel_id=1, source_target_pairs={{0,64},{8,72},{16,80},{24,88},{32,96},{40,104},{48,112},{56,120},{... | collective-permute-start | bytes 786440 | tf_op jit(solution)/shard_map/ppermute | solution.py:43
  51.9 0.1 pad_add_fusion.3.refs_0_
  52.0 2.7 %collective-permute-done.12.refs_1_ = bf16[256,1024]{1,0:T(8,128)(2,1)} collective-permute-done((bf16[256,1024]{1,0:T(8,128)(2,1)S(1)}, bf16[256,1024]{1,0:T(8,128)(2,1)}, u32[]{:S(2)}, u32[]{:S(2)}) %collective-permute-start.12) | collective-permute-done | bytes 524320 | tf_op jit(solution)/shard_map/ppermute | solution.py:29
  54.7 4.6 %project.9.refs_7_ = f32[256,768]{1,0:T(8,128)S(1)} custom-call(s32[3]{0:T(128)S(1)} %pad_add_fusion.3.refs_0_, bf16[256,1024]{1,0:T(8,128)(2,1)S(1)} %bitcast.28, bf16[256,1024]{1,0:T(8,128)(2,1)} %collective-permute-done.6.refs_2_, bf16[256,1024]{1,0:T(8,128)(2,1)} %collective-permute-done.7.refs_3_, bf16[8192,512]{1,0:T(8,128)(2,1)} %refs_3_.3, ...), custom_call_target="tpu_custom_call" | custom-call | flops 1 | bytes 1 | tf_op jit(solution)/shard_map/project/pallas_call | solution.py:164
  59.4 1.2 collective-permute-done.9
  60.6 1.7 %collective-permute-start.15 = (bf16[256,1024]{1,0:T(8,128)(2,1)S(1)}, bf16[256,1024]{1,0:T(8,128)(2,1)S(1)}, u32[]{:S(2)}, u32[]{:S(2)}) collective-permute-start(bf16[256,1024]{1,0:T(8,128)(2,1)S(1)} %collective-permute-done.11.refs_3_), channel_id=1, source_target_pairs={{0,6},{1,7},{2,0},{3,1},{4,2},{5,3},{6,4},{7,5},{8,14},{9,15},{10,... | collective-permute-start | bytes 1572872 | tf_op jit(solution)/shard_map/ppermute | solution.py:29
  62.5 1.9 %collective-permute-start.13 = (bf16[640,256]{1,0:T(8,128)(2,1)S(1)}, bf16[640,256]{1,0:T(8,128)(2,1)S(1)}, u32[]{:S(2)}, u32[]{:S(2)}) collective-permute-start(bf16[640,256]{1,0:T(8,128)(2,1)S(1)} %get-tuple-element.82), channel_id=1, source_target_pairs={{0,16},{8,24},{16,32},{24,40},{32,48},{40,56},{48,0},{56,8},{64,80... | collective-permute-start | bytes 983048 | tf_op jit(solution)/shard_map/ppermute | solution.py:43
  64.4 3.3 %collective-permute-start.17 = (bf16[640,256]{1,0:T(8,128)(2,1)S(1)}, bf16[640,256]{1,0:T(8,128)(2,1)S(1)}, u32[]{:S(2)}, u32[]{:S(2)}) collective-permute-start(bf16[640,256]{1,0:T(8,128)(2,1)S(1)} %get-tuple-element.95), channel_id=1, source_target_pairs={{0,32},{8,40},{16,48},{24,56},{32,0},{40,8},{48,16},{56,24},{64,96... | collective-permute-start | bytes 983048 | tf_op jit(solution)/shard_map/ppermute | solution.py:43
  67.7 0.7 collective-permute-start.18
  68.5 0.1 add_add_fusion.1.refs_0_
  68.6 4.6 %project.10.refs_6_ = f32[256,768]{1,0:T(8,128)S(1)} custom-call(s32[3]{0:T(128)S(1)} %add_add_fusion.1.refs_0_, bf16[256,1024]{1,0:T(8,128)(2,1)} %collective-permute-done.12.refs_1_, bf16[256,1024]{1,0:T(8,128)(2,1)} %collective-permute-done.10.refs_2_, bf16[256,1024]{1,0:T(8,128)(2,1)S(1)} %collective-permute-done.11.refs_3_, bf16[8192,512]{1,0:T(8,128)(2,1)} %refs_3_.3, ...), custom_call_target="tpu_custom_call" | custom-call | flops 1 | bytes 1 | tf_op jit(solution)/shard_map/project/pallas_call | solution.py:164
  73.3 3.3 %project.11 = (bf16[320,256]{1,0:T(8,128)(2,1)S(1)}, bf16[320,256]{1,0:T(8,128)(2,1)S(1)}, bf16[320,256]{1,0:T(8,128)(2,1)S(1)}, bf16[320,256]{1,0:T(8,128)(2,1)...) custom-call(s32[2]{0:T(128)S(1)} %pad_add_fusion.4.refs_0_, ...), custom_call_target="tpu_custom_call" | custom-call | flops 1 | bytes 1 | tf_op jit(solution)/shard_map/project/pallas_call | solution.py:164
  76.6 3.0 %collective-permute-start.16 = (bf16[320,256]{1,0:T(8,128)(2,1)S(1)}, bf16[320,256]{1,0:T(8,128)(2,1)S(1)}, u32[]{:S(2)}, u32[]{:S(2)}) collective-permute-start(bf16[320,256]{1,0:T(8,128)(2,1)S(1)} %get-tuple-element.89), channel_id=1, source_target_pairs={{0,64},{8,72},{16,80},{24,88},{32,96},{40,104},{48,112},{56,120},{... | collective-permute-start | bytes 491528 | tf_op jit(solution)/shard_map/ppermute | solution.py:43
  79.6 0.5 collective-permute-start.23
  80.1 3.0 %collective-permute-start.24 = (bf16[320,256]{1,0:T(8,128)(2,1)S(1)}, bf16[320,256]{1,0:T(8,128)(2,1)S(1)}, u32[]{:S(2)}, u32[]{:S(2)}) collective-permute-start(bf16[320,256]{1,0:T(8,128)(2,1)S(1)} %get-tuple-element.103), channel_id=1, source_target_pairs={{0,96},{8,104},{16,112},{24,120},{32,64},{40,72},{48,80},{56,88},{... | collective-permute-start | bytes 491528 | tf_op jit(solution)/shard_map/ppermute | solution.py:43
  83.2 2.0 %collective-permute-start.25 = (bf16[320,256]{1,0:T(8,128)(2,1)S(1)}, bf16[320,256]{1,0:T(8,128)(2,1)S(1)}, u32[]{:S(2)}, u32[]{:S(2)}) collective-permute-start(bf16[320,256]{1,0:T(8,128)(2,1)S(1)} %get-tuple-element.104), channel_id=1, source_target_pairs={{0,112},{8,120},{16,64},{24,72},{32,80},{40,88},{48,96},{56,104},{... | collective-permute-start | bytes 491528 | tf_op jit(solution)/shard_map/ppermute | solution.py:43
  85.2 0.1 pad_maximum_fusion
  85.3 0.6 copy-done.12
  85.9 6.8 %collective-permute-start.19 = (bf16[2560,256]{1,0:T(8,128)(2,1)S(1)}, bf16[2560,256]{1,0:T(8,128)(2,1)}, u32[]{:S(2)}, u32[]{:S(2)}) collective-permute-start(bf16[2560,256]{1,0:T(8,128)(2,1)S(1)} %pad_maximum_fusion), channel_id=1, source_target_pairs={{0,8},{8,0},{16,24},{24,16},{32,40},{40,32},{48,56},{56,48},{64,72... | collective-permute-start | bytes 3932168 | tf_op jit(solution)/shard_map/ppermute | solution.py:55
  92.7 0.1 collective-permute-start.20
  92.9 2.4 %collective-permute-start.21 = (bf16[320,256]{1,0:T(8,128)(2,1)S(1)}, bf16[320,256]{1,0:T(8,128)(2,1)S(1)}, u32[]{:S(2)}, u32[]{:S(2)}) collective-permute-start(bf16[320,256]{1,0:T(8,128)(2,1)S(1)} %get-tuple-element.99), channel_id=1, source_target_pairs={{0,32},{8,40},{16,48},{24,56},{32,0},{40,8},{48,16},{56,24},{64,96... | collective-permute-start | bytes 491528 | tf_op jit(solution)/shard_map/ppermute | solution.py:43
  95.3 1.9 %collective-permute-start.22 = (bf16[320,256]{1,0:T(8,128)(2,1)S(1)}, bf16[320,256]{1,0:T(8,128)(2,1)S(1)}, u32[]{:S(2)}, u32[]{:S(2)}) collective-permute-start(bf16[320,256]{1,0:T(8,128)(2,1)S(1)} %get-tuple-element.100), channel_id=1, source_target_pairs={{0,48},{8,56},{16,0},{24,8},{32,16},{40,24},{48,32},{56,40},{64,11... | collective-permute-start | bytes 491528 | tf_op jit(solution)/shard_map/ppermute | solution.py:43
  97.3 1.4 %collective-permute-start.27 = (bf16[1280,256]{1,0:T(8,128)(2,1)S(1)}, bf16[1280,256]{1,0:T(8,128)(2,1)}, u32[]{:S(2)}, u32[]{:S(2)}) collective-permute-start(bf16[1280,256]{1,0:T(8,128)(2,1)S(1)} %pad_maximum_fusion.2), channel_id=1, source_target_pairs={{0,8},{8,0},{16,24},{24,16},{32,40},{40,32},{48,56},{56,48},{64,72... | collective-permute-start | bytes 1966088 | tf_op jit(solution)/shard_map/ppermute | solution.py:55
  98.7 1.2 collective-permute-done.20.refs_6_
  99.9 3.2 %collective-permute-done.21.refs_7_ = bf16[320,256]{1,0:T(8,128)(2,1)S(1)} collective-permute-done((bf16[320,256]{1,0:T(8,128)(2,1)S(1)}, bf16[320,256]{1,0:T(8,128)(2,1)S(1)}, u32[]{:S(2)}, u32[]{:S(2)}) %collective-permute-start.21) | collective-permute-done | bytes 163872 | tf_op jit(solution)/shard_map/ppermute | solution.py:43
  103.1 0.4 collective-permute-done.22.refs_8_
  103.6 1.3 collective-permute-start.26
  104.8 1.9 %collective-permute-done.26.refs_13_ = bf16[1280,256]{1,0:T(8,128)(2,1)} collective-permute-done((bf16[1280,256]{1,0:T(8,128)(2,1)S(1)}, bf16[1280,256]{1,0:T(8,128)(2,1)}, u32[]{:S(2)}, u32[]{:S(2)}) %collective-permute-start.26) | collective-permute-done | bytes 655392 | tf_op jit(solution)/shard_map/ppermute | solution.py:55
  106.7 20.0 %attend.1 = bf16[512,512]{1,0:T(8,128)(2,1)} custom-call(s32[19]{0:T(128)} %pad_add_fusion.1.info, s32[256]{0:T(256)} %reshape.65.old_map, bf16[640,256]{1,0:T(8,128)(2,1)} %copy-done.9, bf16[640,256]{1,0:T(8,128)(2,1)} %copy-done.10, bf16[640,256]{1,0:T(8,128)(2,1)} %copy-done.11, bf16[640,256]{1,0:T(8,128)(2,1)} %copy-done.12, ...), custom_call_target="tpu_custom_call" | custom-call | tf_op jit(solution)/shard_map/attend/pallas_call | solution.py:244
  (77 shorter events, 0.7 us)
Async XLA Ops:
  0.0 6.2 %copy-start.21 = (s32[16,16]{1,0:T(8,128)S(1)}, s32[16,16]{1,0:T(8,128)}, u32[]{:S(2)}) copy-start(s32[16,16]{1,0:T(8,128)} %param.8) | copy-start | bytes 3076
  0.0 11.8 %copy-start.20 = (s32[16,16]{1,0:T(8,128)S(1)}, s32[16,16]{1,0:T(8,128)}, u32[]{:S(2)}) copy-start(s32[16,16]{1,0:T(8,128)} %param.7) | copy-start | bytes 3076
  1.3 19.9 %copy-start.3 = (bf16[16,1,16,1024]{3,2,1,0:T(8,128)(2,1)}, bf16[16,1,16,1024]{3,2,1,0:T(8,128)(2,1)S(1)}, u32[]{:S(2)}) copy-start(bf16[16,1,16,1024]{3,2,1,0:T(8,128)(2,1)S(1)} %get-tuple-element.107) | copy-start | bytes 1572868
  1.3 20.0 %copy-start = (bf16[8192,128]{1,0:T(8,128)(2,1)S(1)}, bf16[8192,128]{1,0:T(8,128)(2,1)}, u32[]{:S(2)}) copy-start(bf16[8192,128]{1,0:T(8,128)(2,1)} %refs_4_.9) | copy-start | bytes 6291460
  1.3 15.4 %collective-permute-start = (bf16[256,1024]{1,0:T(8,128)(2,1)S(1)}, bf16[256,1024]{1,0:T(8,128)(2,1)}, u32[]{:S(2)}, u32[]{:S(2)}) collective-permute-start(bf16[256,1024]{1,0:T(8,128)(2,1)S(1)} %bitcast.29), channel_id=1, source_target_pairs={{0,2},{1,3},{2,4},{3,5},{4,6},{5,7},{6,0},{7,1},{8,10},{9,11},{10,... | collective-permute-start | bytes 1572872 | tf_op jit(solution)/shard_map/ppermute | solution.py:29
  3.4 13.3 %collective-permute-start.1 = (bf16[256,1024]{1,0:T(8,128)(2,1)S(1)}, bf16[256,1024]{1,0:T(8,128)(2,1)}, u32[]{:S(2)}, u32[]{:S(2)}) collective-permute-start(bf16[256,1024]{1,0:T(8,128)(2,1)S(1)} %bitcast.30), channel_id=1, source_target_pairs={{0,6},{1,7},{2,0},{3,1},{4,2},{5,3},{6,4},{7,5},{8,14},{9,15},{10,... | collective-permute-start | bytes 1572872 | tf_op jit(solution)/shard_map/ppermute | solution.py:29
  4.8 12.3 %collective-permute-start.2 = (bf16[256,1024]{1,0:T(8,128)(2,1)S(1)}, bf16[256,1024]{1,0:T(8,128)(2,1)}, u32[]{:S(2)}, u32[]{:S(2)}) collective-permute-start(bf16[256,1024]{1,0:T(8,128)(2,1)S(1)} %bitcast.31), channel_id=1, source_target_pairs={{0,1},{1,0},{2,3},{3,2},{4,5},{5,4},{6,7},{7,6},{8,9},{9,8},{10,11... | collective-permute-start | bytes 1572872 | tf_op jit(solution)/shard_map/ppermute | solution.py:33
  17.1 12.8 %collective-permute-start.3 = (bf16[256,1024]{1,0:T(8,128)(2,1)}, bf16[256,1024]{1,0:T(8,128)(2,1)}, u32[]{:S(2)}, u32[]{:S(2)}) collective-permute-start(bf16[256,1024]{1,0:T(8,128)(2,1)} %collective-permute-done.2.refs_4_), channel_id=1, source_target_pairs={{0,2},{1,3},{2,4},{3,5},{4,6},{5,7},{6,0},{7,1},{8,10},{9,11},{10,... | collective-permute-start | bytes 1572872 | tf_op jit(solution)/shard_map/ppermute | solution.py:29
  17.2 12.6 %collective-permute-start.4 = (bf16[256,1024]{1,0:T(8,128)(2,1)}, bf16[256,1024]{1,0:T(8,128)(2,1)}, u32[]{:S(2)}, u32[]{:S(2)}) collective-permute-start(bf16[256,1024]{1,0:T(8,128)(2,1)} %collective-permute-done.1.refs_3_), channel_id=1, source_target_pairs={{0,6},{1,7},{2,0},{3,1},{4,2},{5,3},{6,4},{7,5},{8,14},{9,15},{10,... | collective-permute-start | bytes 1572872 | tf_op jit(solution)/shard_map/ppermute | solution.py:29
  19.7 12.5 %collective-permute-start.8 = (bf16[256,1024]{1,0:T(8,128)(2,1)}, bf16[256,1024]{1,0:T(8,128)(2,1)}, u32[]{:S(2)}, u32[]{:S(2)}) collective-permute-start(bf16[256,1024]{1,0:T(8,128)(2,1)} %collective-permute-done.1.refs_3_), channel_id=1, source_target_pairs={{0,1},{1,0},{2,3},{3,2},{4,5},{5,4},{6,7},{7,6},{8,9},{9,8},{10,11... | collective-permute-start | bytes 1572872 | tf_op jit(solution)/shard_map/ppermute | solution.py:33
  21.3 20.7 %collective-permute-start.7 = (bf16[256,1024]{1,0:T(8,128)(2,1)S(1)}, bf16[256,1024]{1,0:T(8,128)(2,1)}, u32[]{:S(2)}, u32[]{:S(2)}) collective-permute-start(bf16[256,1024]{1,0:T(8,128)(2,1)S(1)} %bitcast.25), channel_id=1, source_target_pairs={{0,1},{1,0},{2,3},{3,2},{4,5},{5,4},{6,7},{7,6},{8,9},{9,8},{10,11... | collective-permute-start | bytes 1572872 | tf_op jit(solution)/shard_map/ppermute | solution.py:33
  21.3 1.0 copy-start.4
  29.8 12.2 %collective-permute-start.6 = (bf16[256,1024]{1,0:T(8,128)(2,1)S(1)}, bf16[256,1024]{1,0:T(8,128)(2,1)}, u32[]{:S(2)}, u32[]{:S(2)}) collective-permute-start(bf16[256,1024]{1,0:T(8,128)(2,1)S(1)} %bitcast.26), channel_id=1, source_target_pairs={{0,6},{1,7},{2,0},{3,1},{4,2},{5,3},{6,4},{7,5},{8,14},{9,15},{10,... | collective-permute-start | bytes 1572872 | tf_op jit(solution)/shard_map/ppermute | solution.py:29
  32.2 12.8 %collective-permute-start.5 = (bf16[256,1024]{1,0:T(8,128)(2,1)}, bf16[256,1024]{1,0:T(8,128)(2,1)}, u32[]{:S(2)}, u32[]{:S(2)}) collective-permute-start(bf16[256,1024]{1,0:T(8,128)(2,1)} %collective-permute-done.3.refs_1_), channel_id=1, source_target_pairs={{0,2},{1,3},{2,4},{3,5},{4,6},{5,7},{6,0},{7,1},{8,10},{9,11},{10,... | collective-permute-start | bytes 1572872 | tf_op jit(solution)/shard_map/ppermute | solution.py:29
  32.2 22.5 %collective-permute-start.12 = (bf16[256,1024]{1,0:T(8,128)(2,1)S(1)}, bf16[256,1024]{1,0:T(8,128)(2,1)}, u32[]{:S(2)}, u32[]{:S(2)}) collective-permute-start(bf16[256,1024]{1,0:T(8,128)(2,1)S(1)} %bitcast.27), channel_id=1, source_target_pairs={{0,2},{1,3},{2,4},{3,5},{4,6},{5,7},{6,0},{7,1},{8,10},{9,11},{10,... | collective-permute-start | bytes 1572872 | tf_op jit(solution)/shard_map/ppermute | solution.py:29
  37.1 0.9 copy-start.1
  42.0 18.7 %collective-permute-start.10 = (bf16[256,1024]{1,0:T(8,128)(2,1)}, bf16[256,1024]{1,0:T(8,128)(2,1)}, u32[]{:S(2)}, u32[]{:S(2)}) collective-permute-start(bf16[256,1024]{1,0:T(8,128)(2,1)} %collective-permute-done.6.refs_2_), channel_id=1, source_target_pairs={{0,6},{1,7},{2,0},{3,1},{4,2},{5,3},{6,4},{7,5},{8,14},{9,15},{10,... | collective-permute-start | bytes 1572872 | tf_op jit(solution)/shard_map/ppermute | solution.py:29
  43.6 17.1 %collective-permute-start.11 = (bf16[256,1024]{1,0:T(8,128)(2,1)}, bf16[256,1024]{1,0:T(8,128)(2,1)S(1)}, u32[]{:S(2)}, u32[]{:S(2)}) collective-permute-start(bf16[256,1024]{1,0:T(8,128)(2,1)} %collective-permute-done.6.refs_2_), channel_id=1, source_target_pairs={{0,1},{1,0},{2,3},{3,2},{4,5},{5,4},{6,7},{7,6},{8,9},{9,8},{10,11... | collective-permute-start | bytes 1572872 | tf_op jit(solution)/shard_map/ppermute | solution.py:33
  45.0 1.1 copy-start.2
  46.2 0.9 copy-start.6
  49.2 11.3 %collective-permute-start.9 = (bf16[512,256]{1,0:T(8,128)(2,1)S(1)}, bf16[512,256]{1,0:T(8,128)(2,1)S(1)}, u32[]{:S(2)}, u32[]{:S(2)}) collective-permute-start(bf16[512,256]{1,0:T(8,128)(2,1)S(1)} %get-tuple-element.73), channel_id=1, source_target_pairs={{0,64},{8,72},{16,80},{24,88},{32,96},{40,104},{48,112},{56,120},{... | collective-permute-start | bytes 786440 | tf_op jit(solution)/shard_map/ppermute | solution.py:43
  54.7 18.5 %collective-permute-start.14 = (bf16[256,1024]{1,0:T(8,128)(2,1)}, bf16[256,1024]{1,0:T(8,128)(2,1)S(1)}, u32[]{:S(2)}, u32[]{:S(2)}) collective-permute-start(bf16[256,1024]{1,0:T(8,128)(2,1)} %collective-permute-done.7.refs_3_), channel_id=1, source_target_pairs={{0,2},{1,3},{2,4},{3,5},{4,6},{5,7},{6,0},{7,1},{8,10},{9,11},{10,... | collective-permute-start | bytes 1572872 | tf_op jit(solution)/shard_map/ppermute | solution.py:29
  60.6 12.6 %collective-permute-start.15 = (bf16[256,1024]{1,0:T(8,128)(2,1)S(1)}, bf16[256,1024]{1,0:T(8,128)(2,1)S(1)}, u32[]{:S(2)}, u32[]{:S(2)}) collective-permute-start(bf16[256,1024]{1,0:T(8,128)(2,1)S(1)} %collective-permute-done.11.refs_3_), channel_id=1, source_target_pairs={{0,6},{1,7},{2,0},{3,1},{4,2},{5,3},{6,4},{7,5},{8,14},{9,15},{10,... | collective-permute-start | bytes 1572872 | tf_op jit(solution)/shard_map/ppermute | solution.py:29
  62.4 22.8 %copy-start.9 = (bf16[640,256]{1,0:T(8,128)(2,1)}, bf16[640,256]{1,0:T(8,128)(2,1)S(1)}, u32[]{:S(2)}) copy-start(bf16[640,256]{1,0:T(8,128)(2,1)S(1)} %pad_maximum_fusion.6.refs_0_) | copy-start | bytes 983044
  62.5 17.6 %collective-permute-start.13 = (bf16[640,256]{1,0:T(8,128)(2,1)S(1)}, bf16[640,256]{1,0:T(8,128)(2,1)S(1)}, u32[]{:S(2)}, u32[]{:S(2)}) collective-permute-start(bf16[640,256]{1,0:T(8,128)(2,1)S(1)} %get-tuple-element.82), channel_id=1, source_target_pairs={{0,16},{8,24},{16,32},{24,40},{32,48},{40,56},{48,0},{56,8},{64,80... | collective-permute-start | bytes 983048 | tf_op jit(solution)/shard_map/ppermute | solution.py:43
  64.4 18.8 %collective-permute-start.17 = (bf16[640,256]{1,0:T(8,128)(2,1)S(1)}, bf16[640,256]{1,0:T(8,128)(2,1)S(1)}, u32[]{:S(2)}, u32[]{:S(2)}) collective-permute-start(bf16[640,256]{1,0:T(8,128)(2,1)S(1)} %get-tuple-element.95), channel_id=1, source_target_pairs={{0,32},{8,40},{16,48},{24,56},{32,0},{40,8},{48,16},{56,24},{64,96... | collective-permute-start | bytes 983048 | tf_op jit(solution)/shard_map/ppermute | solution.py:43
  67.7 17.5 %collective-permute-start.18 = (bf16[640,256]{1,0:T(8,128)(2,1)S(1)}, bf16[640,256]{1,0:T(8,128)(2,1)S(1)}, u32[]{:S(2)}, u32[]{:S(2)}) collective-permute-start(bf16[640,256]{1,0:T(8,128)(2,1)S(1)} %get-tuple-element.96), channel_id=1, source_target_pairs={{0,48},{8,56},{16,0},{24,8},{32,16},{40,24},{48,32},{56,40},{64,11... | collective-permute-start | bytes 983048 | tf_op jit(solution)/shard_map/ppermute | solution.py:43
  68.6 4.7 %copy-start.7 = (f32[256,128]{1,0:T(8,128)S(1)}, f32[256,128]{1,0:T(8,128)}, u32[]{:S(2)}) copy-start(f32[256,128]{1,0:T(8,128)} %get-tuple-element.87.refs_8_) | copy-start | bytes 393220
  68.6 4.7 %copy-start.8 = (f32[256,128]{1,0:T(8,128)S(1)}, f32[256,128]{1,0:T(8,128)}, u32[]{:S(2)}) copy-start(f32[256,128]{1,0:T(8,128)} %get-tuple-element.88.refs_9_) | copy-start | bytes 393220
  76.6 26.9 %copy-start.5 = (bf16[320,256]{1,0:T(8,128)(2,1)}, bf16[320,256]{1,0:T(8,128)(2,1)S(1)}, u32[]{:S(2)}) copy-start(bf16[320,256]{1,0:T(8,128)(2,1)S(1)} %get-tuple-element.97.refs_5_) | copy-start | bytes 491524
  76.6 16.2 %collective-permute-start.16 = (bf16[320,256]{1,0:T(8,128)(2,1)S(1)}, bf16[320,256]{1,0:T(8,128)(2,1)S(1)}, u32[]{:S(2)}, u32[]{:S(2)}) collective-permute-start(bf16[320,256]{1,0:T(8,128)(2,1)S(1)} %get-tuple-element.89), channel_id=1, source_target_pairs={{0,64},{8,72},{16,80},{24,88},{32,96},{40,104},{48,112},{56,120},{... | collective-permute-start | bytes 491528 | tf_op jit(solution)/shard_map/ppermute | solution.py:43
  79.6 13.3 %collective-permute-start.23 = (bf16[320,256]{1,0:T(8,128)(2,1)S(1)}, bf16[320,256]{1,0:T(8,128)(2,1)S(1)}, u32[]{:S(2)}, u32[]{:S(2)}) collective-permute-start(bf16[320,256]{1,0:T(8,128)(2,1)S(1)} %get-tuple-element.102), channel_id=1, source_target_pairs={{0,80},{8,88},{16,96},{24,104},{32,112},{40,120},{48,64},{56,72},{... | collective-permute-start | bytes 491528 | tf_op jit(solution)/shard_map/ppermute | solution.py:43
  80.1 5.2 %copy-start.10 = (bf16[640,256]{1,0:T(8,128)(2,1)}, bf16[640,256]{1,0:T(8,128)(2,1)S(1)}, u32[]{:S(2)}) copy-start(bf16[640,256]{1,0:T(8,128)(2,1)S(1)} %collective-permute-done.13.refs_1_) | copy-start | bytes 983044
  80.1 15.2 %collective-permute-start.24 = (bf16[320,256]{1,0:T(8,128)(2,1)S(1)}, bf16[320,256]{1,0:T(8,128)(2,1)S(1)}, u32[]{:S(2)}, u32[]{:S(2)}) collective-permute-start(bf16[320,256]{1,0:T(8,128)(2,1)S(1)} %get-tuple-element.103), channel_id=1, source_target_pairs={{0,96},{8,104},{16,112},{24,120},{32,64},{40,72},{48,80},{56,88},{... | collective-permute-start | bytes 491528 | tf_op jit(solution)/shard_map/ppermute | solution.py:43
  83.2 2.1 %copy-start.11 = (bf16[640,256]{1,0:T(8,128)(2,1)}, bf16[640,256]{1,0:T(8,128)(2,1)S(1)}, u32[]{:S(2)}) copy-start(bf16[640,256]{1,0:T(8,128)(2,1)S(1)} %collective-permute-done.17.refs_2_) | copy-start | bytes 983044
  83.2 14.0 %collective-permute-start.25 = (bf16[320,256]{1,0:T(8,128)(2,1)S(1)}, bf16[320,256]{1,0:T(8,128)(2,1)S(1)}, u32[]{:S(2)}, u32[]{:S(2)}) collective-permute-start(bf16[320,256]{1,0:T(8,128)(2,1)S(1)} %get-tuple-element.104), channel_id=1, source_target_pairs={{0,112},{8,120},{16,64},{24,72},{32,80},{40,88},{48,96},{56,104},{... | collective-permute-start | bytes 491528 | tf_op jit(solution)/shard_map/ppermute | solution.py:43
  85.2 0.7 copy-start.12
  85.9 20.8 %collective-permute-start.19 = (bf16[2560,256]{1,0:T(8,128)(2,1)S(1)}, bf16[2560,256]{1,0:T(8,128)(2,1)}, u32[]{:S(2)}, u32[]{:S(2)}) collective-permute-start(bf16[2560,256]{1,0:T(8,128)(2,1)S(1)} %pad_maximum_fusion), channel_id=1, source_target_pairs={{0,8},{8,0},{16,24},{24,16},{32,40},{40,32},{48,56},{56,48},{64,72... | collective-permute-start | bytes 3932168 | tf_op jit(solution)/shard_map/ppermute | solution.py:55
  92.7 10.8 %copy-start.13 = (bf16[320,256]{1,0:T(8,128)(2,1)}, bf16[320,256]{1,0:T(8,128)(2,1)S(1)}, u32[]{:S(2)}) copy-start(bf16[320,256]{1,0:T(8,128)(2,1)S(1)} %collective-permute-done.16.refs_9_) | copy-start | bytes 491524
  92.7 7.1 %collective-permute-start.20 = (bf16[320,256]{1,0:T(8,128)(2,1)S(1)}, bf16[320,256]{1,0:T(8,128)(2,1)S(1)}, u32[]{:S(2)}, u32[]{:S(2)}) collective-permute-start(bf16[320,256]{1,0:T(8,128)(2,1)S(1)} %get-tuple-element.98), channel_id=1, source_target_pairs={{0,16},{8,24},{16,32},{24,40},{32,48},{40,56},{48,0},{56,8},{64,80... | collective-permute-start | bytes 491528 | tf_op jit(solution)/shard_map/ppermute | solution.py:43
  92.9 10.7 %copy-start.14 = (bf16[320,256]{1,0:T(8,128)(2,1)}, bf16[320,256]{1,0:T(8,128)(2,1)S(1)}, u32[]{:S(2)}) copy-start(bf16[320,256]{1,0:T(8,128)(2,1)S(1)} %collective-permute-done.23.refs_10_) | copy-start | bytes 491524
  92.9 10.2 %collective-permute-start.21 = (bf16[320,256]{1,0:T(8,128)(2,1)S(1)}, bf16[320,256]{1,0:T(8,128)(2,1)S(1)}, u32[]{:S(2)}, u32[]{:S(2)}) collective-permute-start(bf16[320,256]{1,0:T(8,128)(2,1)S(1)} %get-tuple-element.99), channel_id=1, source_target_pairs={{0,32},{8,40},{16,48},{24,56},{32,0},{40,8},{48,16},{56,24},{64,96... | collective-permute-start | bytes 491528 | tf_op jit(solution)/shard_map/ppermute | solution.py:43
  95.3 8.3 %copy-start.15 = (bf16[320,256]{1,0:T(8,128)(2,1)}, bf16[320,256]{1,0:T(8,128)(2,1)S(1)}, u32[]{:S(2)}) copy-start(bf16[320,256]{1,0:T(8,128)(2,1)S(1)} %collective-permute-done.24.refs_11_) | copy-start | bytes 491524
  95.3 8.2 %collective-permute-start.22 = (bf16[320,256]{1,0:T(8,128)(2,1)S(1)}, bf16[320,256]{1,0:T(8,128)(2,1)S(1)}, u32[]{:S(2)}, u32[]{:S(2)}) collective-permute-start(bf16[320,256]{1,0:T(8,128)(2,1)S(1)} %get-tuple-element.100), channel_id=1, source_target_pairs={{0,48},{8,56},{16,0},{24,8},{32,16},{40,24},{48,32},{56,40},{64,11... | collective-permute-start | bytes 491528 | tf_op jit(solution)/shard_map/ppermute | solution.py:43
  97.2 6.4 %copy-start.16 = (bf16[320,256]{1,0:T(8,128)(2,1)}, bf16[320,256]{1,0:T(8,128)(2,1)S(1)}, u32[]{:S(2)}) copy-start(bf16[320,256]{1,0:T(8,128)(2,1)S(1)} %collective-permute-done.25.refs_12_) | copy-start | bytes 491524
  97.3 7.6 %collective-permute-start.27 = (bf16[1280,256]{1,0:T(8,128)(2,1)S(1)}, bf16[1280,256]{1,0:T(8,128)(2,1)}, u32[]{:S(2)}, u32[]{:S(2)}) collective-permute-start(bf16[1280,256]{1,0:T(8,128)(2,1)S(1)} %pad_maximum_fusion.2), channel_id=1, source_target_pairs={{0,8},{8,0},{16,24},{24,16},{32,40},{40,32},{48,56},{56,48},{64,72... | collective-permute-start | bytes 1966088 | tf_op jit(solution)/shard_map/ppermute | solution.py:55
  99.9 6.8 %copy-start.17 = (bf16[320,256]{1,0:T(8,128)(2,1)}, bf16[320,256]{1,0:T(8,128)(2,1)S(1)}, u32[]{:S(2)}) copy-start(bf16[320,256]{1,0:T(8,128)(2,1)S(1)} %collective-permute-done.20.refs_6_) | copy-start | bytes 491524
  103.1 3.6 %copy-start.18 = (bf16[320,256]{1,0:T(8,128)(2,1)}, bf16[320,256]{1,0:T(8,128)(2,1)S(1)}, u32[]{:S(2)}) copy-start(bf16[320,256]{1,0:T(8,128)(2,1)S(1)} %collective-permute-done.21.refs_7_) | copy-start | bytes 491524
  103.5 3.2 %copy-start.19 = (bf16[320,256]{1,0:T(8,128)(2,1)}, bf16[320,256]{1,0:T(8,128)(2,1)S(1)}, u32[]{:S(2)}) copy-start(bf16[320,256]{1,0:T(8,128)(2,1)S(1)} %collective-permute-done.22.refs_8_) | copy-start | bytes 491524
  103.6 3.1 %collective-permute-start.26 = (bf16[1280,256]{1,0:T(8,128)(2,1)S(1)}, bf16[1280,256]{1,0:T(8,128)(2,1)}, u32[]{:S(2)}, u32[]{:S(2)}) collective-permute-start(bf16[1280,256]{1,0:T(8,128)(2,1)S(1)} %pad_maximum_fusion.1), channel_id=1, source_target_pairs={{0,8},{8,0},{16,24},{24,16},{32,40},{40,32},{48,56},{56,48},{64,72... | collective-permute-start | bytes 1966088 | tf_op jit(solution)/shard_map/ppermute | solution.py:55

commit v11 on v10

--- a/solution.py
+++ b/solution.py
@@ -190,7 +190,12 @@
                 if j == 0:
                     ref, base = (packed_other, (dz * 2 + dh) * PAYLOAD) if swapped else (packed[dz], dh * PAYLOAD)
                 else:
-                    ref, base = (late_other[r // 4], (r % 4) * PAYLOAD) if swapped else (late[r], 0)
+                    if not swapped:
+                        ref, base = late[r], 0
+                    elif 1 <= r <= 3:
+                        ref, base = late_other[0], (r - 1) * PAYLOAD
+                    else:
+                        ref, base = late_other[1], max(r - 3, 0) * PAYLOAD
                 for k in range(16):
                     at = pl.ds(pl.multiple_of(old_map[source * 16 + k] * FINE + j * W, W), W)
                     rows = slice(base + k * W, base + (k + 1) * W)
@@ -345,7 +350,8 @@
     late_parts = [shift_ctx(sent[r], *CHIPS[r]) for r in range(4, 8)]
     early_parts[1], late_parts[0], *sent[:4] = together(early_parts[1], late_parts[0], *sent[:4])
     late_parts = [sent[0]] + [shift_ctx(sent[r], *CHIPS[r]) for r in range(1, 4)] + late_parts
-    late_other = [swap_core(jnp.concatenate(late_parts[at : at + 4], axis=0)) for at in (0, 4)]
+    groups = [late_parts[1:4], late_parts[:1] + late_parts[4:]]
+    late_other = [swap_core(jnp.concatenate(group, axis=0)) for group in groups]
     return attend(attend_info, old_flat, [*early_parts, early_other, *late_parts, *late_other])
 
 

time: 127 us -> 138 us (1.087)
  waiting for transfers between devices: 16.8 us -> 25 us
  starting transfers between devices: 47.4 us -> 49.7 us
    ppermute x11, waiting for transfers between devices: 6.05 us -> 14.4 us  [shift_ctx(): return lax.ppermute(block, 'ctx', perm)]
    ppermute x11, starting transfers between devices: 21.7 us -> 25.4 us  [shift_ctx(): return lax.ppermute(block, 'ctx', perm)]
    ppermute x3, starting transfers between devices: 9.47 us -> 8.05 us  [swap_core(): return lax.ppermute(block, 'ctx', [(i, i ^ 1) for i in range(16)])]
    unnamed x44 -> x50, local copies, waits for them, and re-layouts: 4.67 us -> 4.81 us
  transfers between devices with their start and end apart: 28 -> 28, of which waited for: 9 -> 11; matrix products, arithmetic and copies ran while one was open for 5% -> 4% of each run, Pallas kernels for 20% -> 18%
where the time goes in v11:
time: 138 us; the launch traced here: 137 us
  starting transfers between devices  49.7 us (36%)
  Pallas kernels  45 us (33%)
  waiting for transfers between devices  25 us (18%)
  local copies, waits for them, and re-layouts  7.66 us (6%)
  between operations  5.33 us (4%)
  other arithmetic  4.61 us (3%)
    ppermute x11, starting transfers between devices, shift_ctx(): return lax.ppermute(block, 'ctx', perm)  25.4 us
    pallas_call x6, Pallas kernels, project(): pl.pallas_call(functools.partial(project_kernel, groups, acc is not None,...  25 us
    pallas_call x1, Pallas kernels, attend(): pl.pallas_call(attend_kernel, out_shape=jax.ShapeDtypeStruct((512, 512),...  20 us
    ppermute x11, waiting for transfers between devices, shift_ctx(): return lax.ppermute(block, 'ctx', perm)  14.4 us
    ppermute x10, starting transfers between devices, shift_x(): return lax.ppermute(block, 'tp', perm)  11.9 us
    ppermute x3, starting transfers between devices, swap_core(): return lax.ppermute(block, 'ctx', [(i, i ^ 1) for i in range(16)])  8.05 us
    unnamed x50, local copies, waits for them, and re-layouts  4.81 us
    ppermute x10, waiting for transfers between devices, shift_x(): return lax.ppermute(block, 'tp', perm)  4.67 us
  transfers between devices with their start and end apart: 28, of which 11 were waited for; matrix products, arithmetic and copies ran while one was open for 4% of the time, Pallas kernels for 18%

profile of v11, /device:TPU:1, one launch (start us, length us, event | category | flops | bytes accessed | tf_op | source)
XLA Modules:
  0.0 137.3 jit_solution(15837831081165782321)
XLA Ops:
  0.0 1.4 %fusion.5 = (bf16[16,1,16,1024]{3,2,1,0:T(8,128)(2,1)S(1)}, bf16[16,1,16,1024]{3,2,1,0:T(8,128)(2,1)S(1)}) fusion(bf16[16,2,16,1024]{3,2,1,0:T(8,128)(2,1)} %bitcast.33), kind=kLoop, calls=%fused_computation.42 | loop fusion | bytes 2097152 | tf_op jit(solution)/shard_map/slice | solution.py:301
  1.5 2.1 %collective-permute-start = (bf16[256,1024]{1,0:T(8,128)(2,1)S(1)}, bf16[256,1024]{1,0:T(8,128)(2,1)}, u32[]{:S(2)}, u32[]{:S(2)}) collective-permute-start(bf16[256,1024]{1,0:T(8,128)(2,1)S(1)} %bitcast.29), channel_id=1, source_target_pairs={{0,2},{1,3},{2,4},{3,5},{4,6},{5,7},{6,0},{7,1},{8,10},{9,11},{10,... | collective-permute-start | bytes 1572872 | tf_op jit(solution)/shard_map/ppermute | solution.py:29
  3.6 1.4 collective-permute-start.1
  4.9 1.4 %collective-permute-start.2 = (bf16[256,1024]{1,0:T(8,128)(2,1)S(1)}, bf16[256,1024]{1,0:T(8,128)(2,1)}, u32[]{:S(2)}, u32[]{:S(2)}) collective-permute-start(bf16[256,1024]{1,0:T(8,128)(2,1)S(1)} %bitcast.31), channel_id=1, source_target_pairs={{0,1},{1,0},{2,3},{3,2},{4,5},{5,4},{6,7},{7,6},{8,9},{9,8},{10,11... | collective-permute-start | bytes 1572872 | tf_op jit(solution)/shard_map/ppermute | solution.py:33
  6.4 0.6 fusion.7
  11.8 0.1 compare_reduce_fusion.1
  12.0 0.1 select_reduce_fusion.1
  12.1 0.1 compare_reduce_fusion
  12.2 0.1 select_reduce_fusion
  12.6 0.7 pad_add_fusion.1.info
  13.3 0.6 reshape.65.old_map
  13.9 0.1 convert_element_type.25
  13.9 0.1 convert_element_type.23
  14.0 1.0 fusion.4
  15.0 0.8 pad_maximum_fusion.6
  15.8 0.8 pad_maximum_fusion.8
  16.7 0.5 collective-permute-done.2.refs_4_
  17.2 0.2 collective-permute-start.3
  17.4 2.5 %collective-permute-start.4 = (bf16[256,1024]{1,0:T(8,128)(2,1)}, bf16[256,1024]{1,0:T(8,128)(2,1)}, u32[]{:S(2)}, u32[]{:S(2)}) collective-permute-start(bf16[256,1024]{1,0:T(8,128)(2,1)} %collective-permute-done.1.refs_3_), channel_id=1, source_target_pairs={{0,6},{1,7},{2,0},{3,1},{4,2},{5,3},{6,4},{7,5},{8,14},{9,15},{10,... | collective-permute-start | bytes 1572872 | tf_op jit(solution)/shard_map/ppermute | solution.py:29
  19.9 1.4 %collective-permute-start.8 = (bf16[256,1024]{1,0:T(8,128)(2,1)}, bf16[256,1024]{1,0:T(8,128)(2,1)}, u32[]{:S(2)}, u32[]{:S(2)}) collective-permute-start(bf16[256,1024]{1,0:T(8,128)(2,1)} %collective-permute-done.1.refs_3_), channel_id=1, source_target_pairs={{0,1},{1,0},{2,3},{3,2},{4,5},{5,4},{6,7},{7,6},{8,9},{9,8},{10,11... | collective-permute-start | bytes 1572872 | tf_op jit(solution)/shard_map/ppermute | solution.py:33
  21.3 0.1 pad_add_fusion.2.refs_0_
  21.4 1.0 copy-done.4
  22.5 5.5 %project.6.refs_7_ = f32[256,768]{1,0:T(8,128)S(1)} custom-call(s32[4]{0:T(128)S(1)} %pad_add_fusion.2.refs_0_, bf16[256,1024]{1,0:T(8,128)(2,1)S(1)} %bitcast.32, bf16[256,1024]{1,0:T(8,128)(2,1)} %collective-permute-done.refs_2_, bf16[256,1024]{1,0:T(8,128)(2,1)} %collective-permute-done.1.refs_3_, bf16[256,1024]{1,0:T(8,128)(2,1)} %collective-permute-done.2.refs_4_, ...), custom_call_target="tpu_custom_call" | custom-call | flops 1 | bytes 1 | tf_op jit(solution)/shard_map/project/pallas_call | solution.py:164
  28.0 1.9 %collective-permute-done.3.refs_1_ = bf16[256,1024]{1,0:T(8,128)(2,1)} collective-permute-done((bf16[256,1024]{1,0:T(8,128)(2,1)}, bf16[256,1024]{1,0:T(8,128)(2,1)}, u32[]{:S(2)}, u32[]{:S(2)}) %collective-permute-start.3) | collective-permute-done | bytes 524320 | tf_op jit(solution)/shard_map/ppermute | solution.py:29
  29.9 2.4 %collective-permute-start.6 = (bf16[256,1024]{1,0:T(8,128)(2,1)S(1)}, bf16[256,1024]{1,0:T(8,128)(2,1)}, u32[]{:S(2)}, u32[]{:S(2)}) collective-permute-start(bf16[256,1024]{1,0:T(8,128)(2,1)S(1)} %bitcast.26), channel_id=1, source_target_pairs={{0,6},{1,7},{2,0},{3,1},{4,2},{5,3},{6,4},{7,5},{8,14},{9,15},{10,... | collective-permute-start | bytes 1572872 | tf_op jit(solution)/shard_map/ppermute | solution.py:29
  32.4 0.1 add_add_fusion.refs_0_
  32.5 4.8 %project.7.refs_5_ = f32[256,768]{1,0:T(8,128)S(1)} custom-call(s32[3]{0:T(128)S(1)} %add_add_fusion.refs_0_, bf16[256,1024]{1,0:T(8,128)(2,1)} %collective-permute-done.3.refs_1_, bf16[256,1024]{1,0:T(8,128)(2,1)} %collective-permute-done.4.refs_2_, bf16[256,1024]{1,0:T(8,128)(2,1)} %collective-permute-done.8.refs_3_, bf16[8192,512]{1,0:T(8,128)(2,1)} %refs_3_.3, ...), custom_call_target="tpu_custom_call" | custom-call | flops 1 | bytes 1 | tf_op jit(solution)/shard_map/project/pallas_call | solution.py:164
  37.3 0.9 copy-done.1
  38.2 3.9 %collective-permute-done.7.refs_3_ = bf16[256,1024]{1,0:T(8,128)(2,1)} collective-permute-done((bf16[256,1024]{1,0:T(8,128)(2,1)S(1)}, bf16[256,1024]{1,0:T(8,128)(2,1)}, u32[]{:S(2)}, u32[]{:S(2)}) %collective-permute-start.7) | collective-permute-done | bytes 524320 | tf_op jit(solution)/shard_map/ppermute | solution.py:33
  42.1 1.6 %collective-permute-start.10 = (bf16[256,1024]{1,0:T(8,128)(2,1)}, bf16[256,1024]{1,0:T(8,128)(2,1)}, u32[]{:S(2)}, u32[]{:S(2)}) collective-permute-start(bf16[256,1024]{1,0:T(8,128)(2,1)} %collective-permute-done.6.refs_2_), channel_id=1, source_target_pairs={{0,6},{1,7},{2,0},{3,1},{4,2},{5,3},{6,4},{7,5},{8,14},{9,15},{10,... | collective-permute-start | bytes 1572872 | tf_op jit(solution)/shard_map/ppermute | solution.py:29
  43.7 1.5 %collective-permute-start.11 = (bf16[256,1024]{1,0:T(8,128)(2,1)}, bf16[256,1024]{1,0:T(8,128)(2,1)S(1)}, u32[]{:S(2)}, u32[]{:S(2)}) collective-permute-start(bf16[256,1024]{1,0:T(8,128)(2,1)} %collective-permute-done.6.refs_2_), channel_id=1, source_target_pairs={{0,1},{1,0},{2,3},{3,2},{4,5},{5,4},{6,7},{7,6},{8,9},{9,8},{10,11... | collective-permute-start | bytes 1572872 | tf_op jit(solution)/shard_map/ppermute | solution.py:33
  45.2 1.1 copy-done.2
  46.3 0.9 copy-done.6
  47.2 2.1 %project.8 = (bf16[320,256]{1,0:T(8,128)(2,1)S(1)}, bf16[320,256]{1,0:T(8,128)(2,1)S(1)}, bf16[320,256]{1,0:T(8,128)(2,1)S(1)}, bf16[320,256]{1,0:T(8,128)(2,1)S(1)}, bf16[512,256]{1,0:T(8,128)(2,1)S(1)}) custom-call(s32[1]{0:T(128)} %bitcast.10.refs_0_, bf16[256,1024]{1,0:T(8,128)(2,1)} %collective-permute-done.5.refs_1_, bf16[8192,512]{1,0:T(8,128)(2,1)} %refs_3_.3, ...), custom_call_target="tpu_custom_call" | custom-call | flops 1 | bytes 1 | tf_op jit(solution)/shard_map/project/pallas_call | solution.py:164
  49.4 2.7 %collective-permute-start.9 = (bf16[512,256]{1,0:T(8,128)(2,1)S(1)}, bf16[512,256]{1,0:T(8,128)(2,1)S(1)}, u32[]{:S(2)}, u32[]{:S(2)}) collective-permute-start(bf16[512,256]{1,0:T(8,128)(2,1)S(1)} %get-tuple-element.73), channel_id=1, source_target_pairs={{0,64},{8,72},{16,80},{24,88},{32,96},{40,104},{48,112},{56,120},{... | collective-permute-start | bytes 786440 | tf_op jit(solution)/shard_map/ppermute | solution.py:43
  52.1 0.1 pad_add_fusion.3.refs_0_
  52.1 2.7 %collective-permute-done.12.refs_1_ = bf16[256,1024]{1,0:T(8,128)(2,1)} collective-permute-done((bf16[256,1024]{1,0:T(8,128)(2,1)S(1)}, bf16[256,1024]{1,0:T(8,128)(2,1)}, u32[]{:S(2)}, u32[]{:S(2)}) %collective-permute-start.12) | collective-permute-done | bytes 524320 | tf_op jit(solution)/shard_map/ppermute | solution.py:29
  54.9 4.6 %project.9.refs_7_ = f32[256,768]{1,0:T(8,128)S(1)} custom-call(s32[3]{0:T(128)S(1)} %pad_add_fusion.3.refs_0_, bf16[256,1024]{1,0:T(8,128)(2,1)S(1)} %bitcast.28, bf16[256,1024]{1,0:T(8,128)(2,1)} %collective-permute-done.6.refs_2_, bf16[256,1024]{1,0:T(8,128)(2,1)} %collective-permute-done.7.refs_3_, bf16[8192,512]{1,0:T(8,128)(2,1)} %refs_3_.3, ...), custom_call_target="tpu_custom_call" | custom-call | flops 1 | bytes 1 | tf_op jit(solution)/shard_map/project/pallas_call | solution.py:164
  59.5 1.2 collective-permute-done.9
  60.8 1.7 %collective-permute-start.15 = (bf16[256,1024]{1,0:T(8,128)(2,1)S(1)}, bf16[256,1024]{1,0:T(8,128)(2,1)S(1)}, u32[]{:S(2)}, u32[]{:S(2)}) collective-permute-start(bf16[256,1024]{1,0:T(8,128)(2,1)S(1)} %collective-permute-done.11.refs_3_), channel_id=1, source_target_pairs={{0,6},{1,7},{2,0},{3,1},{4,2},{5,3},{6,4},{7,5},{8,14},{9,15},{10,... | collective-permute-start | bytes 1572872 | tf_op jit(solution)/shard_map/ppermute | solution.py:29
  62.6 1.9 %collective-permute-start.13 = (bf16[640,256]{1,0:T(8,128)(2,1)S(1)}, bf16[640,256]{1,0:T(8,128)(2,1)S(1)}, u32[]{:S(2)}, u32[]{:S(2)}) collective-permute-start(bf16[640,256]{1,0:T(8,128)(2,1)S(1)} %get-tuple-element.82), channel_id=1, source_target_pairs={{0,16},{8,24},{16,32},{24,40},{32,48},{40,56},{48,0},{56,8},{64,80... | collective-permute-start | bytes 983048 | tf_op jit(solution)/shard_map/ppermute | solution.py:43
  64.5 3.3 %collective-permute-start.17 = (bf16[640,256]{1,0:T(8,128)(2,1)S(1)}, bf16[640,256]{1,0:T(8,128)(2,1)S(1)}, u32[]{:S(2)}, u32[]{:S(2)}) collective-permute-start(bf16[640,256]{1,0:T(8,128)(2,1)S(1)} %get-tuple-element.95), channel_id=1, source_target_pairs={{0,32},{8,40},{16,48},{24,56},{32,0},{40,8},{48,16},{56,24},{64,96... | collective-permute-start | bytes 983048 | tf_op jit(solution)/shard_map/ppermute | solution.py:43
  67.8 0.7 collective-permute-start.18
  68.7 4.6 %project.10.refs_6_ = f32[256,768]{1,0:T(8,128)S(1)} custom-call(s32[3]{0:T(128)S(1)} %add_add_fusion.1.refs_0_, bf16[256,1024]{1,0:T(8,128)(2,1)} %collective-permute-done.12.refs_1_, bf16[256,1024]{1,0:T(8,128)(2,1)} %collective-permute-done.10.refs_2_, bf16[256,1024]{1,0:T(8,128)(2,1)S(1)} %collective-permute-done.11.refs_3_, bf16[8192,512]{1,0:T(8,128)(2,1)} %refs_3_.3, ...), custom_call_target="tpu_custom_call" | custom-call | flops 1 | bytes 1 | tf_op jit(solution)/shard_map/project/pallas_call | solution.py:164
  73.4 3.3 %project.11 = (bf16[320,256]{1,0:T(8,128)(2,1)S(1)}, bf16[320,256]{1,0:T(8,128)(2,1)S(1)}, bf16[320,256]{1,0:T(8,128)(2,1)S(1)}, bf16[320,256]{1,0:T(8,128)(2,1)...) custom-call(s32[2]{0:T(128)S(1)} %pad_add_fusion.4.refs_0_, ...), custom_call_target="tpu_custom_call" | custom-call | flops 1 | bytes 1 | tf_op jit(solution)/shard_map/project/pallas_call | solution.py:164
  76.7 3.0 %collective-permute-start.16 = (bf16[320,256]{1,0:T(8,128)(2,1)S(1)}, bf16[320,256]{1,0:T(8,128)(2,1)S(1)}, u32[]{:S(2)}, u32[]{:S(2)}) collective-permute-start(bf16[320,256]{1,0:T(8,128)(2,1)S(1)} %get-tuple-element.89), channel_id=1, source_target_pairs={{0,64},{8,72},{16,80},{24,88},{32,96},{40,104},{48,112},{56,120},{... | collective-permute-start | bytes 491528 | tf_op jit(solution)/shard_map/ppermute | solution.py:43
  79.7 0.1 pad_maximum_fusion
  79.8 6.3 %collective-permute-start.19 = (bf16[2560,256]{1,0:T(8,128)(2,1)S(1)}, bf16[2560,256]{1,0:T(8,128)(2,1)}, u32[]{:S(2)}, u32[]{:S(2)}) collective-permute-start(bf16[2560,256]{1,0:T(8,128)(2,1)S(1)} %pad_maximum_fusion), channel_id=1, source_target_pairs={{0,8},{8,0},{16,24},{24,16},{32,40},{40,32},{48,56},{56,48},{64,72... | collective-permute-start | bytes 3932168 | tf_op jit(solution)/shard_map/ppermute | solution.py:55
  86.1 1.1 collective-permute-start.23
  87.3 2.2 %collective-permute-start.24 = (bf16[320,256]{1,0:T(8,128)(2,1)S(1)}, bf16[320,256]{1,0:T(8,128)(2,1)S(1)}, u32[]{:S(2)}, u32[]{:S(2)}) collective-permute-start(bf16[320,256]{1,0:T(8,128)(2,1)S(1)} %get-tuple-element.103), channel_id=1, source_target_pairs={{0,96},{8,104},{16,112},{24,120},{32,64},{40,72},{48,80},{56,88},{... | collective-permute-start | bytes 491528 | tf_op jit(solution)/shard_map/ppermute | solution.py:43
  89.5 3.3 %collective-permute-start.25 = (bf16[320,256]{1,0:T(8,128)(2,1)S(1)}, bf16[320,256]{1,0:T(8,128)(2,1)S(1)}, u32[]{:S(2)}, u32[]{:S(2)}) collective-permute-start(bf16[320,256]{1,0:T(8,128)(2,1)S(1)} %get-tuple-element.104), channel_id=1, source_target_pairs={{0,112},{8,120},{16,64},{24,72},{32,80},{40,88},{48,96},{56,104},{... | collective-permute-start | bytes 491528 | tf_op jit(solution)/shard_map/ppermute | solution.py:43
  92.8 3.6 %collective-permute-done.23.refs_10_ = bf16[320,256]{1,0:T(8,128)(2,1)S(1)} collective-permute-done((bf16[320,256]{1,0:T(8,128)(2,1)S(1)}, bf16[320,256]{1,0:T(8,128)(2,1)S(1)}, u32[]{:S(2)}, u32[]{:S(2)}) %collective-permute-start.23) | collective-permute-done | bytes 163872 | tf_op jit(solution)/shard_map/ppermute | solution.py:43
  96.5 2.3 %collective-permute-done.24.refs_11_ = bf16[320,256]{1,0:T(8,128)(2,1)S(1)} collective-permute-done((bf16[320,256]{1,0:T(8,128)(2,1)S(1)}, bf16[320,256]{1,0:T(8,128)(2,1)S(1)}, u32[]{:S(2)}, u32[]{:S(2)}) %collective-permute-start.24) | collective-permute-done | bytes 163872 | tf_op jit(solution)/shard_map/ppermute | solution.py:43
  98.8 1.3 collective-permute-done.25.refs_12_
  100.2 1.0 collective-permute-start.27
  101.2 3.0 %collective-permute-start.20 = (bf16[320,256]{1,0:T(8,128)(2,1)S(1)}, bf16[320,256]{1,0:T(8,128)(2,1)S(1)}, u32[]{:S(2)}, u32[]{:S(2)}) collective-permute-start(bf16[320,256]{1,0:T(8,128)(2,1)S(1)} %get-tuple-element.98), channel_id=1, source_target_pairs={{0,16},{8,24},{16,32},{24,40},{32,48},{40,56},{48,0},{56,8},{64,80... | collective-permute-start | bytes 491528 | tf_op jit(solution)/shard_map/ppermute | solution.py:43
  104.1 2.1 %collective-permute-start.21 = (bf16[320,256]{1,0:T(8,128)(2,1)S(1)}, bf16[320,256]{1,0:T(8,128)(2,1)S(1)}, u32[]{:S(2)}, u32[]{:S(2)}) collective-permute-start(bf16[320,256]{1,0:T(8,128)(2,1)S(1)} %get-tuple-element.99), channel_id=1, source_target_pairs={{0,32},{8,40},{16,48},{24,56},{32,0},{40,8},{48,16},{56,24},{64,96... | collective-permute-start | bytes 491528 | tf_op jit(solution)/shard_map/ppermute | solution.py:43
  106.2 2.1 %collective-permute-start.22 = (bf16[320,256]{1,0:T(8,128)(2,1)S(1)}, bf16[320,256]{1,0:T(8,128)(2,1)S(1)}, u32[]{:S(2)}, u32[]{:S(2)}) collective-permute-start(bf16[320,256]{1,0:T(8,128)(2,1)S(1)} %get-tuple-element.100), channel_id=1, source_target_pairs={{0,48},{8,56},{16,0},{24,8},{32,16},{40,24},{48,32},{56,40},{64,11... | collective-permute-start | bytes 491528 | tf_op jit(solution)/shard_map/ppermute | solution.py:43
  108.3 0.5 collective-permute-done.20.refs_6_
  108.8 5.4 %collective-permute-done.21.refs_7_ = bf16[320,256]{1,0:T(8,128)(2,1)S(1)} collective-permute-done((bf16[320,256]{1,0:T(8,128)(2,1)S(1)}, bf16[320,256]{1,0:T(8,128)(2,1)S(1)}, u32[]{:S(2)}, u32[]{:S(2)}) %collective-permute-start.21) | collective-permute-done | bytes 163872 | tf_op jit(solution)/shard_map/ppermute | solution.py:43
  114.3 0.7 collective-permute-start.26
  115.0 1.5 %collective-permute-done.26.refs_13_ = bf16[960,256]{1,0:T(8,128)(2,1)S(1)} collective-permute-done((bf16[960,256]{1,0:T(8,128)(2,1)S(1)}, bf16[960,256]{1,0:T(8,128)(2,1)S(1)}, u32[]{:S(2)}, u32[]{:S(2)}) %collective-permute-start.26) | collective-permute-done | bytes 491552 | tf_op jit(solution)/shard_map/ppermute | solution.py:55
  116.6 0.7 copy-done.20
  117.3 20.0 %attend.1 = bf16[512,512]{1,0:T(8,128)(2,1)} custom-call(s32[19]{0:T(128)} %pad_add_fusion.1.info, s32[256]{0:T(256)} %reshape.65.old_map, bf16[640,256]{1,0:T(8,128)(2,1)} %copy-done.9, bf16[640,256]{1,0:T(8,128)(2,1)} %copy-done.10, bf16[640,256]{1,0:T(8,128)(2,1)} %copy-done.11, bf16[640,256]{1,0:T(8,128)(2,1)} %copy-done.12, ...), custom_call_target="tpu_custom_call" | custom-call | tf_op jit(solution)/shard_map/attend/pallas_call | solution.py:249
  (83 shorter events, 0.8 us)
Async XLA Ops:
  0.0 6.3 %copy-start.22 = (s32[16,16]{1,0:T(8,128)S(1)}, s32[16,16]{1,0:T(8,128)}, u32[]{:S(2)}) copy-start(s32[16,16]{1,0:T(8,128)} %param.8) | copy-start | bytes 3076
  0.0 11.8 %copy-start.21 = (s32[16,16]{1,0:T(8,128)S(1)}, s32[16,16]{1,0:T(8,128)}, u32[]{:S(2)}) copy-start(s32[16,16]{1,0:T(8,128)} %param.7) | copy-start | bytes 3076
  0.0 21.4 %copy-start = (bf16[8192,128]{1,0:T(8,128)(2,1)S(1)}, bf16[8192,128]{1,0:T(8,128)(2,1)}, u32[]{:S(2)}) copy-start(bf16[8192,128]{1,0:T(8,128)(2,1)} %refs_4_.9) | copy-start | bytes 6291460
  1.4 19.9 %copy-start.3 = (bf16[16,1,16,1024]{3,2,1,0:T(8,128)(2,1)}, bf16[16,1,16,1024]{3,2,1,0:T(8,128)(2,1)S(1)}, u32[]{:S(2)}) copy-start(bf16[16,1,16,1024]{3,2,1,0:T(8,128)(2,1)S(1)} %get-tuple-element.107) | copy-start | bytes 1572868
  1.5 15.2 %collective-permute-start = (bf16[256,1024]{1,0:T(8,128)(2,1)S(1)}, bf16[256,1024]{1,0:T(8,128)(2,1)}, u32[]{:S(2)}, u32[]{:S(2)}) collective-permute-start(bf16[256,1024]{1,0:T(8,128)(2,1)S(1)} %bitcast.29), channel_id=1, source_target_pairs={{0,2},{1,3},{2,4},{3,5},{4,6},{5,7},{6,0},{7,1},{8,10},{9,11},{10,... | collective-permute-start | bytes 1572872 | tf_op jit(solution)/shard_map/ppermute | solution.py:29
  3.6 13.1 %collective-permute-start.1 = (bf16[256,1024]{1,0:T(8,128)(2,1)S(1)}, bf16[256,1024]{1,0:T(8,128)(2,1)}, u32[]{:S(2)}, u32[]{:S(2)}) collective-permute-start(bf16[256,1024]{1,0:T(8,128)(2,1)S(1)} %bitcast.30), channel_id=1, source_target_pairs={{0,6},{1,7},{2,0},{3,1},{4,2},{5,3},{6,4},{7,5},{8,14},{9,15},{10,... | collective-permute-start | bytes 1572872 | tf_op jit(solution)/shard_map/ppermute | solution.py:29
  4.9 12.3 %collective-permute-start.2 = (bf16[256,1024]{1,0:T(8,128)(2,1)S(1)}, bf16[256,1024]{1,0:T(8,128)(2,1)}, u32[]{:S(2)}, u32[]{:S(2)}) collective-permute-start(bf16[256,1024]{1,0:T(8,128)(2,1)S(1)} %bitcast.31), channel_id=1, source_target_pairs={{0,1},{1,0},{2,3},{3,2},{4,5},{5,4},{6,7},{7,6},{8,9},{9,8},{10,11... | collective-permute-start | bytes 1572872 | tf_op jit(solution)/shard_map/ppermute | solution.py:33
  17.2 12.8 %collective-permute-start.3 = (bf16[256,1024]{1,0:T(8,128)(2,1)}, bf16[256,1024]{1,0:T(8,128)(2,1)}, u32[]{:S(2)}, u32[]{:S(2)}) collective-permute-start(bf16[256,1024]{1,0:T(8,128)(2,1)} %collective-permute-done.2.refs_4_), channel_id=1, source_target_pairs={{0,2},{1,3},{2,4},{3,5},{4,6},{5,7},{6,0},{7,1},{8,10},{9,11},{10,... | collective-permute-start | bytes 1572872 | tf_op jit(solution)/shard_map/ppermute | solution.py:29
  17.4 12.6 %collective-permute-start.4 = (bf16[256,1024]{1,0:T(8,128)(2,1)}, bf16[256,1024]{1,0:T(8,128)(2,1)}, u32[]{:S(2)}, u32[]{:S(2)}) collective-permute-start(bf16[256,1024]{1,0:T(8,128)(2,1)} %collective-permute-done.1.refs_3_), channel_id=1, source_target_pairs={{0,6},{1,7},{2,0},{3,1},{4,2},{5,3},{6,4},{7,5},{8,14},{9,15},{10,... | collective-permute-start | bytes 1572872 | tf_op jit(solution)/shard_map/ppermute | solution.py:29
  19.9 12.5 %collective-permute-start.8 = (bf16[256,1024]{1,0:T(8,128)(2,1)}, bf16[256,1024]{1,0:T(8,128)(2,1)}, u32[]{:S(2)}, u32[]{:S(2)}) collective-permute-start(bf16[256,1024]{1,0:T(8,128)(2,1)} %collective-permute-done.1.refs_3_), channel_id=1, source_target_pairs={{0,1},{1,0},{2,3},{3,2},{4,5},{5,4},{6,7},{7,6},{8,9},{9,8},{10,11... | collective-permute-start | bytes 1572872 | tf_op jit(solution)/shard_map/ppermute | solution.py:33
  21.4 20.7 %collective-permute-start.7 = (bf16[256,1024]{1,0:T(8,128)(2,1)S(1)}, bf16[256,1024]{1,0:T(8,128)(2,1)}, u32[]{:S(2)}, u32[]{:S(2)}) collective-permute-start(bf16[256,1024]{1,0:T(8,128)(2,1)S(1)} %bitcast.25), channel_id=1, source_target_pairs={{0,1},{1,0},{2,3},{3,2},{4,5},{5,4},{6,7},{7,6},{8,9},{9,8},{10,11... | collective-permute-start | bytes 1572872 | tf_op jit(solution)/shard_map/ppermute | solution.py:33
  21.4 1.0 copy-start.4
  29.9 12.1 %collective-permute-start.6 = (bf16[256,1024]{1,0:T(8,128)(2,1)S(1)}, bf16[256,1024]{1,0:T(8,128)(2,1)}, u32[]{:S(2)}, u32[]{:S(2)}) collective-permute-start(bf16[256,1024]{1,0:T(8,128)(2,1)S(1)} %bitcast.26), channel_id=1, source_target_pairs={{0,6},{1,7},{2,0},{3,1},{4,2},{5,3},{6,4},{7,5},{8,14},{9,15},{10,... | collective-permute-start | bytes 1572872 | tf_op jit(solution)/shard_map/ppermute | solution.py:29
  32.3 12.8 %collective-permute-start.5 = (bf16[256,1024]{1,0:T(8,128)(2,1)}, bf16[256,1024]{1,0:T(8,128)(2,1)}, u32[]{:S(2)}, u32[]{:S(2)}) collective-permute-start(bf16[256,1024]{1,0:T(8,128)(2,1)} %collective-permute-done.3.refs_1_), channel_id=1, source_target_pairs={{0,2},{1,3},{2,4},{3,5},{4,6},{5,7},{6,0},{7,1},{8,10},{9,11},{10,... | collective-permute-start | bytes 1572872 | tf_op jit(solution)/shard_map/ppermute | solution.py:29
  32.3 22.5 %collective-permute-start.12 = (bf16[256,1024]{1,0:T(8,128)(2,1)S(1)}, bf16[256,1024]{1,0:T(8,128)(2,1)}, u32[]{:S(2)}, u32[]{:S(2)}) collective-permute-start(bf16[256,1024]{1,0:T(8,128)(2,1)S(1)} %bitcast.27), channel_id=1, source_target_pairs={{0,2},{1,3},{2,4},{3,5},{4,6},{5,7},{6,0},{7,1},{8,10},{9,11},{10,... | collective-permute-start | bytes 1572872 | tf_op jit(solution)/shard_map/ppermute | solution.py:29
  37.3 0.9 copy-start.1
  42.1 18.7 %collective-permute-start.10 = (bf16[256,1024]{1,0:T(8,128)(2,1)}, bf16[256,1024]{1,0:T(8,128)(2,1)}, u32[]{:S(2)}, u32[]{:S(2)}) collective-permute-start(bf16[256,1024]{1,0:T(8,128)(2,1)} %collective-permute-done.6.refs_2_), channel_id=1, source_target_pairs={{0,6},{1,7},{2,0},{3,1},{4,2},{5,3},{6,4},{7,5},{8,14},{9,15},{10,... | collective-permute-start | bytes 1572872 | tf_op jit(solution)/shard_map/ppermute | solution.py:29
  43.7 17.1 %collective-permute-start.11 = (bf16[256,1024]{1,0:T(8,128)(2,1)}, bf16[256,1024]{1,0:T(8,128)(2,1)S(1)}, u32[]{:S(2)}, u32[]{:S(2)}) collective-permute-start(bf16[256,1024]{1,0:T(8,128)(2,1)} %collective-permute-done.6.refs_2_), channel_id=1, source_target_pairs={{0,1},{1,0},{2,3},{3,2},{4,5},{5,4},{6,7},{7,6},{8,9},{9,8},{10,11... | collective-permute-start | bytes 1572872 | tf_op jit(solution)/shard_map/ppermute | solution.py:33
  45.2 1.1 copy-start.2
  46.3 0.9 copy-start.6
  49.4 11.3 %collective-permute-start.9 = (bf16[512,256]{1,0:T(8,128)(2,1)S(1)}, bf16[512,256]{1,0:T(8,128)(2,1)S(1)}, u32[]{:S(2)}, u32[]{:S(2)}) collective-permute-start(bf16[512,256]{1,0:T(8,128)(2,1)S(1)} %get-tuple-element.73), channel_id=1, source_target_pairs={{0,64},{8,72},{16,80},{24,88},{32,96},{40,104},{48,112},{56,120},{... | collective-permute-start | bytes 786440 | tf_op jit(solution)/shard_map/ppermute | solution.py:43
  54.9 18.5 %collective-permute-start.14 = (bf16[256,1024]{1,0:T(8,128)(2,1)}, bf16[256,1024]{1,0:T(8,128)(2,1)S(1)}, u32[]{:S(2)}, u32[]{:S(2)}) collective-permute-start(bf16[256,1024]{1,0:T(8,128)(2,1)} %collective-permute-done.7.refs_3_), channel_id=1, source_target_pairs={{0,2},{1,3},{2,4},{3,5},{4,6},{5,7},{6,0},{7,1},{8,10},{9,11},{10,... | collective-permute-start | bytes 1572872 | tf_op jit(solution)/shard_map/ppermute | solution.py:29
  60.8 12.6 %collective-permute-start.15 = (bf16[256,1024]{1,0:T(8,128)(2,1)S(1)}, bf16[256,1024]{1,0:T(8,128)(2,1)S(1)}, u32[]{:S(2)}, u32[]{:S(2)}) collective-permute-start(bf16[256,1024]{1,0:T(8,128)(2,1)S(1)} %collective-permute-done.11.refs_3_), channel_id=1, source_target_pairs={{0,6},{1,7},{2,0},{3,1},{4,2},{5,3},{6,4},{7,5},{8,14},{9,15},{10,... | collective-permute-start | bytes 1572872 | tf_op jit(solution)/shard_map/ppermute | solution.py:29
  62.5 17.2 %copy-start.9 = (bf16[640,256]{1,0:T(8,128)(2,1)}, bf16[640,256]{1,0:T(8,128)(2,1)S(1)}, u32[]{:S(2)}) copy-start(bf16[640,256]{1,0:T(8,128)(2,1)S(1)} %pad_maximum_fusion.5.refs_0_) | copy-start | bytes 983044
  62.6 17.1 %collective-permute-start.13 = (bf16[640,256]{1,0:T(8,128)(2,1)S(1)}, bf16[640,256]{1,0:T(8,128)(2,1)S(1)}, u32[]{:S(2)}, u32[]{:S(2)}) collective-permute-start(bf16[640,256]{1,0:T(8,128)(2,1)S(1)} %get-tuple-element.82), channel_id=1, source_target_pairs={{0,16},{8,24},{16,32},{24,40},{32,48},{40,56},{48,0},{56,8},{64,80... | collective-permute-start | bytes 983048 | tf_op jit(solution)/shard_map/ppermute | solution.py:43
  64.5 15.2 %collective-permute-start.17 = (bf16[640,256]{1,0:T(8,128)(2,1)S(1)}, bf16[640,256]{1,0:T(8,128)(2,1)S(1)}, u32[]{:S(2)}, u32[]{:S(2)}) collective-permute-start(bf16[640,256]{1,0:T(8,128)(2,1)S(1)} %get-tuple-element.95), channel_id=1, source_target_pairs={{0,32},{8,40},{16,48},{24,56},{32,0},{40,8},{48,16},{56,24},{64,96... | collective-permute-start | bytes 983048 | tf_op jit(solution)/shard_map/ppermute | solution.py:43
  67.8 11.9 %collective-permute-start.18 = (bf16[640,256]{1,0:T(8,128)(2,1)S(1)}, bf16[640,256]{1,0:T(8,128)(2,1)S(1)}, u32[]{:S(2)}, u32[]{:S(2)}) collective-permute-start(bf16[640,256]{1,0:T(8,128)(2,1)S(1)} %get-tuple-element.96), channel_id=1, source_target_pairs={{0,48},{8,56},{16,0},{24,8},{32,16},{40,24},{48,32},{56,40},{64,11... | collective-permute-start | bytes 983048 | tf_op jit(solution)/shard_map/ppermute | solution.py:43
  68.7 4.7 %copy-start.7 = (f32[256,128]{1,0:T(8,128)S(1)}, f32[256,128]{1,0:T(8,128)}, u32[]{:S(2)}) copy-start(f32[256,128]{1,0:T(8,128)} %get-tuple-element.87.refs_8_) | copy-start | bytes 393220
  68.7 4.7 %copy-start.8 = (f32[256,128]{1,0:T(8,128)S(1)}, f32[256,128]{1,0:T(8,128)}, u32[]{:S(2)}) copy-start(f32[256,128]{1,0:T(8,128)} %get-tuple-element.88.refs_9_) | copy-start | bytes 393220
  76.7 23.5 %copy-start.5 = (bf16[320,256]{1,0:T(8,128)(2,1)}, bf16[320,256]{1,0:T(8,128)(2,1)S(1)}, u32[]{:S(2)}) copy-start(bf16[320,256]{1,0:T(8,128)(2,1)S(1)} %get-tuple-element.97.refs_5_) | copy-start | bytes 491524
  76.7 16.1 %collective-permute-start.16 = (bf16[320,256]{1,0:T(8,128)(2,1)S(1)}, bf16[320,256]{1,0:T(8,128)(2,1)S(1)}, u32[]{:S(2)}, u32[]{:S(2)}) collective-permute-start(bf16[320,256]{1,0:T(8,128)(2,1)S(1)} %get-tuple-element.89), channel_id=1, source_target_pairs={{0,64},{8,72},{16,80},{24,88},{32,96},{40,104},{48,112},{56,120},{... | collective-permute-start | bytes 491528 | tf_op jit(solution)/shard_map/ppermute | solution.py:43
  79.7 20.5 %copy-start.10 = (bf16[640,256]{1,0:T(8,128)(2,1)}, bf16[640,256]{1,0:T(8,128)(2,1)S(1)}, u32[]{:S(2)}) copy-start(bf16[640,256]{1,0:T(8,128)(2,1)S(1)} %collective-permute-done.13.refs_1_) | copy-start | bytes 983044
  79.7 20.5 %copy-start.11 = (bf16[640,256]{1,0:T(8,128)(2,1)}, bf16[640,256]{1,0:T(8,128)(2,1)S(1)}, u32[]{:S(2)}) copy-start(bf16[640,256]{1,0:T(8,128)(2,1)S(1)} %collective-permute-done.17.refs_2_) | copy-start | bytes 983044
  79.7 20.4 %copy-start.12 = (bf16[640,256]{1,0:T(8,128)(2,1)}, bf16[640,256]{1,0:T(8,128)(2,1)S(1)}, u32[]{:S(2)}) copy-start(bf16[640,256]{1,0:T(8,128)(2,1)S(1)} %collective-permute-done.18.refs_3_) | copy-start | bytes 983044
  79.8 36.7 %collective-permute-start.19 = (bf16[2560,256]{1,0:T(8,128)(2,1)S(1)}, bf16[2560,256]{1,0:T(8,128)(2,1)}, u32[]{:S(2)}, u32[]{:S(2)}) collective-permute-start(bf16[2560,256]{1,0:T(8,128)(2,1)S(1)} %pad_maximum_fusion), channel_id=1, source_target_pairs={{0,8},{8,0},{16,24},{24,16},{32,40},{40,32},{48,56},{56,48},{64,72... | collective-permute-start | bytes 3932168 | tf_op jit(solution)/shard_map/ppermute | solution.py:55
  86.1 10.3 %collective-permute-start.23 = (bf16[320,256]{1,0:T(8,128)(2,1)S(1)}, bf16[320,256]{1,0:T(8,128)(2,1)S(1)}, u32[]{:S(2)}, u32[]{:S(2)}) collective-permute-start(bf16[320,256]{1,0:T(8,128)(2,1)S(1)} %get-tuple-element.102), channel_id=1, source_target_pairs={{0,80},{8,88},{16,96},{24,104},{32,112},{40,120},{48,64},{56,72},{... | collective-permute-start | bytes 491528 | tf_op jit(solution)/shard_map/ppermute | solution.py:43
  87.3 11.5 %collective-permute-start.24 = (bf16[320,256]{1,0:T(8,128)(2,1)S(1)}, bf16[320,256]{1,0:T(8,128)(2,1)S(1)}, u32[]{:S(2)}, u32[]{:S(2)}) collective-permute-start(bf16[320,256]{1,0:T(8,128)(2,1)S(1)} %get-tuple-element.103), channel_id=1, source_target_pairs={{0,96},{8,104},{16,112},{24,120},{32,64},{40,72},{48,80},{56,88},{... | collective-permute-start | bytes 491528 | tf_op jit(solution)/shard_map/ppermute | solution.py:43
  89.5 10.6 %collective-permute-start.25 = (bf16[320,256]{1,0:T(8,128)(2,1)S(1)}, bf16[320,256]{1,0:T(8,128)(2,1)S(1)}, u32[]{:S(2)}, u32[]{:S(2)}) collective-permute-start(bf16[320,256]{1,0:T(8,128)(2,1)S(1)} %get-tuple-element.104), channel_id=1, source_target_pairs={{0,112},{8,120},{16,64},{24,72},{32,80},{40,88},{48,96},{56,104},{... | collective-permute-start | bytes 491528 | tf_op jit(solution)/shard_map/ppermute | solution.py:43
  92.8 23.7 %copy-start.13 = (bf16[320,256]{1,0:T(8,128)(2,1)}, bf16[320,256]{1,0:T(8,128)(2,1)S(1)}, u32[]{:S(2)}) copy-start(bf16[320,256]{1,0:T(8,128)(2,1)S(1)} %collective-permute-done.16.refs_9_) | copy-start | bytes 491524
  96.4 20.1 %copy-start.14 = (bf16[320,256]{1,0:T(8,128)(2,1)}, bf16[320,256]{1,0:T(8,128)(2,1)S(1)}, u32[]{:S(2)}) copy-start(bf16[320,256]{1,0:T(8,128)(2,1)S(1)} %collective-permute-done.23.refs_10_) | copy-start | bytes 491524
  98.8 17.8 %copy-start.15 = (bf16[320,256]{1,0:T(8,128)(2,1)}, bf16[320,256]{1,0:T(8,128)(2,1)S(1)}, u32[]{:S(2)}) copy-start(bf16[320,256]{1,0:T(8,128)(2,1)S(1)} %collective-permute-done.24.refs_11_) | copy-start | bytes 491524
  100.1 16.4 %copy-start.16 = (bf16[320,256]{1,0:T(8,128)(2,1)}, bf16[320,256]{1,0:T(8,128)(2,1)S(1)}, u32[]{:S(2)}) copy-start(bf16[320,256]{1,0:T(8,128)(2,1)S(1)} %collective-permute-done.25.refs_12_) | copy-start | bytes 491524
  100.2 16.4 %collective-permute-start.27 = (bf16[1600,256]{1,0:T(8,128)(2,1)S(1)}, bf16[1600,256]{1,0:T(8,128)(2,1)}, u32[]{:S(2)}, u32[]{:S(2)}) collective-permute-start(bf16[1600,256]{1,0:T(8,128)(2,1)S(1)} %constant_dynamic-update-slice_fusion), channel_id=1, source_target_pairs={{0,8},{8,0},{16,24},{24,16},{32,40},{40,32},{48,56},{56,48},{64,72... | collective-permute-start | bytes 2457608 | tf_op jit(solution)/shard_map/ppermute | solution.py:55
  101.2 7.6 %collective-permute-start.20 = (bf16[320,256]{1,0:T(8,128)(2,1)S(1)}, bf16[320,256]{1,0:T(8,128)(2,1)S(1)}, u32[]{:S(2)}, u32[]{:S(2)}) collective-permute-start(bf16[320,256]{1,0:T(8,128)(2,1)S(1)} %get-tuple-element.98), channel_id=1, source_target_pairs={{0,16},{8,24},{16,32},{24,40},{32,48},{40,56},{48,0},{56,8},{64,80... | collective-permute-start | bytes 491528 | tf_op jit(solution)/shard_map/ppermute | solution.py:43
  104.1 10.1 %collective-permute-start.21 = (bf16[320,256]{1,0:T(8,128)(2,1)S(1)}, bf16[320,256]{1,0:T(8,128)(2,1)S(1)}, u32[]{:S(2)}, u32[]{:S(2)}) collective-permute-start(bf16[320,256]{1,0:T(8,128)(2,1)S(1)} %get-tuple-element.99), channel_id=1, source_target_pairs={{0,32},{8,40},{16,48},{24,56},{32,0},{40,8},{48,16},{56,24},{64,96... | collective-permute-start | bytes 491528 | tf_op jit(solution)/shard_map/ppermute | solution.py:43
  106.2 8.0 %collective-permute-start.22 = (bf16[320,256]{1,0:T(8,128)(2,1)S(1)}, bf16[320,256]{1,0:T(8,128)(2,1)S(1)}, u32[]{:S(2)}, u32[]{:S(2)}) collective-permute-start(bf16[320,256]{1,0:T(8,128)(2,1)S(1)} %get-tuple-element.100), channel_id=1, source_target_pairs={{0,48},{8,56},{16,0},{24,8},{32,16},{40,24},{48,32},{56,40},{64,11... | collective-permute-start | bytes 491528 | tf_op jit(solution)/shard_map/ppermute | solution.py:43
  108.8 7.8 %copy-start.17 = (bf16[320,256]{1,0:T(8,128)(2,1)}, bf16[320,256]{1,0:T(8,128)(2,1)S(1)}, u32[]{:S(2)}) copy-start(bf16[320,256]{1,0:T(8,128)(2,1)S(1)} %collective-permute-done.20.refs_6_) | copy-start | bytes 491524
  114.2 2.3 %copy-start.18 = (bf16[320,256]{1,0:T(8,128)(2,1)}, bf16[320,256]{1,0:T(8,128)(2,1)S(1)}, u32[]{:S(2)}) copy-start(bf16[320,256]{1,0:T(8,128)(2,1)S(1)} %collective-permute-done.21.refs_7_) | copy-start | bytes 491524
  114.2 2.3 %copy-start.19 = (bf16[320,256]{1,0:T(8,128)(2,1)}, bf16[320,256]{1,0:T(8,128)(2,1)S(1)}, u32[]{:S(2)}) copy-start(bf16[320,256]{1,0:T(8,128)(2,1)S(1)} %collective-permute-done.22.refs_8_) | copy-start | bytes 491524
  114.3 2.2 %collective-permute-start.26 = (bf16[960,256]{1,0:T(8,128)(2,1)S(1)}, bf16[960,256]{1,0:T(8,128)(2,1)S(1)}, u32[]{:S(2)}, u32[]{:S(2)}) collective-permute-start(bf16[960,256]{1,0:T(8,128)(2,1)S(1)} %pad_maximum_fusion.1), channel_id=1, source_target_pairs={{0,8},{8,0},{16,24},{24,16},{32,40},{40,32},{48,56},{56,48},{64,72... | collective-permute-start | bytes 1474568 | tf_op jit(solution)/shard_map/ppermute | solution.py:55
  116.5 0.8 copy-start.20
